TPU v7x, 32 devices: a whole 2x2x4 slice. The times are simulated.
32 devices in a mesh: clip: 8 (over z, core), seq: 4 (over y, x).
Axes of the slice: x: 2, y: 2, z: 4, core: 2. Of those that a mesh axis runs over, the one named last changes fastest.
Arguments:
- video_latents: bfloat16 [8, 16, 256, 1152], P('clip', 'seq'), may hold values from -6 to 6
- conditioning: float32 [8, 1152], P('clip'), may hold values from -6 to 6
- ada_weight: bfloat16 [2, 1152, 6912], P(None, None, ('clip', 'seq')), may hold values from -0.1875 to 0.1875
- ada_bias: float32 [2, 6912], P(None, ('clip', 'seq')), may hold values from -3 to 3
- qkv_weight: bfloat16 [2, 1152, 3456], P(None, 'clip', 'seq'), may hold values from -1 to 1
- out_weight: bfloat16 [2, 1152, 1152], P(None, 'clip', 'seq'), may hold values from -0.75 to 0.75
- up_weight: bfloat16 [2, 1152, 4608], P(None, 'clip', 'seq'), may hold values from -0.1875 to 0.1875
- down_weight: bfloat16 [2, 4608, 1152], P(None, 'clip', 'seq'), may hold values from -0.09375 to 0.09375
- attention_bias: float32 [2, 3, 1152], replicated, may hold values from -3 to 3
- up_bias: float32 [2, 4608], replicated, may hold values from -3 to 3
- down_bias: float32 [2, 1152], replicated, may hold values from -3 to 3
- cotangent: bfloat16 [8, 16, 256, 1152], P('clip', 'seq'), may hold values from -6 to 6
Outputs:
- output_latents: bfloat16 [8, 16, 256, 1152], P('clip', 'seq')
- latents_grad: float32 [8, 16, 256, 1152], P('clip', 'seq')
- conditioning_grad: float32 [8, 1152], P('clip')
- ada_weight_grad: float32 [2, 1152, 6912], P(None, None, ('clip', 'seq'))
- ada_bias_grad: float32 [2, 6912], P(None, ('clip', 'seq'))
- qkv_weight_grad: float32 [2, 1152, 3456], P(None, 'clip', 'seq')
- out_weight_grad: float32 [2, 1152, 1152], P(None, 'clip', 'seq')
- up_weight_grad: float32 [2, 1152, 4608], P(None, 'clip', 'seq')
- down_weight_grad: float32 [2, 4608, 1152], P(None, 'clip', 'seq')
- attention_bias_grad: float32 [2, 3, 1152], replicated
- up_bias_grad: float32 [2, 4608], replicated
- down_bias_grad: float32 [2, 1152], replicated
- clipped_qkv: float32 [2, 1152, 3456], P(None, 'clip', 'seq')
- logit_peak: float32 [2, 16], replicated
All inputs are finite; a program needn't handle non-finite values.
Results may differ from a plain program's by a relative error of at most 0.023.
Values may be sent and summed in bfloat16 or wider, within the bound.
No kernel may reach another device: no remote copies, remote signals or barrier semaphores. Data moves between devices by JAX's collectives and lax.ppermute only.
A program may use at most 512 MiB of HBM per device.

v0:
```python
from functools import partial

import jax
import jax.numpy as jnp
from jax import lax
from jax.sharding import PartitionSpec as P

HEADS = 16


clip_limit = 8.0
spatial_forms = ("cabhe,cakhe->cahbk", "cahbk,cakhe->cabhe", "cahbk,cabhe->cakhe")
temporal_forms = ("cabhe,ckbhe->cbhak", "cbhak,ckbhe->cabhe", "cbhak,cabhe->ckbhe")


def normalize(stream):
    centred = stream - jnp.mean(stream, axis=-1, keepdims=True)
    return centred * lax.rsqrt(jnp.mean(centred * centred, axis=-1, keepdims=True) + 1e-06)


def modulated(stream, shift, stretch):
    return normalize(stream) * (1.0 + stretch) + shift


def layer_forward(stream, modulation, weights, biases, forms):
    qkv_full, out_full, up_full, down_full = weights
    attention_b, up_b, down_b = biases
    model_width = stream.shape[-1]
    token_shape = stream.shape[:-1]
    pieces = [
        modulation[:, None, None, slot * model_width : (slot + 1) * model_width]
        for slot in range(6)
    ]
    hidden = modulated(stream, pieces[0], pieces[1]).astype(jnp.bfloat16)
    qkv_bias = jnp.concatenate([attention_b[0], jnp.zeros_like(attention_b[0]), attention_b[1]])
    projected = (
        jnp.dot(hidden.reshape(-1, model_width), qkv_full, preferred_element_type=jnp.float32)
        + qkv_bias
    )
    heads_shape = token_shape + (HEADS, model_width // HEADS)
    query_heads = projected[:, :model_width].astype(jnp.bfloat16).reshape(heads_shape)
    key_heads = (
        projected[:, model_width : 2 * model_width].astype(jnp.bfloat16).reshape(heads_shape)
    )
    value_heads = projected[:, 2 * model_width :].astype(jnp.bfloat16).reshape(heads_shape)
    score_scale = (model_width // HEADS) ** (-0.5)
    scores = (
        jnp.einsum(forms[0], query_heads, key_heads, preferred_element_type=jnp.float32)
        * score_scale
    )
    head_peak = jnp.max(scores, axis=(0, 1, 3, 4))
    row_top = jnp.max(scores, axis=-1, keepdims=True)
    exponent = jnp.exp(scores - row_top)
    row_total = jnp.sum(exponent, axis=-1, keepdims=True)
    probs_low = (exponent / row_total).astype(jnp.bfloat16)
    log_total = row_top + jnp.log(row_total)
    attended = jnp.einsum(forms[1], probs_low, value_heads, preferred_element_type=jnp.float32)
    attended = attended.astype(jnp.bfloat16).reshape(-1, model_width)
    branch = jnp.dot(attended, out_full, preferred_element_type=jnp.float32) + attention_b[2]
    branch = branch.reshape(token_shape + (model_width,))
    middle = stream + pieces[2] * branch
    hidden_two = (
        modulated(middle, pieces[3], pieces[4]).astype(jnp.bfloat16).reshape(-1, model_width)
    )
    inner_pre = jnp.dot(hidden_two, up_full, preferred_element_type=jnp.float32) + up_b
    active = jax.nn.gelu(inner_pre, approximate=True).astype(jnp.bfloat16)
    update = (jnp.dot(active, down_full, preferred_element_type=jnp.float32) + down_b).reshape(
        token_shape + (model_width,)
    )
    result = middle + pieces[5] * update
    kept = (
        stream,
        hidden,
        query_heads,
        key_heads,
        value_heads,
        log_total,
        attended,
        branch,
        middle,
        hidden_two,
        inner_pre,
        active,
        update,
    )
    return (result, kept, head_peak)


def layer_backward(grad_out, kept, modulation, weights, forms):
    (
        stream,
        hidden,
        query_heads,
        key_heads,
        value_heads,
        log_total,
        attended,
        branch,
        middle,
        hidden_two,
        inner_pre,
        active,
        update,
    ) = kept
    qkv_full, out_full, up_full, down_full = weights
    model_width = stream.shape[-1]
    token_shape = stream.shape[:-1]
    clip_count = stream.shape[0]
    pieces = [
        modulation[:, None, None, slot * model_width : (slot + 1) * model_width]
        for slot in range(6)
    ]
    heads_shape = token_shape + (HEADS, model_width // HEADS)
    score_scale = (model_width // HEADS) ** (-0.5)
    grad_update = (pieces[5] * grad_out).astype(jnp.bfloat16).reshape(-1, model_width)
    gate_m_grad = jnp.sum(grad_out * update, axis=(1, 2))
    down_grad = jnp.einsum("nf,nd->fd", active, grad_update, preferred_element_type=jnp.float32)
    down_bias_grad = jnp.sum(grad_update.astype(jnp.float32), axis=0)
    active_grad = jnp.einsum(
        "nd,fd->nf", grad_update, down_full, preferred_element_type=jnp.float32
    )
    gelu_value, gelu_pull = jax.vjp(partial(jax.nn.gelu, approximate=True), inner_pre)
    inner_grad = gelu_pull(active_grad)[0].astype(jnp.bfloat16)
    up_grad = jnp.einsum("nd,nf->df", hidden_two, inner_grad, preferred_element_type=jnp.float32)
    up_bias_grad = jnp.sum(inner_grad.astype(jnp.float32), axis=0)
    hidden_two_grad = jnp.einsum(
        "nf,df->nd", inner_grad, up_full, preferred_element_type=jnp.float32
    )
    norm_value, norm_pull = jax.vjp(modulated, middle, pieces[3], pieces[4])
    middle_grad, shift_m_grad, scale_m_grad = norm_pull(
        hidden_two_grad.reshape(token_shape + (model_width,))
    )
    middle_grad = middle_grad + grad_out
    branch_grad = (pieces[2] * middle_grad).astype(jnp.bfloat16).reshape(-1, model_width)
    gate_a_grad = jnp.sum(middle_grad * branch, axis=(1, 2))
    out_grad = jnp.einsum("nd,ne->de", attended, branch_grad, preferred_element_type=jnp.float32)
    out_bias_grad = jnp.sum(branch_grad.astype(jnp.float32), axis=0)
    attended_grad = jnp.einsum(
        "ne,de->nd", branch_grad, out_full, preferred_element_type=jnp.float32
    )
    attended_grad = attended_grad.astype(jnp.bfloat16).reshape(heads_shape)
    scores = (
        jnp.einsum(forms[0], query_heads, key_heads, preferred_element_type=jnp.float32)
        * score_scale
    )
    probs = jnp.exp(scores - log_total)
    probs_grad = jnp.einsum(
        forms[0], attended_grad, value_heads, preferred_element_type=jnp.float32
    )
    value_grad = jnp.einsum(
        forms[2], probs.astype(jnp.bfloat16), attended_grad, preferred_element_type=jnp.float32
    )
    scores_grad = (
        probs * (probs_grad - jnp.sum(probs * probs_grad, axis=-1, keepdims=True))
    ).astype(jnp.bfloat16)
    query_grad = (
        jnp.einsum(forms[1], scores_grad, key_heads, preferred_element_type=jnp.float32)
        * score_scale
    )
    key_grad = (
        jnp.einsum(forms[2], scores_grad, query_heads, preferred_element_type=jnp.float32)
        * score_scale
    )
    stacked_grad = jnp.concatenate(
        [
            query_grad.reshape(-1, model_width),
            key_grad.reshape(-1, model_width),
            value_grad.reshape(-1, model_width),
        ],
        axis=1,
    ).astype(jnp.bfloat16)
    qkv_grad = jnp.einsum(
        "nd,ne->de",
        hidden.reshape(-1, model_width),
        stacked_grad,
        preferred_element_type=jnp.float32,
    )
    column_sums = jnp.sum(stacked_grad.astype(jnp.float32), axis=0)
    attention_bias_grad = jnp.stack(
        [column_sums[:model_width], column_sums[2 * model_width :], out_bias_grad]
    )
    hidden_grad = jnp.einsum(
        "ne,de->nd", stacked_grad, qkv_full, preferred_element_type=jnp.float32
    )
    first_value, first_pull = jax.vjp(modulated, stream, pieces[0], pieces[1])
    stream_grad, shift_a_grad, scale_a_grad = first_pull(
        hidden_grad.reshape(token_shape + (model_width,))
    )
    stream_grad = stream_grad + middle_grad
    members = (shift_a_grad, scale_a_grad, gate_a_grad, shift_m_grad, scale_m_grad, gate_m_grad)
    modulation_grad = jnp.concatenate(
        [member.reshape(clip_count, model_width) for member in members], axis=1
    )
    return (
        stream_grad,
        modulation_grad,
        (qkv_grad, out_grad, up_grad, down_grad),
        (attention_bias_grad, up_bias_grad, down_bias_grad),
    )


def on_device(
    video_latents,
    conditioning,
    ada_weight,
    ada_bias,
    qkv_weight,
    out_weight,
    up_weight,
    down_weight,
    attention_bias,
    up_bias,
    down_bias,
    cotangent,
):
    clip_rows = video_latents.shape[0]
    clip_start = lax.axis_index("clip") * clip_rows
    every_condition = lax.all_gather(conditioning, "clip", axis=0, tiled=True)
    squashed = jax.nn.silu(every_condition).astype(jnp.bfloat16)
    local_mods = (
        jnp.einsum("kd,ldc->lkc", squashed, ada_weight, preferred_element_type=jnp.float32)
        + ada_bias[:, None, :]
    )
    every_mod = lax.all_gather(local_mods, ("clip", "seq"), axis=2, tiled=True)
    modulation = lax.dynamic_slice_in_dim(every_mod, clip_start, clip_rows, axis=1)

    def fetch(layer):
        row_full = (
            lax.all_gather(qkv_weight[layer], "clip", axis=0, tiled=True),
            lax.all_gather(out_weight[layer], "clip", axis=0, tiled=True),
            lax.all_gather(up_weight[layer], "clip", axis=0, tiled=True),
            lax.all_gather(down_weight[layer], "clip", axis=0, tiled=True),
        )
        return (
            lax.all_gather(row_full[0], "seq", axis=1, tiled=True),
            lax.all_gather(row_full[1], "seq", axis=1, tiled=True),
            lax.all_gather(row_full[2], "seq", axis=1, tiled=True),
            lax.all_gather(row_full[3], "seq", axis=1, tiled=True),
        )

    def to_places(tokens_block):
        return lax.all_to_all(tokens_block, "seq", split_axis=2, concat_axis=1, tiled=True)

    def to_frames(tokens_block):
        return lax.all_to_all(tokens_block, "seq", split_axis=1, concat_axis=2, tiled=True)

    def global_peak(local_peak):
        return lax.pmax(local_peak, ("clip", "seq"))

    def shed(gradients):
        column_part = (
            lax.psum_scatter(
                gradients[0].astype(jnp.bfloat16), "seq", scatter_dimension=1, tiled=True
            ).astype(jnp.float32),
            lax.psum_scatter(
                gradients[1].astype(jnp.bfloat16), "seq", scatter_dimension=1, tiled=True
            ).astype(jnp.float32),
            lax.psum_scatter(
                gradients[2].astype(jnp.bfloat16), "seq", scatter_dimension=1, tiled=True
            ).astype(jnp.float32),
            lax.psum_scatter(
                gradients[3].astype(jnp.bfloat16), "seq", scatter_dimension=1, tiled=True
            ).astype(jnp.float32),
        )
        return (
            lax.psum_scatter(
                column_part[0].astype(jnp.bfloat16), "clip", scatter_dimension=0, tiled=True
            ).astype(jnp.float32),
            lax.psum_scatter(
                column_part[1].astype(jnp.bfloat16), "clip", scatter_dimension=0, tiled=True
            ).astype(jnp.float32),
            lax.psum_scatter(
                column_part[2].astype(jnp.bfloat16), "clip", scatter_dimension=0, tiled=True
            ).astype(jnp.float32),
            lax.psum_scatter(
                column_part[3].astype(jnp.bfloat16), "clip", scatter_dimension=0, tiled=True
            ).astype(jnp.float32),
        )

    def layer_biases(layer):
        return (attention_bias[layer], up_bias[layer], down_bias[layer])

    first_weights = fetch(0)
    first_out, first_kept, first_peak = layer_forward(
        video_latents.astype(jnp.float32),
        modulation[0],
        first_weights,
        layer_biases(0),
        spatial_forms,
    )
    first_peak = global_peak(first_peak)
    second_in = to_places(first_out.astype(jnp.bfloat16)).astype(jnp.float32)
    second_weights = fetch(1)
    second_out, second_kept, second_peak = layer_forward(
        second_in, modulation[1], second_weights, layer_biases(1), temporal_forms
    )
    second_peak = global_peak(second_peak)
    output_latents = to_frames(second_out.astype(jnp.bfloat16))
    second_grad_out = to_places(cotangent).astype(jnp.float32)
    second_back = fetch(1)
    second_grad_in, second_mod_grad, second_weight_grads, second_bias_grads = layer_backward(
        second_grad_out, second_kept, modulation[1], second_back, temporal_forms
    )
    second_shed = shed(second_weight_grads)
    first_grad_out = to_frames(second_grad_in.astype(jnp.bfloat16)).astype(jnp.float32)
    first_back = fetch(0)
    latents_grad, first_mod_grad, first_weight_grads, first_bias_grads = layer_backward(
        first_grad_out, first_kept, modulation[0], first_back, spatial_forms
    )
    first_shed = shed(first_weight_grads)
    every_count = every_condition.shape[0]
    mod_grads = jnp.stack([first_mod_grad, second_mod_grad])
    placed = lax.dynamic_update_slice_in_dim(
        jnp.zeros((2, every_count, mod_grads.shape[2]), jnp.float32), mod_grads, clip_start, axis=1
    )
    own_mod_grad = lax.psum_scatter(placed, ("clip", "seq"), scatter_dimension=2, tiled=True)
    ada_bias_grad = jnp.sum(own_mod_grad, axis=1)
    rounded_mod = own_mod_grad.astype(jnp.bfloat16)
    ada_weight_grad = jnp.einsum(
        "kd,lkc->ldc", squashed, rounded_mod, preferred_element_type=jnp.float32
    )
    squash_part = jnp.einsum(
        "lkc,ldc->kd", rounded_mod, ada_weight, preferred_element_type=jnp.float32
    )
    summed = lax.psum(
        (
            squash_part,
            jnp.stack([first_bias_grads[0], second_bias_grads[0]]),
            jnp.stack([first_bias_grads[1], second_bias_grads[1]]),
            jnp.stack([first_bias_grads[2], second_bias_grads[2]]),
        ),
        ("clip", "seq"),
    )
    own_squash = lax.dynamic_slice_in_dim(summed[0], clip_start, clip_rows, axis=0)
    silu_value, silu_pull = jax.vjp(jax.nn.silu, conditioning)
    conditioning_grad = silu_pull(own_squash)[0]
    logit_peak = jnp.stack([first_peak, second_peak])
    model_width = video_latents.shape[-1]
    own_columns = qkv_weight.shape[2]
    column_index = lax.axis_index("seq") * own_columns + jnp.arange(own_columns, dtype=jnp.int32)
    head_of = column_index % model_width // (model_width // HEADS)
    head_match = (head_of[:, None] == jnp.arange(HEADS, dtype=jnp.int32)[None, :]).astype(
        jnp.float32
    )
    roots = jnp.sqrt(clip_limit / jnp.maximum(logit_peak, clip_limit))
    column_roots = jnp.sum(roots[:, None, :] * head_match[None, :, :], axis=-1)
    column_scale = jnp.where(column_index[None, :] < 2 * model_width, column_roots, 1.0)
    clipped_qkv = qkv_weight.astype(jnp.float32) * column_scale[:, None, :]
    return (
        output_latents,
        latents_grad,
        conditioning_grad,
        ada_weight_grad,
        ada_bias_grad,
        jnp.stack([first_shed[0], second_shed[0]]),
        jnp.stack([first_shed[1], second_shed[1]]),
        jnp.stack([first_shed[2], second_shed[2]]),
        jnp.stack([first_shed[3], second_shed[3]]),
        summed[1],
        summed[2],
        summed[3],
        clipped_qkv,
        logit_peak,
    )


def solution(mesh):
    return jax.shard_map(
        on_device,
        mesh=mesh,
        in_specs=(
            P("clip", "seq", None, None),
            P("clip", None),
            P(None, None, ("clip", "seq")),
            P(None, ("clip", "seq")),
            P(None, "clip", "seq"),
            P(None, "clip", "seq"),
            P(None, "clip", "seq"),
            P(None, "clip", "seq"),
            P(),
            P(),
            P(),
            P("clip", "seq", None, None),
        ),
        out_specs=(
            P("clip", "seq", None, None),
            P("clip", "seq", None, None),
            P("clip", None),
            P(None, None, ("clip", "seq")),
            P(None, ("clip", "seq")),
            P(None, "clip", "seq"),
            P(None, "clip", "seq"),
            P(None, "clip", "seq"),
            P(None, "clip", "seq"),
            P(),
            P(),
            P(),
            P(None, "clip", "seq"),
            P(),
        ),
        check_vma=False,
    )
```

profile of v0, /device:TPU:0, one launch (start us, length us, event | category | flops | bytes accessed | tf_op | source)
XLA Modules:
  0.0 2761.4 jit_solution(15402832805448616372)
XLA Ops:
  17.7 24.1 all-gather.32.cloned.1.call-done
  46.0 19.1 all-gather.2
  66.3 14.7 all-gather.38.cloned.1.call-done
  81.1 73.3 %all-gather.42.cloned.1.call-done = bf16[1,4608,288]{2,0,1:T(2,128)(2,1)} async-done(((bf16[1,576,288]{2,0,1:T(2,128)(2,1)}), bf16[1,4608,288]{2,0,1:T(2,128)(2,1)}) %all-gather.42.cloned.1.call-update) | async-done | bytes 2654224 | tf_op jit(solution)/shard_map/all_gather | solution.py:232
  154.3 15.7 copy.322
  188.1 19.2 all-gather.10
  208.5 14.5 all-gather.52.cloned.1.call-done
  246.4 245.3 %all_gather.71 = f32[2,8,6912]{1,0,2:T(2,128)S(1)} all-gather(f32[2,8,216]{1,0,2:T(2,128)S(1)} %copy.310), channel_id=1, replica_groups=mesh['clip'=8,'seq'=4] {'clip','seq'}, dimensions={2}, use_global_device_ids=true | all-gather | bytes 456192 | tf_op jit(solution)/shard_map/all_gather | solution.py:224
  491.7 195.8 %dynamic-slice_reduce_fusion = (f32[6912]{0:T(1024)}, f32[6912]{0:T(1024)S(1)}) fusion(f32[2,8,6912]{1,0,2:T(2,128)S(1)} %all_gather.71, s32[]{:T(128)S(6)} %add.551, s32[]{:T(128)S(6)} %select_n.33), kind=kLoop, calls=%fused_computation.181 | loop fusion | bytes 110600 | tf_op jit(solution)/shard_map/slice | solution.py:295
  693.6 15.9 copy.335
  806.9 19.5 fusion.34
  826.5 22.3 fusion.61
  867.5 44.7 %all-to-all-done = bf16[1,4,256,1152]{3,1,0,2:T(4,128)(2,1)S(1)} async-done(((bf16[1,4,256,1152]{3,1,0,2:T(4,128)(2,1)}), bf16[1,4,256,1152]{3,1,0,2:T(4,128)(2,1)S(1)}, u32[]{:S(2)}, u32[]{:S(2)}) %all-to-all-start) | async-done | bytes 2359328 | tf_op jit(solution)/shard_map/all_to_all | solution.py:242
  1025.4 22.1 fusion.30
  1047.4 37.3 %all-gather.58.cloned.1.call-done = bf16[1,4608,1152]{1,2,0:T(8,128)(2,1)} async-done(((bf16[1,4608,288]{1,2,0:T(8,128)(2,1)}), bf16[1,4608,1152]{1,2,0:T(8,128)(2,1)}) %all-gather.58.cloned.1.call-update) | async-done | bytes 10616848 | tf_op jit(solution)/shard_map/all_gather | solution.py:238
  1084.7 30.5 %convert_reduce_fusion = (f32[4608]{0:T(1024)}, bf16[1024,4608]{1,0:T(8,128)(2,1)}) fusion(f32[1024,4608]{1,0:T(8,128)} %fusion.30, f32[4608]{0:T(1024)S(1)} %copy-done.99, bf16[1024,1152]{1,0:T(8,128)(2,1)} %fusion.79, bf16[1,4608,1152]{1,2,0:T(8,128)(2,1)} %all-gather.58.cloned.1.call-done), kind=kOutput, calls=%fused_computation.22 | convolution fusion | flops 10980159488 | bytes 41324544 | tf_op jit(solution)/shard_map/nd,fd->nf/dot_general | solution.py:119
  1115.2 15.0 fusion.28
  1141.1 25.2 fusion.80
  1194.0 16.1 multiply_reduce_fusion.3
  1266.6 15.8 fusion.41
  1316.3 20.1 all-to-all-done.3
  1341.1 29.8 %convert_reduce_fusion.1 = (f32[4608]{0:T(1024)}, bf16[1024,4608]{1,0:T(8,128)(2,1)}) fusion(f32[1024,4608]{1,0:T(8,128)} %fusion.34, f32[4608]{0:T(1024)S(1)} %copy-done.97, bf16[1024,1152]{1,0:T(8,128)(2,1)S(1)} %get-tuple-element.183, bf16[1,4608,1152]{1,2,0:T(8,128)(2,1)} %all-gather.44.cloned.1.call-done), kind=kOutput, calls=%fused_computation.23 | convolution fusion | flops 10980159488 | bytes 41324544 | tf_op jit(solution)/shard_map/nd,fd->nf/dot_general | solution.py:119
  1370.9 16.1 fusion.170
  1460.5 16.3 fusion.169
  1500.9 14.8 convolution_convert_fusion.5
  1532.6 18.6 convolution_convert_fusion
  1552.9 18.5 convolution_convert_fusion.1
  1572.1 18.4 convolution_convert_fusion.2
  1590.5 15.3 copy.388
  1607.5 17.2 convolution_convert_fusion.3
  1624.7 15.4 copy.386
  1659.3 40.5 %reduce-scatter.38.cloned.1.call-done = bf16[1152,288]{0,1:T(8,128)(2,1)} async-done(((bf16[1152,1152]{0,1:T(8,128)(2,1)}), bf16[1152,288]{0,1:T(8,128)(2,1)}) %reduce-scatter.38.cloned.1.call-update) | async-done | bytes 663568 | tf_op jit(solution)/shard_map/reduce_scatter | solution.py:255
  1702.2 84.2 %reduce-scatter.36.cloned.1.call-done = bf16[1152,864]{0,1:T(8,128)(2,1)} async-done(((bf16[1152,3456]{0,1:T(8,128)(2,1)}), bf16[1152,864]{0,1:T(8,128)(2,1)}) %reduce-scatter.36.cloned.1.call-update) | async-done | bytes 1990672 | tf_op jit(solution)/shard_map/reduce_scatter | solution.py:252
  1790.5 82.2 %reduce-scatter.34.cloned.1.call-done = bf16[1152,864]{0,1:T(8,128)(2,1)} async-done(((bf16[1152,3456]{0,1:T(8,128)(2,1)}), bf16[1152,864]{0,1:T(8,128)(2,1)}) %reduce-scatter.34.cloned.1.call-update) | async-done | bytes 1990672 | tf_op jit(solution)/shard_map/reduce_scatter | solution.py:252
  1876.9 103.8 %reduce-scatter.48.cloned.1.call-done = bf16[4608,288]{0,1:T(8,128)(2,1)} async-done(((bf16[4608,1152]{0,1:T(8,128)(2,1)}), bf16[4608,288]{0,1:T(8,128)(2,1)}) %reduce-scatter.48.cloned.1.call-update) | async-done | bytes 2654224 | tf_op jit(solution)/shard_map/reduce_scatter | solution.py:261
  1985.4 103.3 %reduce-scatter.46.cloned.1.call-done = bf16[4608,288]{0,1:T(8,128)(2,1)} async-done(((bf16[4608,1152]{0,1:T(8,128)(2,1)}), bf16[4608,288]{0,1:T(8,128)(2,1)}) %reduce-scatter.46.cloned.1.call-update) | async-done | bytes 2654224 | tf_op jit(solution)/shard_map/reduce_scatter | solution.py:261
  2093.5 103.3 %reduce-scatter.60.cloned.1.call-done = bf16[1152,1152]{1,0:T(8,128)(2,1)} async-done(((bf16[4608,1152]{1,0:T(8,128)(2,1)}), bf16[1152,1152]{1,0:T(8,128)(2,1)}) %reduce-scatter.60.cloned.1.call-update) | async-done | bytes 2654224
  2202.1 102.7 %reduce-scatter.58.cloned.1.call-done = bf16[1152,1152]{1,0:T(8,128)(2,1)} async-done(((bf16[4608,1152]{1,0:T(8,128)(2,1)}), bf16[1152,1152]{1,0:T(8,128)(2,1)}) %reduce-scatter.58.cloned.1.call-update) | async-done | bytes 2654224
  2313.8 62.4 %all-reduce.2 = (f32[1,16]{1,0:T(1,128)S(1)}, f32[1,16]{1,0:T(1,128)S(1)}) all-reduce(f32[1,16]{1,0:T(1,128)S(1)} %bitcast.396, f32[1,16]{1,0:T(1,128)S(1)} %bitcast.395), channel_id=1, replica_groups=mesh['clip'=8,'seq'=4] {'clip','seq'}, use_global_device_ids=true, to_apply=%region_67.68 | all-reduce | flops 32 | bytes 256 | tf_op jit(solution)/shard_map/pmax | solution.py:248
  2384.6 58.4 %all-reduce.8.cloned.1.call-done = (f32[8,1152]{1,0:T(8,128)}, f32[2,3,1152]{2,1,0:T(4,128)}, f32[2,4608]{1,0:T(2,128)}, f32[2,1152]{1,0:T(2,128)}) async-done(((f32[8,1152]{1,0:T(8,128)}, f32[2,3,1152]{2,1,0:T(4,128)}, f32[2,4608]{1,0:T(2,128)}, f32[2,1152]{1,0:T(2,128)}), (f32[8,1152]{1,0:T(8,128)}, f32[2,3,1152]{2,1,0:T(4,128)}, f32[2,4608]{1,0:T(2,128)}, ...) | async-done | bytes 110608 | tf_op jit(solution)/shard_map/psum | solution.py:325
  2445.8 32.1 %reduce-scatter.56.cloned.1.call-done = bf16[144,288]{1,0:T(8,128)(2,1)} async-done(((bf16[1152,288]{1,0:T(8,128)(2,1)}), bf16[144,288]{1,0:T(8,128)(2,1)}) %reduce-scatter.56.cloned.1.call-update) | async-done | bytes 82960
  2478.9 31.9 %reduce-scatter.54.cloned.1.call-done = bf16[144,288]{1,0:T(8,128)(2,1)} async-done(((bf16[1152,288]{1,0:T(8,128)(2,1)}), bf16[144,288]{1,0:T(8,128)(2,1)}) %reduce-scatter.54.cloned.1.call-update) | async-done | bytes 82960
  2512.9 34.2 %reduce-scatter.52.cloned.1.call-done = bf16[144,864]{1,0:T(8,128)(2,1)} async-done(((bf16[1152,864]{1,0:T(8,128)(2,1)}), bf16[144,864]{1,0:T(8,128)(2,1)}) %reduce-scatter.52.cloned.1.call-update) | async-done | bytes 248848
  2548.3 35.6 %reduce-scatter.50.cloned.1.call-done = bf16[144,864]{1,0:T(8,128)(2,1)} async-done(((bf16[1152,864]{1,0:T(8,128)(2,1)}), bf16[144,864]{1,0:T(8,128)(2,1)}) %reduce-scatter.50.cloned.1.call-update) | async-done | bytes 248848
  2588.5 40.3 %reduce-scatter.64.cloned.1.call-done = bf16[576,288]{1,0:T(8,128)(2,1)} async-done(((bf16[4608,288]{1,0:T(8,128)(2,1)}), bf16[576,288]{1,0:T(8,128)(2,1)}) %reduce-scatter.64.cloned.1.call-update) | async-done | bytes 331792
  2630.0 43.3 %reduce-scatter.62.cloned.1.call-done = bf16[576,288]{1,0:T(8,128)(2,1)} async-done(((bf16[4608,288]{1,0:T(8,128)(2,1)}), bf16[576,288]{1,0:T(8,128)(2,1)}) %reduce-scatter.62.cloned.1.call-update) | async-done | bytes 331792
  2675.7 36.3 %reduce-scatter.44.cloned.1.call-done = bf16[144,1152]{1,0:T(8,128)(2,1)} async-done(((bf16[1152,1152]{1,0:T(8,128)(2,1)}), bf16[144,1152]{1,0:T(8,128)(2,1)}) %reduce-scatter.44.cloned.1.call-update) | async-done | bytes 331792 | tf_op jit(solution)/shard_map/reduce_scatter | solution.py:272
  2712.0 39.2 %reduce-scatter.42.cloned.1.call-done = bf16[144,1152]{1,0:T(8,128)(2,1)} async-done(((bf16[1152,1152]{1,0:T(8,128)(2,1)}), bf16[144,1152]{1,0:T(8,128)(2,1)}) %reduce-scatter.42.cloned.1.call-update) | async-done | bytes 331792 | tf_op jit(solution)/shard_map/reduce_scatter | solution.py:272
  (571 shorter events, 624.6 us)
Async XLA Ops:
  7.2 238.7 %copy-start = (bf16[2,1152,216]{1,2,0:T(8,128)(2,1)S(1)}, bf16[2,1152,216]{1,2,0:T(8,128)(2,1)}, u32[]{:S(2)}) copy-start(bf16[2,1152,216]{1,2,0:T(8,128)(2,1)} %param.14) | copy-start | bytes 2985988
  7.2 34.6 %all-gather.32.cloned.1.call-start = ((), (), s32[]{:S(2)}) async-start(), calls=%async_computation.28 | async-start | bytes 2322432 | tf_op jit(solution)/shard_map/all_gather | solution.py:229
  9.2 71.8 %all-gather.38.cloned.1.call-start = ((), (), s32[]{:S(2)}) async-start(), calls=%async_computation.31 | async-start | bytes 2985984 | tf_op jit(solution)/shard_map/all_gather | solution.py:231
  11.3 143.1 %all-gather.42.cloned.1.call-start = ((), (), s32[]{:S(2)}) async-start(), calls=%async_computation.33 | async-start | bytes 7962624 | tf_op jit(solution)/shard_map/all_gather | solution.py:232
  14.5 169.4 %all-gather.46.cloned.1.call-start = ((), (), s32[]{:S(2)}) async-start(), calls=%async_computation.35 | async-start | bytes 2322432 | tf_op jit(solution)/shard_map/all_gather | solution.py:229
  15.0 207.9 %all-gather.52.cloned.1.call-start = ((), (), s32[]{:S(2)}) async-start(), calls=%async_computation.38 | async-start | bytes 2985984 | tf_op jit(solution)/shard_map/all_gather | solution.py:231
  15.6 678.0 %all-gather.56.cloned.1.call-start = ((), (), s32[]{:S(2)}) async-start(), calls=%async_computation.40 | async-start | bytes 7962624 | tf_op jit(solution)/shard_map/all_gather | solution.py:232
  17.6 692.0 %all-gather.34.cloned.1.call-start = ((), (), s32[]{:S(2)}) async-start(), calls=%async_computation.29 | async-start | bytes 9953280 | tf_op jit(solution)/shard_map/all_gather | solution.py:235
  45.9 749.5 %all-gather.36.cloned.1.call-start = ((), (), s32[]{:S(2)}) async-start(), calls=%async_computation.30 | async-start | bytes 3317760 | tf_op jit(solution)/shard_map/all_gather | solution.py:236
  66.3 740.6 %all-gather.40.cloned.1.call-start = ((), (), s32[]{:S(2)}) async-start(), calls=%async_computation.32 | async-start | bytes 13271040 | tf_op jit(solution)/shard_map/all_gather | solution.py:237
  81.0 745.4 %all-gather.44.cloned.1.call-start = ((), (), s32[]{:S(2)}) async-start(), calls=%async_computation.34 | async-start | bytes 13271040 | tf_op jit(solution)/shard_map/all_gather | solution.py:238
  170.1 755.3 %all-gather.48.cloned.1.call-start = ((), (), s32[]{:S(2)}) async-start(), calls=%async_computation.36 | async-start | bytes 9953280 | tf_op jit(solution)/shard_map/all_gather | solution.py:235
  188.0 817.1 %all-gather.50.cloned.1.call-start = ((), (), s32[]{:S(2)}) async-start(), calls=%async_computation.37 | async-start | bytes 3317760 | tf_op jit(solution)/shard_map/all_gather | solution.py:236
  208.4 816.9 %all-gather.54.cloned.1.call-start = ((), (), s32[]{:S(2)}) async-start(), calls=%async_computation.39 | async-start | bytes 13271040 | tf_op jit(solution)/shard_map/all_gather | solution.py:237
  226.3 630.1 %all-to-all-start.2 = ((bf16[1,4,256,1152]{3,1,0,2:T(4,128)(2,1)}), bf16[1,4,256,1152]{3,1,0,2:T(4,128)(2,1)}, u32[]{:S(2)}, u32[]{:S(2)}) async-start(bf16[1,4,256,1152]{3,1,0,2:T(4,128)(2,1)} %copy.339), calls=%async_computation.2 | async-start | bytes 4718592 | tf_op jit(solution)/shard_map/all_to_all | solution.py:242
  230.8 854.0 %all-gather.58.cloned.1.call-start = ((), (), s32[]{:S(2)}) async-start(), calls=%async_computation.41 | async-start | bytes 13271040 | tf_op jit(solution)/shard_map/all_gather | solution.py:238
  491.7 195.9 %copy-start.93 = (f32[2,3,1152]{2,0,1:T(2,128)S(1)}, f32[2,3,1152]{2,0,1:T(2,128)}, u32[]{:S(2)}) copy-start(f32[2,3,1152]{2,0,1:T(2,128)} %param.20) | copy-start | bytes 82948
  491.7 197.1 %copy-start.106 = (f32[2,1152]{1,0:T(2,128)S(1)}, f32[2,1152]{1,0:T(2,128)}, u32[]{:S(2)}) copy-start(f32[2,1152]{1,0:T(2,128)} %param.22) | copy-start | bytes 27652
  491.7 198.4 %copy-start.87 = (f32[2,4608]{1,0:T(2,128)S(1)}, f32[2,4608]{1,0:T(2,128)}, u32[]{:S(2)}) copy-start(f32[2,4608]{1,0:T(2,128)} %param.21) | copy-start | bytes 110596
  491.7 199.1 %copy-start.5 = (bf16[1,4,256,1152]{3,2,1,0:T(8,128)(2,1)S(1)}, bf16[1,4,256,1152]{3,2,1,0:T(8,128)(2,1)}, u32[]{:S(2)}) copy-start(bf16[1,4,256,1152]{3,2,1,0:T(8,128)(2,1)} %param.12) | copy-start | bytes 7077892
  856.3 55.8 %all-to-all-start = ((bf16[1,4,256,1152]{3,1,0,2:T(4,128)(2,1)}), bf16[1,4,256,1152]{3,1,0,2:T(4,128)(2,1)S(1)}, u32[]{:S(2)}, u32[]{:S(2)}) async-start(bf16[1,4,256,1152]{3,1,0,2:T(4,128)(2,1)} %copy.324), calls=%async_computation | async-start | bytes 4718592 | tf_op jit(solution)/shard_map/all_to_all | solution.py:242
  860.7 164.7 %copy-start.108 = (f32[1152]{0:T(1024)}, f32[1152]{0:T(1024)S(1)}, u32[]{:S(2)}) copy-start(f32[1152]{0:T(1024)S(1)} %get-tuple-element.132) | copy-start | bytes 13828
  860.7 430.6 %copy-start.64 = (f32[1152]{0:T(1024)}, f32[1152]{0:T(1024)S(1)}, u32[]{:S(2)}) copy-start(f32[1152]{0:T(1024)S(1)} %get-tuple-element.133) | copy-start | bytes 13828
  1018.0 115.6 %copy-start.104 = (f32[1024]{0:T(1024)}, f32[1024]{0:T(1024)S(1)}, u32[]{:S(2)}) copy-start(f32[1024]{0:T(1024)S(1)} %rsqrt.59) | copy-start | bytes 12292
  1025.3 107.1 %slice-start.6 = ((s8[4718592]{0:T(1024)(128)(4,1)}), s8[524288]{0:T(1024)(128)(4,1)S(1)}, s32[]{:S(2)}) async-start(s8[4718592]{0:T(1024)(128)(4,1)} %bitcast.345), calls=%async_computation.58 | async-start | bytes 1048576
  1304.6 31.7 %all-to-all-start.3 = ((bf16[1,16,64,1152]{3,2,0,1:T(8,128)(2,1)}), bf16[1,16,64,1152]{3,2,0,1:T(8,128)(2,1)S(1)}, u32[]{:S(2)}, u32[]{:S(2)}) async-start(bf16[1,16,64,1152]{3,2,0,1:T(8,128)(2,1)} %get-tuple-element.170), calls=%async_computation.3 | async-start | bytes 4718592 | tf_op jit(solution)/shard_map/all_to_all | solution.py:245
  1308.4 346.7 %all-reduce.6.cloned.1.call-start = ((), (), s32[]{:S(2)}) async-start(), calls=%async_computation.50 | async-start | bytes 884736
  1486.8 170.1 %reduce-scatter.40.cloned.1.call-start = ((), (), s32[]{:S(2)}) async-start(), calls=%async_computation.23 | async-start | bytes 3317760 | tf_op jit(solution)/shard_map/reduce_scatter | solution.py:255
  1494.2 205.6 %reduce-scatter.38.cloned.1.call-start = ((), (), s32[]{:S(2)}) async-start(), calls=%async_computation.22 | async-start | bytes 3317760 | tf_op jit(solution)/shard_map/reduce_scatter | solution.py:255
  1500.9 285.5 %reduce-scatter.36.cloned.1.call-start = ((), (), s32[]{:S(2)}) async-start(), calls=%async_computation.21 | async-start | bytes 9953280 | tf_op jit(solution)/shard_map/reduce_scatter | solution.py:252
  1515.8 357.0 %reduce-scatter.34.cloned.1.call-start = ((), (), s32[]{:S(2)}) async-start(), calls=%async_computation.20 | async-start | bytes 9953280 | tf_op jit(solution)/shard_map/reduce_scatter | solution.py:252
  1530.9 449.7 %reduce-scatter.48.cloned.1.call-start = ((), (), s32[]{:S(2)}) async-start(), calls=%async_computation.27 | async-start | bytes 13271040 | tf_op jit(solution)/shard_map/reduce_scatter | solution.py:261
  1551.2 537.5 %reduce-scatter.46.cloned.1.call-start = ((), (), s32[]{:S(2)}) async-start(), calls=%async_computation.26 | async-start | bytes 13271040 | tf_op jit(solution)/shard_map/reduce_scatter | solution.py:261
  1571.5 625.3 %reduce-scatter.60.cloned.1.call-start = ((), (), s32[]{:S(2)}) async-start(), calls=%async_computation.47 | async-start | bytes 13271040
  1605.8 699.0 %reduce-scatter.58.cloned.1.call-start = ((), (), s32[]{:S(2)}) async-start(), calls=%async_computation.46 | async-start | bytes 13271040
  1640.1 802.9 %all-reduce.8.cloned.1.call-start = ((), (), s32[]{:S(2)}) async-start(), calls=%async_computation.51 | async-start | bytes 239616 | tf_op jit(solution)/shard_map/psum | solution.py:325
  1656.8 821.1 %reduce-scatter.56.cloned.1.call-start = ((), (), s32[]{:S(2)}) async-start(), calls=%async_computation.45 | async-start | bytes 995328
  1659.2 851.6 %reduce-scatter.54.cloned.1.call-start = ((), (), s32[]{:S(2)}) async-start(), calls=%async_computation.44 | async-start | bytes 995328
  1702.2 845.0 %reduce-scatter.52.cloned.1.call-start = ((), (), s32[]{:S(2)}) async-start(), calls=%async_computation.43 | async-start | bytes 2322432
  1790.5 793.3 %reduce-scatter.50.cloned.1.call-start = ((), (), s32[]{:S(2)}) async-start(), calls=%async_computation.42 | async-start | bytes 2322432
  1876.9 751.9 %reduce-scatter.64.cloned.1.call-start = ((), (), s32[]{:S(2)}) async-start(), calls=%async_computation.49 | async-start | bytes 3981312
  1985.4 687.9 %reduce-scatter.62.cloned.1.call-start = ((), (), s32[]{:S(2)}) async-start(), calls=%async_computation.48 | async-start | bytes 3981312
  2093.4 618.6 %reduce-scatter.44.cloned.1.call-start = ((), (), s32[]{:S(2)}) async-start(), calls=%async_computation.25 | async-start | bytes 2985984 | tf_op jit(solution)/shard_map/reduce_scatter | solution.py:272
  2202.1 549.2 %reduce-scatter.42.cloned.1.call-start = ((), (), s32[]{:S(2)}) async-start(), calls=%async_computation.24 | async-start | bytes 2985984 | tf_op jit(solution)/shard_map/reduce_scatter | solution.py:272
  2310.1 68.9 %all-to-all-start.1 = ((bf16[1,16,64,1152]{3,2,0,1:T(8,128)(2,1)}), bf16[1,16,64,1152]{3,2,0,1:T(8,128)(2,1)S(1)}, u32[]{:S(2)}, u32[]{:S(2)}) async-start(bf16[1,16,64,1152]{3,2,0,1:T(8,128)(2,1)} %get-tuple-element.171), calls=%async_computation.1 | async-start | bytes 4718592 | tf_op jit(solution)/shard_map/all_to_all | solution.py:245
  2313.8 130.6 %copy-start.102 = (f32[1,1152]{1,0:T(1,128)S(1)}, f32[1,1152]{1,0:T(1,128)}, u32[]{:S(2)}) copy-start(f32[1,1152]{1,0:T(1,128)} %param.13) | copy-start | bytes 13828
  2587.0 166.4 %copy-start.88 = (f32[2,4608]{1,0:T(2,128)S(1)}, f32[2,4608]{1,0:T(2,128)}, u32[]{:S(2)}) copy-start(f32[2,4608]{1,0:T(2,128)} %get-tuple-element.233) | copy-start | bytes 110596
  2587.0 167.1 %copy-start.107 = (f32[2,1152]{1,0:T(2,128)S(1)}, f32[2,1152]{1,0:T(2,128)}, u32[]{:S(2)}) copy-start(f32[2,1152]{1,0:T(2,128)} %get-tuple-element.234) | copy-start | bytes 27652
  (122 other events, 1152.7 us)
Sparse Core Ops, SparseCore 0:
  10.2 31.5 all-gather.31
  44.0 36.9 all-gather.37
  83.2 71.0 all-gather.41
  156.4 27.4 all-gather.45
  185.9 36.9 all-gather.51
  225.0 78.7 all-gather.55
  306.2 146.5 all-gather.33
  455.3 48.6 all-gather.35
  505.8 106.1 all-gather.39
  613.7 106.1 all-gather.43
  721.8 84.0 all-gather.47
  808.1 39.9 all-gather.49
  849.9 126.8 all-gather.53
  978.5 106.1 all-gather.57
  1487.0 125.8 all-reduce.5
  1616.0 40.7 reduce-scatter.39
  1659.9 39.8 reduce-scatter.37
  1703.1 83.2 reduce-scatter.35
  1789.5 83.2 reduce-scatter.33
  1876.0 104.6 reduce-scatter.47
  1984.1 104.6 reduce-scatter.45
  2092.1 104.6 reduce-scatter.59
  2200.2 104.6 reduce-scatter.57
  2312.4 130.5 all-reduce.7
  2446.0 31.8 reduce-scatter.55
  2480.6 30.1 reduce-scatter.53
  2513.1 34.0 reduce-scatter.51
  2549.5 34.2 reduce-scatter.49
  2586.3 42.4 reduce-scatter.63
  2630.9 42.2 reduce-scatter.61
  2675.7 36.2 reduce-scatter.43
  2714.4 36.7 reduce-scatter.41
where the time goes:
time: 2770 us; the launch traced here: 2760 us
  waiting for transfers between devices  1220 us (44%)
  local copies, waits for them, and re-layouts  546 us (20%)
  matrix products  470 us (17%)
  blocking collectives  360 us (13%)
  other arithmetic  136 us (5%)
    unnamed x41, waiting for transfers between devices  425 us
    all_gather x1, blocking collectives, on_device(): every_mod = lax.all_gather(local_mods, ('clip', 'seq'), axis=2, tiled=True)  245 us
    reduce_scatter x2, waiting for transfers between devices, shed(): lax.psum_scatter(gradients[3].astype(jnp.bfloat16), 'seq', scatter_dimens...  207 us
    slice x1, local copies, waits for them, and re-layouts, on_device(): modulation[1]  196 us
    reduce_scatter x2, waiting for transfers between devices, shed(): lax.psum_scatter(gradients[0].astype(jnp.bfloat16), 'seq', scatter_dimens...  166 us
    unnamed x310, local copies, waits for them, and re-layouts  122 us
    another operation x13, local copies, waits for them, and re-layouts  101 us
    reduce_scatter x2, waiting for transfers between devices, shed(): lax.psum_scatter(column_part[2].astype(jnp.bfloat16), 'clip', scatter_dim...  75.5 us
  transfers between devices with their start and end apart: 36, of which 24 were waited for; matrix products, arithmetic and copies ran while one was open for 27% of the time, Pallas kernels for 0%

commit v1 on v0

v1 whole, which is shorter than its diff:
```python
from functools import partial

import jax
import jax.numpy as jnp
from jax import lax
from jax.experimental import pallas as pl
from jax.experimental.pallas import tpu as pltpu
from jax.sharding import PartitionSpec as P

HEADS = 16
F32 = jnp.float32
BF16 = jnp.bfloat16
NN = (((1,), (0,)), ((), ()))
NT = (((1,), (1,)), ((), ()))
TN = (((0,), (0,)), ((), ()))
VMEM_BYTES = 56 * 1024 * 1024


def mm(a, b, dims=NN):
    return lax.dot_general(a, b, dims, preferred_element_type=F32)


def call(body, grid, in_specs, out_specs, out_shape, scratch=(), scalars=0, flops=0, nbytes=0):
    return pl.pallas_call(
        body,
        grid_spec=pltpu.PrefetchScalarGridSpec(
            num_scalar_prefetch=scalars,
            grid=grid,
            in_specs=in_specs,
            out_specs=out_specs,
            scratch_shapes=list(scratch),
        ),
        out_shape=out_shape,
        compiler_params=pltpu.CompilerParams(
            dimension_semantics=("arbitrary",) * len(grid), vmem_limit_bytes=VMEM_BYTES
        ),
        cost_estimate=pl.CostEstimate(flops=flops, bytes_accessed=nbytes, transcendentals=0),
    )


def whole(shape):
    return pl.BlockSpec(shape, lambda *_: (0,) * len(shape))


def sds(shape, dtype):
    return jax.ShapeDtypeStruct(shape, dtype)


def standard(x):
    centred = x - jnp.mean(x, axis=-1, keepdims=True)
    r = lax.rsqrt(jnp.mean(centred * centred, axis=-1, keepdims=True) + 1e-06)
    return centred * r, r


def fold(n, limit=512):
    return min(n, limit)


def qkv_forward(x, mods, w, bias):
    n, d = x.shape
    wide = w.shape[1]
    mt = fold(n)

    def body(x_ref, mod_ref, w_ref, b_ref, hid_ref, out_ref):
        m = pl.program_id(1)
        rows = pl.ds(pl.multiple_of(m * mt, mt), mt)

        @pl.when(pl.program_id(0) == 0)
        def _():
            v, _ = standard(x_ref[...].astype(F32))
            hid_ref[rows, :] = (v * (1.0 + mod_ref[1:2, :]) + mod_ref[0:1, :]).astype(BF16)

        out_ref[...] = (mm(hid_ref[rows, :], w_ref[...]) + b_ref[...]).astype(BF16)

    return call(
        body,
        (wide // d, n // mt),
        [
            pl.BlockSpec((mt, d), lambda j, m: (jnp.where(j == 0, m, n // mt - 1), 0)),
            whole((8, d)),
            pl.BlockSpec((d, d), lambda j, m: (0, j)),
            pl.BlockSpec((1, d), lambda j, m: (0, j)),
        ],
        [whole((n, d)), pl.BlockSpec((mt, d), lambda j, m: (m, j))],
        [sds((n, d), BF16), sds((n, wide), BF16)],
        flops=2 * n * d * wide,
        nbytes=2 * (d * wide + n * wide + 2 * n * d),
    )(x, mods, w, bias)


def window(h, size, d):
    lo = h * size
    start = lo // 128 * 128
    stop = min(-(-(lo + size) // 128) * 128, d)
    return start, stop, lo - start


def head_mask(start, stop, off, size, rows):
    lane = lax.broadcasted_iota(jnp.int32, (rows, stop - start), 1)
    return (lane >= off) & (lane < off + size)


def attention_forward(qkv, temporal):
    a, g, p, wide = qkv.shape
    d = wide // 3
    size = d // HEADS
    t = a * p
    scale = size ** (-0.5)

    def body(qkv_ref, att_ref, lse_ref, peak_ref, acc):
        acc[...] = jnp.zeros_like(acc)
        if temporal:
            qi = lax.broadcasted_iota(jnp.int32, (t, t), 0)
            ki = lax.broadcasted_iota(jnp.int32, (t, t), 1)
            same = lax.rem(qi, p) == lax.rem(ki, p)
        tops, totals = [], []
        for h in range(HEADS):
            lo, hi, off = window(h, size, d)
            keep = head_mask(lo, hi, off, size, t)
            q = qkv_ref[:, 0, :, lo:hi].reshape(t, hi - lo)
            k = qkv_ref[:, 0, :, d + lo : d + hi].reshape(t, hi - lo)
            v = qkv_ref[:, 0, :, 2 * d + lo : 2 * d + hi].reshape(t, hi - lo)
            zero = jnp.zeros_like(q)
            s = mm(jnp.where(keep, q, zero), k, NT) * scale
            if temporal:
                s = jnp.where(same, s, -1e30)
            top = jnp.max(s, axis=-1, keepdims=True)
            e = jnp.exp(s - top)
            total = jnp.sum(e, axis=-1, keepdims=True)
            probs = (e / total).astype(BF16)
            acc[:, lo:hi] += mm(probs, jnp.where(keep, v, zero))
            tops.append(top)
            totals.append(total)
        top = jnp.concatenate(tops, axis=1)
        lse_ref[0] = (top + jnp.log(jnp.concatenate(totals, axis=1))).T
        peak_ref[...] = jnp.max(top, axis=0, keepdims=True)[None]
        att_ref[...] = acc[...].astype(BF16).reshape(a, 1, p, d)

    return call(
        body,
        (g,),
        [pl.BlockSpec((a, 1, p, wide), lambda i: (0, i, 0, 0))],
        [
            pl.BlockSpec((a, 1, p, d), lambda i: (0, i, 0, 0)),
            pl.BlockSpec((1, HEADS, t), lambda i: (i, 0, 0)),
            pl.BlockSpec((1, 1, HEADS), lambda i: (i, 0, 0)),
        ],
        [sds((a, g, p, d), BF16), sds((g, HEADS, t), F32), sds((g, 1, HEADS), F32)],
        [pltpu.VMEM((t, d), F32)],
        flops=4 * g * HEADS * t * t * 256,
        nbytes=2 * a * g * p * (wide + d),
    )(qkv)


def out_forward(att, x, mods, w, bias):
    n, d = att.shape
    mt = fold(n, 256)

    def body(att_ref, x_ref, mod_ref, w_ref, b_ref, branch_ref, mid_ref, hid_ref):
        branch = mm(att_ref[...], w_ref[...]) + b_ref[...]
        branch_ref[...] = branch.astype(BF16)
        mid = x_ref[...].astype(F32) + mod_ref[2:3, :] * branch
        mid_ref[...] = mid
        v, _ = standard(mid)
        hid_ref[...] = (v * (1.0 + mod_ref[4:5, :]) + mod_ref[3:4, :]).astype(BF16)

    tile = pl.BlockSpec((mt, d), lambda m: (m, 0))
    return call(
        body,
        (n // mt,),
        [tile, tile, whole((8, d)), whole((d, d)), whole((1, d))],
        [tile, tile, tile],
        [sds((n, d), BF16), sds((n, d), F32), sds((n, d), BF16)],
        flops=2 * n * d * d,
        nbytes=2 * (d * d + 6 * n * d),
    )(att, x, mods, w, bias)


GELU_A = 0.7978845608028654
GELU_B = 0.044715


def up_forward(hid, w, bias):
    n, d = hid.shape
    ff = w.shape[1]
    mt = fold(n)
    ft = d
    cuts = 3

    def body(hid_ref, w_ref, b_ref, act_ref, slope_ref):
        for c in range(cuts):
            cols = slice(c * ft // cuts, (c + 1) * ft // cuts)
            u = mm(hid_ref[...], w_ref[:, cols]) + b_ref[:, cols]
            square = u * u
            tanh = jnp.tanh(u * (GELU_A + (GELU_A * GELU_B) * square))
            half = 0.5 + 0.5 * tanh
            act_ref[:, cols] = (u * half).astype(BF16)
            bend = GELU_A + (3.0 * GELU_A * GELU_B) * square
            slope_ref[:, cols] = (half + (u * half) * ((1.0 - tanh) * bend)).astype(BF16)

    tile = pl.BlockSpec((mt, ft), lambda f, m: (m, f))
    return call(
        body,
        (ff // ft, n // mt),
        [
            pl.BlockSpec((mt, d), lambda f, m: (m, 0)),
            pl.BlockSpec((d, ft), lambda f, m: (0, f)),
            pl.BlockSpec((1, ft), lambda f, m: (0, f)),
        ],
        [tile, tile],
        [sds((n, ff), BF16), sds((n, ff), BF16)],
        flops=2 * n * d * ff,
        nbytes=2 * (d * ff + 2 * n * ff + n * d),
    )(hid, w, bias)


def down_forward(act, mid, mods, w, bias):
    n, ff = act.shape
    d = w.shape[1]
    mt = fold(n)
    last = ff // d - 1

    def body(act_ref, mid_ref, mod_ref, w_ref, b_ref, upd_ref, out_ref, acc):
        k = pl.program_id(0)
        rows = pl.ds(pl.multiple_of(pl.program_id(1) * mt, mt), mt)
        part = mm(act_ref[...], w_ref[...])

        @pl.when(k == 0)
        def _():
            acc[rows, :] = part

        @pl.when((k > 0) & (k < last))
        def _():
            acc[rows, :] += part

        @pl.when(k == last)
        def _():
            upd = acc[rows, :] + part + b_ref[...]
            upd_ref[...] = upd.astype(BF16)
            out_ref[...] = (mid_ref[...] + mod_ref[5:6, :] * upd).astype(BF16)

    late = pl.BlockSpec((mt, d), lambda k, m: (jnp.where(k == last, m, 0), 0))
    return call(
        body,
        (ff // d, n // mt),
        [
            pl.BlockSpec((mt, d), lambda k, m: (m, k)),
            late,
            whole((8, d)),
            pl.BlockSpec((d, d), lambda k, m: (k, 0)),
            whole((1, d)),
        ],
        [late, late],
        [sds((n, d), BF16), sds((n, d), BF16)],
        [pltpu.VMEM((n, d), F32)],
        flops=2 * n * d * ff,
        nbytes=2 * (d * ff + n * ff + 4 * n * d),
    )(act, mid, mods, w, bias)


def column_sum(v):
    return jnp.sum(v, axis=0, keepdims=True)


def update_back(go, upd, mods):
    n, d = go.shape
    mt = fold(n, 256)

    def body(go_ref, upd_ref, mod_ref, gu_ref, sum_ref):
        @pl.when(pl.program_id(0) == 0)
        def _():
            sum_ref[...] = jnp.zeros_like(sum_ref)

        g = go_ref[...].astype(F32)
        low = (mod_ref[5:6, :] * g).astype(BF16)
        gu_ref[...] = low
        sum_ref[0:1, :] += column_sum(g * upd_ref[...].astype(F32))
        sum_ref[1:2, :] += column_sum(low.astype(F32))

    tile = pl.BlockSpec((mt, d), lambda m: (m, 0))
    return call(
        body,
        (n // mt,),
        [tile, tile, whole((8, d))],
        [tile, whole((8, d))],
        [sds((n, d), BF16), sds((8, d), F32)],
        flops=n * d,
        nbytes=6 * n * d,
    )(go, upd, mods)


def shed_specs(seq, zs, rows, d):
    return sds((seq, zs, rows, d), BF16)


def down_grad(place, act, gu, seq, zs):
    n, ff = act.shape
    d = gu.shape[1]
    rows, quarter = d // (2 * zs), d // seq
    parts = ff // (2 * zs) // rows

    def body(place_ref, act_ref, gu_ref, mine_ref, other_ref, full):
        core = place_ref[0]
        cuts = 3
        for c in range(cuts):
            span = slice(c * d // cuts, (c + 1) * d // cuts)
            full[span, :] = mm(act_ref[:, span], gu_ref[...], TN).astype(BF16)
        for c in range(2):
            for target, flag in ((mine_ref, core == c), (other_ref, core != c)):

                @pl.when(flag)
                def _(target=target, c=c):
                    for q in range(parts):
                        base = (c * parts + q) * rows
                        for s in range(seq):
                            target[s, 0, :, q * quarter : (q + 1) * quarter] = full[
                                base : base + rows, s * quarter : (s + 1) * quarter
                            ]

    piece = pl.BlockSpec((seq, 1, rows, d), lambda i, place_ref: (0, i, 0, 0))
    return call(
        body,
        (zs,),
        [
            pl.BlockSpec((n, ff // zs), lambda i, place_ref: (0, i ^ place_ref[1])),
            whole((n, d)),
        ],
        [piece, piece],
        [shed_specs(seq, zs, rows, d)] * 2,
        [pltpu.VMEM((ff // zs, d), BF16)],
        scalars=1,
        flops=2 * n * d * ff,
        nbytes=2 * (d * ff + n * ff + n * d),
    )(place, act, gu)


def spread(place_ref, full, mine_ref, other_ref, zs, rows, cols):
    core, z = place_ref[0], place_ref[1]
    for c in range(2):
        for target, flag in ((mine_ref, core == c), (other_ref, core != c)):

            @pl.when(flag)
            def _(target=target, c=c):
                for zz in range(zs):
                    base = (zz * 2 + c) * rows
                    target[0, zz ^ z, :, cols] = full[base : base + rows, cols]


def up_grad(place, hid, gi, seq, zs):
    n, d = hid.shape
    ff = gi.shape[1]
    rows, wide = d // (2 * zs), ff // seq

    def body(place_ref, hid_ref, gi_ref, mine_ref, other_ref, hid_t, full):
        cuts = 3

        @pl.when(pl.program_id(0) == 0)
        def _():
            for c in range(cuts):
                span = slice(c * d // cuts, (c + 1) * d // cuts)
                hid_t[span, :] = hid_ref[:, span].T

        for c in range(cuts):
            span = slice(c * d // cuts, (c + 1) * d // cuts)
            full[span, :] = mm(hid_t[span, :], gi_ref[...]).astype(BF16)
        spread(place_ref, full, mine_ref, other_ref, zs, rows, slice(0, wide))

    piece = pl.BlockSpec((1, zs, rows, wide), lambda i, place_ref: (i, 0, 0, 0))
    return call(
        body,
        (seq,),
        [whole((n, d)), pl.BlockSpec((n, wide), lambda i, place_ref: (0, i))],
        [piece, piece],
        [shed_specs(seq, zs, rows, wide)] * 2,
        [pltpu.VMEM((d, n), BF16), pltpu.VMEM((d, wide), BF16)],
        scalars=1,
        flops=2 * n * d * ff,
        nbytes=2 * (d * ff + n * ff + n * d),
    )(place, hid, gi)


def qkv_out_grad(place, hid, att, gqkv, gb, zs):
    n, d = hid.shape
    seq, _, wa = gqkv.shape
    wb = gb.shape[2]
    rows = d // (2 * zs)

    def body(place_ref, hid_ref, att_ref, gqkv_ref, gb_ref, mine_ref, other_ref, hid_t, att_t, full):
        cuts = 3

        @pl.when(pl.program_id(0) == 0)
        def _():
            for c in range(cuts):
                span = slice(c * d // cuts, (c + 1) * d // cuts)
                hid_t[span, :] = hid_ref[:, span].T
                att_t[span, :] = att_ref[:, span].T

        for c in range(cuts):
            span = slice(c * d // cuts, (c + 1) * d // cuts)
            full[span, :] = jnp.concatenate(
                [
                    mm(hid_t[span, :], gqkv_ref[0]).astype(BF16),
                    mm(att_t[span, :], gb_ref[0]).astype(BF16),
                ],
                axis=1,
            )
        spread(place_ref, full, mine_ref, other_ref, zs, rows, slice(0, wa + wb))

    piece = pl.BlockSpec((1, zs, rows, wa + wb), lambda i, place_ref: (i, 0, 0, 0))
    return call(
        body,
        (seq,),
        [
            whole((n, d)),
            whole((n, d)),
            pl.BlockSpec((1, n, wa), lambda i, place_ref: (i, 0, 0)),
            pl.BlockSpec((1, n, wb), lambda i, place_ref: (i, 0, 0)),
        ],
        [piece, piece],
        [shed_specs(seq, zs, rows, wa + wb)] * 2,
        [pltpu.VMEM((d, n), BF16), pltpu.VMEM((d, n), BF16), pltpu.VMEM((d, wa + wb), BF16)],
        scalars=1,
        flops=2 * n * d * seq * (wa + wb),
        nbytes=2 * seq * (d + n) * (wa + wb),
    )(place, hid, att, gqkv, gb)


def feed_back(gu, slope, w_down, w_up):
    n, d = gu.shape
    ff = slope.shape[1]
    mt = fold(n)
    last = ff // d - 1

    def body(gu_ref, slope_ref, wd_ref, wu_ref, gi_ref, bias_ref, out_ref, acc):
        f = pl.program_id(0)
        m = pl.program_id(1)
        rows = pl.ds(pl.multiple_of(m * mt, mt), mt)
        gi = (mm(gu_ref[...], wd_ref[...], NT) * slope_ref[...].astype(F32)).astype(BF16)
        gi_ref[...] = gi
        total = column_sum(gi.astype(F32))

        @pl.when(m == 0)
        def _():
            bias_ref[...] = total

        @pl.when(m > 0)
        def _():
            bias_ref[...] += total

        part = mm(gi, wu_ref[...], NT)

        @pl.when(f == 0)
        def _():
            acc[rows, :] = part

        @pl.when((f > 0) & (f < last))
        def _():
            acc[rows, :] += part

        @pl.when(f == last)
        def _():
            out_ref[...] = acc[rows, :] + part

    return call(
        body,
        (ff // d, n // mt),
        [
            pl.BlockSpec((mt, d), lambda f, m: (m, 0)),
            pl.BlockSpec((mt, d), lambda f, m: (m, f)),
            pl.BlockSpec((d, d), lambda f, m: (f, 0)),
            pl.BlockSpec((d, d), lambda f, m: (0, f)),
        ],
        [
            pl.BlockSpec((mt, d), lambda f, m: (m, f)),
            pl.BlockSpec((1, d), lambda f, m: (0, f)),
            pl.BlockSpec((mt, d), lambda f, m: (jnp.where(f == last, m, 0), 0)),
        ],
        [sds((n, ff), BF16), sds((1, ff), F32), sds((n, d), F32)],
        [pltpu.VMEM((n, d), F32)],
        flops=4 * n * d * ff,
        nbytes=2 * (2 * d * ff + 2 * n * ff + 3 * n * d),
    )(gu, slope, w_down, w_up)


def norm_back(grad, v, r, stretch):
    dn = grad * stretch
    return r * (
        dn - jnp.mean(dn, axis=-1, keepdims=True) - v * jnp.mean(dn * v, axis=-1, keepdims=True)
    )


def middle_back(gh, mid, branch, go, mods, w, seq):
    n, d = gh.shape
    mt = fold(n, 256)
    wide = d // seq

    def body(gh_ref, mid_ref, branch_ref, go_ref, mod_ref, w_ref, gmid_ref, gb_ref, cut_ref, ga_ref, sum_ref):
        @pl.when(pl.program_id(0) == 0)
        def _():
            sum_ref[...] = jnp.zeros_like(sum_ref)

        g = gh_ref[...]
        v, r = standard(mid_ref[...])
        sum_ref[0:1, :] += column_sum(g * v)
        sum_ref[1:2, :] += column_sum(g)
        gmid = go_ref[...].astype(F32) + norm_back(g, v, r, 1.0 + mod_ref[4:5, :])
        gmid_ref[...] = gmid
        sum_ref[2:3, :] += column_sum(gmid * branch_ref[...].astype(F32))
        low = (mod_ref[2:3, :] * gmid).astype(BF16)
        gb_ref[...] = low
        for s in range(seq):
            cut_ref[s] = low[:, s * wide : (s + 1) * wide]
        sum_ref[3:4, :] += column_sum(low.astype(F32))
        ga_ref[...] = mm(low, w_ref[...], NT).astype(BF16)

    tile = pl.BlockSpec((mt, d), lambda m: (m, 0))
    return call(
        body,
        (n // mt,),
        [tile, tile, tile, tile, whole((8, d)), whole((d, d))],
        [tile, tile, pl.BlockSpec((seq, mt, wide), lambda m: (0, m, 0)), tile, whole((8, d))],
        [
            sds((n, d), F32),
            sds((n, d), BF16),
            sds((seq, n, wide), BF16),
            sds((n, d), BF16),
            sds((8, d), F32),
        ],
        flops=2 * n * d * d,
        nbytes=2 * (d * d + 11 * n * d),
    )(gh, mid, branch, go, mods, w)


def attention_back(qkv, ga, lse, temporal, seq):
    a, g, p, wide = qkv.shape
    d = wide // 3
    size = d // HEADS
    t = a * p
    scale = size ** (-0.5)
    cut = wide // seq

    def body(qkv_ref, ga_ref, lse_ref, out_ref, cut_ref, sum_ref, acc):
        acc[...] = jnp.zeros_like(acc)
        if temporal:
            ki = lax.broadcasted_iota(jnp.int32, (t, t), 0)
            qi = lax.broadcasted_iota(jnp.int32, (t, t), 1)
            same = lax.rem(qi, p) == lax.rem(ki, p)
        for h in range(HEADS):
            lo, hi, off = window(h, size, d)
            keep = head_mask(lo, hi, off, size, t)
            q = qkv_ref[:, 0, :, lo:hi].reshape(t, hi - lo)
            k = qkv_ref[:, 0, :, d + lo : d + hi].reshape(t, hi - lo)
            v = qkv_ref[:, 0, :, 2 * d + lo : 2 * d + hi].reshape(t, hi - lo)
            o = ga_ref[:, 0, :, lo:hi].reshape(t, hi - lo)
            zero = jnp.zeros_like(q)
            q, o = jnp.where(keep, q, zero), jnp.where(keep, o, zero)
            s = mm(k, q, NT) * scale
            probs = jnp.exp(s - lse_ref[0, h : h + 1, :])
            if temporal:
                probs = jnp.where(same, probs, 0.0)
            dp = mm(v, o, NT)
            acc[:, 2 * d + lo : 2 * d + hi] += mm(probs.astype(BF16), o)
            ds = (probs * (dp - column_sum(probs * dp))).astype(BF16)
            acc[:, d + lo : d + hi] += mm(ds, q) * scale
            acc[:, lo:hi] += mm(ds, jnp.where(keep, k, zero), TN) * scale
        low = acc[...].astype(BF16)
        out_ref[...] = low.reshape(a, 1, p, wide)
        for s in range(seq):
            cut_ref[s] = low[:, s * cut : (s + 1) * cut].reshape(a, 1, p, cut)
        total = column_sum(low.astype(F32))

        @pl.when(pl.program_id(0) == 0)
        def _():
            sum_ref[...] = total

        @pl.when(pl.program_id(0) > 0)
        def _():
            sum_ref[...] += total

    return call(
        body,
        (g,),
        [
            pl.BlockSpec((a, 1, p, wide), lambda i: (0, i, 0, 0)),
            pl.BlockSpec((a, 1, p, d), lambda i: (0, i, 0, 0)),
            pl.BlockSpec((1, HEADS, t), lambda i: (i, 0, 0)),
        ],
        [
            pl.BlockSpec((a, 1, p, wide), lambda i: (0, i, 0, 0)),
            pl.BlockSpec((seq, a, 1, p, cut), lambda i: (0, 0, i, 0, 0)),
            whole((1, wide)),
        ],
        [sds((a, g, p, wide), BF16), sds((seq, a, g, p, cut), BF16), sds((1, wide), F32)],
        [pltpu.VMEM((t, wide), F32)],
        flops=12 * g * HEADS * t * t * 256,
        nbytes=2 * a * g * p * (3 * wide + d),
    )(qkv, ga, lse)


def stream_back(gqkv, w, x, gmid, mods, out_dtype):
    n, wide = gqkv.shape
    d = w.shape[0]
    mt = fold(n)
    last = wide // d - 1

    def body(g_ref, w_ref, x_ref, gmid_ref, mod_ref, out_ref, sum_ref, acc):
        k = pl.program_id(0)
        m = pl.program_id(1)
        rows = pl.ds(pl.multiple_of(m * mt, mt), mt)
        part = mm(g_ref[...], w_ref[...], NT)

        @pl.when(k == 0)
        def _():
            acc[rows, :] = part

        @pl.when((k > 0) & (k < last))
        def _():
            acc[rows, :] += part

        @pl.when((k == last) & (m == 0))
        def _():
            sum_ref[...] = jnp.zeros_like(sum_ref)

        @pl.when(k == last)
        def _():
            grad = acc[rows, :] + part
            v, r = standard(x_ref[...].astype(F32))
            sum_ref[0:1, :] += column_sum(grad * v)
            sum_ref[1:2, :] += column_sum(grad)
            out_ref[...] = (gmid_ref[...] + norm_back(grad, v, r, 1.0 + mod_ref[1:2, :])).astype(
                out_dtype
            )

    late = pl.BlockSpec((mt, d), lambda k, m: (jnp.where(k == last, m, 0), 0))
    return call(
        body,
        (wide // d, n // mt),
        [
            pl.BlockSpec((mt, d), lambda k, m: (m, k)),
            pl.BlockSpec((d, d), lambda k, m: (0, k)),
            late,
            late,
            whole((8, d)),
        ],
        [late, whole((8, d))],
        [sds((n, d), out_dtype), sds((8, d), F32)],
        [pltpu.VMEM((n, d), F32)],
        flops=2 * n * d * wide,
        nbytes=2 * (d * wide + n * wide + 5 * n * d),
    )(gqkv, w, x, gmid, mods)


def join_qkv_out(place, own, got):
    seq, zs, rows, d = own.shape
    wide = d * 3 // 4

    def body(place_ref, own_ref, got_ref, qkv_ref, out_ref):
        def put(c, src):
            span = slice(c * rows, (c + 1) * rows)
            qkv_ref[span, :] = jnp.concatenate([src[s, 0, :, :wide] for s in range(seq)], axis=1)
            out_ref[span, :] = jnp.concatenate([src[s, 0, :, wide:] for s in range(seq)], axis=1)

        for c in range(2):

            @pl.when(place_ref[0] == c)
            def _(c=c):
                put(c, own_ref)
                put(1 - c, got_ref)

    piece = pl.BlockSpec((seq, 1, rows, d), lambda i, place_ref: (0, i ^ place_ref[1], 0, 0))
    return call(
        body,
        (zs,),
        [piece, piece],
        [
            pl.BlockSpec((2 * rows, seq * wide), lambda i, place_ref: (i, 0)),
            pl.BlockSpec((2 * rows, d), lambda i, place_ref: (i, 0)),
        ],
        [sds((2 * rows * zs, seq * wide), BF16), sds((2 * rows * zs, d), BF16)],
        scalars=1,
        nbytes=8 * seq * zs * rows * d,
    )(place, own, got)


def join_up(place, own, got):
    seq, zs, rows, d = own.shape

    def body(place_ref, own_ref, got_ref, up_ref):
        for c in range(2):

            @pl.when(place_ref[0] == c)
            def _(c=c):
                for s in range(seq):
                    cols = slice(s * d, (s + 1) * d)
                    up_ref[c * rows : (c + 1) * rows, cols] = own_ref[s, 0]
                    up_ref[(1 - c) * rows : (2 - c) * rows, cols] = got_ref[s, 0]

    piece = pl.BlockSpec((seq, 1, rows, d), lambda i, place_ref: (0, i ^ place_ref[1], 0, 0))
    return call(
        body,
        (zs,),
        [piece, piece],
        pl.BlockSpec((2 * rows, seq * d), lambda i, place_ref: (i, 0)),
        sds((2 * rows * zs, seq * d), BF16),
        scalars=1,
        nbytes=8 * seq * zs * rows * d,
    )(place, own, got)


def join_down(place, own, got):
    seq, zs, rows, d = own.shape
    quarter = d // seq
    parts = d // quarter

    def body(place_ref, own_ref, got_ref, down_ref):
        def put(c, src):
            for q in range(parts):
                base = (c * parts + q) * rows
                cols = slice(q * quarter, (q + 1) * quarter)
                down_ref[base : base + rows, :] = jnp.concatenate(
                    [src[s, 0, :, cols] for s in range(seq)], axis=1
                )

        for c in range(2):

            @pl.when(place_ref[0] == c)
            def _(c=c):
                put(c, own_ref)
                put(1 - c, got_ref)

    piece = pl.BlockSpec((seq, 1, rows, d), lambda i, place_ref: (0, i ^ place_ref[1], 0, 0))
    return call(
        body,
        (zs,),
        [piece, piece],
        pl.BlockSpec((2 * parts * rows, d), lambda i, place_ref: (i, 0)),
        sds((2 * parts * rows * zs, d), BF16),
        scalars=1,
        nbytes=8 * seq * zs * rows * d,
    )(place, own, got)


clip_limit = 8.0


def hop(x, distance, count):
    return lax.ppermute(x, "clip", [(i, i ^ distance) for i in range(count)])


def on_device(
    video_latents,
    conditioning,
    ada_weight,
    ada_bias,
    qkv_weight,
    out_weight,
    up_weight,
    down_weight,
    attention_bias,
    up_bias,
    down_bias,
    cotangent,
    *,
    clips,
    seq,
):
    zs = clips // 2
    layers, rows, own_columns = qkv_weight.shape
    d = video_latents.shape[-1]
    frames, places = video_latents.shape[1:3]
    n = frames * places
    ff = up_bias.shape[1]
    clip_index = lax.axis_index("clip")
    place = jnp.stack([clip_index % 2, clip_index // 2]).astype(jnp.int32)
    packed = rows % 16 == 0 and down_weight.shape[1] % rows == 0 and d % seq == 0
    cuts = seq if packed else 1

    every_condition = lax.all_gather(conditioning, "clip", axis=0, tiled=True)
    squashed = jax.nn.silu(every_condition).astype(BF16)
    local_mods = (
        jnp.einsum("kd,ldc->klc", squashed, ada_weight, preferred_element_type=F32)
        + ada_bias[None, :, :]
    )
    own_mods = lax.all_to_all(local_mods, "clip", 0, 0, tiled=True)
    every_mod = lax.all_gather(own_mods, "seq", axis=0, tiled=False)
    modulation = every_mod.transpose(2, 1, 0, 3).reshape(layers, 6, d)
    modulation = jnp.pad(modulation, ((0, 0), (0, 2), (0, 0)))

    def spread_out(block):
        blocks = block[None]
        step = 1
        while step < zs:
            blocks = jnp.concatenate([blocks, hop(blocks, 2 * step, clips)], axis=0)
            step *= 2
        own = lax.all_gather(blocks, "seq", axis=0, tiled=False)
        return own, hop(own, 1, clips)

    def fetch(layer):
        if packed:
            tall = down_weight[layer].reshape(-1, rows, d // seq)
            qkv_full, out_full = join_qkv_out(
                place,
                *spread_out(jnp.concatenate([qkv_weight[layer], out_weight[layer]], axis=1)),
            )
            up_full = join_up(place, *spread_out(up_weight[layer]))
            down_full = join_down(
                place,
                *spread_out(tall.transpose(1, 0, 2).reshape(rows, d)),
            )
            return qkv_full, out_full, up_full, down_full
        return tuple(
            lax.all_gather(
                lax.all_gather(item[layer], "clip", axis=0, tiled=True), "seq", axis=1, tiled=True
            )
            for item in (qkv_weight, out_weight, up_weight, down_weight)
        )

    def gather_in(mine, other):
        half = mine + hop(other, 1, clips)
        flat = lax.psum_scatter(half.reshape(-1, d), "seq", scatter_dimension=0, tiled=True)
        part = flat.reshape(zs, rows, d)
        step = zs // 2
        while step >= 1:
            part = part[:step].astype(F32) + hop(part[step:], 2 * step, clips).astype(F32)
            if step > 1:
                part = part.astype(BF16)
            step //= 2
        return part[0]

    def shed_natural(left, right):
        full = mm(left, right, TN).astype(BF16)
        part = lax.psum_scatter(full, "seq", scatter_dimension=1, tiled=True)
        return lax.psum_scatter(part, "clip", scatter_dimension=0, tiled=True).astype(F32)

    def swap_tokens(x):
        block = x.reshape(seq, n // seq, d)
        return lax.all_to_all(block, "seq", 0, 0, tiled=True).reshape(n, d)

    def by_places(x):
        return x.reshape(frames, seq, places // seq, d).transpose(1, 0, 2, 3).reshape(n, d)

    def by_frames(x):
        return (
            x.reshape(seq, frames, places // seq, d)
            .transpose(1, 0, 2, 3)
            .reshape(1, frames, places, d)
        )

    shapes = (
        (seq, frames, places // seq),
        (seq * frames, places // seq // 16, 16),
    )

    def forward(layer, x, weights):
        qkv_full, out_full, up_full, down_full = weights
        temporal = layer == 1
        mods = modulation[layer]
        bias = attention_bias[layer]
        qkv_bias = jnp.concatenate([bias[0], jnp.zeros_like(bias[0]), bias[1]])[None]
        hidden, qkv = qkv_forward(x, mods, qkv_full, qkv_bias)
        qkv = qkv.reshape(shapes[layer] + (3 * d,))
        attended, lse, peak = attention_forward(qkv, temporal)
        attended = attended.reshape(n, d)
        branch, middle, hidden_two = out_forward(attended, x, mods, out_full, bias[2:3])
        active, slope = up_forward(hidden_two, up_full, up_bias[layer : layer + 1])
        update, result = down_forward(
            active, middle, mods, down_full, down_bias[layer : layer + 1]
        )
        kept = (x, hidden, qkv, lse, attended, branch, middle, hidden_two, active, slope, update)
        return result, kept, jnp.max(peak, axis=(0, 1))

    def backward(layer, grad_out, kept, weights):
        x, hidden, qkv, lse, attended, branch, middle, hidden_two, active, slope, update = kept
        qkv_full, out_full, up_full, down_full = weights
        temporal = layer == 1
        mods = modulation[layer]
        grad_update, update_sums = update_back(grad_out, update, mods)
        if packed:
            down_g = gather_in(*down_grad(place, active, grad_update, seq, zs))
            down_g = down_g.reshape(rows, -1, d // seq).transpose(1, 0, 2).reshape(-1, d // seq)
        else:
            down_g = shed_natural(active, grad_update)
        inner_grad, up_sums, hidden_grad = feed_back(grad_update, slope, down_full, up_full)
        if packed:
            up_g = gather_in(*up_grad(place, hidden_two, inner_grad, seq, zs))
        else:
            up_g = shed_natural(hidden_two, inner_grad)
        middle_grad, branch_grad, branch_cut, attended_grad, middle_sums = middle_back(
            hidden_grad, middle, branch, grad_out, mods, out_full, cuts
        )
        qkv_grad, qkv_cut, qkv_sums = attention_back(
            qkv, attended_grad.reshape(shapes[layer] + (d,)), lse, temporal, cuts
        )
        qkv_grad = qkv_grad.reshape(n, 3 * d)
        stream_grad, stream_sums = stream_back(
            qkv_grad, qkv_full, x, middle_grad, mods, BF16 if temporal else F32
        )
        if packed:
            both = gather_in(
                *qkv_out_grad(
                    place, hidden, attended, qkv_cut.reshape(seq, n, -1), branch_cut, zs
                )
            )
            qkv_g, out_g = both[:, :own_columns], both[:, own_columns:]
        else:
            qkv_g = shed_natural(hidden, qkv_grad)
            out_g = shed_natural(attended, branch_grad)
        mod_grad = jnp.concatenate(
            [
                stream_sums[1:2],
                stream_sums[0:1],
                middle_sums[2:3],
                middle_sums[1:2],
                middle_sums[0:1],
                update_sums[0:1],
            ],
            axis=0,
        )
        bias_grad = jnp.concatenate(
            [
                qkv_sums[:, :d],
                qkv_sums[:, 2 * d :],
                middle_sums[3:4],
                update_sums[1:2],
                up_sums.reshape(-1, d),
            ],
            axis=0,
        )
        return stream_grad, mod_grad, bias_grad, (qkv_g, out_g, up_g, down_g)

    first_weights = fetch(0)
    second_weights = fetch(1)
    first_in = by_places(video_latents)
    second_go = swap_tokens(by_places(cotangent))
    first_out, first_kept, first_peak = forward(0, first_in, first_weights)
    second_out, second_kept, second_peak = forward(1, swap_tokens(first_out), second_weights)
    output_latents = by_frames(swap_tokens(second_out))

    peaks = lax.all_gather(jnp.stack([first_peak, second_peak]), ("clip", "seq"), axis=0)
    logit_peak = jnp.max(peaks, axis=0)
    column_index = lax.axis_index("seq") * own_columns + jnp.arange(own_columns, dtype=jnp.int32)
    head_of = column_index % d // (d // HEADS)
    head_match = (head_of[:, None] == jnp.arange(HEADS, dtype=jnp.int32)[None, :]).astype(F32)
    roots = jnp.sqrt(clip_limit / jnp.maximum(logit_peak, clip_limit))
    column_roots = jnp.sum(roots[:, None, :] * head_match[None, :, :], axis=-1)
    column_scale = jnp.where(column_index[None, :] < 2 * d, column_roots, 1.0)
    clipped_qkv = qkv_weight.astype(F32) * column_scale[:, None, :]

    second_grad, second_mod, second_bias, second_shed = backward(
        1, second_go, second_kept, second_weights
    )
    latents_grad, first_mod, first_bias, first_shed = backward(
        0, swap_tokens(second_grad), first_kept, first_weights
    )

    mod_grads = jnp.stack([first_mod, second_mod]).reshape(layers, clips, seq, -1)
    of_columns = lax.psum_scatter(
        mod_grads.transpose(2, 1, 0, 3), "seq", scatter_dimension=0, tiled=False
    )
    own_mod_grad = lax.all_to_all(of_columns, "clip", 0, 0, tiled=True)
    ada_bias_grad = jnp.sum(own_mod_grad, axis=0)
    rounded_mod = own_mod_grad.astype(BF16)
    ada_weight_grad = jnp.einsum("kd,klc->ldc", squashed, rounded_mod, preferred_element_type=F32)
    squash_part = jnp.einsum("klc,ldc->kd", rounded_mod, ada_weight, preferred_element_type=F32)
    bias_rows = first_bias.shape[0]
    summed = lax.psum(
        jnp.concatenate([first_bias, second_bias, squash_part], axis=0), ("clip", "seq")
    )
    bias_sums = summed[: 2 * bias_rows].reshape(layers, bias_rows, d)
    own_squash = lax.dynamic_slice_in_dim(summed[2 * bias_rows :], clip_index, 1, axis=0)
    silu_value, silu_pull = jax.vjp(jax.nn.silu, conditioning)
    conditioning_grad = silu_pull(own_squash)[0]
    return (
        output_latents,
        latents_grad.reshape(seq, frames, places // seq, d)
        .transpose(1, 0, 2, 3)
        .reshape(1, frames, places, d),
        conditioning_grad,
        ada_weight_grad,
        ada_bias_grad,
        jnp.stack([first_shed[0], second_shed[0]]),
        jnp.stack([first_shed[1], second_shed[1]]),
        jnp.stack([first_shed[2], second_shed[2]]),
        jnp.stack([first_shed[3], second_shed[3]]),
        bias_sums[:, :3],
        bias_sums[:, 4:].reshape(layers, ff),
        bias_sums[:, 3],
        clipped_qkv,
        logit_peak,
    )


def solution(mesh):
    return jax.shard_map(
        partial(on_device, clips=mesh.shape["clip"], seq=mesh.shape["seq"]),
        mesh=mesh,
        in_specs=(
            P("clip", "seq", None, None),
            P("clip", None),
            P(None, None, ("clip", "seq")),
            P(None, ("clip", "seq")),
            P(None, "clip", "seq"),
            P(None, "clip", "seq"),
            P(None, "clip", "seq"),
            P(None, "clip", "seq"),
            P(),
            P(),
            P(),
            P("clip", "seq", None, None),
        ),
        out_specs=(
            P("clip", "seq", None, None),
            P("clip", "seq", None, None),
            P("clip", None),
            P(None, None, ("clip", "seq")),
            P(None, ("clip", "seq")),
            P(None, "clip", "seq"),
            P(None, "clip", "seq"),
            P(None, "clip", "seq"),
            P(None, "clip", "seq"),
            P(),
            P(),
            P(),
            P(None, "clip", "seq"),
            P(),
        ),
        check_vma=False,
    )
```

time: 2770 us -> 1570 us (0.57)
  waiting for transfers between devices: 1220 us -> 637 us
  Pallas kernels: 0 us -> 575 us
  local copies, waits for them, and re-layouts: 546 us -> 53.7 us
  matrix products: 470 us -> 2.41 us
  blocking collectives: 360 us -> 144 us
  other arithmetic: 136 us -> 67.9 us
  starting transfers between devices: 17.6 us -> 67.9 us
    pallas_call x0 -> x32, Pallas kernels: none -> 575 us  [the longest x2 83.5 us: feed_back(): call(body, (ff // d, n // mt), [pl.BlockSpec((mt, d), lambda f, m: (m, 0)...]
    dot_general x39 -> x3, matrix products: 470 us -> 2.41 us  [the longest x1 1.77 us: on_device(): jnp.einsum('kd,klc->ldc', squashed, rounded_mod, preferred_element_type=F32)]
    unnamed x41 -> x15, waiting for transfers between devices: 425 us -> 24 us
    reduce_scatter x8 -> x6, waiting for transfers between devices: 490 us -> 122 us  [gather_in(): lax.psum_scatter(half.reshape(-1, d), 'seq', scatter_dimension=0, tiled=T...]
    ppermute x0 -> x36, waiting for transfers between devices: none -> 367 us  [hop(): return lax.ppermute(x, 'clip', [(i, i ^ distance) for i in range(count)])]
    slice x12 -> x27, local copies, waits for them, and re-layouts: 208 us -> 18.5 us  [the longest x12 11.2 us: gather_in(): part[step:]]
    all_gather x3 -> x2, blocking collectives: 284 us -> 113 us  [the longest x1 105 us: on_device(): lax.all_gather(jnp.stack([first_peak, second_peak]), ('clip', 'seq'), axi...]
    unnamed x310 -> x57, local copies, waits for them, and re-layouts: 122 us -> 7.53 us
  transfers between devices with their start and end apart: 36 -> 56, of which waited for: 24 -> 32; matrix products, arithmetic and copies ran while one was open for 27% -> 7% of each run, Pallas kernels for 0% -> 30%
where the time goes in v1:
time: 1570 us; the launch traced here: 1560 us
  waiting for transfers between devices  637 us (41%)
  Pallas kernels  575 us (37%)
  blocking collectives  144 us (9%)
  starting transfers between devices  67.9 us (4%)
  other arithmetic  67.9 us (4%)
  local copies, waits for them, and re-layouts  53.7 us (3%)
    ppermute x36, waiting for transfers between devices, hop(): return lax.ppermute(x, 'clip', [(i, i ^ distance) for i in range(count)])  367 us
    reduce_scatter x6, waiting for transfers between devices, gather_in(): lax.psum_scatter(half.reshape(-1, d), 'seq', scatter_dimension=0, tiled=T...  122 us
    all_gather x6, waiting for transfers between devices, spread_out(): own = lax.all_gather(blocks, 'seq', axis=0, tiled=False)  116 us
    all_gather x1, blocking collectives, on_device(): lax.all_gather(jnp.stack([first_peak, second_peak]), ('clip', 'seq'), axi...  105 us
    pallas_call x2, Pallas kernels, feed_back(): call(body, (ff // d, n // mt), [pl.BlockSpec((mt, d), lambda f, m: (m, 0)...  83.5 us
    pallas_call x2, Pallas kernels, up_forward(): call(body, (ff // ft, n // mt), [pl.BlockSpec((mt, d), lambda f, m: (m, 0...  53.3 us
    pallas_call x2, Pallas kernels, attention_back(): call(body, (g,), [pl.BlockSpec((a, 1, p, wide), lambda i: (0, i, 0, 0)),...  51.9 us
    pallas_call x2, Pallas kernels, qkv_out_grad(): call(body, (seq,), [whole((n, d)), whole((n, d)), pl.BlockSpec((1, n, wa)...  46.7 us
  transfers between devices with their start and end apart: 56, of which 32 were waited for; matrix products, arithmetic and copies ran while one was open for 7% of the time, Pallas kernels for 30%

profile of v1, /device:TPU:0, one launch (start us, length us, event | category | flops | bytes accessed | tf_op | source)
XLA Modules:
  0.0 1563.0 jit_solution(15794009036481608532)
XLA Ops:
  23.3 28.5 %collective-permute-done.1 = bf16[2,144,1152]{2,1,0:T(8,128)(2,1)S(1)} collective-permute-done((bf16[2,144,1152]{2,1,0:T(8,128)(2,1)S(1)}, bf16[2,144,1152]{2,1,0:T(8,128)(2,1)S(1)}, u32[]{:S(2)}, u32[]{:S(2)}) %collective-permute-start.1) | collective-permute-done | bytes 663584 | tf_op jit(solution)/shard_map/ppermute | solution.py:747
  65.2 28.8 %collective-permute-done.4 = bf16[2,144,1152]{2,1,0:T(8,128)(2,1)S(1)} collective-permute-done((bf16[2,144,1152]{2,1,0:T(8,128)(2,1)S(1)}, bf16[2,144,1152]{2,1,0:T(8,128)(2,1)S(1)}, u32[]{:S(2)}, u32[]{:S(2)}) %collective-permute-start.4) | collective-permute-done | bytes 663584 | tf_op jit(solution)/shard_map/ppermute | solution.py:747
  109.4 28.8 %collective-permute-done.7 = bf16[2,144,1152]{2,1,0:T(8,128)(2,1)S(1)} collective-permute-done((bf16[2,144,1152]{2,1,0:T(8,128)(2,1)S(1)}, bf16[2,144,1152]{2,1,0:T(8,128)(2,1)S(1)}, u32[]{:S(2)}, u32[]{:S(2)}) %collective-permute-start.7) | collective-permute-done | bytes 663584 | tf_op jit(solution)/shard_map/ppermute | solution.py:747
  151.8 28.7 %collective-permute-done.10 = bf16[2,144,1152]{2,1,0:T(8,128)(2,1)S(1)} collective-permute-done((bf16[2,144,1152]{2,1,0:T(8,128)(2,1)S(1)}, bf16[2,144,1152]{2,1,0:T(8,128)(2,1)S(1)}, u32[]{:S(2)}, u32[]{:S(2)}) %collective-permute-start.10) | collective-permute-done | bytes 663584 | tf_op jit(solution)/shard_map/ppermute | solution.py:747
  194.1 28.7 %collective-permute-done.13 = bf16[2,144,1152]{2,1,0:T(8,128)(2,1)S(1)} collective-permute-done((bf16[2,144,1152]{2,1,0:T(8,128)(2,1)S(1)}, bf16[2,144,1152]{2,1,0:T(8,128)(2,1)S(1)}, u32[]{:S(2)}, u32[]{:S(2)}) %collective-permute-start.13) | collective-permute-done | bytes 663584 | tf_op jit(solution)/shard_map/ppermute | solution.py:747
  237.1 28.8 %collective-permute-done.16 = bf16[2,144,1152]{2,1,0:T(8,128)(2,1)S(1)} collective-permute-done((bf16[2,144,1152]{2,1,0:T(8,128)(2,1)S(1)}, bf16[2,144,1152]{2,1,0:T(8,128)(2,1)S(1)}, u32[]{:S(2)}, u32[]{:S(2)}) %collective-permute-start.16) | collective-permute-done | bytes 663584 | tf_op jit(solution)/shard_map/ppermute | solution.py:747
  267.9 31.2 %all-gather.8 = f32[8,1,1152]{2,1,0:T(1,128)S(1)} all-gather(f32[1,1,1152]{2,1,0:T(1,128)S(1)} %bitcast.211), channel_id=1, replica_groups=mesh['clip'=8,'seq'=4] {'clip'}, dimensions={0}, use_global_device_ids=true | all-gather | bytes 41472 | tf_op jit(solution)/shard_map/all_gather | solution.py:778
  320.4 52.5 %all-gather.25.cloned.1.call-done = bf16[16,144,1152]{2,1,0:T(8,128)(2,1)} async-done(((bf16[4,144,1152]{2,1,0:T(8,128)(2,1)}), bf16[16,144,1152]{2,1,0:T(8,128)(2,1)}) %all-gather.25.cloned.1.call-update) | async-done | bytes 5308432 | tf_op jit(solution)/shard_map/all_gather | solution.py:795
  373.0 63.7 %all-gather.27.cloned.1.call-done = bf16[16,144,1152]{2,1,0:T(8,128)(2,1)} async-done(((bf16[4,144,1152]{2,1,0:T(8,128)(2,1)}), bf16[16,144,1152]{2,1,0:T(8,128)(2,1)}) %all-gather.27.cloned.1.call-update) | async-done | bytes 5308432 | tf_op jit(solution)/shard_map/all_gather | solution.py:795
  437.3 10.0 shard_map.227
  456.3 10.0 shard_map.233.w_ref.wd_ref
  466.3 16.5 %shard_map.228 = (bf16[1024,1152]{1,0:T(8,128)(2,1)}, bf16[1024,3456]{1,0:T(8,128)(2,1)}) custom-call(bf16[1024,1152]{1,0:T(8,128)(2,1)} %bitcast.196, f32[8,1152]{1,0:T(8,128)} %get-tuple-element.245.mod_ref, bf16[1152,3456]{1,0:T(8,128)(2,1)} %get-tuple-element.82.w_ref, f32[1,3456]{1,0:T(1,128)} %broadcast_in_dim.32.b_ref), custom_call_target="tpu_custom_call" | custom-call | flops 8153726976 | bytes 19759104 | tf_op jit(solution)/shard_map/pallas_call | solution.py:75
  482.8 12.9 shard_map.229
  495.7 9.1 shard_map.230
  504.8 26.6 %shard_map.232 = (bf16[1024,4608]{1,0:T(8,128)(2,1)}, bf16[1024,4608]{1,0:T(8,128)(2,1)}) custom-call(bf16[1024,1152]{1,0:T(8,128)(2,1)} %get-tuple-element.86.hid_ref, bf16[1152,4608]{1,0:T(8,128)(2,1)} %shard_map.231.w_ref.wu_ref, f32[1,4608]{1,0:T(1,128)} %get-tuple-element.263.b_ref), custom_call_target="tpu_custom_call" | custom-call | flops 10871635968 | bytes 31850496 | tf_op jit(solution)/shard_map/pallas_call | solution.py:202
  531.4 22.5 %shard_map.234 = (bf16[1024,1152]{1,0:T(8,128)(2,1)}, bf16[1024,1152]{1,0:T(8,128)(2,1)}) custom-call(bf16[1024,4608]{1,0:T(8,128)(2,1)} %get-tuple-element.87.act_ref, f32[1024,1152]{1,0:T(8,128)} %get-tuple-element.88.mid_ref, f32[8,1152]{1,0:T(8,128)} %get-tuple-element.245.mod_ref, bf16[4608,1152]{1,0:T(8,128)(2,1)} %shard_map.233.w_ref.wd_ref, ...), custom_call_target="tpu_custom_call" | custom-call | flops 10871635968 | bytes 29491200 | tf_op jit(solution)/shard_map/pallas_call | solution.py:243
  560.7 9.7 shard_map.235
  579.3 10.0 shard_map.241.w_ref.wd_ref
  593.5 16.5 %shard_map.236 = (bf16[1024,1152]{1,0:T(8,128)(2,1)}, bf16[1024,3456]{1,0:T(8,128)(2,1)}) custom-call(bf16[1024,1152]{1,0:T(8,128)(2,1)} %bitcast.22.x_ref, f32[8,1152]{1,0:T(8,128)} %get-tuple-element.244.mod_ref, bf16[1152,3456]{1,0:T(8,128)(2,1)} %get-tuple-element.90.w_ref, f32[1,3456]{1,0:T(1,128)} %broadcast_in_dim.34.b_ref), custom_call_target="tpu_custom_call" | custom-call | flops 8153726976 | bytes 19759104 | tf_op jit(solution)/shard_map/pallas_call | solution.py:75
  610.0 12.8 shard_map.237
  622.9 9.2 shard_map.238
  632.0 26.7 %shard_map.240 = (bf16[1024,4608]{1,0:T(8,128)(2,1)}, bf16[1024,4608]{1,0:T(8,128)(2,1)}) custom-call(bf16[1024,1152]{1,0:T(8,128)(2,1)} %get-tuple-element.94.hid_ref, bf16[1152,4608]{1,0:T(8,128)(2,1)} %shard_map.239.w_ref.wu_ref, f32[1,4608]{1,0:T(1,128)} %get-tuple-element.262.b_ref), custom_call_target="tpu_custom_call" | custom-call | flops 10871635968 | bytes 31850496 | tf_op jit(solution)/shard_map/pallas_call | solution.py:202
  658.7 22.0 %shard_map.242 = (bf16[1024,1152]{1,0:T(8,128)(2,1)}, bf16[1024,1152]{1,0:T(8,128)(2,1)}) custom-call(bf16[1024,4608]{1,0:T(8,128)(2,1)} %get-tuple-element.95.act_ref, f32[1024,1152]{1,0:T(8,128)} %get-tuple-element.96.mid_ref, f32[8,1152]{1,0:T(8,128)} %get-tuple-element.244.mod_ref, bf16[4608,1152]{1,0:T(8,128)(2,1)} %shard_map.241.w_ref.wd_ref, ...), custom_call_target="tpu_custom_call" | custom-call | flops 10871635968 | bytes 29491200 | tf_op jit(solution)/shard_map/pallas_call | solution.py:243
  686.8 41.9 %shard_map.244 = (bf16[1024,4608]{1,0:T(8,128)(2,1)}, f32[1,4608]{1,0:T(1,128)}, f32[1024,1152]{1,0:T(8,128)}) custom-call(bf16[1024,1152]{1,0:T(8,128)(2,1)} %get-tuple-element.99.gu_ref, bf16[1024,4608]{1,0:T(8,128)(2,1)} %get-tuple-element.100.slope_ref, bf16[4608,1152]{1,0:T(8,128)(2,1)} %shard_map.241.w_ref.wd_ref, ...), custom_call_target="tpu_custom_call" | custom-call | flops 21743271936 | bytes 47185920 | tf_op jit(solution)/shard_map/pallas_call | solution.py:464
  728.7 13.5 shard_map.245
  742.2 26.0 %shard_map.246 = (bf16[16,4,16,3456]{3,2,1,0:T(8,128)(2,1)}, bf16[4,16,4,16,864]{4,3,2,1,0:T(8,128)(2,1)}, f32[1,3456]{1,0:T(1,128)}) custom-call(bf16[16,4,16,3456]{3,2,1,0:T(8,128)(2,1)} %bitcast.223, bf16[16,4,16,1152]{3,2,1,0:T(8,128)(2,1)} %bitcast.217, f32[4,16,256]{2,1,0:T(8,128)} %get-tuple-element.104.lse_ref), custom_call_target="tpu_custom_call" | custom-call | flops 12884901888 | bytes 23592960 | tf_op jit(solution)/shard_map/pallas_call | solution.py:580
  768.2 21.0 %shard_map.247 = (bf16[1024,1152]{1,0:T(8,128)(2,1)}, f32[8,1152]{1,0:T(8,128)}) custom-call(bf16[1024,3456]{1,0:T(8,128)(2,1)} %bitcast.224, bf16[1152,3456]{1,0:T(8,128)(2,1)} %get-tuple-element.90.w_ref, bf16[1024,1152]{1,0:T(8,128)(2,1)} %bitcast.22.x_ref, f32[1024,1152]{1,0:T(8,128)} %get-tuple-element.106.gmid_ref, f32[8,1152]{1,0:T(8,128)} %get-tuple-element.244.mod_ref), custom_call_target="tpu_custom_call" | custom-call | flops 8153726976 | bytes 26836992 | tf_op jit(solution)/shard_map/pallas_call | solution.py:635
  795.4 23.2 %shard_map.254 = (bf16[4,4,144,1152]{3,2,1,0:T(8,128)(2,1)}, bf16[4,4,144,1152]{3,2,1,0:T(8,128)(2,1)}) custom-call(s32[2]{0:T(128)} %pad_add_fusion.place_ref, bf16[1024,1152]{1,0:T(8,128)(2,1)} %get-tuple-element.133.hid_ref, bf16[1024,1152]{1,0:T(8,128)(2,1)} %bitcast.229, bf16[4,1024,864]{2,1,0:T(8,128)(2,1)} %bitcast.219, ...), custom_call_target="tpu_custom_call" | custom-call | flops 10871635968 | bytes 20054016 | tf_op jit(solution)/shard_map/pallas_call | solution.py:410
  827.0 41.6 %shard_map.249 = (bf16[1024,4608]{1,0:T(8,128)(2,1)}, f32[1,4608]{1,0:T(1,128)}, f32[1024,1152]{1,0:T(8,128)}) custom-call(bf16[1024,1152]{1,0:T(8,128)(2,1)} %get-tuple-element.109.gu_ref, bf16[1024,4608]{1,0:T(8,128)(2,1)} %get-tuple-element.110.slope_ref, bf16[4608,1152]{1,0:T(8,128)(2,1)} %shard_map.233.w_ref.wd_ref, ...), custom_call_target="tpu_custom_call" | custom-call | flops 21743271936 | bytes 47185920 | tf_op jit(solution)/shard_map/pallas_call | solution.py:464
  868.7 13.6 shard_map.250
  883.1 25.9 %shard_map.251 = (bf16[4,4,64,3456]{3,2,1,0:T(8,128)(2,1)}, bf16[4,4,4,64,864]{4,3,2,1,0:T(8,128)(2,1)}, f32[1,3456]{1,0:T(1,128)}) custom-call(bf16[4,4,64,3456]{3,2,1,0:T(8,128)(2,1)} %bitcast.221, bf16[4,4,64,1152]{3,2,1,0:T(8,128)(2,1)} %bitcast.216, f32[4,16,256]{2,1,0:T(8,128)} %get-tuple-element.114.lse_ref), custom_call_target="tpu_custom_call" | custom-call | flops 12884901888 | bytes 23592960 | tf_op jit(solution)/shard_map/pallas_call | solution.py:580
  909.0 21.0 %shard_map.252 = (f32[1024,1152]{1,0:T(8,128)}, f32[8,1152]{1,0:T(8,128)}) custom-call(bf16[1024,3456]{1,0:T(8,128)(2,1)} %bitcast.225, bf16[1152,3456]{1,0:T(8,128)(2,1)} %get-tuple-element.82.w_ref, bf16[1024,1152]{1,0:T(8,128)(2,1)} %bitcast.198, f32[1024,1152]{1,0:T(8,128)} %get-tuple-element.116.gmid_ref, f32[8,1152]{1,0:T(8,128)} %get-tuple-element.245.mod_ref), custom_call_target="tpu_custom_call" | custom-call | flops 8153726976 | bytes 26836992 | tf_op jit(solution)/shard_map/pallas_call | solution.py:635
  931.9 23.7 %reduce-scatter.22.cloned.1.call-done = f32[1,8,2,216]{3,1,2,0:T(8,128)} async-done(((f32[4,8,2,216]{3,1,2,0:T(8,128)}), f32[1,8,2,216]{3,1,2,0:T(8,128)}) %reduce-scatter.22.cloned.1.call-update) | async-done | bytes 13840
  977.3 19.2 %shard_map.256 = (bf16[4,4,144,1152]{3,2,1,0:T(8,128)(2,1)}, bf16[4,4,144,1152]{3,2,1,0:T(8,128)(2,1)}) custom-call(s32[2]{0:T(128)} %pad_add_fusion.place_ref, bf16[1024,1152]{1,0:T(8,128)(2,1)} %get-tuple-element.94.hid_ref, bf16[1024,4608]{1,0:T(8,128)(2,1)} %get-tuple-element.141.gi_ref), custom_call_target="tpu_custom_call" | custom-call | flops 10871635968 | bytes 22413312 | tf_op jit(solution)/shard_map/pallas_call | solution.py:369
  996.5 9.0 collective-permute-done.27
  1011.7 21.9 %shard_map.258 = (bf16[4,4,144,1152]{3,2,1,0:T(8,128)(2,1)}, bf16[4,4,144,1152]{3,2,1,0:T(8,128)(2,1)}) custom-call(s32[2]{0:T(128)} %pad_add_fusion.place_ref, bf16[1024,4608]{1,0:T(8,128)(2,1)} %get-tuple-element.95.act_ref, bf16[1024,1152]{1,0:T(8,128)(2,1)} %get-tuple-element.99.gu_ref), custom_call_target="tpu_custom_call" | custom-call | flops 10871635968 | bytes 22413312 | tf_op jit(solution)/shard_map/pallas_call | solution.py:321
  1048.8 23.5 %shard_map.253 = (bf16[4,4,144,1152]{3,2,1,0:T(8,128)(2,1)}, bf16[4,4,144,1152]{3,2,1,0:T(8,128)(2,1)}) custom-call(s32[2]{0:T(128)} %pad_add_fusion.place_ref, bf16[1024,1152]{1,0:T(8,128)(2,1)} %get-tuple-element.128.hid_ref, bf16[1024,1152]{1,0:T(8,128)(2,1)} %bitcast.227, bf16[4,1024,864]{2,1,0:T(8,128)(2,1)} %bitcast.218, ...), custom_call_target="tpu_custom_call" | custom-call | flops 10871635968 | bytes 20054016 | tf_op jit(solution)/shard_map/pallas_call | solution.py:410
  1087.6 19.0 %shard_map.255 = (bf16[4,4,144,1152]{3,2,1,0:T(8,128)(2,1)}, bf16[4,4,144,1152]{3,2,1,0:T(8,128)(2,1)}) custom-call(s32[2]{0:T(128)} %pad_add_fusion.place_ref, bf16[1024,1152]{1,0:T(8,128)(2,1)} %get-tuple-element.86.hid_ref, bf16[1024,4608]{1,0:T(8,128)(2,1)} %get-tuple-element.138.gi_ref), custom_call_target="tpu_custom_call" | custom-call | flops 10871635968 | bytes 22413312 | tf_op jit(solution)/shard_map/pallas_call | solution.py:369
  1122.0 22.1 %shard_map.257 = (bf16[4,4,144,1152]{3,2,1,0:T(8,128)(2,1)}, bf16[4,4,144,1152]{3,2,1,0:T(8,128)(2,1)}) custom-call(s32[2]{0:T(128)} %pad_add_fusion.place_ref, bf16[1024,4608]{1,0:T(8,128)(2,1)} %get-tuple-element.87.act_ref, bf16[1024,1152]{1,0:T(8,128)(2,1)} %get-tuple-element.109.gu_ref), custom_call_target="tpu_custom_call" | custom-call | flops 10871635968 | bytes 22413312 | tf_op jit(solution)/shard_map/pallas_call | solution.py:321
  1163.9 105.0 %all-gather.9 = f32[32,2,16]{2,1,0:T(2,128)S(1)} all-gather(f32[1,2,16]{2,1,0:T(2,128)S(1)} %maximum_bitcast_fusion.3), channel_id=9, replica_groups=mesh['clip'=8,'seq'=4] {'clip','seq'}, dimensions={0}, use_global_device_ids=true | all-gather | bytes 4224 | tf_op jit(solution)/shard_map/all_gather | solution.py:939
  1291.1 17.3 %reduce-scatter.20.cloned.1.call-done = bf16[576,1152]{1,0:T(8,128)(2,1)} async-done(((bf16[2304,1152]{1,0:T(8,128)(2,1)}), bf16[576,1152]{1,0:T(8,128)(2,1)}) %reduce-scatter.20.cloned.1.call-update) | async-done | bytes 1327120 | tf_op jit(solution)/shard_map/reduce_scatter | solution.py:820
  1312.3 24.4 %collective-permute-done.22 = bf16[2,144,1152]{2,1,0:T(8,128)(2,1)} collective-permute-done((bf16[2,144,1152]{2,1,0:T(8,128)(2,1)}, bf16[2,144,1152]{2,1,0:T(8,128)(2,1)}, u32[]{:S(2)}, u32[]{:S(2)}) %collective-permute-start.22) | collective-permute-done | bytes 663584 | tf_op jit(solution)/shard_map/ppermute | solution.py:747
  1338.1 12.9 collective-permute-done.28
  1352.4 12.6 collective-permute-done.34
  1372.2 14.1 collective-permute-done.35
  1395.8 43.1 %reduce-scatter.14.cloned.1.call-done = bf16[576,1152]{1,0:T(8,128)(2,1)} async-done(((bf16[2304,1152]{1,0:T(8,128)(2,1)}), bf16[576,1152]{1,0:T(8,128)(2,1)}) %reduce-scatter.14.cloned.1.call-update) | async-done | bytes 1327120 | tf_op jit(solution)/shard_map/reduce_scatter | solution.py:820
  1442.7 61.3 %reduce-scatter.18.cloned.1.call-done = bf16[576,1152]{1,0:T(8,128)(2,1)} async-done(((bf16[2304,1152]{1,0:T(8,128)(2,1)}), bf16[576,1152]{1,0:T(8,128)(2,1)}) %reduce-scatter.18.cloned.1.call-update) | async-done | bytes 1327120 | tf_op jit(solution)/shard_map/reduce_scatter | solution.py:820
  1513.4 24.0 %collective-permute-done.31 = bf16[2,144,1152]{2,1,0:T(8,128)(2,1)S(1)} collective-permute-done((bf16[2,144,1152]{2,1,0:T(8,128)(2,1)S(1)}, bf16[2,144,1152]{2,1,0:T(8,128)(2,1)S(1)}, u32[]{:S(2)}, u32[]{:S(2)}) %collective-permute-start.31) | collective-permute-done | bytes 663584 | tf_op jit(solution)/shard_map/ppermute | solution.py:747
  (290 shorter events, 333.0 us)
Async XLA Ops:
  7.2 260.0 %all-gather.17.cloned.1.call-start = ((), (), s32[]{:S(2)}) async-start(), calls=%async_computation.20 | async-start | bytes 6635520 | tf_op jit(solution)/shard_map/all_gather | solution.py:795
  9.5 10.9 collective-permute-start
  20.5 31.3 %collective-permute-start.1 = (bf16[2,144,1152]{2,1,0:T(8,128)(2,1)S(1)}, bf16[2,144,1152]{2,1,0:T(8,128)(2,1)S(1)}, u32[]{:S(2)}, u32[]{:S(2)}) collective-permute-start(bf16[2,144,1152]{2,1,0:T(8,128)(2,1)S(1)} %pad_maximum_fusion.9), channel_id=1, source_target_pairs={{0,16},{4,20},{8,24},{12,28},{16,0},{20,4},{24,8},{28,12},{1,17},{... | collective-permute-start | bytes 1990664 | tf_op jit(solution)/shard_map/ppermute | solution.py:747
  53.0 214.3 %all-gather.19.cloned.1.call-start = ((), (), s32[]{:S(2)}) async-start(), calls=%async_computation.21 | async-start | bytes 6635520 | tf_op jit(solution)/shard_map/all_gather | solution.py:795
  62.1 31.9 %collective-permute-start.4 = (bf16[2,144,1152]{2,1,0:T(8,128)(2,1)S(1)}, bf16[2,144,1152]{2,1,0:T(8,128)(2,1)S(1)}, u32[]{:S(2)}, u32[]{:S(2)}) collective-permute-start(bf16[2,144,1152]{2,1,0:T(8,128)(2,1)S(1)} %pad_maximum_fusion.10), channel_id=1, source_target_pairs={{0,16},{4,20},{8,24},{12,28},{16,0},{20,4},{24,8},{28,12},{1,17},{... | collective-permute-start | bytes 1990664 | tf_op jit(solution)/shard_map/ppermute | solution.py:747
  95.2 172.6 %all-gather.21.cloned.1.call-start = ((), (), s32[]{:S(2)}) async-start(), calls=%async_computation.22 | async-start | bytes 6635520 | tf_op jit(solution)/shard_map/all_gather | solution.py:795
  106.2 32.1 %collective-permute-start.7 = (bf16[2,144,1152]{2,1,0:T(8,128)(2,1)S(1)}, bf16[2,144,1152]{2,1,0:T(8,128)(2,1)S(1)}, u32[]{:S(2)}, u32[]{:S(2)}) collective-permute-start(bf16[2,144,1152]{2,1,0:T(8,128)(2,1)S(1)} %pad_maximum_fusion.11), channel_id=1, source_target_pairs={{0,16},{4,20},{8,24},{12,28},{16,0},{20,4},{24,8},{28,12},{1,17},{... | collective-permute-start | bytes 1990664 | tf_op jit(solution)/shard_map/ppermute | solution.py:747
  139.5 180.8 %all-gather.23.cloned.1.call-start = ((), (), s32[]{:S(2)}) async-start(), calls=%async_computation.23 | async-start | bytes 6635520 | tf_op jit(solution)/shard_map/all_gather | solution.py:795
  148.6 31.9 %collective-permute-start.10 = (bf16[2,144,1152]{2,1,0:T(8,128)(2,1)S(1)}, bf16[2,144,1152]{2,1,0:T(8,128)(2,1)S(1)}, u32[]{:S(2)}, u32[]{:S(2)}) collective-permute-start(bf16[2,144,1152]{2,1,0:T(8,128)(2,1)S(1)} %pad_maximum_fusion.12), channel_id=1, source_target_pairs={{0,16},{4,20},{8,24},{12,28},{16,0},{20,4},{24,8},{28,12},{1,17},{... | collective-permute-start | bytes 1990664 | tf_op jit(solution)/shard_map/ppermute | solution.py:747
  181.8 191.2 %all-gather.25.cloned.1.call-start = ((), (), s32[]{:S(2)}) async-start(), calls=%async_computation.24 | async-start | bytes 6635520 | tf_op jit(solution)/shard_map/all_gather | solution.py:795
  190.8 32.0 %collective-permute-start.13 = (bf16[2,144,1152]{2,1,0:T(8,128)(2,1)S(1)}, bf16[2,144,1152]{2,1,0:T(8,128)(2,1)S(1)}, u32[]{:S(2)}, u32[]{:S(2)}) collective-permute-start(bf16[2,144,1152]{2,1,0:T(8,128)(2,1)S(1)} %pad_maximum_fusion.13), channel_id=1, source_target_pairs={{0,16},{4,20},{8,24},{12,28},{16,0},{20,4},{24,8},{28,12},{1,17},{... | collective-permute-start | bytes 1990664 | tf_op jit(solution)/shard_map/ppermute | solution.py:747
  224.1 212.6 %all-gather.27.cloned.1.call-start = ((), (), s32[]{:S(2)}) async-start(), calls=%async_computation.25 | async-start | bytes 6635520 | tf_op jit(solution)/shard_map/all_gather | solution.py:795
  233.9 32.0 %collective-permute-start.16 = (bf16[2,144,1152]{2,1,0:T(8,128)(2,1)S(1)}, bf16[2,144,1152]{2,1,0:T(8,128)(2,1)S(1)}, u32[]{:S(2)}, u32[]{:S(2)}) collective-permute-start(bf16[2,144,1152]{2,1,0:T(8,128)(2,1)S(1)} %pad_maximum_fusion.14), channel_id=1, source_target_pairs={{0,16},{4,20},{8,24},{12,28},{16,0},{20,4},{24,8},{28,12},{1,17},{... | collective-permute-start | bytes 1990664 | tf_op jit(solution)/shard_map/ppermute | solution.py:747
  267.2 169.4 %collective-permute-start.2 = (bf16[4,4,144,1152]{3,2,1,0:T(8,128)(2,1)}, bf16[4,4,144,1152]{3,2,1,0:T(8,128)(2,1)}, u32[]{:S(2)}, u32[]{:S(2)}) collective-permute-start(bf16[4,4,144,1152]{3,2,1,0:T(8,128)(2,1)} %bitcast.169), channel_id=1, source_target_pairs={{0,4},{4,0},{8,12},{12,8},{16,20},{20,16},{24,28},{28,24},{1,5},{5... | collective-permute-start | bytes 15925256 | tf_op jit(solution)/shard_map/ppermute | solution.py:747
  267.3 180.0 %collective-permute-start.5 = (bf16[4,4,144,1152]{3,2,1,0:T(8,128)(2,1)}, bf16[4,4,144,1152]{3,2,1,0:T(8,128)(2,1)}, u32[]{:S(2)}, u32[]{:S(2)}) collective-permute-start(bf16[4,4,144,1152]{3,2,1,0:T(8,128)(2,1)} %bitcast.173), channel_id=1, source_target_pairs={{0,4},{4,0},{8,12},{12,8},{16,20},{20,16},{24,28},{28,24},{1,5},{5... | collective-permute-start | bytes 15925256 | tf_op jit(solution)/shard_map/ppermute | solution.py:747
  267.8 188.5 %collective-permute-start.8 = (bf16[4,4,144,1152]{3,2,1,0:T(8,128)(2,1)}, bf16[4,4,144,1152]{3,2,1,0:T(8,128)(2,1)}, u32[]{:S(2)}, u32[]{:S(2)}) collective-permute-start(bf16[4,4,144,1152]{3,2,1,0:T(8,128)(2,1)} %bitcast.175), channel_id=1, source_target_pairs={{0,4},{4,0},{8,12},{12,8},{16,20},{20,16},{24,28},{28,24},{1,5},{5... | collective-permute-start | bytes 15925256 | tf_op jit(solution)/shard_map/ppermute | solution.py:747
  300.7 11.2 all-to-all-start
  320.3 240.4 %collective-permute-start.11 = (bf16[4,4,144,1152]{3,2,1,0:T(8,128)(2,1)}, bf16[4,4,144,1152]{3,2,1,0:T(8,128)(2,1)}, u32[]{:S(2)}, u32[]{:S(2)}) collective-permute-start(bf16[4,4,144,1152]{3,2,1,0:T(8,128)(2,1)} %bitcast.171), channel_id=1, source_target_pairs={{0,4},{4,0},{8,12},{12,8},{16,20},{20,16},{24,28},{28,24},{1,5},{5... | collective-permute-start | bytes 15925256 | tf_op jit(solution)/shard_map/ppermute | solution.py:747
  373.0 197.5 %collective-permute-start.14 = (bf16[4,4,144,1152]{3,2,1,0:T(8,128)(2,1)}, bf16[4,4,144,1152]{3,2,1,0:T(8,128)(2,1)}, u32[]{:S(2)}, u32[]{:S(2)}) collective-permute-start(bf16[4,4,144,1152]{3,2,1,0:T(8,128)(2,1)} %bitcast.177), channel_id=1, source_target_pairs={{0,4},{4,0},{8,12},{12,8},{16,20},{20,16},{24,28},{28,24},{1,5},{5... | collective-permute-start | bytes 15925256 | tf_op jit(solution)/shard_map/ppermute | solution.py:747
  436.7 142.7 %collective-permute-start.17 = (bf16[4,4,144,1152]{3,2,1,0:T(8,128)(2,1)}, bf16[4,4,144,1152]{3,2,1,0:T(8,128)(2,1)}, u32[]{:S(2)}, u32[]{:S(2)}) collective-permute-start(bf16[4,4,144,1152]{3,2,1,0:T(8,128)(2,1)} %bitcast.179), channel_id=1, source_target_pairs={{0,4},{4,0},{8,12},{12,8},{16,20},{20,16},{24,28},{28,24},{1,5},{5... | collective-permute-start | bytes 15925256 | tf_op jit(solution)/shard_map/ppermute | solution.py:747
  553.9 35.5 %all-to-all-start.1 = ((bf16[4,256,1152]{2,1,0:T(8,128)(2,1)}), bf16[4,256,1152]{2,1,0:T(8,128)(2,1)}, u32[]{:S(2)}, u32[]{:S(2)}) async-start(bf16[4,256,1152]{2,1,0:T(8,128)(2,1)} %bitcast.201), calls=%async_computation.1 | async-start | bytes 4718592 | tf_op jit(solution)/shard_map/all_to_all | solution.py:837
  589.4 91.4 %all-to-all-start.3 = ((bf16[4,256,1152]{2,1,0:T(8,128)(2,1)}), bf16[4,256,1152]{2,1,0:T(8,128)(2,1)S(1)}, u32[]{:S(2)}, u32[]{:S(2)}) async-start(bf16[4,256,1152]{2,1,0:T(8,128)(2,1)} %bitcast.167), calls=%async_computation.3 | async-start | bytes 4718592 | tf_op jit(solution)/shard_map/all_to_all | solution.py:837
  789.2 31.8 %all-to-all-start.4 = ((bf16[4,256,1152]{2,1,0:T(8,128)(2,1)}), bf16[4,256,1152]{2,1,0:T(8,128)(2,1)S(1)}, u32[]{:S(2)}, u32[]{:S(2)}) async-start(bf16[4,256,1152]{2,1,0:T(8,128)(2,1)} %bitcast.200), calls=%async_computation.4 | async-start | bytes 4718592 | tf_op jit(solution)/shard_map/all_to_all | solution.py:837
  793.5 162.1 %reduce-scatter.22.cloned.1.call-start = ((), (), s32[]{:S(2)}) async-start(), calls=%async_computation.26 | async-start | bytes 81920
  818.6 150.9 %collective-permute-start.21 = (bf16[4,4,144,1152]{3,2,1,0:T(8,128)(2,1)}, bf16[4,4,144,1152]{3,2,1,0:T(8,128)(2,1)}, u32[]{:S(2)}, u32[]{:S(2)}) collective-permute-start(bf16[4,4,144,1152]{3,2,1,0:T(8,128)(2,1)} %get-tuple-element.137), channel_id=1, source_target_pairs={{0,4},{4,0},{8,12},{12,8},{16,20},{20,16},{24,28},{28,24},{1,5},{5... | collective-permute-start | bytes 15925256 | tf_op jit(solution)/shard_map/ppermute | solution.py:747
  956.9 10.3 all-to-all-start.5
  961.5 318.7 %all-reduce.4.cloned.1.call-start = ((), (), s32[]{:S(2)}) async-start(), calls=%async_computation.13 | async-start | bytes 221184 | tf_op jit(solution)/shard_map/psum | solution.py:966
  969.4 315.0 %reduce-scatter.12.cloned.1.call-start = ((), (), s32[]{:S(2)}) async-start(), calls=%async_computation.15 | async-start | bytes 6635520 | tf_op jit(solution)/shard_map/reduce_scatter | solution.py:820
  977.3 309.5 %reduce-scatter.16.cloned.1.call-start = ((), (), s32[]{:S(2)}) async-start(), calls=%async_computation.17 | async-start | bytes 6635520 | tf_op jit(solution)/shard_map/reduce_scatter | solution.py:820
  1011.7 296.8 %reduce-scatter.20.cloned.1.call-start = ((), (), s32[]{:S(2)}) async-start(), calls=%async_computation.19 | async-start | bytes 6635520 | tf_op jit(solution)/shard_map/reduce_scatter | solution.py:820
  1033.6 9.0 collective-permute-start.33
  1048.8 344.6 %reduce-scatter.10.cloned.1.call-start = ((), (), s32[]{:S(2)}) async-start(), calls=%async_computation.14 | async-start | bytes 6635520 | tf_op jit(solution)/shard_map/reduce_scatter | solution.py:820
  1072.3 9.0 collective-permute-start.18
  1087.6 351.3 %reduce-scatter.14.cloned.1.call-start = ((), (), s32[]{:S(2)}) async-start(), calls=%async_computation.16 | async-start | bytes 6635520 | tf_op jit(solution)/shard_map/reduce_scatter | solution.py:820
  1121.9 382.1 %reduce-scatter.18.cloned.1.call-start = ((), (), s32[]{:S(2)}) async-start(), calls=%async_computation.18 | async-start | bytes 6635520 | tf_op jit(solution)/shard_map/reduce_scatter | solution.py:820
  1144.1 9.6 collective-permute-start.30
  1160.1 111.1 %all-to-all-start.2 = ((bf16[4,256,1152]{2,1,0:T(8,128)(2,1)}), bf16[4,256,1152]{2,1,0:T(8,128)(2,1)S(1)}, u32[]{:S(2)}, u32[]{:S(2)}) async-start(bf16[4,256,1152]{2,1,0:T(8,128)(2,1)} %bitcast.195), calls=%async_computation.2 | async-start | bytes 4718592 | tf_op jit(solution)/shard_map/all_to_all | solution.py:837
  1286.7 50.0 %collective-permute-start.22 = (bf16[2,144,1152]{2,1,0:T(8,128)(2,1)}, bf16[2,144,1152]{2,1,0:T(8,128)(2,1)}, u32[]{:S(2)}, u32[]{:S(2)}) collective-permute-start(bf16[2,144,1152]{2,1,0:T(8,128)(2,1)} %bitcast.66), channel_id=1, source_target_pairs={{0,16},{4,20},{8,24},{12,28},{16,0},{20,4},{24,8},{28,12},{1,17},{... | collective-permute-start | bytes 1990664 | tf_op jit(solution)/shard_map/ppermute | solution.py:747
  1288.1 62.9 %collective-permute-start.28 = (bf16[2,144,1152]{2,1,0:T(8,128)(2,1)S(1)}, bf16[2,144,1152]{2,1,0:T(8,128)(2,1)}, u32[]{:S(2)}, u32[]{:S(2)}) collective-permute-start(bf16[2,144,1152]{2,1,0:T(8,128)(2,1)S(1)} %bitcast.206), channel_id=1, source_target_pairs={{0,16},{4,20},{8,24},{12,28},{16,0},{20,4},{24,8},{28,12},{1,17},{... | collective-permute-start | bytes 1990664 | tf_op jit(solution)/shard_map/ppermute | solution.py:747
  1309.8 55.2 %collective-permute-start.34 = (bf16[2,144,1152]{2,1,0:T(8,128)(2,1)S(1)}, bf16[2,144,1152]{2,1,0:T(8,128)(2,1)S(1)}, u32[]{:S(2)}, u32[]{:S(2)}) collective-permute-start(bf16[2,144,1152]{2,1,0:T(8,128)(2,1)S(1)} %bitcast.204), channel_id=1, source_target_pairs={{0,16},{4,20},{8,24},{12,28},{16,0},{20,4},{24,8},{28,12},{1,17},{... | collective-permute-start | bytes 1990664 | tf_op jit(solution)/shard_map/ppermute | solution.py:747
  1338.0 34.1 %collective-permute-start.23 = (bf16[1,144,1152]{2,1,0:T(8,128)(2,1)S(1)}, bf16[1,144,1152]{2,1,0:T(8,128)(2,1)S(1)}, u32[]{:S(2)}, u32[]{:S(2)}) collective-permute-start(bf16[1,144,1152]{2,1,0:T(8,128)(2,1)S(1)} %slice.353), channel_id=1, source_target_pairs={{0,8},{4,12},{8,0},{12,4},{16,24},{20,28},{24,16},{28,20},{1,9},{5... | collective-permute-start | bytes 995336 | tf_op jit(solution)/shard_map/ppermute | solution.py:747
  1352.3 39.1 %collective-permute-start.29 = (bf16[1,144,1152]{2,1,0:T(8,128)(2,1)S(1)}, bf16[1,144,1152]{2,1,0:T(8,128)(2,1)}, u32[]{:S(2)}, u32[]{:S(2)}) collective-permute-start(bf16[1,144,1152]{2,1,0:T(8,128)(2,1)S(1)} %slice.364), channel_id=1, source_target_pairs={{0,8},{4,12},{8,0},{12,4},{16,24},{20,28},{24,16},{28,20},{1,9},{5... | collective-permute-start | bytes 995336 | tf_op jit(solution)/shard_map/ppermute | solution.py:747
  1365.2 21.0 %collective-permute-start.35 = (bf16[1,144,1152]{2,1,0:T(8,128)(2,1)S(1)}, bf16[1,144,1152]{2,1,0:T(8,128)(2,1)S(1)}, u32[]{:S(2)}, u32[]{:S(2)}) collective-permute-start(bf16[1,144,1152]{2,1,0:T(8,128)(2,1)S(1)} %slice.372), channel_id=1, source_target_pairs={{0,8},{4,12},{8,0},{12,4},{16,24},{20,28},{24,16},{28,20},{1,9},{5... | collective-permute-start | bytes 995336 | tf_op jit(solution)/shard_map/ppermute | solution.py:747
  1395.8 112.1 %collective-permute-start.19 = (bf16[2,144,1152]{2,1,0:T(8,128)(2,1)}, bf16[2,144,1152]{2,1,0:T(8,128)(2,1)}, u32[]{:S(2)}, u32[]{:S(2)}) collective-permute-start(bf16[2,144,1152]{2,1,0:T(8,128)(2,1)} %bitcast.60), channel_id=1, source_target_pairs={{0,16},{4,20},{8,24},{12,28},{16,0},{20,4},{24,8},{28,12},{1,17},{... | collective-permute-start | bytes 1990664 | tf_op jit(solution)/shard_map/ppermute | solution.py:747
  1440.2 70.5 %collective-permute-start.25 = (bf16[2,144,1152]{2,1,0:T(8,128)(2,1)S(1)}, bf16[2,144,1152]{2,1,0:T(8,128)(2,1)}, u32[]{:S(2)}, u32[]{:S(2)}) collective-permute-start(bf16[2,144,1152]{2,1,0:T(8,128)(2,1)S(1)} %bitcast.207), channel_id=1, source_target_pairs={{0,16},{4,20},{8,24},{12,28},{16,0},{20,4},{24,8},{28,12},{1,17},{... | collective-permute-start | bytes 1990664 | tf_op jit(solution)/shard_map/ppermute | solution.py:747
  1505.4 31.9 %collective-permute-start.31 = (bf16[2,144,1152]{2,1,0:T(8,128)(2,1)S(1)}, bf16[2,144,1152]{2,1,0:T(8,128)(2,1)S(1)}, u32[]{:S(2)}, u32[]{:S(2)}) collective-permute-start(bf16[2,144,1152]{2,1,0:T(8,128)(2,1)S(1)} %bitcast.205), channel_id=1, source_target_pairs={{0,16},{4,20},{8,24},{12,28},{16,0},{20,4},{24,8},{28,12},{1,17},{... | collective-permute-start | bytes 1990664 | tf_op jit(solution)/shard_map/ppermute | solution.py:747
  1509.1 28.9 %collective-permute-start.20 = (bf16[1,144,1152]{2,1,0:T(8,128)(2,1)S(1)}, bf16[1,144,1152]{2,1,0:T(8,128)(2,1)S(1)}, u32[]{:S(2)}, u32[]{:S(2)}) collective-permute-start(bf16[1,144,1152]{2,1,0:T(8,128)(2,1)S(1)} %slice.348), channel_id=1, source_target_pairs={{0,8},{4,12},{8,0},{12,4},{16,24},{20,28},{24,16},{28,20},{1,9},{5... | collective-permute-start | bytes 995336 | tf_op jit(solution)/shard_map/ppermute | solution.py:747
  1512.8 41.2 %collective-permute-start.26 = (bf16[1,144,1152]{2,1,0:T(8,128)(2,1)}, bf16[1,144,1152]{2,1,0:T(8,128)(2,1)}, u32[]{:S(2)}, u32[]{:S(2)}) collective-permute-start(bf16[1,144,1152]{2,1,0:T(8,128)(2,1)} %slice.360), channel_id=1, source_target_pairs={{0,8},{4,12},{8,0},{12,4},{16,24},{20,28},{24,16},{28,20},{1,9},{5... | collective-permute-start | bytes 995336 | tf_op jit(solution)/shard_map/ppermute | solution.py:747
  (33 other events, 1016.2 us)
Sparse Core Ops, SparseCore 0:
  53.1 62.9 all-gather.16
  118.5 61.9 all-gather.18
  183.0 61.9 all-gather.20
  247.2 61.9 all-gather.22
  310.9 61.9 all-gather.24
  374.7 61.9 all-gather.26
  931.9 23.6 reduce-scatter.21
  969.6 126.7 all-reduce.3
  1099.7 62.4 reduce-scatter.11
  1165.3 77.6 reduce-scatter.15
  1246.3 62.0 reduce-scatter.19
  1311.6 61.9 reduce-scatter.9
  1376.8 61.9 reduce-scatter.13
  1442.0 61.9 reduce-scatter.17

commit v2 on v1

v2 whole, which is shorter than its diff:
```python
from functools import partial

import jax
import jax.numpy as jnp
from jax import lax
from jax.experimental import pallas as pl
from jax.experimental.pallas import tpu as pltpu
from jax.sharding import PartitionSpec as P

HEADS = 16
F32 = jnp.float32
BF16 = jnp.bfloat16
NN = (((1,), (0,)), ((), ()))
NT = (((1,), (1,)), ((), ()))
TN = (((0,), (0,)), ((), ()))
VMEM_BYTES = 56 * 1024 * 1024
FEED_ROWS = 1024
UP_ROWS, UP_CUTS = 1024, 1
QKV_ROWS = 512


def mm(a, b, dims=NN):
    return lax.dot_general(a, b, dims, preferred_element_type=F32)


def call(
    body, grid, in_specs, out_specs, out_shape, scratch=(), scalars=0, flops=0, nbytes=0, deps=()
):
    first = scalars + len(in_specs)

    def run(*refs):
        body(*refs[:first], *refs[first + len(deps) :])

    kernel = pl.pallas_call(
        run,
        grid_spec=pltpu.PrefetchScalarGridSpec(
            num_scalar_prefetch=scalars,
            grid=grid,
            in_specs=[*in_specs, *[pl.BlockSpec(memory_space=pl.ANY)] * len(deps)],
            out_specs=out_specs,
            scratch_shapes=list(scratch),
        ),
        out_shape=out_shape,
        compiler_params=pltpu.CompilerParams(
            dimension_semantics=("arbitrary",) * len(grid), vmem_limit_bytes=VMEM_BYTES
        ),
        cost_estimate=pl.CostEstimate(flops=flops, bytes_accessed=nbytes, transcendentals=0),
    )
    return lambda *args: kernel(*args, *deps)


def gate(x, deps):
    def body(*refs):
        pass

    anywhere = pl.BlockSpec(memory_space=pl.ANY)
    return pl.pallas_call(
        body,
        in_specs=[anywhere] * (1 + len(deps)),
        out_specs=anywhere,
        out_shape=sds(x.shape, x.dtype),
        input_output_aliases={0: 0},
    )(x, *deps)


def joint(*arrays):
    def body(*refs):
        pass

    anywhere = pl.BlockSpec(memory_space=pl.ANY)
    return pl.pallas_call(
        body,
        in_specs=[anywhere] * len(arrays),
        out_specs=[anywhere] * len(arrays),
        out_shape=[sds(x.shape, x.dtype) for x in arrays],
        input_output_aliases={k: k for k in range(len(arrays))},
    )(*arrays)


def whole(shape):
    return pl.BlockSpec(shape, lambda *_: (0,) * len(shape))


def sds(shape, dtype):
    return jax.ShapeDtypeStruct(shape, dtype)


def standard(x):
    centred = x - jnp.mean(x, axis=-1, keepdims=True)
    r = lax.rsqrt(jnp.mean(centred * centred, axis=-1, keepdims=True) + 1e-06)
    return centred * r, r


def fold(n, limit=512):
    return min(n, limit)


def qkv_forward(x, mods, w, bias, deps=()):
    n, d = x.shape
    wide = w.shape[1]
    mt = fold(n, QKV_ROWS)

    def body(x_ref, mod_ref, w_ref, b_ref, hid_ref, out_ref):
        m = pl.program_id(1)
        rows = pl.ds(pl.multiple_of(m * mt, mt), mt)

        @pl.when(pl.program_id(0) == 0)
        def _():
            v, _ = standard(x_ref[...].astype(F32))
            hid_ref[rows, :] = (v * (1.0 + mod_ref[1:2, :]) + mod_ref[0:1, :]).astype(BF16)

        out_ref[...] = (mm(hid_ref[rows, :], w_ref[...]) + b_ref[...]).astype(BF16)

    return call(
        body,
        (wide // d, n // mt),
        [
            pl.BlockSpec((mt, d), lambda j, m: (jnp.where(j == 0, m, n // mt - 1), 0)),
            whole((8, d)),
            pl.BlockSpec((d, d), lambda j, m: (0, j)),
            pl.BlockSpec((1, d), lambda j, m: (0, j)),
        ],
        [whole((n, d)), pl.BlockSpec((mt, d), lambda j, m: (m, j))],
        [sds((n, d), BF16), sds((n, wide), BF16)],
        flops=2 * n * d * wide,
        nbytes=2 * (d * wide + n * wide + 2 * n * d),
        deps=deps,
    )(x, mods, w, bias)


def window(h, size, d):
    lo = h * size
    start = lo // 128 * 128
    stop = min(-(-(lo + size) // 128) * 128, d)
    return start, stop, lo - start


def head_mask(start, stop, off, size, rows):
    lane = lax.broadcasted_iota(jnp.int32, (rows, stop - start), 1)
    return (lane >= off) & (lane < off + size)


def attention_forward(qkv, temporal, deps=()):
    a, g, p, wide = qkv.shape
    d = wide // 3
    size = d // HEADS
    t = a * p
    scale = size ** (-0.5)

    def body(qkv_ref, att_ref, lse_ref, peak_ref, acc):
        acc[...] = jnp.zeros_like(acc)
        if temporal:
            qi = lax.broadcasted_iota(jnp.int32, (t, t), 0)
            ki = lax.broadcasted_iota(jnp.int32, (t, t), 1)
            same = lax.rem(qi, p) == lax.rem(ki, p)
        tops, totals = [], []
        for h in range(HEADS):
            lo, hi, off = window(h, size, d)
            keep = head_mask(lo, hi, off, size, t)
            q = qkv_ref[:, 0, :, lo:hi].reshape(t, hi - lo)
            k = qkv_ref[:, 0, :, d + lo : d + hi].reshape(t, hi - lo)
            v = qkv_ref[:, 0, :, 2 * d + lo : 2 * d + hi].reshape(t, hi - lo)
            zero = jnp.zeros_like(q)
            s = mm(jnp.where(keep, q, zero), k, NT) * scale
            if temporal:
                s = jnp.where(same, s, -1e30)
            top = jnp.max(s, axis=-1, keepdims=True)
            e = jnp.exp(s - top)
            total = jnp.sum(e, axis=-1, keepdims=True)
            probs = (e / total).astype(BF16)
            acc[:, lo:hi] += mm(probs, jnp.where(keep, v, zero))
            tops.append(top)
            totals.append(total)
        top = jnp.concatenate(tops, axis=1)
        lse_ref[0] = (top + jnp.log(jnp.concatenate(totals, axis=1))).T
        peak_ref[...] = jnp.max(top, axis=0, keepdims=True)[None]
        att_ref[...] = acc[...].astype(BF16).reshape(a, 1, p, d)

    return call(
        body,
        (g,),
        [pl.BlockSpec((a, 1, p, wide), lambda i: (0, i, 0, 0))],
        [
            pl.BlockSpec((a, 1, p, d), lambda i: (0, i, 0, 0)),
            pl.BlockSpec((1, HEADS, t), lambda i: (i, 0, 0)),
            pl.BlockSpec((1, 1, HEADS), lambda i: (i, 0, 0)),
        ],
        [sds((a, g, p, d), BF16), sds((g, HEADS, t), F32), sds((g, 1, HEADS), F32)],
        [pltpu.VMEM((t, d), F32)],
        flops=4 * g * HEADS * t * t * 256,
        nbytes=2 * a * g * p * (wide + d),
        deps=deps,
    )(qkv)


def out_forward(att, x, mods, w, bias, deps=()):
    n, d = att.shape
    mt = fold(n, 256)

    def body(att_ref, x_ref, mod_ref, w_ref, b_ref, branch_ref, mid_ref, hid_ref):
        branch = mm(att_ref[...], w_ref[...]) + b_ref[...]
        branch_ref[...] = branch.astype(BF16)
        mid = x_ref[...].astype(F32) + mod_ref[2:3, :] * branch
        mid_ref[...] = mid
        v, _ = standard(mid)
        hid_ref[...] = (v * (1.0 + mod_ref[4:5, :]) + mod_ref[3:4, :]).astype(BF16)

    tile = pl.BlockSpec((mt, d), lambda m: (m, 0))
    return call(
        body,
        (n // mt,),
        [tile, tile, whole((8, d)), whole((d, d)), whole((1, d))],
        [tile, tile, tile],
        [sds((n, d), BF16), sds((n, d), F32), sds((n, d), BF16)],
        flops=2 * n * d * d,
        nbytes=2 * (d * d + 6 * n * d),
        deps=deps,
    )(att, x, mods, w, bias)


GELU_A = 0.7978845608028654
GELU_B = 0.044715


def up_forward(hid, w, bias, deps=()):
    n, d = hid.shape
    ff = w.shape[1]
    mt = fold(n, UP_ROWS)
    ft = d
    cuts = UP_CUTS

    def body(hid_ref, w_ref, b_ref, act_ref, slope_ref):
        for c in range(cuts):
            cols = slice(c * ft // cuts, (c + 1) * ft // cuts)
            u = mm(hid_ref[...], w_ref[:, cols]) + b_ref[:, cols]
            square = u * u
            tanh = jnp.tanh(u * (GELU_A + (GELU_A * GELU_B) * square))
            half = 0.5 + 0.5 * tanh
            act_ref[:, cols] = (u * half).astype(BF16)
            bend = GELU_A + (3.0 * GELU_A * GELU_B) * square
            slope_ref[:, cols] = (half + (u * half) * ((1.0 - tanh) * bend)).astype(BF16)

    tile = pl.BlockSpec((mt, ft), lambda f, m: (m, f))
    return call(
        body,
        (ff // ft, n // mt),
        [
            pl.BlockSpec((mt, d), lambda f, m: (m, 0)),
            pl.BlockSpec((d, ft), lambda f, m: (0, f)),
            pl.BlockSpec((1, ft), lambda f, m: (0, f)),
        ],
        [tile, tile],
        [sds((n, ff), BF16), sds((n, ff), BF16)],
        flops=2 * n * d * ff,
        nbytes=2 * (d * ff + 2 * n * ff + n * d),
        deps=deps,
    )(hid, w, bias)


def down_forward(act, mid, mods, w, bias, deps=()):
    n, ff = act.shape
    d = w.shape[1]
    mt = fold(n, 256)

    def body(act_ref, mid_ref, mod_ref, w_ref, b_ref, upd_ref, out_ref):
        upd = mm(act_ref[...], w_ref[...]) + b_ref[...]
        upd_ref[...] = upd.astype(BF16)
        out_ref[...] = (mid_ref[...] + mod_ref[5:6, :] * upd).astype(BF16)

    tile = pl.BlockSpec((mt, d), lambda m: (m, 0))
    return call(
        body,
        (n // mt,),
        [
            pl.BlockSpec((mt, ff), lambda m: (m, 0)),
            tile,
            whole((8, d)),
            whole((ff, d)),
            whole((1, d)),
        ],
        [tile, tile],
        [sds((n, d), BF16), sds((n, d), BF16)],
        flops=2 * n * d * ff,
        nbytes=2 * (d * ff + n * ff + 4 * n * d),
        deps=deps,
    )(act, mid, mods, w, bias)


def column_sum(v):
    return jnp.sum(v, axis=0, keepdims=True)


def update_back(go, mods, deps=()):
    n, d = go.shape
    mt = fold(n, 256)

    def body(go_ref, mod_ref, gu_ref, sum_ref):
        @pl.when(pl.program_id(0) == 0)
        def _():
            sum_ref[...] = jnp.zeros_like(sum_ref)

        low = (mod_ref[5:6, :] * go_ref[...].astype(F32)).astype(BF16)
        gu_ref[...] = low
        sum_ref[0:1, :] += column_sum(low.astype(F32))

    tile = pl.BlockSpec((mt, d), lambda m: (m, 0))
    return call(
        body,
        (n // mt,),
        [tile, whole((8, d))],
        [tile, whole((8, d))],
        [sds((n, d), BF16), sds((8, d), F32)],
        flops=n * d,
        nbytes=4 * n * d,
        deps=deps,
    )(go, mods)


def shed_specs(seq, zs, rows, d):
    return sds((seq, zs, rows, d), BF16)


def shares(start, stop, rows):
    found = []
    while start < stop:
        block = start // rows
        end = min(stop, (block + 1) * rows)
        found.append((block, start - block * rows, start, end))
        start = end
    return found


def down_grad(place, act, gu, seq, zs, deps=()):
    n, ff = act.shape
    d = gu.shape[1]
    rows, quarter = d // (2 * zs), d // seq
    parts = ff // (2 * zs) // rows
    cuts = 3

    def body(place_ref, act_ref, gu_ref, mine_ref, other_ref):
        def fill(targets):
            for c in range(cuts):
                first, stop = c * (ff // zs) // cuts, (c + 1) * (ff // zs) // cuts
                full = mm(act_ref[:, first:stop], gu_ref[...], TN).astype(BF16)
                for block, at, lo, hi in shares(first, stop, rows):
                    target, q = targets[block // parts], block % parts
                    for s in range(seq):
                        target[s, 0, at : at + hi - lo, q * quarter : (q + 1) * quarter] = full[
                            lo - first : hi - first, s * quarter : (s + 1) * quarter
                        ]

        @pl.when(place_ref[0] == 0)
        def _():
            fill((mine_ref, other_ref))

        @pl.when(place_ref[0] == 1)
        def _():
            fill((other_ref, mine_ref))

    piece = pl.BlockSpec((seq, 1, rows, d), lambda i, place_ref: (0, i, 0, 0))
    return call(
        body,
        (zs,),
        [
            pl.BlockSpec((n, ff // zs), lambda i, place_ref: (0, i ^ place_ref[1])),
            whole((n, d)),
        ],
        [piece, piece],
        [shed_specs(seq, zs, rows, d)] * 2,
        scalars=1,
        flops=2 * n * d * ff,
        nbytes=2 * (d * ff + n * ff + n * d),
        deps=deps,
    )(place, act, gu)


def up_grad(place, hid, gi, seq, zs, deps=()):
    n, d = hid.shape
    ff = gi.shape[1]
    rows, wide = d // (2 * zs), ff // seq
    cuts = 3

    def body(place_ref, hid_ref, gi_ref, mine_ref, other_ref):
        z = place_ref[1]

        def fill(targets):
            for c in range(cuts):
                first, stop = c * d // cuts, (c + 1) * d // cuts
                full = mm(hid_ref[:, first:stop], gi_ref[...], TN).astype(BF16)
                for block, at, lo, hi in shares(first, stop, rows):
                    targets[block % 2][0, (block // 2) ^ z, at : at + hi - lo, :] = full[
                        lo - first : hi - first
                    ]

        @pl.when(place_ref[0] == 0)
        def _():
            fill((mine_ref, other_ref))

        @pl.when(place_ref[0] == 1)
        def _():
            fill((other_ref, mine_ref))

    piece = pl.BlockSpec((1, zs, rows, wide), lambda i, place_ref: (i, 0, 0, 0))
    return call(
        body,
        (seq,),
        [whole((n, d)), pl.BlockSpec((n, wide), lambda i, place_ref: (0, i))],
        [piece, piece],
        [shed_specs(seq, zs, rows, wide)] * 2,
        scalars=1,
        flops=2 * n * d * ff,
        nbytes=2 * (d * ff + n * ff + n * d),
        deps=deps,
    )(place, hid, gi)


def qkv_out_grad(place, hid, att, gqkv, gb, zs, deps=()):
    n, d = hid.shape
    seq, _, wa = gqkv.shape
    wb = gb.shape[2]
    rows = d // (2 * zs)
    cuts = 3

    def body(place_ref, hid_ref, att_ref, gqkv_ref, gb_ref, mine_ref, other_ref):
        z = place_ref[1]

        def fill(targets):
            for c in range(cuts):
                first, stop = c * d // cuts, (c + 1) * d // cuts
                left = mm(hid_ref[:, first:stop], gqkv_ref[0], TN).astype(BF16)
                right = mm(att_ref[:, first:stop], gb_ref[0], TN).astype(BF16)
                full = jnp.concatenate([left, right], axis=1)
                for block, at, lo, hi in shares(first, stop, rows):
                    targets[block % 2][0, (block // 2) ^ z, at : at + hi - lo, :] = full[
                        lo - first : hi - first
                    ]

        @pl.when(place_ref[0] == 0)
        def _():
            fill((mine_ref, other_ref))

        @pl.when(place_ref[0] == 1)
        def _():
            fill((other_ref, mine_ref))

    piece = pl.BlockSpec((1, zs, rows, wa + wb), lambda i, place_ref: (i, 0, 0, 0))
    return call(
        body,
        (seq,),
        [
            whole((n, d)),
            whole((n, d)),
            pl.BlockSpec((1, n, wa), lambda i, place_ref: (i, 0, 0)),
            pl.BlockSpec((1, n, wb), lambda i, place_ref: (i, 0, 0)),
        ],
        [piece, piece],
        [shed_specs(seq, zs, rows, wa + wb)] * 2,
        scalars=1,
        flops=2 * n * d * seq * (wa + wb),
        nbytes=2 * seq * (d + n) * (wa + wb),
        deps=deps,
    )(place, hid, att, gqkv, gb)


def feed_back(gu, slope, w_down, w_up, deps=()):
    n, d = gu.shape
    ff = slope.shape[1]
    mt = fold(n, FEED_ROWS)
    last = ff // d - 1

    def body(gu_ref, slope_ref, wd_ref, wu_ref, gi_ref, bias_ref, out_ref, acc):
        f = pl.program_id(0)
        m = pl.program_id(1)
        rows = pl.ds(pl.multiple_of(m * mt, mt), mt)
        gi = (mm(gu_ref[...], wd_ref[...], NT) * slope_ref[...].astype(F32)).astype(BF16)
        gi_ref[...] = gi
        total = column_sum(gi.astype(F32))

        @pl.when(m == 0)
        def _():
            bias_ref[...] = total

        @pl.when(m > 0)
        def _():
            bias_ref[...] += total

        part = mm(gi, wu_ref[...], NT)

        @pl.when(f == 0)
        def _():
            acc[rows, :] = part

        @pl.when((f > 0) & (f < last))
        def _():
            acc[rows, :] += part

        @pl.when(f == last)
        def _():
            out_ref[...] = acc[rows, :] + part

    return call(
        body,
        (ff // d, n // mt),
        [
            pl.BlockSpec((mt, d), lambda f, m: (m, 0)),
            pl.BlockSpec((mt, d), lambda f, m: (m, f)),
            pl.BlockSpec((d, d), lambda f, m: (f, 0)),
            pl.BlockSpec((d, d), lambda f, m: (0, f)),
        ],
        [
            pl.BlockSpec((mt, d), lambda f, m: (m, f)),
            pl.BlockSpec((1, d), lambda f, m: (0, f)),
            pl.BlockSpec((mt, d), lambda f, m: (jnp.where(f == last, m, 0), 0)),
        ],
        [sds((n, ff), BF16), sds((1, ff), F32), sds((n, d), F32)],
        [pltpu.VMEM((n, d), F32)],
        flops=4 * n * d * ff,
        nbytes=2 * (2 * d * ff + 2 * n * ff + 3 * n * d),
        deps=deps,
    )(gu, slope, w_down, w_up)


def norm_back(grad, v, r, stretch):
    dn = grad * stretch
    return r * (
        dn - jnp.mean(dn, axis=-1, keepdims=True) - v * jnp.mean(dn * v, axis=-1, keepdims=True)
    )


def middle_back(gh, mid, branch, go, upd, mods, w, seq, deps=()):
    n, d = gh.shape
    mt = fold(n, 256)
    wide = d // seq

    def body(
        gh_ref, mid_ref, branch_ref, go_ref, upd_ref, mod_ref, w_ref,
        gmid_ref, gb_ref, cut_ref, ga_ref, sum_ref,
    ):
        @pl.when(pl.program_id(0) == 0)
        def _():
            sum_ref[...] = jnp.zeros_like(sum_ref)

        g = gh_ref[...]
        v, r = standard(mid_ref[...])
        sum_ref[0:1, :] += column_sum(g * v)
        sum_ref[1:2, :] += column_sum(g)
        go = go_ref[...].astype(F32)
        sum_ref[4:5, :] += column_sum(go * upd_ref[...].astype(F32))
        gmid = go + norm_back(g, v, r, 1.0 + mod_ref[4:5, :])
        gmid_ref[...] = gmid
        sum_ref[2:3, :] += column_sum(gmid * branch_ref[...].astype(F32))
        low = (mod_ref[2:3, :] * gmid).astype(BF16)
        gb_ref[...] = low
        for s in range(seq):
            cut_ref[s] = low[:, s * wide : (s + 1) * wide]
        sum_ref[3:4, :] += column_sum(low.astype(F32))
        ga_ref[...] = mm(low, w_ref[...], NT).astype(BF16)

    tile = pl.BlockSpec((mt, d), lambda m: (m, 0))
    return call(
        body,
        (n // mt,),
        [tile, tile, tile, tile, tile, whole((8, d)), whole((d, d))],
        [tile, tile, pl.BlockSpec((seq, mt, wide), lambda m: (0, m, 0)), tile, whole((8, d))],
        [
            sds((n, d), F32),
            sds((n, d), BF16),
            sds((seq, n, wide), BF16),
            sds((n, d), BF16),
            sds((8, d), F32),
        ],
        flops=2 * n * d * d,
        nbytes=2 * (d * d + 11 * n * d),
        deps=deps,
    )(gh, mid, branch, go, upd, mods, w)


def attention_back(qkv, ga, lse, temporal, seq, deps=()):
    a, g, p, wide = qkv.shape
    d = wide // 3
    size = d // HEADS
    t = a * p
    scale = size ** (-0.5)
    cut = wide // seq

    def body(qkv_ref, ga_ref, lse_ref, out_ref, cut_ref, sum_ref, acc):
        acc[...] = jnp.zeros_like(acc)
        if temporal:
            ki = lax.broadcasted_iota(jnp.int32, (t, t), 0)
            qi = lax.broadcasted_iota(jnp.int32, (t, t), 1)
            same = lax.rem(qi, p) == lax.rem(ki, p)
        for h in range(HEADS):
            lo, hi, off = window(h, size, d)
            keep = head_mask(lo, hi, off, size, t)
            q = qkv_ref[:, 0, :, lo:hi].reshape(t, hi - lo)
            k = qkv_ref[:, 0, :, d + lo : d + hi].reshape(t, hi - lo)
            v = qkv_ref[:, 0, :, 2 * d + lo : 2 * d + hi].reshape(t, hi - lo)
            o = ga_ref[:, 0, :, lo:hi].reshape(t, hi - lo)
            zero = jnp.zeros_like(q)
            q, o = jnp.where(keep, q, zero), jnp.where(keep, o, zero)
            s = mm(k, q, NT) * scale
            probs = jnp.exp(s - lse_ref[0, h : h + 1, :])
            if temporal:
                probs = jnp.where(same, probs, 0.0)
            dp = mm(v, o, NT)
            acc[:, 2 * d + lo : 2 * d + hi] += mm(probs.astype(BF16), o)
            ds = (probs * (dp - column_sum(probs * dp))).astype(BF16)
            acc[:, d + lo : d + hi] += mm(ds, q) * scale
            acc[:, lo:hi] += mm(ds, jnp.where(keep, k, zero), TN) * scale
        low = acc[...].astype(BF16)
        out_ref[...] = low.reshape(a, 1, p, wide)
        for s in range(seq):
            cut_ref[s] = low[:, s * cut : (s + 1) * cut].reshape(a, 1, p, cut)
        total = column_sum(low.astype(F32))

        @pl.when(pl.program_id(0) == 0)
        def _():
            sum_ref[...] = total

        @pl.when(pl.program_id(0) > 0)
        def _():
            sum_ref[...] += total

    return call(
        body,
        (g,),
        [
            pl.BlockSpec((a, 1, p, wide), lambda i: (0, i, 0, 0)),
            pl.BlockSpec((a, 1, p, d), lambda i: (0, i, 0, 0)),
            pl.BlockSpec((1, HEADS, t), lambda i: (i, 0, 0)),
        ],
        [
            pl.BlockSpec((a, 1, p, wide), lambda i: (0, i, 0, 0)),
            pl.BlockSpec((seq, a, 1, p, cut), lambda i: (0, 0, i, 0, 0)),
            whole((1, wide)),
        ],
        [sds((a, g, p, wide), BF16), sds((seq, a, g, p, cut), BF16), sds((1, wide), F32)],
        [pltpu.VMEM((t, wide), F32)],
        flops=12 * g * HEADS * t * t * 256,
        nbytes=2 * a * g * p * (3 * wide + d),
        deps=deps,
    )(qkv, ga, lse)


def stream_back(gqkv, w, x, gmid, mods, out_dtype, deps=()):
    n, wide = gqkv.shape
    d = w.shape[0]
    mt = fold(n, 256)

    def body(g_ref, w_ref, x_ref, gmid_ref, mod_ref, out_ref, sum_ref):
        @pl.when(pl.program_id(0) == 0)
        def _():
            sum_ref[...] = jnp.zeros_like(sum_ref)

        grad = mm(g_ref[...], w_ref[...], NT)
        v, r = standard(x_ref[...].astype(F32))
        sum_ref[0:1, :] += column_sum(grad * v)
        sum_ref[1:2, :] += column_sum(grad)
        out_ref[...] = (gmid_ref[...] + norm_back(grad, v, r, 1.0 + mod_ref[1:2, :])).astype(
            out_dtype
        )

    tile = pl.BlockSpec((mt, d), lambda m: (m, 0))
    return call(
        body,
        (n // mt,),
        [
            pl.BlockSpec((mt, wide), lambda m: (m, 0)),
            whole((d, wide)),
            tile,
            tile,
            whole((8, d)),
        ],
        [tile, whole((8, d))],
        [sds((n, d), out_dtype), sds((8, d), F32)],
        flops=2 * n * d * wide,
        nbytes=2 * (d * wide + n * wide + 5 * n * d),
        deps=deps,
    )(gqkv, w, x, gmid, mods)


def add_pieces(left, right, deps=()):
    seq, zs, rows, d = left.shape

    def body(left_ref, right_ref, out_ref):
        out_ref[...] = (left_ref[...].astype(F32) + right_ref[...].astype(F32)).astype(BF16)

    piece = pl.BlockSpec((1, zs, rows, d), lambda i: (i, 0, 0, 0))
    return call(
        body,
        (seq,),
        [piece, piece],
        piece,
        sds(left.shape, BF16),
        nbytes=6 * seq * zs * rows * d,
        deps=deps,
    )(left, right)


def join_qkv_out(place, own, got, deps=()):
    seq, zs, rows, d = own.shape
    wide = d * 3 // 4

    def body(place_ref, own_ref, got_ref, qkv_ref, out_ref):
        def put(c, src):
            span = slice(c * rows, (c + 1) * rows)
            qkv_ref[span, :] = jnp.concatenate([src[s, 0, :, :wide] for s in range(seq)], axis=1)
            out_ref[span, :] = jnp.concatenate([src[s, 0, :, wide:] for s in range(seq)], axis=1)

        for c in range(2):

            @pl.when(place_ref[0] == c)
            def _(c=c):
                put(c, own_ref)
                put(1 - c, got_ref)

    piece = pl.BlockSpec((seq, 1, rows, d), lambda i, place_ref: (0, i ^ place_ref[1], 0, 0))
    return call(
        body,
        (zs,),
        [piece, piece],
        [
            pl.BlockSpec((2 * rows, seq * wide), lambda i, place_ref: (i, 0)),
            pl.BlockSpec((2 * rows, d), lambda i, place_ref: (i, 0)),
        ],
        [sds((2 * rows * zs, seq * wide), BF16), sds((2 * rows * zs, d), BF16)],
        scalars=1,
        nbytes=8 * seq * zs * rows * d,
        deps=deps,
    )(place, own, got)


def join_up(place, own, got, deps=()):
    seq, zs, rows, d = own.shape

    def body(place_ref, own_ref, got_ref, up_ref):
        for c in range(2):

            @pl.when(place_ref[0] == c)
            def _(c=c):
                for s in range(seq):
                    cols = slice(s * d, (s + 1) * d)
                    up_ref[c * rows : (c + 1) * rows, cols] = own_ref[s, 0]
                    up_ref[(1 - c) * rows : (2 - c) * rows, cols] = got_ref[s, 0]

    piece = pl.BlockSpec((seq, 1, rows, d), lambda i, place_ref: (0, i ^ place_ref[1], 0, 0))
    return call(
        body,
        (zs,),
        [piece, piece],
        pl.BlockSpec((2 * rows, seq * d), lambda i, place_ref: (i, 0)),
        sds((2 * rows * zs, seq * d), BF16),
        scalars=1,
        nbytes=8 * seq * zs * rows * d,
        deps=deps,
    )(place, own, got)


def join_down(place, own, got, deps=()):
    seq, zs, rows, d = own.shape
    quarter = d // seq
    parts = d // quarter

    def body(place_ref, own_ref, got_ref, down_ref):
        def put(c, src):
            for q in range(parts):
                base = (c * parts + q) * rows
                cols = slice(q * quarter, (q + 1) * quarter)
                down_ref[base : base + rows, :] = jnp.concatenate(
                    [src[s, 0, :, cols] for s in range(seq)], axis=1
                )

        for c in range(2):

            @pl.when(place_ref[0] == c)
            def _(c=c):
                put(c, own_ref)
                put(1 - c, got_ref)

    piece = pl.BlockSpec((seq, 1, rows, d), lambda i, place_ref: (0, i ^ place_ref[1], 0, 0))
    return call(
        body,
        (zs,),
        [piece, piece],
        pl.BlockSpec((2 * parts * rows, d), lambda i, place_ref: (i, 0)),
        sds((2 * parts * rows * zs, d), BF16),
        scalars=1,
        nbytes=8 * seq * zs * rows * d,
        deps=deps,
    )(place, own, got)


clip_limit = 8.0
CLIP = ("z", "core")


def hop(x, distance, count):
    return lax.ppermute(x, CLIP, [(i, i ^ distance) for i in range(count)])


def on_device(
    video_latents,
    conditioning,
    ada_weight,
    ada_bias,
    qkv_weight,
    out_weight,
    up_weight,
    down_weight,
    attention_bias,
    up_bias,
    down_bias,
    cotangent,
    *,
    clips,
    seq,
):
    zs = clips // 2
    layers, rows, own_columns = qkv_weight.shape
    d = video_latents.shape[-1]
    frames, places = video_latents.shape[1:3]
    n = frames * places
    ff = up_bias.shape[1]
    clip_index = lax.axis_index(CLIP)
    place = jnp.stack([clip_index % 2, clip_index // 2]).astype(jnp.int32)
    packed = zs == 4 and rows % 16 == 0 and down_weight.shape[1] % rows == 0 and d % seq == 0
    cuts = seq if packed else 1

    every_condition = lax.all_gather(conditioning, CLIP, axis=0, tiled=True)
    squashed = jax.nn.silu(every_condition).astype(BF16)
    local_mods = (
        jnp.einsum("kd,ldc->klc", squashed, ada_weight, preferred_element_type=F32)
        + ada_bias[None, :, :]
    )
    own_mods = lax.all_to_all(local_mods, CLIP, 0, 0, tiled=True)
    every_mod = lax.all_gather(own_mods, "seq", axis=0, tiled=False)
    modulation = every_mod.transpose(2, 1, 0, 3).reshape(layers, 6, d)
    modulation = jnp.pad(modulation, ((0, 0), (0, 2), (0, 0)))

    def pair_of(block, got):
        return jnp.concatenate([block[None], got[None]], axis=0)

    def line_of(pair, got):
        return jnp.concatenate([pair, got], axis=0)

    def pack_rows(layer):
        tall = down_weight[layer].reshape(-1, rows, d // seq)
        return (
            jnp.concatenate([qkv_weight[layer], out_weight[layer]], axis=1),
            up_weight[layer],
            tall.transpose(1, 0, 2).reshape(rows, d),
        )

    def along_seq(blocks):
        return lax.all_gather(blocks, "seq", axis=0, tiled=False)

    def both_cores(own, deps):
        own = gate(own, deps)
        return own, hop(own, 1, clips)

    def fetch_natural(layer):
        return tuple(
            lax.all_gather(
                lax.all_gather(item[layer], CLIP, axis=0, tiled=True), "seq", axis=1, tiled=True
            )
            for item in (qkv_weight, out_weight, up_weight, down_weight)
        )

    def reduce_seq(half):
        flat = lax.psum_scatter(half.reshape(-1, d), "seq", scatter_dimension=0, tiled=True)
        return flat.reshape(zs, rows, d)

    def far_half(part):
        return hop(part[2:], 4, clips)

    def add_far(part, got):
        return (part[:2].astype(F32) + got.astype(F32)).astype(BF16)

    def near_half(part):
        return hop(part[1], 2, clips)

    def add_near(part, got):
        return part[0].astype(F32) + got.astype(F32)

    def shed_natural(left, right):
        full = mm(left, right, TN).astype(BF16)
        part = lax.psum_scatter(full, "seq", scatter_dimension=1, tiled=True)
        return lax.psum_scatter(part, CLIP, scatter_dimension=0, tiled=True).astype(F32)

    def swap_tokens(x):
        block = x.reshape(seq, n // seq, d)
        return lax.all_to_all(block, "seq", 0, 0, tiled=True).reshape(n, d)

    def by_places(x):
        return x.reshape(frames, seq, places // seq, d).transpose(1, 0, 2, 3).reshape(n, d)

    def by_frames(x):
        return (
            x.reshape(seq, frames, places // seq, d)
            .transpose(1, 0, 2, 3)
            .reshape(1, frames, places, d)
        )

    shapes = (
        (seq, frames, places // seq),
        (seq * frames, places // seq // 16, 16),
    )

    def qkv_bias_of(layer):
        bias = attention_bias[layer]
        return jnp.concatenate([bias[0], jnp.zeros_like(bias[0]), bias[1]])[None]

    def forward_natural(layer, x):
        mods = modulation[layer]
        qkv_full, out_full, up_full, down_full = fetch_natural(layer)
        hidden, qkv = qkv_forward(x, mods, qkv_full, qkv_bias_of(layer))
        qkv = qkv.reshape(shapes[layer] + (3 * d,))
        attended, lse, peak = attention_forward(qkv, layer == 1)
        attended = attended.reshape(n, d)
        out_bias = attention_bias[layer, 2:3]
        branch, middle, hidden_two = out_forward(attended, x, mods, out_full, out_bias)
        active, slope = up_forward(hidden_two, up_full, up_bias[layer : layer + 1])
        update, result = down_forward(
            active, middle, mods, down_full, down_bias[layer : layer + 1]
        )
        kept = (x, hidden, qkv, lse, attended, branch, middle, hidden_two, active, slope, update)
        weights = (qkv_full, out_full, up_full, down_full)
        return result, kept, weights, jnp.max(peak, axis=(0, 1))

    def backward_natural(layer, grad_out, kept, weights):
        x, hidden, qkv, lse, attended, branch, middle, hidden_two, active, slope, update = kept
        qkv_full, out_full, up_full, down_full = weights
        mods = modulation[layer]
        grad_update, update_sums = update_back(grad_out, mods)
        inner_grad, up_sums, hidden_grad = feed_back(grad_update, slope, down_full, up_full)
        middle_grad, branch_grad, _, attended_grad, middle_sums = middle_back(
            hidden_grad, middle, branch, grad_out, update, mods, out_full, 1
        )
        qkv_grad, _, qkv_sums = attention_back(
            qkv, attended_grad.reshape(shapes[layer] + (d,)), lse, layer == 1, 1
        )
        qkv_grad = qkv_grad.reshape(n, 3 * d)
        stream_grad, stream_sums = stream_back(
            qkv_grad, qkv_full, x, middle_grad, mods, BF16 if layer == 1 else F32
        )
        parts = (
            shed_natural(hidden, qkv_grad),
            shed_natural(attended, branch_grad),
            shed_natural(hidden_two, inner_grad),
            shed_natural(active, grad_update),
        )
        return stream_grad, (stream_sums, middle_sums, update_sums, qkv_sums, up_sums), parts

    def mod_rows(sums):
        stream_sums, middle_sums, _, _, _ = sums
        return jnp.concatenate(
            [
                stream_sums[1:2],
                stream_sums[0:1],
                middle_sums[2:3],
                middle_sums[1:2],
                middle_sums[0:1],
                middle_sums[4:5],
            ],
            axis=0,
        )

    def bias_rows_of(sums):
        _, middle_sums, update_sums, qkv_sums, up_sums = sums
        return jnp.concatenate(
            [
                qkv_sums[:, :d],
                qkv_sums[:, 2 * d :],
                middle_sums[3:4],
                update_sums[0:1],
                up_sums.reshape(-1, d),
            ],
            axis=0,
        )

    def unpack(parts):
        down_g, up_g, both = parts
        down_g = down_g.reshape(rows, -1, d // seq).transpose(1, 0, 2).reshape(-1, d // seq)
        return both[:, :own_columns], both[:, own_columns:], up_g, down_g

    def run_natural():
        first_in = by_places(video_latents)
        second_go = swap_tokens(by_places(cotangent))
        first_out, first_kept, first_weights, first_peak = forward_natural(0, first_in)
        second_in = swap_tokens(first_out)
        second_out, second_kept, second_weights, second_peak = forward_natural(1, second_in)
        second_grad, second_sums, second_parts = backward_natural(
            1, second_go, second_kept, second_weights
        )
        first_grad, first_sums, first_parts = backward_natural(
            0, swap_tokens(second_grad), first_kept, first_weights
        )
        peaks = (first_peak, second_peak)
        sums = (first_sums, second_sums)
        second_out = swap_tokens(second_out)
        return second_out, first_grad, peaks, sums, first_parts, second_parts

    def run_packed():
        first_pack, second_pack = pack_rows(0), pack_rows(1)
        first_in = by_places(video_latents)
        second_go = swap_tokens(by_places(cotangent))

        pair = pair_of(first_pack[0], hop(first_pack[0], 2, clips))
        line_q0 = line_of(pair, gate(hop(pair, 4, clips), (second_go,)))
        block = gate(first_pack[1], (line_q0,))
        pair = pair_of(block, hop(block, 2, clips))
        line_u0 = line_of(pair, gate(hop(pair, 4, clips), (modulation,)))
        block = gate(first_pack[2], (line_u0,))
        pair_d0 = pair_of(block, hop(block, 2, clips))
        whole_q0, whole_u0 = along_seq(line_q0), along_seq(line_u0)

        def attention_part(layer, x, qkv, out_full):
            qkv = qkv.reshape(shapes[layer] + (3 * d,))
            attended, lse, peak = attention_forward(qkv, layer == 1)
            return qkv, attended.reshape(n, d), lse, jnp.max(peak, axis=(0, 1))

        mods = modulation[0]
        qkv_full, out_full = join_qkv_out(place, *both_cores(whole_q0, (pair_d0,)))
        hidden, qkv = qkv_forward(first_in, mods, qkv_full, qkv_bias_of(0))
        hidden, qkv, got = joint(hidden, qkv, hop(pair_d0, 4, clips))
        line_d0 = line_of(pair_d0, got)
        block_q1 = gate(second_pack[0], (hidden,))
        qkv, attended, lse, peak0 = attention_part(0, first_in, qkv, out_full)
        attended, lse, got = joint(attended, lse, hop(block_q1, 2, clips))
        pair_q1 = pair_of(block_q1, got)
        block_u1, block_d1 = gate(second_pack[1], (attended,)), gate(second_pack[2], (attended,))
        branch, middle, hidden_two = out_forward(
            attended, first_in, mods, out_full, attention_bias[0, 2:3]
        )
        branch, middle, hidden_two, got, got2 = joint(
            branch, middle, hidden_two, hop(block_u1, 2, clips), hop(block_d1, 2, clips)
        )
        pair_u1, pair_d1 = pair_of(block_u1, got), pair_of(block_d1, got2)
        whole_d0 = along_seq(line_d0)
        up_full = join_up(
            place, *both_cores(whole_u0, (branch,)), deps=(pair_q1, pair_u1, pair_d1, line_d0)
        )
        active, slope = up_forward(hidden_two, up_full, up_bias[:1])
        active, slope, got = joint(active, slope, hop(pair_q1, 4, clips))
        line_q1 = line_of(pair_q1, got)
        whole_q1 = along_seq(line_q1)
        down_full = join_down(place, *both_cores(whole_d0, (active,)), deps=(line_q1,))
        update, result = down_forward(active, middle, mods, down_full, down_bias[:1])
        update, result, got = joint(update, result, hop(pair_u1, 4, clips))
        line_u1 = line_of(pair_u1, got)
        whole_u1 = along_seq(line_u1)
        kept0 = (
            first_in, hidden, qkv, lse, attended, branch, middle, hidden_two, active, slope, update
        )
        weights0 = (qkv_full, out_full, up_full, down_full)
        second_in, got = joint(swap_tokens(result), hop(gate(pair_d1, (line_u1,)), 4, clips))
        line_d1 = line_of(pair_d1, got)
        whole_d1 = along_seq(line_d1)

        mods = modulation[1]
        qkv_full, out_full = join_qkv_out(
            place, *both_cores(whole_q1, (result, line_u1))
        )
        hidden, qkv = qkv_forward(second_in, mods, qkv_full, qkv_bias_of(1))
        qkv, attended, lse, peak1 = attention_part(1, second_in, qkv, out_full)
        branch, middle, hidden_two = out_forward(
            attended, second_in, mods, out_full, attention_bias[1, 2:3]
        )
        up_full = join_up(place, *both_cores(whole_u1, (branch,)))
        active, slope = up_forward(hidden_two, up_full, up_bias[1:2])
        grad_update, update_sums1 = update_back(second_go, mods, deps=(active,))
        own, got = both_cores(whole_d1, (grad_update,))
        down_m, down_o = down_grad(place, active, grad_update, seq, zs, deps=(own,))
        down_m, down_o, got = joint(down_m, down_o, got)
        down_full = join_down(place, own, got)
        half_d1 = add_pieces(down_m, hop(down_o, 1, clips), deps=(down_full,))
        part_d1 = reduce_seq(half_d1)
        update, result = down_forward(
            active, middle, mods, down_full, down_bias[1:2], deps=(half_d1,)
        )
        kept1 = (
            second_in, hidden, qkv, lse, attended, branch, middle, hidden_two, active, slope, update
        )
        weights1 = (qkv_full, out_full, up_full, down_full)
        kept, weights = (kept0, kept1), (weights0, weights1)

        def up_stage(layer, hidden_grad, inner_grad, grad_out, deps):
            _, _, _, _, _, branch, middle, hidden_two, _, _, update = kept[layer]
            up_m, up_o = up_grad(place, hidden_two, inner_grad, seq, zs, deps=deps)
            middle_grad, _, branch_cut, attended_grad, middle_sums = middle_back(
                hidden_grad, middle, branch, grad_out, update, modulation[layer],
                weights[layer][1], cuts, deps=(up_m,),
            )
            half_u = add_pieces(up_m, hop(up_o, 1, clips), deps=(middle_grad,))
            return half_u, reduce_seq(half_u), middle_grad, branch_cut, attended_grad, middle_sums

        def attention_stage(layer, attended_grad, deps):
            _, _, qkv, lse = kept[layer][:4]
            grad = attended_grad.reshape(shapes[layer] + (d,))
            qkv_grad, qkv_cut, qkv_sums = attention_back(
                qkv, grad, lse, layer == 1, cuts, deps=deps
            )
            return qkv_grad.reshape(n, 3 * d), qkv_cut.reshape(seq, n, -1), qkv_sums

        def last_grad(layer, qkv_cut, branch_cut, deps):
            hidden, attended = kept[layer][1], kept[layer][4]
            return qkv_out_grad(place, hidden, attended, qkv_cut, branch_cut, zs, deps=deps)

        inner_grad, up_sums, hidden_grad = feed_back(
            grad_update, kept1[9], weights1[3], weights1[2], deps=(result,)
        )
        inner_grad, hidden_grad, second_out = joint(inner_grad, hidden_grad, swap_tokens(result))
        half_u, part_u1, middle_grad, branch_cut, attended_grad, middle_sums = up_stage(
            1, hidden_grad, inner_grad, second_go, ()
        )
        qkv_grad, qkv_cut, qkv_sums = attention_stage(1, attended_grad, (half_u, part_d1))
        qkv_grad, qkv_cut, got = joint(qkv_grad, qkv_cut, far_half(part_d1))
        sum_d1 = add_far(part_d1, got)
        stream_grad, stream_sums = stream_back(
            qkv_grad, weights1[0], kept1[0], middle_grad, modulation[1], BF16
        )
        stream_grad, stream_sums, got = joint(stream_grad, stream_sums, near_half(sum_d1))
        down_g1 = add_near(sum_d1, got)
        second_sums = (stream_sums, middle_sums, update_sums1, qkv_sums, up_sums)
        last_m, last_o = last_grad(1, qkv_cut, branch_cut, (stream_grad,))
        last_m, last_o, first_go = joint(last_m, last_o, swap_tokens(stream_grad))

        grad_update, update_sums = update_back(first_go, modulation[0])
        half_q1 = add_pieces(last_m, hop(last_o, 1, clips), deps=(grad_update,))
        part_q1 = reduce_seq(half_q1)
        down_m, down_o = down_grad(place, kept0[8], grad_update, seq, zs, deps=(half_q1,))
        inner_grad, up_sums, hidden_grad = feed_back(
            grad_update, kept0[9], weights0[3], weights0[2], deps=(down_m, part_u1)
        )
        inner_grad, hidden_grad, got = joint(inner_grad, hidden_grad, far_half(part_u1))
        sum_u1 = add_far(part_u1, got)
        half_d0 = add_pieces(down_m, hop(down_o, 1, clips), deps=(hidden_grad, part_q1))
        part_d0 = reduce_seq(half_d0)
        half_u, part_u0, middle_grad, branch_cut, attended_grad, middle_sums = up_stage(
            0, hidden_grad, inner_grad, first_go, (half_d0, sum_u1)
        )
        qkv_grad, qkv_cut, qkv_sums = attention_stage(0, attended_grad, (half_u,))
        qkv_grad, qkv_cut, got, got2 = joint(
            qkv_grad, qkv_cut, far_half(part_q1), near_half(sum_u1)
        )
        sum_q1 = add_far(part_q1, got)
        up_g1 = add_near(sum_u1, got2)
        last_m, last_o = last_grad(0, qkv_cut, branch_cut, (part_d0, sum_q1))
        last_m, last_o, got, got2 = joint(last_m, last_o, far_half(part_d0), near_half(sum_q1))
        sum_d0 = add_far(part_d0, got)
        both_g1 = add_near(sum_q1, got2)
        first_grad, stream_sums = stream_back(
            qkv_grad, weights0[0], kept0[0], middle_grad, modulation[0], F32, deps=(last_m, sum_d0)
        )
        first_grad, stream_sums, got, got2 = joint(
            first_grad, stream_sums, near_half(sum_d0), far_half(part_u0)
        )
        down_g0 = add_near(sum_d0, got)
        sum_u0 = add_far(part_u0, got2)
        first_sums = (stream_sums, middle_sums, update_sums, qkv_sums, up_sums)
        half = add_pieces(last_m, hop(last_o, 1, clips), deps=(first_grad,))
        part_q0 = reduce_seq(half)
        up_g0 = add_near(sum_u0, near_half(sum_u0))
        part_q0 = gate(part_q0, (up_g0,))
        sum_q0 = add_far(part_q0, far_half(part_q0))
        both_g0 = add_near(sum_q0, near_half(sum_q0))
        sums = (first_sums, second_sums)
        first_parts = unpack((down_g0, up_g0, both_g0))
        second_parts = unpack((down_g1, up_g1, both_g1))
        return second_out, first_grad, (peak0, peak1), sums, first_parts, second_parts

    run = run_packed if packed else run_natural
    second_out, latents_grad, peaks, sums, first_shed, second_shed = run()
    output_latents = by_frames(second_out)

    def total(v, *axes):
        for axis, count in axes:
            step = 1
            while step < count:
                v = v + lax.ppermute(v, axis, [(i, i ^ step) for i in range(count)])
                step *= 2
        return v

    mod_grads = total(jnp.stack([mod_rows(sums[0]), mod_rows(sums[1])]), ("seq", seq))
    mod_grads = mod_grads.reshape(layers, clips, seq, -1)
    of_columns = lax.dynamic_index_in_dim(mod_grads, lax.axis_index("seq"), 2, keepdims=False)
    own_mod_grad = lax.all_to_all(of_columns.transpose(1, 0, 2), CLIP, 0, 0, tiled=True)
    ada_bias_grad = jnp.sum(own_mod_grad, axis=0)
    rounded_mod = own_mod_grad.astype(BF16)
    ada_weight_grad = jnp.einsum("kd,klc->ldc", squashed, rounded_mod, preferred_element_type=F32)
    squash_part = jnp.einsum("klc,ldc->kd", rounded_mod, ada_weight, preferred_element_type=F32)
    bias_sums = [bias_rows_of(sums[0]), bias_rows_of(sums[1])]
    bias_rows = bias_sums[0].shape[0]
    devices = clips * seq
    device = clip_index * seq + lax.axis_index("seq")
    peak_rows = -(-devices * layers * HEADS // d)
    own_peaks = jnp.concatenate(peaks)[None]
    placed = lax.dynamic_update_slice(
        jnp.zeros((devices, layers * HEADS), F32), own_peaks, (device, 0)
    ).reshape(-1)
    placed = jnp.pad(placed, (0, peak_rows * d - placed.shape[0])).reshape(peak_rows, d)
    summed = total(
        jnp.concatenate([*bias_sums, squash_part, placed], axis=0), (CLIP, clips), ("seq", seq)
    )
    bias_sums = summed[: 2 * bias_rows].reshape(layers, bias_rows, d)
    own_squash = lax.dynamic_slice_in_dim(summed, 2 * bias_rows + clip_index, 1, axis=0)
    peaks = summed[2 * bias_rows + clips :].reshape(-1)[: devices * layers * HEADS]
    logit_peak = jnp.max(peaks.reshape(devices, layers, HEADS), axis=0)
    column_index = lax.axis_index("seq") * own_columns + jnp.arange(own_columns, dtype=jnp.int32)
    head_of = column_index % d // (d // HEADS)
    head_match = (head_of[:, None] == jnp.arange(HEADS, dtype=jnp.int32)[None, :]).astype(F32)
    roots = jnp.sqrt(clip_limit / jnp.maximum(logit_peak, clip_limit))
    column_roots = jnp.sum(roots[:, None, :] * head_match[None, :, :], axis=-1)
    column_scale = jnp.where(column_index[None, :] < 2 * d, column_roots, 1.0)
    clipped_qkv = qkv_weight.astype(F32) * column_scale[:, None, :]
    silu_value, silu_pull = jax.vjp(jax.nn.silu, conditioning)
    conditioning_grad = silu_pull(own_squash)[0]
    return (
        output_latents,
        latents_grad.reshape(seq, frames, places // seq, d)
        .transpose(1, 0, 2, 3)
        .reshape(1, frames, places, d),
        conditioning_grad,
        ada_weight_grad,
        ada_bias_grad,
        jnp.stack([first_shed[0], second_shed[0]]),
        jnp.stack([first_shed[1], second_shed[1]]),
        jnp.stack([first_shed[2], second_shed[2]]),
        jnp.stack([first_shed[3], second_shed[3]]),
        bias_sums[:, :3],
        bias_sums[:, 4:].reshape(layers, ff),
        bias_sums[:, 3],
        clipped_qkv,
        logit_peak,
    )


def solution(mesh):
    clips, seq = mesh.shape["clip"], mesh.shape["seq"]
    finer = jax.sharding.Mesh(
        mesh.devices.reshape(clips // 2, 2, seq), ("z", "core", "seq")
    )
    every = (*CLIP, "seq")
    tokens = P(CLIP, "seq", None, None)
    matrix = P(None, CLIP, "seq")
    return jax.shard_map(
        partial(on_device, clips=clips, seq=seq),
        mesh=finer,
        in_specs=(
            tokens,
            P(CLIP, None),
            P(None, None, every),
            P(None, every),
            matrix,
            matrix,
            matrix,
            matrix,
            P(),
            P(),
            P(),
            tokens,
        ),
        out_specs=(
            tokens,
            tokens,
            P(CLIP, None),
            P(None, None, every),
            P(None, every),
            matrix,
            matrix,
            matrix,
            matrix,
            P(),
            P(),
            P(),
            matrix,
            P(),
        ),
        check_vma=False,
    )
```

time: 1570 us -> 1110 us (0.71)
  waiting for transfers between devices: 637 us -> 245 us
  blocking collectives: 144 us -> 53.2 us
  local copies, waits for them, and re-layouts: 53.7 us -> 89.7 us
  other arithmetic: 67.9 us -> 47.1 us
    ppermute x36 -> x43, waiting for transfers between devices: 367 us -> 196 us  [the longest x36 178 us: hop(): return lax.ppermute(x, CLIP, [(i, i ^ distance) for i in range(count)])]
    reduce_scatter x6, waiting for transfers between devices: 122 us -> 9.92 us  [reduce_seq(): lax.psum_scatter(half.reshape(-1, d), 'seq', scatter_dimension=0, tiled=T...]
    all_gather x2 -> x1, blocking collectives: 136 us -> 37.2 us  [on_device(): every_condition = lax.all_gather(conditioning, CLIP, axis=0, tiled=True)]
    all_gather x6, waiting for transfers between devices: 116 us -> 17.7 us  [along_seq(): return lax.all_gather(blocks, 'seq', axis=0, tiled=False)]
    add x10 -> x11, other arithmetic: 43 us -> 4.86 us  [the longest x7 2.68 us: total(): v = v + lax.ppermute(v, axis, [(i, i ^ step) for i in range(count)])]
    unnamed x57 -> x174, local copies, waits for them, and re-layouts: 7.53 us -> 38.4 us
    unnamed x15 -> x12, waiting for transfers between devices: 24 us -> 0.2 us
    all_to_all x4, waiting for transfers between devices: 2.41 us -> 18.3 us  [swap_tokens(): return lax.all_to_all(block, 'seq', 0, 0, tiled=True).reshape(n, d)]
  transfers between devices with their start and end apart: 56 -> 60, of which waited for: 32 -> 30; matrix products, arithmetic and copies ran while one was open for 7% -> 9% of each run, Pallas kernels for 30% -> 51%
where the time goes in v2:
time: 1110 us; the launch traced here: 1100 us
  Pallas kernels  579 us (52%)
  waiting for transfers between devices  245 us (22%)
  local copies, waits for them, and re-layouts  89.7 us (8%)
  starting transfers between devices  66 us (6%)
  blocking collectives  53.2 us (5%)
  other arithmetic  47.1 us (4%)
  between operations  15.5 us (1%)
    pallas_call x38, Pallas kernels, call(): return lambda *args: kernel(*args, *deps)  579 us
    ppermute x36, waiting for transfers between devices, hop(): return lax.ppermute(x, CLIP, [(i, i ^ distance) for i in range(count)])  178 us
    unnamed x174, local copies, waits for them, and re-layouts  38.4 us
    all_gather x1, blocking collectives, on_device(): every_condition = lax.all_gather(conditioning, CLIP, axis=0, tiled=True)  37.2 us
    ppermute x36, starting transfers between devices, hop(): return lax.ppermute(x, CLIP, [(i, i ^ distance) for i in range(count)])  37.2 us
  transfers between devices with their start and end apart: 60, of which 30 were waited for; matrix products, arithmetic and copies ran while one was open for 9% of the time, Pallas kernels for 51%

profile of v2, /device:TPU:0, one launch (start us, length us, event | category | flops | bytes accessed | tf_op | source)
XLA Modules:
  0.0 1098.0 jit_solution(1357462934116328519)
XLA Ops:
  21.0 7.7 collective-permute-done
  31.6 28.3 %collective-permute-done.1.refs_0_ = bf16[2,144,1152]{2,1,0:T(8,128)(2,1)} collective-permute-done((bf16[2,144,1152]{2,1,0:T(8,128)(2,1)S(1)}, bf16[2,144,1152]{2,1,0:T(8,128)(2,1)}, u32[]{:S(2)}, u32[]{:S(2)}) %collective-permute-start.1) | collective-permute-done | bytes 663584 | tf_op jit(solution)/shard_map/ppermute | solution.py:798
  65.5 8.2 collective-permute-done.2
  79.2 37.2 %all-gather.7 = f32[8,1,1152]{2,1,0:T(1,128)S(1)} all-gather(f32[1,1,1152]{2,1,0:T(1,128)S(1)} %bitcast.308), channel_id=1, replica_groups=mesh['z'=4,'core'=2,'seq'=4] {'z','core'}, dimensions={0}, use_global_device_ids=true | all-gather | bytes 41472 | tf_op jit(solution)/shard_map/all_gather | solution.py:829
  116.8 8.0 all_to_all.30
  124.9 8.0 all-gather
  139.1 7.1 collective-permute-done.4
  157.2 10.0 shard_map.232
  167.2 16.6 %shard_map.233 = (bf16[1024,1152]{1,0:T(8,128)(2,1)}, bf16[1024,3456]{1,0:T(8,128)(2,1)}) custom-call(bf16[1024,1152]{1,0:T(8,128)(2,1)} %bitcast.277, f32[8,1152]{1,0:T(8,128)} %get-tuple-element.342.refs_1_.refs_2_.refs_5_.refs_4_, bf16[1152,3456]{1,0:T(8,128)(2,1)} %get-tuple-element.131.refs_2_.refs_1_, f32[1,3456]{1,0:T(1,128)} %broadcast_in_dim.73.refs_3_), custom_call_target="tpu_custom_call" | custom-call | flops 8153726976 | bytes 19759104 | tf_op jit(solution)/shard_map/pallas_call | solution.py:49
  193.1 13.0 %shard_map.235 = (bf16[4,4,64,1152]{3,2,1,0:T(8,128)(2,1)}, f32[4,16,256]{2,1,0:T(8,128)}, f32[4,1,16]{2,1,0:T(1,128)}) custom-call(bf16[4,4,64,3456]{3,2,1,0:T(8,128)(2,1)} %bitcast.247), custom_call_target="tpu_custom_call" | custom-call | flops 4294967296 | bytes 9437184 | tf_op jit(solution)/shard_map/pallas_call | solution.py:49
  208.8 9.1 shard_map.238
  235.8 9.0 shard_map.243.refs_1_.refs_3_
  244.9 23.1 %shard_map.244 = (bf16[1024,4608]{1,0:T(8,128)(2,1)}, bf16[1024,4608]{1,0:T(8,128)(2,1)}) custom-call(bf16[1024,1152]{1,0:T(8,128)(2,1)} %get-tuple-element.143.refs_0_.refs_1_, bf16[1152,4608]{1,0:T(8,128)(2,1)} %shard_map.243.refs_1_.refs_3_, f32[1,4608]{1,0:T(1,128)} %get-tuple-element.359.refs_2_), custom_call_target="tpu_custom_call" | custom-call | flops 10871635968 | bytes 31850496 | tf_op jit(solution)/shard_map/pallas_call | solution.py:49
  281.7 10.0 shard_map.247.refs_3_.refs_2_
  291.7 19.1 %shard_map.248 = (bf16[1024,1152]{1,0:T(8,128)(2,1)}, bf16[1024,1152]{1,0:T(8,128)(2,1)}) custom-call(bf16[1024,4608]{1,0:T(8,128)(2,1)} %get-tuple-element.151.refs_1_.refs_0_, f32[1024,1152]{1,0:T(8,128)} %get-tuple-element.152.refs_1_, f32[8,1152]{1,0:T(8,128)} %get-tuple-element.342.refs_1_.refs_2_.refs_5_.refs_4_, ...), custom_call_target="tpu_custom_call" | custom-call | flops 10871635968 | bytes 29491200 | tf_op jit(solution)/shard_map/pallas_call | solution.py:49
  313.1 17.6 %all-gather.21.cloned.1.call-done = bf16[16,144,1152]{2,1,0:T(8,128)(2,1)} async-done(((bf16[4,144,1152]{2,1,0:T(8,128)(2,1)}), bf16[16,144,1152]{2,1,0:T(8,128)(2,1)}) %all-gather.21.cloned.1.call-update) | async-done | bytes 5308432 | tf_op jit(solution)/shard_map/all_gather | solution.py:855
  336.9 30.3 %collective-permute-done.14.refs_1_ = bf16[2,144,1152]{2,1,0:T(8,128)(2,1)} collective-permute-done((bf16[2,144,1152]{2,1,0:T(8,128)(2,1)}, bf16[2,144,1152]{2,1,0:T(8,128)(2,1)}, u32[]{:S(2)}, u32[]{:S(2)}) %collective-permute-start.14) | collective-permute-done | bytes 663584 | tf_op jit(solution)/shard_map/ppermute | solution.py:798
  367.3 9.9 all-to-all-done.2
  381.9 10.7 shard_map.253
  392.6 16.5 %shard_map.254 = (bf16[1024,1152]{1,0:T(8,128)(2,1)}, bf16[1024,3456]{1,0:T(8,128)(2,1)}) custom-call(bf16[1024,1152]{1,0:T(8,128)(2,1)} %get-tuple-element.158.refs_0_.refs_1_.refs_2_, f32[8,1152]{1,0:T(8,128)} %get-tuple-element.343.refs_1_.refs_2_.refs_5_.refs_4_, bf16[1152,3456]{1,0:T(8,128)(2,1)} %get-tuple-element.159.refs_2_.refs_1_, ...), custom_call_target="tpu_custom_call" | custom-call | flops 8153726976 | bytes 19759104 | tf_op jit(solution)/shard_map/pallas_call | solution.py:49
  409.1 12.9 %shard_map.255 = (bf16[16,4,16,1152]{3,2,1,0:T(8,128)(2,1)}, f32[4,16,256]{2,1,0:T(8,128)}, f32[4,1,16]{2,1,0:T(1,128)}) custom-call(bf16[16,4,16,3456]{3,2,1,0:T(8,128)(2,1)} %bitcast.312), custom_call_target="tpu_custom_call" | custom-call | flops 4294967296 | bytes 9437184 | tf_op jit(solution)/shard_map/pallas_call | solution.py:49
  422.0 9.6 shard_map.256
  431.8 8.9 collective-permute-done.16.refs_2_
  442.9 9.0 shard_map.258.refs_1_.refs_3_
  452.0 23.1 %shard_map.259 = (bf16[1024,4608]{1,0:T(8,128)(2,1)}, bf16[1024,4608]{1,0:T(8,128)(2,1)}) custom-call(bf16[1024,1152]{1,0:T(8,128)(2,1)} %get-tuple-element.163.refs_0_.refs_1_, bf16[1152,4608]{1,0:T(8,128)(2,1)} %shard_map.258.refs_1_.refs_3_, f32[1,4608]{1,0:T(1,128)} %get-tuple-element.358.refs_2_), custom_call_target="tpu_custom_call" | custom-call | flops 10871635968 | bytes 31850496 | tf_op jit(solution)/shard_map/pallas_call | solution.py:49
  479.7 18.2 %shard_map.262 = (bf16[4,4,144,1152]{3,2,1,0:T(8,128)(2,1)}, bf16[4,4,144,1152]{3,2,1,0:T(8,128)(2,1)}) custom-call(s32[2]{0:T(128)} %pad_add_fusion.refs_0_, bf16[1024,4608]{1,0:T(8,128)(2,1)} %get-tuple-element.165.refs_2_.refs_1_.refs_0_, bf16[1024,1152]{1,0:T(8,128)(2,1)} %get-tuple-element.166.refs_1_.refs_2_.refs_0_, ...), custom_call_target="tpu_custom_call" | custom-call | flops 10871635968 | bytes 22413312 | tf_op jit(solution)/shard_map/pallas_call | solution.py:49
  498.2 10.0 shard_map.264.refs_2_.refs_3_
  517.5 19.1 %shard_map.266 = (bf16[1024,1152]{1,0:T(8,128)(2,1)}, bf16[1024,1152]{1,0:T(8,128)(2,1)}) custom-call(bf16[1024,4608]{1,0:T(8,128)(2,1)} %get-tuple-element.165.refs_2_.refs_1_.refs_0_, f32[1024,1152]{1,0:T(8,128)} %get-tuple-element.172.refs_1_, f32[8,1152]{1,0:T(8,128)} %get-tuple-element.343.refs_1_.refs_2_.refs_5_.refs_4_, ...), custom_call_target="tpu_custom_call" | custom-call | flops 10871635968 | bytes 29491200 | tf_op jit(solution)/shard_map/pallas_call | solution.py:49
  540.5 37.4 %shard_map.267 = (bf16[1024,4608]{1,0:T(8,128)(2,1)}, f32[1,4608]{1,0:T(1,128)}, f32[1024,1152]{1,0:T(8,128)}) custom-call(bf16[1024,1152]{1,0:T(8,128)(2,1)} %get-tuple-element.166.refs_1_.refs_2_.refs_0_, bf16[1024,4608]{1,0:T(8,128)(2,1)} %get-tuple-element.167.refs_1_, bf16[4608,1152]{1,0:T(8,128)(2,1)} %shard_map.264.refs_2_.refs_3_, ...), custom_call_target="tpu_custom_call" | custom-call | flops 21743271936 | bytes 47185920 | tf_op jit(solution)/shard_map/pallas_call | solution.py:49
  581.6 17.8 %shard_map.269 = (bf16[4,4,144,1152]{3,2,1,0:T(8,128)(2,1)}, bf16[4,4,144,1152]{3,2,1,0:T(8,128)(2,1)}) custom-call(s32[2]{0:T(128)} %pad_add_fusion.refs_0_, bf16[1024,1152]{1,0:T(8,128)(2,1)} %get-tuple-element.163.refs_0_.refs_1_, bf16[1024,4608]{1,0:T(8,128)(2,1)} %get-tuple-element.182.refs_2_), custom_call_target="tpu_custom_call" | custom-call | flops 10871635968 | bytes 22413312 | tf_op jit(solution)/shard_map/pallas_call | solution.py:49
  599.4 14.9 %shard_map.270 = (f32[1024,1152]{1,0:T(8,128)}, bf16[1024,1152]{1,0:T(8,128)(2,1)}, bf16[4,1024,288]{2,1,0:T(8,128)(2,1)}, bf16[1024,1152]{1,0:T(8,128)(2,1)}, f32[8,1152]{1,0:T(8,128)}) custom-call(f32[1024,1152]{1,0:T(8,128)} %get-tuple-element.180.refs_0_, f32[1024,1152]{1,0:T(8,128)} %get-tuple-element.172.refs_1_, ...), custom_call_target="tpu_custom_call" | custom-call | flops 2717908992 | bytes 28606464 | tf_op jit(solution)/shard_map/pallas_call | solution.py:49
  627.5 25.9 %shard_map.272 = (bf16[16,4,16,3456]{3,2,1,0:T(8,128)(2,1)}, bf16[4,16,4,16,864]{4,3,2,1,0:T(8,128)(2,1)}, f32[1,3456]{1,0:T(1,128)}) custom-call(bf16[16,4,16,3456]{3,2,1,0:T(8,128)(2,1)} %bitcast.313, bf16[16,4,16,1152]{3,2,1,0:T(8,128)(2,1)} %bitcast.311, f32[4,16,256]{2,1,0:T(8,128)} %get-tuple-element.185.refs_2_, ...), custom_call_target="tpu_custom_call" | custom-call | flops 12884901888 | bytes 23592960 | tf_op jit(solution)/shard_map/pallas_call | solution.py:49
  661.2 17.2 %shard_map.274 = (bf16[1024,1152]{1,0:T(8,128)(2,1)}, f32[8,1152]{1,0:T(8,128)}) custom-call(bf16[1024,3456]{1,0:T(8,128)(2,1)} %get-tuple-element.192.refs_0_, bf16[1152,3456]{1,0:T(8,128)(2,1)} %get-tuple-element.159.refs_2_.refs_1_, bf16[1024,1152]{1,0:T(8,128)(2,1)} %get-tuple-element.158.refs_0_.refs_1_.refs_2_, ...), custom_call_target="tpu_custom_call" | custom-call | flops 8153726976 | bytes 26836992 | tf_op jit(solution)/shard_map/pallas_call | solution.py:49
  682.9 21.8 %shard_map.276 = (bf16[4,4,144,1152]{3,2,1,0:T(8,128)(2,1)}, bf16[4,4,144,1152]{3,2,1,0:T(8,128)(2,1)}) custom-call(s32[2]{0:T(128)} %pad_add_fusion.refs_0_, bf16[1024,1152]{1,0:T(8,128)(2,1)} %get-tuple-element.179.refs_1_, bf16[1024,1152]{1,0:T(8,128)(2,1)} %bitcast.315, bf16[4,1024,864]{2,1,0:T(8,128)(2,1)} %get-tuple-element.190.refs_3_, ...), custom_call_target="tpu_custom_call" | custom-call | flops 10871635968 | bytes 20054016 | tf_op jit(solution)/shard_map/pallas_call | solution.py:49
  723.3 7.0 shard_map.279.refs_3_
  730.4 18.4 %shard_map.280 = (bf16[4,4,144,1152]{3,2,1,0:T(8,128)(2,1)}, bf16[4,4,144,1152]{3,2,1,0:T(8,128)(2,1)}) custom-call(s32[2]{0:T(128)} %pad_add_fusion.refs_0_, bf16[1024,4608]{1,0:T(8,128)(2,1)} %get-tuple-element.151.refs_1_.refs_0_, bf16[1024,1152]{1,0:T(8,128)(2,1)} %get-tuple-element.200.refs_2_.refs_0_, bf16[4,4,144,1152]{3,2,1,0:T(8,128)(2,1)} %shard_map.279.refs_3_), custom_call_target="tpu_custom_call" | custom-call | flops 10871635968 | bytes 22413312 | tf_op jit(solution)/shard_map/pallas_call | solution.py:49
  753.7 37.5 %shard_map.281 = (bf16[1024,4608]{1,0:T(8,128)(2,1)}, f32[1,4608]{1,0:T(1,128)}, f32[1024,1152]{1,0:T(8,128)}) custom-call(bf16[1024,1152]{1,0:T(8,128)(2,1)} %get-tuple-element.200.refs_2_.refs_0_, bf16[1024,4608]{1,0:T(8,128)(2,1)} %get-tuple-element.201.refs_1_, bf16[4608,1152]{1,0:T(8,128)(2,1)} %shard_map.247.refs_3_.refs_2_, ...), custom_call_target="tpu_custom_call" | custom-call | flops 21743271936 | bytes 47185920 | tf_op jit(solution)/shard_map/pallas_call | solution.py:49
  792.5 7.0 shard_map.283.refs_3_
  801.6 18.2 %shard_map.284 = (bf16[4,4,144,1152]{3,2,1,0:T(8,128)(2,1)}, bf16[4,4,144,1152]{3,2,1,0:T(8,128)(2,1)}) custom-call(s32[2]{0:T(128)} %pad_add_fusion.refs_0_, bf16[1024,1152]{1,0:T(8,128)(2,1)} %get-tuple-element.143.refs_0_.refs_1_, bf16[1024,4608]{1,0:T(8,128)(2,1)} %get-tuple-element.209.refs_2_, bf16[4,4,144,1152]{3,2,1,0:T(8,128)(2,1)} %shard_map.283.refs_3_, ...), custom_call_target="tpu_custom_call" | custom-call | flops 10871635968 | bytes 22413312 | tf_op jit(solution)/shard_map/pallas_call | solution.py:49
  819.9 14.9 %shard_map.285 = (f32[1024,1152]{1,0:T(8,128)}, bf16[1024,1152]{1,0:T(8,128)(2,1)}, bf16[4,1024,288]{2,1,0:T(8,128)(2,1)}, bf16[1024,1152]{1,0:T(8,128)(2,1)}, f32[8,1152]{1,0:T(8,128)}) custom-call(f32[1024,1152]{1,0:T(8,128)} %get-tuple-element.207.refs_2_.refs_0_, f32[1024,1152]{1,0:T(8,128)} %get-tuple-element.152.refs_1_, ...), custom_call_target="tpu_custom_call" | custom-call | flops 2717908992 | bytes 28606464 | tf_op jit(solution)/shard_map/pallas_call | solution.py:49
  837.1 7.1 shard_map.286.refs_3_
  849.7 26.0 %shard_map.287 = (bf16[4,4,64,3456]{3,2,1,0:T(8,128)(2,1)}, bf16[4,4,4,64,864]{4,3,2,1,0:T(8,128)(2,1)}, f32[1,3456]{1,0:T(1,128)}) custom-call(bf16[4,4,64,3456]{3,2,1,0:T(8,128)(2,1)} %bitcast.248, bf16[4,4,64,1152]{3,2,1,0:T(8,128)(2,1)} %bitcast.310, f32[4,16,256]{2,1,0:T(8,128)} %get-tuple-element.214.refs_2_, bf16[4,4,144,1152]{3,2,1,0:T(8,128)(2,1)} %shard_map.286.refs_3_), custom_call_target="tpu_custom_call" | custom-call | flops 12884901888 | bytes 23592960 | tf_op jit(solution)/shard_map/pallas_call | solution.py:49
  886.7 22.0 %shard_map.289 = (bf16[4,4,144,1152]{3,2,1,0:T(8,128)(2,1)}, bf16[4,4,144,1152]{3,2,1,0:T(8,128)(2,1)}) custom-call(s32[2]{0:T(128)} %pad_add_fusion.refs_0_, bf16[1024,1152]{1,0:T(8,128)(2,1)} %get-tuple-element.137.refs_1_, bf16[1024,1152]{1,0:T(8,128)(2,1)} %get-tuple-element.138.refs_0_.refs_1_.refs_2_, ...), custom_call_target="tpu_custom_call" | custom-call | flops 10871635968 | bytes 20054016 | tf_op jit(solution)/shard_map/pallas_call | solution.py:49
  917.3 9.4 reduce-scatter.15.cloned.1.call-done
  931.4 17.3 %shard_map.291 = (f32[1024,1152]{1,0:T(8,128)}, f32[8,1152]{1,0:T(8,128)}) custom-call(bf16[1024,3456]{1,0:T(8,128)(2,1)} %get-tuple-element.219.refs_0_, bf16[1152,3456]{1,0:T(8,128)(2,1)} %get-tuple-element.131.refs_2_.refs_1_, bf16[1024,1152]{1,0:T(8,128)(2,1)} %bitcast.279, f32[1024,1152]{1,0:T(8,128)} %get-tuple-element.216.refs_2_.refs_3_, ...), custom_call_target="tpu_custom_call" | custom-call | flops 8153726976 | bytes 26836992 | tf_op jit(solution)/shard_map/pallas_call | solution.py:49
  948.7 12.1 %collective-permute-done.31.refs_3_ = bf16[2,144,1152]{2,1,0:T(8,128)(2,1)S(1)} collective-permute-done((bf16[2,144,1152]{2,1,0:T(8,128)(2,1)S(1)}, bf16[2,144,1152]{2,1,0:T(8,128)(2,1)S(1)}, u32[]{:S(2)}, u32[]{:S(2)}) %collective-permute-start.31) | collective-permute-done | bytes 663584 | tf_op jit(solution)/shard_map/ppermute | solution.py:798
  1029.2 7.2 collective-permute-done.36
  1049.2 28.8 %collective-permute-done.41 = bf16[2,144,1152]{2,1,0:T(8,128)(2,1)S(1)} collective-permute-done((bf16[2,144,1152]{2,1,0:T(8,128)(2,1)S(1)}, bf16[2,144,1152]{2,1,0:T(8,128)(2,1)S(1)}, u32[]{:S(2)}, u32[]{:S(2)}) %collective-permute-start.41) | collective-permute-done | bytes 663584 | tf_op jit(solution)/shard_map/ppermute | solution.py:798
  (456 shorter events, 304.3 us)
Async XLA Ops:
  10.6 49.3 %all-to-all-start = ((bf16[4,256,1152]{2,1,0:T(8,128)(2,1)}), bf16[4,256,1152]{2,1,0:T(8,128)(2,1)S(1)}, u32[]{:S(2)}, u32[]{:S(2)}) async-start(bf16[4,256,1152]{2,1,0:T(8,128)(2,1)} %bitcast.240), calls=%async_computation | async-start | bytes 4718592 | tf_op jit(solution)/shard_map/all_to_all | solution.py:892
  15.7 132.3 %all-gather.15.cloned.1.call-start = ((), (), s32[]{:S(2)}) async-start(), calls=%async_computation.18 | async-start | bytes 6635520 | tf_op jit(solution)/shard_map/all_gather | solution.py:855
  19.3 9.4 collective-permute-start
  28.8 31.1 %collective-permute-start.1 = (bf16[2,144,1152]{2,1,0:T(8,128)(2,1)S(1)}, bf16[2,144,1152]{2,1,0:T(8,128)(2,1)}, u32[]{:S(2)}, u32[]{:S(2)}) collective-permute-start(bf16[2,144,1152]{2,1,0:T(8,128)(2,1)S(1)} %pad_maximum_fusion.9), channel_id=1, source_target_pairs={{0,16},{4,20},{8,24},{12,28},{16,0},{20,4},{24,8},{28,12},{1,17},{... | collective-permute-start | bytes 1990664 | tf_op jit(solution)/shard_map/ppermute | solution.py:798
  63.9 160.5 %all-gather.17.cloned.1.call-start = ((), (), s32[]{:S(2)}) async-start(), calls=%async_computation.19 | async-start | bytes 6635520 | tf_op jit(solution)/shard_map/all_gather | solution.py:855
  75.7 58.0 %collective-permute-start.3 = (bf16[2,144,1152]{2,1,0:T(8,128)(2,1)}, bf16[2,144,1152]{2,1,0:T(8,128)(2,1)S(1)}, u32[]{:S(2)}, u32[]{:S(2)}) collective-permute-start(bf16[2,144,1152]{2,1,0:T(8,128)(2,1)} %pad_maximum_fusion.10), channel_id=1, source_target_pairs={{0,16},{4,20},{8,24},{12,28},{16,0},{20,4},{24,8},{28,12},{1,17},{... | collective-permute-start | bytes 1990664 | tf_op jit(solution)/shard_map/ppermute | solution.py:798
  136.9 133.5 %all-gather.19.cloned.1.call-start = ((), (), s32[]{:S(2)}) async-start(), calls=%async_computation.20 | async-start | bytes 6635520 | tf_op jit(solution)/shard_map/all_gather | solution.py:855
  148.1 9.1 collective-permute-start.5
  154.0 32.4 %collective-permute-start.6 = (bf16[2,144,1152]{2,1,0:T(8,128)(2,1)S(1)}, bf16[2,144,1152]{2,1,0:T(8,128)(2,1)S(1)}, u32[]{:S(2)}, u32[]{:S(2)}) collective-permute-start(bf16[2,144,1152]{2,1,0:T(8,128)(2,1)S(1)} %copy-done.26), channel_id=1, source_target_pairs={{0,16},{4,20},{8,24},{12,28},{16,0},{20,4},{24,8},{28,12},{1,17},{... | collective-permute-start | bytes 1990664 | tf_op jit(solution)/shard_map/ppermute | solution.py:798
  190.5 140.2 %all-gather.21.cloned.1.call-start = ((), (), s32[]{:S(2)}) async-start(), calls=%async_computation.21 | async-start | bytes 6635520 | tf_op jit(solution)/shard_map/all_gather | solution.py:855
  193.1 13.0 %collective-permute-start.7 = (bf16[144,1152]{1,0:T(8,128)(2,1)}, bf16[144,1152]{1,0:T(8,128)(2,1)S(1)}, u32[]{:S(2)}, u32[]{:S(2)}) collective-permute-start(bf16[144,1152]{1,0:T(8,128)(2,1)} %shard_map.236), channel_id=1, source_target_pairs={{0,8},{4,12},{8,0},{12,4},{16,24},{20,28},{24,16},{28,20},{1,9},{5... | collective-permute-start | bytes 995336 | tf_op jit(solution)/shard_map/ppermute | solution.py:798
  206.8 11.1 %collective-permute-start.8 = (bf16[144,1152]{1,0:T(8,128)(2,1)}, bf16[144,1152]{1,0:T(8,128)(2,1)S(1)}, u32[]{:S(2)}, u32[]{:S(2)}) collective-permute-start(bf16[144,1152]{1,0:T(8,128)(2,1)} %shard_map.239), channel_id=1, source_target_pairs={{0,8},{4,12},{8,0},{12,4},{16,24},{20,28},{24,16},{28,20},{1,9},{5... | collective-permute-start | bytes 995336 | tf_op jit(solution)/shard_map/ppermute | solution.py:798
  208.8 14.9 %collective-permute-start.9 = (bf16[144,1152]{1,0:T(8,128)(2,1)}, bf16[144,1152]{1,0:T(8,128)(2,1)S(1)}, u32[]{:S(2)}, u32[]{:S(2)}) collective-permute-start(bf16[144,1152]{1,0:T(8,128)(2,1)} %shard_map.240), channel_id=1, source_target_pairs={{0,8},{4,12},{8,0},{12,4},{16,24},{20,28},{24,16},{28,20},{1,9},{5... | collective-permute-start | bytes 995336 | tf_op jit(solution)/shard_map/ppermute | solution.py:798
  227.1 40.8 %collective-permute-start.11 = (bf16[2,144,1152]{2,1,0:T(8,128)(2,1)}, bf16[2,144,1152]{2,1,0:T(8,128)(2,1)}, u32[]{:S(2)}, u32[]{:S(2)}) collective-permute-start(bf16[2,144,1152]{2,1,0:T(8,128)(2,1)} %pad_maximum_fusion.12.refs_3_), channel_id=1, source_target_pairs={{0,16},{4,20},{8,24},{12,28},{16,0},{20,4},{24,8},{28,12},{1,17},{... | collective-permute-start | bytes 1990664 | tf_op jit(solution)/shard_map/ppermute | solution.py:798
  270.3 161.4 %all-gather.23.cloned.1.call-start = ((), (), s32[]{:S(2)}) async-start(), calls=%async_computation.22 | async-start | bytes 6635520 | tf_op jit(solution)/shard_map/all_gather | solution.py:855
  271.6 39.2 %collective-permute-start.13 = (bf16[2,144,1152]{2,1,0:T(8,128)(2,1)S(1)}, bf16[2,144,1152]{2,1,0:T(8,128)(2,1)}, u32[]{:S(2)}, u32[]{:S(2)}) collective-permute-start(bf16[2,144,1152]{2,1,0:T(8,128)(2,1)S(1)} %copy-done.27), channel_id=1, source_target_pairs={{0,16},{4,20},{8,24},{12,28},{16,0},{20,4},{24,8},{28,12},{1,17},{... | collective-permute-start | bytes 1990664 | tf_op jit(solution)/shard_map/ppermute | solution.py:798
  330.8 51.1 %collective-permute-start.15 = (bf16[4,4,144,1152]{3,2,1,0:T(8,128)(2,1)}, bf16[4,4,144,1152]{3,2,1,0:T(8,128)(2,1)}, u32[]{:S(2)}, u32[]{:S(2)}) collective-permute-start(bf16[4,4,144,1152]{3,2,1,0:T(8,128)(2,1)} %shard_map.252.refs_1_), channel_id=1, source_target_pairs={{0,4},{4,0},{8,12},{12,8},{16,20},{20,16},{24,28},{28,24},{1,5},{5... | collective-permute-start | bytes 15925256 | tf_op jit(solution)/shard_map/ppermute | solution.py:798
  330.8 46.5 %all-to-all-start.2 = ((bf16[4,256,1152]{2,1,0:T(8,128)(2,1)}), bf16[4,256,1152]{2,1,0:T(8,128)(2,1)S(1)}, u32[]{:S(2)}, u32[]{:S(2)}) async-start(bf16[4,256,1152]{2,1,0:T(8,128)(2,1)} %bitcast.43), calls=%async_computation.2 | async-start | bytes 4718592 | tf_op jit(solution)/shard_map/all_to_all | solution.py:892
  334.4 145.1 %all-gather.25.cloned.1.call-start = ((), (), s32[]{:S(2)}) async-start(), calls=%async_computation.23 | async-start | bytes 6635520 | tf_op jit(solution)/shard_map/all_gather | solution.py:855
  334.5 32.8 %collective-permute-start.14 = (bf16[2,144,1152]{2,1,0:T(8,128)(2,1)}, bf16[2,144,1152]{2,1,0:T(8,128)(2,1)}, u32[]{:S(2)}, u32[]{:S(2)}) collective-permute-start(bf16[2,144,1152]{2,1,0:T(8,128)(2,1)} %shard_map.250), channel_id=1, source_target_pairs={{0,16},{4,20},{8,24},{12,28},{16,0},{20,4},{24,8},{28,12},{1,17},{... | collective-permute-start | bytes 1990664 | tf_op jit(solution)/shard_map/ppermute | solution.py:798
  381.2 242.4 %reduce-scatter.7.cloned.1.call-start = ((), (), s32[]{:S(2)}) async-start(), calls=%async_computation.12 | async-start | bytes 6635520 | tf_op jit(solution)/shard_map/reduce_scatter | solution.py:870
  479.5 18.4 %collective-permute-start.17 = (bf16[4,4,144,1152]{3,2,1,0:T(8,128)(2,1)}, bf16[4,4,144,1152]{3,2,1,0:T(8,128)(2,1)}, u32[]{:S(2)}, u32[]{:S(2)}) collective-permute-start(bf16[4,4,144,1152]{3,2,1,0:T(8,128)(2,1)} %shard_map.261.refs_3_.refs_1_), channel_id=1, source_target_pairs={{0,4},{4,0},{8,12},{12,8},{16,20},{20,16},{24,28},{28,24},{1,5},{5... | collective-permute-start | bytes 15925256 | tf_op jit(solution)/shard_map/ppermute | solution.py:798
  497.9 10.4 collective-permute-start.18
  536.7 43.5 %all-to-all-start.3 = ((bf16[4,256,1152]{2,1,0:T(8,128)(2,1)}), bf16[4,256,1152]{2,1,0:T(8,128)(2,1)S(1)}, u32[]{:S(2)}, u32[]{:S(2)}) async-start(bf16[4,256,1152]{2,1,0:T(8,128)(2,1)} %bitcast.281), calls=%async_computation.3 | async-start | bytes 4718592 | tf_op jit(solution)/shard_map/all_to_all | solution.py:892
  540.4 208.5 %reduce-scatter.9.cloned.1.call-start = ((), (), s32[]{:S(2)}) async-start(), calls=%async_computation.13 | async-start | bytes 6635520 | tf_op jit(solution)/shard_map/reduce_scatter | solution.py:870
  599.4 14.9 %collective-permute-start.19 = (bf16[4,4,144,1152]{3,2,1,0:T(8,128)(2,1)}, bf16[4,4,144,1152]{3,2,1,0:T(8,128)(2,1)S(1)}, u32[]{:S(2)}, u32[]{:S(2)}) collective-permute-start(bf16[4,4,144,1152]{3,2,1,0:T(8,128)(2,1)} %get-tuple-element.186), channel_id=1, source_target_pairs={{0,4},{4,0},{8,12},{12,8},{16,20},{20,16},{24,28},{28,24},{1,5},{5... | collective-permute-start | bytes 15925256 | tf_op jit(solution)/shard_map/ppermute | solution.py:798
  625.0 32.6 %collective-permute-start.20 = (bf16[2,144,1152]{2,1,0:T(8,128)(2,1)S(1)}, bf16[2,144,1152]{2,1,0:T(8,128)(2,1)S(1)}, u32[]{:S(2)}, u32[]{:S(2)}) collective-permute-start(bf16[2,144,1152]{2,1,0:T(8,128)(2,1)S(1)} %bitcast.297), channel_id=1, source_target_pairs={{0,16},{4,20},{8,24},{12,28},{16,0},{20,4},{24,8},{28,12},{1,17},{... | collective-permute-start | bytes 1990664 | tf_op jit(solution)/shard_map/ppermute | solution.py:798
  660.7 17.8 %collective-permute-start.21 = (bf16[144,1152]{1,0:T(8,128)(2,1)S(1)}, bf16[144,1152]{1,0:T(8,128)(2,1)S(1)}, u32[]{:S(2)}, u32[]{:S(2)}) collective-permute-start(bf16[144,1152]{1,0:T(8,128)(2,1)S(1)} %slice_bitcast_fusion.13), channel_id=1, source_target_pairs={{0,8},{4,12},{8,0},{12,4},{16,24},{20,28},{24,16},{28,20},{1,9},{5... | collective-permute-start | bytes 995336 | tf_op jit(solution)/shard_map/ppermute | solution.py:798
  679.2 31.5 %all-to-all-start.4 = ((bf16[4,256,1152]{2,1,0:T(8,128)(2,1)}), bf16[4,256,1152]{2,1,0:T(8,128)(2,1)S(1)}, u32[]{:S(2)}, u32[]{:S(2)}) async-start(bf16[4,256,1152]{2,1,0:T(8,128)(2,1)} %bitcast.242), calls=%async_computation.5 | async-start | bytes 4718592 | tf_op jit(solution)/shard_map/all_to_all | solution.py:892
  682.8 109.7 %reduce-scatter.11.cloned.1.call-start = ((), (), s32[]{:S(2)}) async-start(), calls=%async_computation.14 | async-start | bytes 6635520 | tf_op jit(solution)/shard_map/reduce_scatter | solution.py:870
  730.4 151.8 %reduce-scatter.13.cloned.1.call-start = ((), (), s32[]{:S(2)}) async-start(), calls=%async_computation.15 | async-start | bytes 6635520 | tf_op jit(solution)/shard_map/reduce_scatter | solution.py:870
  748.8 43.3 %collective-permute-start.24 = (bf16[4,4,144,1152]{3,2,1,0:T(8,128)(2,1)}, bf16[4,4,144,1152]{3,2,1,0:T(8,128)(2,1)}, u32[]{:S(2)}, u32[]{:S(2)}) collective-permute-start(bf16[4,4,144,1152]{3,2,1,0:T(8,128)(2,1)} %get-tuple-element.210), channel_id=1, source_target_pairs={{0,4},{4,0},{8,12},{12,8},{16,20},{20,16},{24,28},{28,24},{1,5},{5... | collective-permute-start | bytes 15925256 | tf_op jit(solution)/shard_map/ppermute | solution.py:798
  750.4 40.9 %collective-permute-start.23 = (bf16[2,144,1152]{2,1,0:T(8,128)(2,1)S(1)}, bf16[2,144,1152]{2,1,0:T(8,128)(2,1)S(1)}, u32[]{:S(2)}, u32[]{:S(2)}) collective-permute-start(bf16[2,144,1152]{2,1,0:T(8,128)(2,1)S(1)} %bitcast.296), channel_id=1, source_target_pairs={{0,16},{4,20},{8,24},{12,28},{16,0},{20,4},{24,8},{28,12},{1,17},{... | collective-permute-start | bytes 1990664 | tf_op jit(solution)/shard_map/ppermute | solution.py:798
  799.6 127.2 %reduce-scatter.15.cloned.1.call-start = ((), (), s32[]{:S(2)}) async-start(), calls=%async_computation.16 | async-start | bytes 6635520 | tf_op jit(solution)/shard_map/reduce_scatter | solution.py:870
  819.9 14.9 %collective-permute-start.25 = (bf16[4,4,144,1152]{3,2,1,0:T(8,128)(2,1)}, bf16[4,4,144,1152]{3,2,1,0:T(8,128)(2,1)S(1)}, u32[]{:S(2)}, u32[]{:S(2)}) collective-permute-start(bf16[4,4,144,1152]{3,2,1,0:T(8,128)(2,1)} %get-tuple-element.215), channel_id=1, source_target_pairs={{0,4},{4,0},{8,12},{12,8},{16,20},{20,16},{24,28},{28,24},{1,5},{5... | collective-permute-start | bytes 15925256 | tf_op jit(solution)/shard_map/ppermute | solution.py:798
  844.3 203.4 %reduce-scatter.17.cloned.1.call-start = ((), (), s32[]{:S(2)}) async-start(), calls=%async_computation.17 | async-start | bytes 6635520 | tf_op jit(solution)/shard_map/reduce_scatter | solution.py:870
  845.4 30.3 %collective-permute-start.27 = (bf16[144,1152]{1,0:T(8,128)(2,1)S(1)}, bf16[144,1152]{1,0:T(8,128)(2,1)S(1)}, u32[]{:S(2)}, u32[]{:S(2)}) collective-permute-start(bf16[144,1152]{1,0:T(8,128)(2,1)S(1)} %slice_bitcast_fusion.12), channel_id=1, source_target_pairs={{0,8},{4,12},{8,0},{12,4},{16,24},{20,28},{24,16},{28,20},{1,9},{5... | collective-permute-start | bytes 995336 | tf_op jit(solution)/shard_map/ppermute | solution.py:798
  847.2 32.1 %collective-permute-start.26 = (bf16[2,144,1152]{2,1,0:T(8,128)(2,1)S(1)}, bf16[2,144,1152]{2,1,0:T(8,128)(2,1)S(1)}, u32[]{:S(2)}, u32[]{:S(2)}) collective-permute-start(bf16[2,144,1152]{2,1,0:T(8,128)(2,1)S(1)} %bitcast.293), channel_id=1, source_target_pairs={{0,16},{4,20},{8,24},{12,28},{16,0},{20,4},{24,8},{28,12},{1,17},{... | collective-permute-start | bytes 1990664 | tf_op jit(solution)/shard_map/ppermute | solution.py:798
  882.2 26.5 %collective-permute-start.29 = (bf16[144,1152]{1,0:T(8,128)(2,1)}, bf16[144,1152]{1,0:T(8,128)(2,1)S(1)}, u32[]{:S(2)}, u32[]{:S(2)}) collective-permute-start(bf16[144,1152]{1,0:T(8,128)(2,1)} %slice_bitcast_fusion.11), channel_id=1, source_target_pairs={{0,8},{4,12},{8,0},{12,4},{16,24},{20,28},{24,16},{28,20},{1,9},{5... | collective-permute-start | bytes 995336 | tf_op jit(solution)/shard_map/ppermute | solution.py:798
  883.7 31.4 %collective-permute-start.28 = (bf16[2,144,1152]{2,1,0:T(8,128)(2,1)S(1)}, bf16[2,144,1152]{2,1,0:T(8,128)(2,1)S(1)}, u32[]{:S(2)}, u32[]{:S(2)}) collective-permute-start(bf16[2,144,1152]{2,1,0:T(8,128)(2,1)S(1)} %bitcast.294), channel_id=1, source_target_pairs={{0,16},{4,20},{8,24},{12,28},{16,0},{20,4},{24,8},{28,12},{1,17},{... | collective-permute-start | bytes 1990664 | tf_op jit(solution)/shard_map/ppermute | solution.py:798
  915.9 45.7 %collective-permute-start.39 = (bf16[4,4,144,1152]{3,2,1,0:T(8,128)(2,1)}, bf16[4,4,144,1152]{3,2,1,0:T(8,128)(2,1)}, u32[]{:S(2)}, u32[]{:S(2)}) collective-permute-start(bf16[4,4,144,1152]{3,2,1,0:T(8,128)(2,1)} %get-tuple-element.242), channel_id=1, source_target_pairs={{0,4},{4,0},{8,12},{12,8},{16,20},{20,16},{24,28},{28,24},{1,5},{5... | collective-permute-start | bytes 15925256 | tf_op jit(solution)/shard_map/ppermute | solution.py:798
  917.3 31.4 %collective-permute-start.30 = (bf16[144,1152]{1,0:T(8,128)(2,1)S(1)}, bf16[144,1152]{1,0:T(8,128)(2,1)S(1)}, u32[]{:S(2)}, u32[]{:S(2)}) collective-permute-start(bf16[144,1152]{1,0:T(8,128)(2,1)S(1)} %slice_bitcast_fusion.10), channel_id=1, source_target_pairs={{0,8},{4,12},{8,0},{12,4},{16,24},{20,28},{24,16},{28,20},{1,9},{5... | collective-permute-start | bytes 995336 | tf_op jit(solution)/shard_map/ppermute | solution.py:798
  929.0 31.8 %collective-permute-start.31 = (bf16[2,144,1152]{2,1,0:T(8,128)(2,1)S(1)}, bf16[2,144,1152]{2,1,0:T(8,128)(2,1)S(1)}, u32[]{:S(2)}, u32[]{:S(2)}) collective-permute-start(bf16[2,144,1152]{2,1,0:T(8,128)(2,1)S(1)} %bitcast.295), channel_id=1, source_target_pairs={{0,16},{4,20},{8,24},{12,28},{16,0},{20,4},{24,8},{28,12},{1,17},{... | collective-permute-start | bytes 1990664 | tf_op jit(solution)/shard_map/ppermute | solution.py:798
  1002.1 10.8 all-to-all-start.5
  1007.9 29.9 %collective-permute-start.40 = (bf16[144,1152]{1,0:T(8,128)(2,1)}, bf16[144,1152]{1,0:T(8,128)(2,1)}, u32[]{:S(2)}, u32[]{:S(2)}) collective-permute-start(bf16[144,1152]{1,0:T(8,128)(2,1)} %slice_bitcast_fusion.8), channel_id=1, source_target_pairs={{0,8},{4,12},{8,0},{12,4},{16,24},{20,28},{24,16},{28,20},{1,9},{5... | collective-permute-start | bytes 995336 | tf_op jit(solution)/shard_map/ppermute | solution.py:798
  1026.3 10.1 collective-permute-start.36
  1048.9 29.1 %collective-permute-start.41 = (bf16[2,144,1152]{2,1,0:T(8,128)(2,1)S(1)}, bf16[2,144,1152]{2,1,0:T(8,128)(2,1)S(1)}, u32[]{:S(2)}, u32[]{:S(2)}) collective-permute-start(bf16[2,144,1152]{2,1,0:T(8,128)(2,1)S(1)} %slice.352), channel_id=1, source_target_pairs={{0,16},{4,20},{8,24},{12,28},{16,0},{20,4},{24,8},{28,12},{1,17},{... | collective-permute-start | bytes 1990664 | tf_op jit(solution)/shard_map/ppermute | solution.py:798
  1079.3 9.5 collective-permute-start.42
  (95 other events, 873.3 us)
Sparse Core Ops, SparseCore 0:
  64.0 62.8 all-gather.14
  137.0 59.2 all-gather.16
  198.7 61.9 all-gather.18
  270.4 60.3 all-gather.20
  333.0 80.5 all-gather.22
  415.8 61.9 all-gather.24
  517.6 85.6 reduce-scatter.6
  623.7 62.2 reduce-scatter.8
  730.5 62.0 reduce-scatter.10
  799.7 61.9 reduce-scatter.12
  864.7 61.9 reduce-scatter.14
  968.7 63.6 reduce-scatter.16

commit v3 on v2

--- a/solution.py
+++ b/solution.py
@@ -316,6 +316,10 @@
     )(go, mods)
 
 
+def slot(k):
+    return k % 2 * 2 + k // 2
+
+
 def shed_specs(seq, zs, rows, d):
     return sds((seq, zs, rows, d), BF16)
 
@@ -362,7 +366,7 @@
         body,
         (zs,),
         [
-            pl.BlockSpec((n, ff // zs), lambda i, place_ref: (0, i ^ place_ref[1])),
+            pl.BlockSpec((n, ff // zs), lambda i, place_ref: (0, slot(i) ^ place_ref[1])),
             whole((n, d)),
         ],
         [piece, piece],
@@ -388,7 +392,7 @@
                 first, stop = c * d // cuts, (c + 1) * d // cuts
                 full = mm(hid_ref[:, first:stop], gi_ref[...], TN).astype(BF16)
                 for block, at, lo, hi in shares(first, stop, rows):
-                    targets[block % 2][0, (block // 2) ^ z, at : at + hi - lo, :] = full[
+                    targets[block % 2][0, slot((block // 2) ^ z), at : at + hi - lo, :] = full[
                         lo - first : hi - first
                     ]
 
@@ -431,7 +435,7 @@
                 right = mm(att_ref[:, first:stop], gb_ref[0], TN).astype(BF16)
                 full = jnp.concatenate([left, right], axis=1)
                 for block, at, lo, hi in shares(first, stop, rows):
-                    targets[block % 2][0, (block // 2) ^ z, at : at + hi - lo, :] = full[
+                    targets[block % 2][0, slot((block // 2) ^ z), at : at + hi - lo, :] = full[
                         lo - first : hi - first
                     ]
 
@@ -642,10 +646,10 @@
     )(qkv, ga, lse)
 
 
-def stream_back(gqkv, w, x, gmid, mods, out_dtype, deps=()):
+def stream_back(gqkv, w, x, gmid, mods, out_dtype, shape=None, deps=()):
     n, wide = gqkv.shape
     d = w.shape[0]
-    mt = fold(n, 256)
+    mt = fold(n, 256) if shape is None else n // shape[0]
 
     def body(g_ref, w_ref, x_ref, gmid_ref, mod_ref, out_ref, sum_ref):
         @pl.when(pl.program_id(0) == 0)
@@ -656,11 +660,15 @@
         v, r = standard(x_ref[...].astype(F32))
         sum_ref[0:1, :] += column_sum(grad * v)
         sum_ref[1:2, :] += column_sum(grad)
-        out_ref[...] = (gmid_ref[...] + norm_back(grad, v, r, 1.0 + mod_ref[1:2, :])).astype(
-            out_dtype
-        )
+        out = gmid_ref[...] + norm_back(grad, v, r, 1.0 + mod_ref[1:2, :])
+        out_ref[...] = out.astype(out_dtype).reshape(out_ref.shape)
 
     tile = pl.BlockSpec((mt, d), lambda m: (m, 0))
+    result, block = sds((n, d), out_dtype), tile
+    if shape is not None:
+        parts, frames, places = shape
+        result = sds((frames, parts, places, d), out_dtype)
+        block = pl.BlockSpec((frames, 1, places, d), lambda m: (0, m, 0, 0))
     return call(
         body,
         (n // mt,),
@@ -671,12 +679,46 @@
             tile,
             whole((8, d)),
         ],
-        [tile, whole((8, d))],
-        [sds((n, d), out_dtype), sds((8, d), F32)],
+        [block, whole((8, d))],
+        [result, sds((8, d), F32)],
         flops=2 * n * d * wide,
         nbytes=2 * (d * wide + n * wide + 5 * n * d),
         deps=deps,
     )(gqkv, w, x, gmid, mods)
+
+
+def collect(sums, deps=()):
+    flat = [item for layer in sums for item in layer]
+    d = flat[0].shape[1]
+    ups = flat[4].shape[1] // d
+    each = 4 + ups
+
+    def body(*refs):
+        mod_ref, bias_ref = refs[len(flat) :]
+        for k in range(len(sums)):
+            stream, middle, update, qkv, up = refs[5 * k : 5 * k + 5]
+            rows = (
+                (stream, 1), (stream, 0), (middle, 2), (middle, 1), (middle, 0), (middle, 4)
+            )
+            for r, (ref, at) in enumerate(rows):
+                mod_ref[6 * k + r : 6 * k + r + 1, :] = ref[at : at + 1, :]
+            base = each * k
+            bias_ref[base : base + 1, :] = qkv[:, :d]
+            bias_ref[base + 1 : base + 2, :] = qkv[:, 2 * d :]
+            bias_ref[base + 2 : base + 3, :] = middle[3:4, :]
+            bias_ref[base + 3 : base + 4, :] = update[0:1, :]
+            for u in range(ups):
+                bias_ref[base + 4 + u : base + 5 + u, :] = up[:, u * d : (u + 1) * d]
+
+    shapes = [(6 * len(sums), d), (each * len(sums), d)]
+    return call(
+        body,
+        (1,),
+        [whole(item.shape) for item in flat],
+        [whole(shape) for shape in shapes],
+        [sds(shape, F32) for shape in shapes],
+        deps=deps,
+    )(*flat)
 
 
 def add_pieces(left, right, deps=()):
@@ -697,15 +739,15 @@
     )(left, right)
 
 
-def join_qkv_out(place, own, got, deps=()):
-    seq, zs, rows, d = own.shape
+def join_qkv_out(place, own, got, which, deps=()):
+    seq, _, zs, rows, d = own.shape
     wide = d * 3 // 4
 
     def body(place_ref, own_ref, got_ref, qkv_ref, out_ref):
         def put(c, src):
             span = slice(c * rows, (c + 1) * rows)
-            qkv_ref[span, :] = jnp.concatenate([src[s, 0, :, :wide] for s in range(seq)], axis=1)
-            out_ref[span, :] = jnp.concatenate([src[s, 0, :, wide:] for s in range(seq)], axis=1)
+            qkv_ref[span, :] = jnp.concatenate([src[s ^ place_ref[2], 0, 0, :, :wide] for s in range(seq)], axis=1)
+            out_ref[span, :] = jnp.concatenate([src[s ^ place_ref[2], 0, 0, :, wide:] for s in range(seq)], axis=1)
 
         for c in range(2):
 
@@ -714,7 +756,9 @@
                 put(c, own_ref)
                 put(1 - c, got_ref)
 
-    piece = pl.BlockSpec((seq, 1, rows, d), lambda i, place_ref: (0, i ^ place_ref[1], 0, 0))
+    piece = pl.BlockSpec(
+        (seq, 1, 1, rows, d), lambda i, place_ref: (0, which, slot(i ^ place_ref[1]), 0, 0)
+    )
     return call(
         body,
         (zs,),
@@ -730,8 +774,8 @@
     )(place, own, got)
 
 
-def join_up(place, own, got, deps=()):
-    seq, zs, rows, d = own.shape
+def join_up(place, own, got, which, deps=()):
+    seq, _, zs, rows, d = own.shape
 
     def body(place_ref, own_ref, got_ref, up_ref):
         for c in range(2):
@@ -740,10 +784,12 @@
             def _(c=c):
                 for s in range(seq):
                     cols = slice(s * d, (s + 1) * d)
-                    up_ref[c * rows : (c + 1) * rows, cols] = own_ref[s, 0]
-                    up_ref[(1 - c) * rows : (2 - c) * rows, cols] = got_ref[s, 0]
-
-    piece = pl.BlockSpec((seq, 1, rows, d), lambda i, place_ref: (0, i ^ place_ref[1], 0, 0))
+                    up_ref[c * rows : (c + 1) * rows, cols] = own_ref[s ^ place_ref[2], 0, 0]
+                    up_ref[(1 - c) * rows : (2 - c) * rows, cols] = got_ref[s ^ place_ref[2], 0, 0]
+
+    piece = pl.BlockSpec(
+        (seq, 1, 1, rows, d), lambda i, place_ref: (0, which, slot(i ^ place_ref[1]), 0, 0)
+    )
     return call(
         body,
         (zs,),
@@ -756,8 +802,8 @@
     )(place, own, got)
 
 
-def join_down(place, own, got, deps=()):
-    seq, zs, rows, d = own.shape
+def join_down(place, own, got, which, deps=()):
+    seq, _, zs, rows, d = own.shape
     quarter = d // seq
     parts = d // quarter
 
@@ -767,7 +813,7 @@
                 base = (c * parts + q) * rows
                 cols = slice(q * quarter, (q + 1) * quarter)
                 down_ref[base : base + rows, :] = jnp.concatenate(
-                    [src[s, 0, :, cols] for s in range(seq)], axis=1
+                    [src[s ^ place_ref[2], 0, 0, :, cols] for s in range(seq)], axis=1
                 )
 
         for c in range(2):
@@ -777,7 +823,9 @@
                 put(c, own_ref)
                 put(1 - c, got_ref)
 
-    piece = pl.BlockSpec((seq, 1, rows, d), lambda i, place_ref: (0, i ^ place_ref[1], 0, 0))
+    piece = pl.BlockSpec(
+        (seq, 1, 1, rows, d), lambda i, place_ref: (0, which, slot(i ^ place_ref[1]), 0, 0)
+    )
     return call(
         body,
         (zs,),
@@ -822,11 +870,26 @@
     n = frames * places
     ff = up_bias.shape[1]
     clip_index = lax.axis_index(CLIP)
-    place = jnp.stack([clip_index % 2, clip_index // 2]).astype(jnp.int32)
-    packed = zs == 4 and rows % 16 == 0 and down_weight.shape[1] % rows == 0 and d % seq == 0
+    seq_index = lax.axis_index("seq")
+    place = jnp.stack([clip_index % 2, clip_index // 2, 0 * seq_index]).astype(jnp.int32)
+    turned = jnp.stack([clip_index % 2, clip_index // 2, seq_index]).astype(jnp.int32)
+    packed = zs == 4 and seq == 4 and rows % 16 == 0 and down_weight.shape[1] % rows == 0 and d % seq == 0
     cuts = seq if packed else 1
 
-    every_condition = lax.all_gather(conditioning, CLIP, axis=0, tiled=True)
+    def total(v, *axes):
+        for axis, count in axes:
+            step = 1
+            while step < count:
+                v = v + lax.ppermute(v, axis, [(i, i ^ step) for i in range(count)])
+                step *= 2
+        return v
+
+    every_condition = total(
+        lax.dynamic_update_slice(
+            jnp.zeros((clips, d), F32), conditioning, (clip_index, jnp.zeros_like(clip_index))
+        ),
+        (CLIP, clips),
+    )
     squashed = jax.nn.silu(every_condition).astype(BF16)
     local_mods = (
         jnp.einsum("kd,ldc->klc", squashed, ada_weight, preferred_element_type=F32)
@@ -837,11 +900,17 @@
     modulation = every_mod.transpose(2, 1, 0, 3).reshape(layers, 6, d)
     modulation = jnp.pad(modulation, ((0, 0), (0, 2), (0, 0)))
 
-    def pair_of(block, got):
-        return jnp.concatenate([block[None], got[None]], axis=0)
-
-    def line_of(pair, got):
-        return jnp.concatenate([pair, got], axis=0)
+    def far(block):
+        return hop(block, 4, clips)
+
+    def near(block):
+        return hop(block, 2, clips)
+
+    def side(block, distance):
+        return lax.ppermute(block, "seq", [(i, i ^ distance) for i in range(seq)])
+
+    def put(*parts):
+        return jnp.concatenate(parts, axis=1)
 
     def pack_rows(layer):
         tall = down_weight[layer].reshape(-1, rows, d // seq)
@@ -854,6 +923,17 @@
     def along_seq(blocks):
         return lax.all_gather(blocks, "seq", axis=0, tiled=False)
 
+    def across(upper, lower):
+        upper_x, lower_y = side(upper, 1), side(lower, 2)
+        upper_y, lower_x = side(upper, 2), side(lower, 1)
+        blocks = (
+            (upper, lower),
+            (upper_x, lower_x),
+            (upper_y, lower_y),
+            (side(upper_x, 2), side(lower_y, 1)),
+        )
+        return jnp.stack([put(*pair) for pair in blocks])
+
     def both_cores(own, deps):
         own = gate(own, deps)
         return own, hop(own, 1, clips)
@@ -870,16 +950,16 @@
         flat = lax.psum_scatter(half.reshape(-1, d), "seq", scatter_dimension=0, tiled=True)
         return flat.reshape(zs, rows, d)
 
-    def far_half(part):
-        return hop(part[2:], 4, clips)
-
-    def add_far(part, got):
+    def first_half(part):
+        return hop(part[2:], 2, clips)
+
+    def add_first(part, got):
         return (part[:2].astype(F32) + got.astype(F32)).astype(BF16)
 
-    def near_half(part):
-        return hop(part[1], 2, clips)
-
-    def add_near(part, got):
+    def second_half(part):
+        return hop(part[1], 4, clips)
+
+    def add_second(part, got):
         return part[0].astype(F32) + got.astype(F32)
 
     def shed_natural(left, right):
@@ -949,34 +1029,9 @@
             shed_natural(hidden_two, inner_grad),
             shed_natural(active, grad_update),
         )
+        if layer == 0:
+            stream_grad = by_frames(stream_grad)
         return stream_grad, (stream_sums, middle_sums, update_sums, qkv_sums, up_sums), parts
-
-    def mod_rows(sums):
-        stream_sums, middle_sums, _, _, _ = sums
-        return jnp.concatenate(
-            [
-                stream_sums[1:2],
-                stream_sums[0:1],
-                middle_sums[2:3],
-                middle_sums[1:2],
-                middle_sums[0:1],
-                middle_sums[4:5],
-            ],
-            axis=0,
-        )
-
-    def bias_rows_of(sums):
-        _, middle_sums, update_sums, qkv_sums, up_sums = sums
-        return jnp.concatenate(
-            [
-                qkv_sums[:, :d],
-                qkv_sums[:, 2 * d :],
-                middle_sums[3:4],
-                update_sums[0:1],
-                up_sums.reshape(-1, d),
-            ],
-            axis=0,
-        )
 
     def unpack(parts):
         down_g, up_g, both = parts
@@ -998,21 +1053,27 @@
         peaks = (first_peak, second_peak)
         sums = (first_sums, second_sums)
         second_out = swap_tokens(second_out)
-        return second_out, first_grad, peaks, sums, first_parts, second_parts
+
+        def finish(small, own_mod_grad):
+            return total(small, (CLIP, clips), ("seq", seq)), first_parts
+
+        return second_out, first_grad, peaks, collect(sums), finish, second_parts
 
     def run_packed():
         first_pack, second_pack = pack_rows(0), pack_rows(1)
         first_in = by_places(video_latents)
         second_go = swap_tokens(by_places(cotangent))
 
-        pair = pair_of(first_pack[0], hop(first_pack[0], 2, clips))
-        line_q0 = line_of(pair, gate(hop(pair, 4, clips), (second_go,)))
-        block = gate(first_pack[1], (line_q0,))
-        pair = pair_of(block, hop(block, 2, clips))
-        line_u0 = line_of(pair, gate(hop(pair, 4, clips), (modulation,)))
-        block = gate(first_pack[2], (line_u0,))
-        pair_d0 = pair_of(block, hop(block, 2, clips))
-        whole_q0, whole_u0 = along_seq(line_q0), along_seq(line_u0)
+        block = first_pack[0][None, None]
+        pair = put(block, far(block))
+        rest = gate(near(pair), (second_go,))
+        whole_q0 = across(pair, rest)
+        block = gate(first_pack[1][None, None], (rest,))
+        pair = put(block, far(block))
+        line_u0 = put(pair, near(pair))
+        block = gate(first_pack[2][None, None], (line_u0,))
+        pair_d0 = put(block, gate(far(block), (modulation,)))
+        whole_u0 = along_seq(line_u0)
 
         def attention_part(layer, x, qkv, out_full):
             qkv = qkv.reshape(shapes[layer] + (3 * d,))
@@ -1020,61 +1081,56 @@
             return qkv, attended.reshape(n, d), lse, jnp.max(peak, axis=(0, 1))
 
         mods = modulation[0]
-        qkv_full, out_full = join_qkv_out(place, *both_cores(whole_q0, (pair_d0,)))
+        qkv_full, out_full = join_qkv_out(turned, *both_cores(whole_q0, (pair_d0,)), 0)
         hidden, qkv = qkv_forward(first_in, mods, qkv_full, qkv_bias_of(0))
-        hidden, qkv, got = joint(hidden, qkv, hop(pair_d0, 4, clips))
-        line_d0 = line_of(pair_d0, got)
-        block_q1 = gate(second_pack[0], (hidden,))
+        hidden, qkv, got = joint(hidden, qkv, near(pair_d0))
+        line_d0 = put(pair_d0, got)
+        whole_d0 = along_seq(line_d0)
+        block_q1 = gate(second_pack[0][None, None], (got,))
         qkv, attended, lse, peak0 = attention_part(0, first_in, qkv, out_full)
-        attended, lse, got = joint(attended, lse, hop(block_q1, 2, clips))
-        pair_q1 = pair_of(block_q1, got)
-        block_u1, block_d1 = gate(second_pack[1], (attended,)), gate(second_pack[2], (attended,))
+        attended, lse, got = joint(attended, lse, far(block_q1))
+        pair_q1 = put(block_q1, got)
         branch, middle, hidden_two = out_forward(
             attended, first_in, mods, out_full, attention_bias[0, 2:3]
         )
-        branch, middle, hidden_two, got, got2 = joint(
-            branch, middle, hidden_two, hop(block_u1, 2, clips), hop(block_d1, 2, clips)
-        )
-        pair_u1, pair_d1 = pair_of(block_u1, got), pair_of(block_d1, got2)
-        whole_d0 = along_seq(line_d0)
-        up_full = join_up(
-            place, *both_cores(whole_u0, (branch,)), deps=(pair_q1, pair_u1, pair_d1, line_d0)
-        )
+        branch, middle, hidden_two, got = joint(branch, middle, hidden_two, near(pair_q1))
+        line_q1 = put(pair_q1, got)
+        whole_q1 = along_seq(line_q1)
+        block_f1 = gate(jnp.stack(second_pack[1:])[:, None], (got,))
+        up_full = join_up(place, *both_cores(whole_u0, (branch,)), 0, deps=(line_q1, line_d0))
         active, slope = up_forward(hidden_two, up_full, up_bias[:1])
-        active, slope, got = joint(active, slope, hop(pair_q1, 4, clips))
-        line_q1 = line_of(pair_q1, got)
-        whole_q1 = along_seq(line_q1)
-        down_full = join_down(place, *both_cores(whole_d0, (active,)), deps=(line_q1,))
+        active, slope, got = joint(active, slope, far(block_f1))
+        pair_f1 = put(block_f1, got)
+        down_full = join_down(place, *both_cores(whole_d0, (active,)), 0, deps=(pair_f1,))
         update, result = down_forward(active, middle, mods, down_full, down_bias[:1])
-        update, result, got = joint(update, result, hop(pair_u1, 4, clips))
-        line_u1 = line_of(pair_u1, got)
-        whole_u1 = along_seq(line_u1)
+        update, result, got = joint(update, result, near(pair_f1))
+        line_f1 = put(pair_f1, got)
+        whole_u1, whole_d1 = along_seq(line_f1[:1]), along_seq(line_f1[1:])
         kept0 = (
             first_in, hidden, qkv, lse, attended, branch, middle, hidden_two, active, slope, update
         )
         weights0 = (qkv_full, out_full, up_full, down_full)
-        second_in, got = joint(swap_tokens(result), hop(gate(pair_d1, (line_u1,)), 4, clips))
-        line_d1 = line_of(pair_d1, got)
-        whole_d1 = along_seq(line_d1)
+        second_in = swap_tokens(result)
 
         mods = modulation[1]
-        qkv_full, out_full = join_qkv_out(
-            place, *both_cores(whole_q1, (result, line_u1))
-        )
+        own, got = both_cores(whole_q1, (second_in, line_f1))
+        qkv_full, out_full = join_qkv_out(place, own, got, 0)
         hidden, qkv = qkv_forward(second_in, mods, qkv_full, qkv_bias_of(1))
         qkv, attended, lse, peak1 = attention_part(1, second_in, qkv, out_full)
         branch, middle, hidden_two = out_forward(
             attended, second_in, mods, out_full, attention_bias[1, 2:3]
         )
-        up_full = join_up(place, *both_cores(whole_u1, (branch,)))
+        own, got = both_cores(whole_u1, (attended,))
+        branch, middle, hidden_two, got = joint(branch, middle, hidden_two, got)
+        up_full = join_up(place, own, got, 0)
         active, slope = up_forward(hidden_two, up_full, up_bias[1:2])
         grad_update, update_sums1 = update_back(second_go, mods, deps=(active,))
-        own, got = both_cores(whole_d1, (grad_update,))
-        down_m, down_o = down_grad(place, active, grad_update, seq, zs, deps=(own,))
-        down_m, down_o, got = joint(down_m, down_o, got)
-        down_full = join_down(place, own, got)
-        half_d1 = add_pieces(down_m, hop(down_o, 1, clips), deps=(down_full,))
+        down_m, down_o = down_grad(place, active, grad_update, seq, zs)
+        own, got = both_cores(whole_d1, (down_m,))
+        half_d1 = add_pieces(down_m, hop(down_o, 1, clips), deps=(own,))
+        half_d1, got = joint(half_d1, got)
         part_d1 = reduce_seq(half_d1)
+        down_full = join_down(place, own, got, 0)
         update, result = down_forward(
             active, middle, mods, down_full, down_bias[1:2], deps=(half_d1,)
         )
@@ -1114,13 +1170,13 @@
             1, hidden_grad, inner_grad, second_go, ()
         )
         qkv_grad, qkv_cut, qkv_sums = attention_stage(1, attended_grad, (half_u, part_d1))
-        qkv_grad, qkv_cut, got = joint(qkv_grad, qkv_cut, far_half(part_d1))
-        sum_d1 = add_far(part_d1, got)
+        qkv_grad, qkv_cut, got = joint(qkv_grad, qkv_cut, first_half(part_d1))
+        sum_d1 = add_first(part_d1, got)
         stream_grad, stream_sums = stream_back(
             qkv_grad, weights1[0], kept1[0], middle_grad, modulation[1], BF16
         )
-        stream_grad, stream_sums, got = joint(stream_grad, stream_sums, near_half(sum_d1))
-        down_g1 = add_near(sum_d1, got)
+        stream_grad, stream_sums, got = joint(stream_grad, stream_sums, second_half(sum_d1))
+        down_g1 = add_second(sum_d1, got)
         second_sums = (stream_sums, middle_sums, update_sums1, qkv_sums, up_sums)
         last_m, last_o = last_grad(1, qkv_cut, branch_cut, (stream_grad,))
         last_m, last_o, first_go = joint(last_m, last_o, swap_tokens(stream_grad))
@@ -1132,8 +1188,8 @@
         inner_grad, up_sums, hidden_grad = feed_back(
             grad_update, kept0[9], weights0[3], weights0[2], deps=(down_m, part_u1)
         )
-        inner_grad, hidden_grad, got = joint(inner_grad, hidden_grad, far_half(part_u1))
-        sum_u1 = add_far(part_u1, got)
+        inner_grad, hidden_grad, got = joint(inner_grad, hidden_grad, first_half(part_u1))
+        sum_u1 = add_first(part_u1, got)
         half_d0 = add_pieces(down_m, hop(down_o, 1, clips), deps=(hidden_grad, part_q1))
         part_d0 = reduce_seq(half_d0)
         half_u, part_u0, middle_grad, branch_cut, attended_grad, middle_sums = up_stage(
@@ -1141,56 +1197,49 @@
         )
         qkv_grad, qkv_cut, qkv_sums = attention_stage(0, attended_grad, (half_u,))
         qkv_grad, qkv_cut, got, got2 = joint(
-            qkv_grad, qkv_cut, far_half(part_q1), near_half(sum_u1)
-        )
-        sum_q1 = add_far(part_q1, got)
-        up_g1 = add_near(sum_u1, got2)
+            qkv_grad, qkv_cut, first_half(part_q1), second_half(sum_u1)
+        )
+        sum_q1 = add_first(part_q1, got)
+        up_g1 = add_second(sum_u1, got2)
         last_m, last_o = last_grad(0, qkv_cut, branch_cut, (part_d0, sum_q1))
-        last_m, last_o, got, got2 = joint(last_m, last_o, far_half(part_d0), near_half(sum_q1))
-        sum_d0 = add_far(part_d0, got)
-        both_g1 = add_near(sum_q1, got2)
+        last_m, last_o, got, got2 = joint(last_m, last_o, first_half(part_d0), second_half(sum_q1))
+        sum_d0 = add_first(part_d0, got)
+        both_g1 = add_second(sum_q1, got2)
         first_grad, stream_sums = stream_back(
-            qkv_grad, weights0[0], kept0[0], middle_grad, modulation[0], F32, deps=(last_m, sum_d0)
-        )
-        first_grad, stream_sums, got, got2 = joint(
-            first_grad, stream_sums, near_half(sum_d0), far_half(part_u0)
-        )
-        down_g0 = add_near(sum_d0, got)
-        sum_u0 = add_far(part_u0, got2)
+            qkv_grad, weights0[0], kept0[0], middle_grad, modulation[0], F32, shape=shapes[0],
+            deps=(last_m, sum_d0),
+        )
+        first_grad, stream_sums, got = joint(first_grad, stream_sums, second_half(sum_d0))
+        down_g0 = add_second(sum_d0, got)
         first_sums = (stream_sums, middle_sums, update_sums, qkv_sums, up_sums)
         half = add_pieces(last_m, hop(last_o, 1, clips), deps=(first_grad,))
         part_q0 = reduce_seq(half)
-        up_g0 = add_near(sum_u0, near_half(sum_u0))
-        part_q0 = gate(part_q0, (up_g0,))
-        sum_q0 = add_far(part_q0, far_half(part_q0))
-        both_g0 = add_near(sum_q0, near_half(sum_q0))
-        sums = (first_sums, second_sums)
-        first_parts = unpack((down_g0, up_g0, both_g0))
+        got = first_half(part_u0)
+        rows_of = collect((first_sums, second_sums), deps=(half, got))
+        sum_u0 = add_first(part_u0, got)
         second_parts = unpack((down_g1, up_g1, both_g1))
-        return second_out, first_grad, (peak0, peak1), sums, first_parts, second_parts
+
+        def finish(small, own_mod_grad):
+            up_g0 = add_second(sum_u0, gate(second_half(sum_u0), (own_mod_grad,)))
+            part = gate(part_q0, (up_g0,))
+            sum_q0 = add_first(part, first_half(part))
+            both_g0 = add_second(sum_q0, second_half(sum_q0))
+            return total(small, (CLIP, clips), ("seq", seq)), unpack((down_g0, up_g0, both_g0))
+
+        return second_out, first_grad, (peak0, peak1), rows_of, finish, second_parts
 
     run = run_packed if packed else run_natural
-    second_out, latents_grad, peaks, sums, first_shed, second_shed = run()
+    second_out, latents_grad, peaks, (mod_grads, bias_rows), finish, second_shed = run()
     output_latents = by_frames(second_out)
 
-    def total(v, *axes):
-        for axis, count in axes:
-            step = 1
-            while step < count:
-                v = v + lax.ppermute(v, axis, [(i, i ^ step) for i in range(count)])
-                step *= 2
-        return v
-
-    mod_grads = total(jnp.stack([mod_rows(sums[0]), mod_rows(sums[1])]), ("seq", seq))
-    mod_grads = mod_grads.reshape(layers, clips, seq, -1)
+    mod_grads = total(mod_grads, ("seq", seq)).reshape(layers, clips, seq, -1)
     of_columns = lax.dynamic_index_in_dim(mod_grads, lax.axis_index("seq"), 2, keepdims=False)
     own_mod_grad = lax.all_to_all(of_columns.transpose(1, 0, 2), CLIP, 0, 0, tiled=True)
     ada_bias_grad = jnp.sum(own_mod_grad, axis=0)
     rounded_mod = own_mod_grad.astype(BF16)
     ada_weight_grad = jnp.einsum("kd,klc->ldc", squashed, rounded_mod, preferred_element_type=F32)
     squash_part = jnp.einsum("klc,ldc->kd", rounded_mod, ada_weight, preferred_element_type=F32)
-    bias_sums = [bias_rows_of(sums[0]), bias_rows_of(sums[1])]
-    bias_rows = bias_sums[0].shape[0]
+    bias_count = bias_rows.shape[0]
     devices = clips * seq
     device = clip_index * seq + lax.axis_index("seq")
     peak_rows = -(-devices * layers * HEADS // d)
@@ -1199,12 +1248,12 @@
         jnp.zeros((devices, layers * HEADS), F32), own_peaks, (device, 0)
     ).reshape(-1)
     placed = jnp.pad(placed, (0, peak_rows * d - placed.shape[0])).reshape(peak_rows, d)
-    summed = total(
-        jnp.concatenate([*bias_sums, squash_part, placed], axis=0), (CLIP, clips), ("seq", seq)
+    summed, first_shed = finish(
+        jnp.concatenate([bias_rows, squash_part, placed], axis=0), own_mod_grad
     )
-    bias_sums = summed[: 2 * bias_rows].reshape(layers, bias_rows, d)
-    own_squash = lax.dynamic_slice_in_dim(summed, 2 * bias_rows + clip_index, 1, axis=0)
-    peaks = summed[2 * bias_rows + clips :].reshape(-1)[: devices * layers * HEADS]
+    bias_sums = summed[:bias_count].reshape(layers, -1, d)
+    own_squash = lax.dynamic_slice_in_dim(summed, bias_count + clip_index, 1, axis=0)
+    peaks = summed[bias_count + clips :].reshape(-1)[: devices * layers * HEADS]
     logit_peak = jnp.max(peaks.reshape(devices, layers, HEADS), axis=0)
     column_index = lax.axis_index("seq") * own_columns + jnp.arange(own_columns, dtype=jnp.int32)
     head_of = column_index % d // (d // HEADS)
@@ -1217,9 +1266,7 @@
     conditioning_grad = silu_pull(own_squash)[0]
     return (
         output_latents,
-        latents_grad.reshape(seq, frames, places // seq, d)
-        .transpose(1, 0, 2, 3)
-        .reshape(1, frames, places, d),
+        latents_grad.reshape(1, frames, places, d),
         conditioning_grad,
         ada_weight_grad,
         ada_bias_grad,

time: 1110 us -> 1060 us (0.955)
  blocking collectives: 53.2 us -> 8.86 us
  starting transfers between devices: 66 us -> 88.1 us
  waiting for transfers between devices: 245 us -> 228 us
  local copies, waits for them, and re-layouts: 89.7 us -> 74.7 us
    ppermute x36 -> x34, waiting for transfers between devices: 178 us -> 103 us  [hop(): return lax.ppermute(x, CLIP, [(i, i ^ distance) for i in range(count)])]
    all_gather x1 -> x0, blocking collectives: 37.2 us -> none  [on_device(): every_condition = lax.all_gather(conditioning, CLIP, axis=0, tiled=True)]
    all_to_all x4, waiting for transfers between devices: 18.3 us -> 51.4 us  [swap_tokens(): return lax.all_to_all(block, 'seq', 0, 0, tiled=True).reshape(n, d)]
    ppermute x0 -> x6, waiting for transfers between devices: none -> 24.7 us  [side(): return lax.ppermute(block, 'seq', [(i, i ^ distance) for i in range(seq)])]
    all_gather x6 -> x5, waiting for transfers between devices: 17.7 us -> 0.02 us  [along_seq(): return lax.all_gather(blocks, 'seq', axis=0, tiled=False)]
    ppermute x7 -> x10, waiting for transfers between devices: 18.6 us -> 34.3 us  [total(): v = v + lax.ppermute(v, axis, [(i, i ^ step) for i in range(count)])]
    another operation x2 -> x7, other arithmetic: 0.62 us -> 12.3 us  [the longest x5 11.1 us: across(): return jnp.stack([put(*pair) for pair in blocks])]
    ppermute x36 -> x34, starting transfers between devices: 37.2 us -> 33.3 us  [hop(): return lax.ppermute(x, CLIP, [(i, i ^ distance) for i in range(count)])]
  transfers between devices with their start and end apart: 60 -> 67, of which waited for: 30 -> 29; matrix products, arithmetic and copies ran while one was open for 9% -> 9% of each run, Pallas kernels for 51% -> 55%
where the time goes in v3:
time: 1060 us; the launch traced here: 1050 us
  Pallas kernels  581 us (55%)
  waiting for transfers between devices  228 us (22%)
  starting transfers between devices  88.1 us (8%)
  local copies, waits for them, and re-layouts  74.7 us (7%)
  other arithmetic  53.8 us (5%)
  between operations  15.2 us (1%)
    pallas_call x39, Pallas kernels, call(): return lambda *args: kernel(*args, *deps)  581 us
    ppermute x34, waiting for transfers between devices, hop(): return lax.ppermute(x, CLIP, [(i, i ^ distance) for i in range(count)])  103 us
    all_to_all x4, waiting for transfers between devices, swap_tokens(): return lax.all_to_all(block, 'seq', 0, 0, tiled=True).reshape(n, d)  51.4 us
    unnamed x146, local copies, waits for them, and re-layouts  34.8 us
    ppermute x10, waiting for transfers between devices, total(): v = v + lax.ppermute(v, axis, [(i, i ^ step) for i in range(count)])  34.3 us
    ppermute x34, starting transfers between devices, hop(): return lax.ppermute(x, CLIP, [(i, i ^ distance) for i in range(count)])  33.3 us
    ppermute x6, waiting for transfers between devices, side(): return lax.ppermute(block, 'seq', [(i, i ^ distance) for i in range(seq)])  24.7 us
  transfers between devices with their start and end apart: 67, of which 29 were waited for; matrix products, arithmetic and copies ran while one was open for 9% of the time, Pallas kernels for 55%

profile of v3, /device:TPU:0, one launch (start us, length us, event | category | flops | bytes accessed | tf_op | source)
XLA Modules:
  0.0 1052.4 jit_solution(17142578295838230185)
XLA Ops:
  24.1 13.1 %collective-permute-done.3 = bf16[1,1,144,1152]{3,2,1,0:T(8,128)(2,1)} collective-permute-done((bf16[1,1,144,1152]{3,2,1,0:T(8,128)(2,1)}, bf16[1,1,144,1152]{3,2,1,0:T(8,128)(2,1)}, u32[]{:S(2)}, u32[]{:S(2)}) %collective-permute-start.3) | collective-permute-done | bytes 331808 | tf_op jit(solution)/shard_map/ppermute | solution.py:846
  41.5 14.6 %collective-permute-done.1 = f32[8,1152]{1,0:T(8,128)S(1)} collective-permute-done((f32[8,1152]{1,0:T(8,128)S(1)}, f32[8,1152]{1,0:T(8,128)S(1)}, u32[]{:S(2)}, u32[]{:S(2)}) %collective-permute-start.1) | collective-permute-done | bytes 36896 | tf_op jit(solution)/shard_map/ppermute | solution.py:883
  66.1 13.9 %collective-permute-done.11 = bf16[1,1,144,1152]{3,2,1,0:T(8,128)(2,1)S(1)} collective-permute-done((bf16[1,1,144,1152]{3,2,1,0:T(8,128)(2,1)}, bf16[1,1,144,1152]{3,2,1,0:T(8,128)(2,1)S(1)}, u32[]{:S(2)}, u32[]{:S(2)}) %collective-permute-start.11) | collective-permute-done | bytes 331808 | tf_op jit(solution)/shard_map/ppermute | solution.py:846
  90.4 8.1 all-to-all-done.1
  98.6 8.9 all-gather
  120.7 7.2 collective-permute-done.6
  134.1 17.5 %collective-permute-done.10 = bf16[1,2,144,1152]{3,2,1,0:T(8,128)(2,1)} collective-permute-done((bf16[1,2,144,1152]{3,2,1,0:T(8,128)(2,1)}, bf16[1,2,144,1152]{3,2,1,0:T(8,128)(2,1)}, u32[]{:S(2)}, u32[]{:S(2)}) %collective-permute-start.10) | collective-permute-done | bytes 663584 | tf_op jit(solution)/shard_map/ppermute | solution.py:910
  165.2 9.8 shard_map.232
  175.0 16.6 %shard_map.233 = (bf16[1024,1152]{1,0:T(8,128)(2,1)}, bf16[1024,3456]{1,0:T(8,128)(2,1)}) custom-call(bf16[1024,1152]{1,0:T(8,128)(2,1)} %bitcast.238, f32[8,1152]{1,0:T(8,128)} %get-tuple-element.332.refs_1_.refs_2_.refs_5_.refs_4_, bf16[1152,3456]{1,0:T(8,128)(2,1)} %get-tuple-element.132.refs_2_.refs_1_, f32[1,3456]{1,0:T(1,128)} %broadcast_in_dim.45.refs_3_), custom_call_target="tpu_custom_call" | custom-call | flops 8153726976 | bytes 19759104 | tf_op jit(solution)/shard_map/pallas_call | solution.py:49
  199.7 12.9 %shard_map.235 = (bf16[4,4,64,1152]{3,2,1,0:T(8,128)(2,1)}, f32[4,16,256]{2,1,0:T(8,128)}, f32[4,1,16]{2,1,0:T(1,128)}) custom-call(bf16[4,4,64,3456]{3,2,1,0:T(8,128)(2,1)} %bitcast.222), custom_call_target="tpu_custom_call" | custom-call | flops 4294967296 | bytes 9437184 | tf_op jit(solution)/shard_map/pallas_call | solution.py:49
  217.7 9.1 shard_map.238
  243.2 9.0 shard_map.241.refs_1_.refs_3_
  252.2 23.1 %shard_map.242 = (bf16[1024,4608]{1,0:T(8,128)(2,1)}, bf16[1024,4608]{1,0:T(8,128)(2,1)}) custom-call(bf16[1024,1152]{1,0:T(8,128)(2,1)} %get-tuple-element.145.refs_0_.refs_1_, bf16[1152,4608]{1,0:T(8,128)(2,1)} %shard_map.241.refs_1_.refs_3_, f32[1,4608]{1,0:T(1,128)} %get-tuple-element.335.refs_2_), custom_call_target="tpu_custom_call" | custom-call | flops 10871635968 | bytes 31850496 | tf_op jit(solution)/shard_map/pallas_call | solution.py:49
  285.4 10.8 %shard_map.246.refs_3_.refs_2_ = bf16[4608,1152]{1,0:T(8,128)(2,1)} custom-call(s32[3]{0:T(128)} %pad_add_fusion.2.refs_0_, bf16[4,1,4,144,1152]{4,3,2,1,0:T(8,128)(2,1)} %shard_map.245.refs_1_, bf16[4,1,4,144,1152]{4,3,2,1,0:T(8,128)(2,1)} %collective-permute-done.20.refs_2_, bf16[2,2,144,1152]{3,2,1,0:T(8,128)(2,1)} %copy-done.21), custom_call_target="tpu_custom_call" | custom-call | bytes 21233664 | tf_op jit(solution)/shard_map/pallas_call | solution.py:49
  296.2 19.2 %shard_map.247 = (bf16[1024,1152]{1,0:T(8,128)(2,1)}, bf16[1024,1152]{1,0:T(8,128)(2,1)}) custom-call(bf16[1024,4608]{1,0:T(8,128)(2,1)} %get-tuple-element.150.refs_1_.refs_0_, f32[1024,1152]{1,0:T(8,128)} %get-tuple-element.151.refs_1_, f32[8,1152]{1,0:T(8,128)} %get-tuple-element.332.refs_1_.refs_2_.refs_5_.refs_4_, ...), custom_call_target="tpu_custom_call" | custom-call | flops 10871635968 | bytes 29491200 | tf_op jit(solution)/shard_map/pallas_call | solution.py:49
  323.1 42.4 %all-to-all-done.2 = bf16[4,256,1152]{2,1,0:T(8,128)(2,1)S(1)} async-done(((bf16[4,256,1152]{2,1,0:T(8,128)(2,1)}), bf16[4,256,1152]{2,1,0:T(8,128)(2,1)S(1)}, u32[]{:S(2)}, u32[]{:S(2)}) %all-to-all-start.2) | async-done | bytes 2359328 | tf_op jit(solution)/shard_map/all_to_all | solution.py:972
  367.7 8.7 reduce-scatter.7.cloned.1.call-start
  376.4 9.9 shard_map.250
  386.3 16.5 %shard_map.251 = (bf16[1024,1152]{1,0:T(8,128)(2,1)}, bf16[1024,3456]{1,0:T(8,128)(2,1)}) custom-call(bf16[1024,1152]{1,0:T(8,128)(2,1)} %bitcast.215, f32[8,1152]{1,0:T(8,128)} %get-tuple-element.333.refs_1_.refs_2_.refs_5_.refs_4_, bf16[1152,3456]{1,0:T(8,128)(2,1)} %get-tuple-element.157.refs_2_.refs_1_, f32[1,3456]{1,0:T(1,128)} %broadcast_in_dim.48.refs_3_), custom_call_target="tpu_custom_call" | custom-call | flops 8153726976 | bytes 19759104 | tf_op jit(solution)/shard_map/pallas_call | solution.py:49
  402.8 12.9 %shard_map.252 = (bf16[16,4,16,1152]{3,2,1,0:T(8,128)(2,1)}, f32[4,16,256]{2,1,0:T(8,128)}, f32[4,1,16]{2,1,0:T(1,128)}) custom-call(bf16[16,4,16,3456]{3,2,1,0:T(8,128)(2,1)} %bitcast.260), custom_call_target="tpu_custom_call" | custom-call | flops 4294967296 | bytes 9437184 | tf_op jit(solution)/shard_map/pallas_call | solution.py:49
  416.3 9.1 shard_map.253
  425.3 8.9 shard_map.256.refs_1_.refs_3_
  434.3 23.7 %shard_map.257 = (bf16[1024,4608]{1,0:T(8,128)(2,1)}, bf16[1024,4608]{1,0:T(8,128)(2,1)}) custom-call(bf16[1024,1152]{1,0:T(8,128)(2,1)} %get-tuple-element.164.refs_0_.refs_1_, bf16[1152,4608]{1,0:T(8,128)(2,1)} %shard_map.256.refs_1_.refs_3_, f32[1,4608]{1,0:T(1,128)} %get-tuple-element.334.refs_2_), custom_call_target="tpu_custom_call" | custom-call | flops 10871635968 | bytes 31850496 | tf_op jit(solution)/shard_map/pallas_call | solution.py:49
  462.4 18.2 %shard_map.259 = (bf16[4,4,144,1152]{3,2,1,0:T(8,128)(2,1)}, bf16[4,4,144,1152]{3,2,1,0:T(8,128)(2,1)}) custom-call(s32[3]{0:T(128)} %pad_add_fusion.2.refs_0_, bf16[1024,4608]{1,0:T(8,128)(2,1)} %get-tuple-element.166.refs_2_.refs_1_.refs_0_, bf16[1024,1152]{1,0:T(8,128)(2,1)} %get-tuple-element.167.refs_2_.refs_0_), custom_call_target="tpu_custom_call" | custom-call | flops 10871635968 | bytes 22413312 | tf_op jit(solution)/shard_map/pallas_call | solution.py:49
  481.2 8.6 collective-permute-done.24.refs_1_
  489.8 7.0 shard_map.261.refs_0_
  497.4 10.3 shard_map.263.refs_3_.refs_2_
  507.7 19.4 %shard_map.264 = (bf16[1024,1152]{1,0:T(8,128)(2,1)}, bf16[1024,1152]{1,0:T(8,128)(2,1)}) custom-call(bf16[1024,4608]{1,0:T(8,128)(2,1)} %get-tuple-element.166.refs_2_.refs_1_.refs_0_, f32[1024,1152]{1,0:T(8,128)} %get-tuple-element.172.refs_1_, f32[8,1152]{1,0:T(8,128)} %get-tuple-element.333.refs_1_.refs_2_.refs_5_.refs_4_, ...), custom_call_target="tpu_custom_call" | custom-call | flops 10871635968 | bytes 29491200 | tf_op jit(solution)/shard_map/pallas_call | solution.py:49
  530.8 37.4 %shard_map.265 = (bf16[1024,4608]{1,0:T(8,128)(2,1)}, f32[1,4608]{1,0:T(1,128)}, f32[1024,1152]{1,0:T(8,128)}) custom-call(bf16[1024,1152]{1,0:T(8,128)(2,1)} %get-tuple-element.167.refs_2_.refs_0_, bf16[1024,4608]{1,0:T(8,128)(2,1)} %get-tuple-element.168.refs_1_, bf16[4608,1152]{1,0:T(8,128)(2,1)} %shard_map.263.refs_3_.refs_2_, ...), custom_call_target="tpu_custom_call" | custom-call | flops 21743271936 | bytes 47185920 | tf_op jit(solution)/shard_map/pallas_call | solution.py:49
  569.6 17.7 %shard_map.267 = (bf16[4,4,144,1152]{3,2,1,0:T(8,128)(2,1)}, bf16[4,4,144,1152]{3,2,1,0:T(8,128)(2,1)}) custom-call(s32[3]{0:T(128)} %pad_add_fusion.2.refs_0_, bf16[1024,1152]{1,0:T(8,128)(2,1)} %get-tuple-element.164.refs_0_.refs_1_, bf16[1024,4608]{1,0:T(8,128)(2,1)} %get-tuple-element.182.refs_2_), custom_call_target="tpu_custom_call" | custom-call | flops 10871635968 | bytes 22413312 | tf_op jit(solution)/shard_map/pallas_call | solution.py:49
  587.4 14.7 %shard_map.268 = (f32[1024,1152]{1,0:T(8,128)}, bf16[1024,1152]{1,0:T(8,128)(2,1)}, bf16[4,1024,288]{2,1,0:T(8,128)(2,1)}, bf16[1024,1152]{1,0:T(8,128)(2,1)}, f32[8,1152]{1,0:T(8,128)}) custom-call(f32[1024,1152]{1,0:T(8,128)} %get-tuple-element.179.refs_0_, f32[1024,1152]{1,0:T(8,128)} %get-tuple-element.172.refs_1_, ...), custom_call_target="tpu_custom_call" | custom-call | flops 2717908992 | bytes 28606464 | tf_op jit(solution)/shard_map/pallas_call | solution.py:49
  613.7 26.0 %shard_map.270 = (bf16[16,4,16,3456]{3,2,1,0:T(8,128)(2,1)}, bf16[4,16,4,16,864]{4,3,2,1,0:T(8,128)(2,1)}, f32[1,3456]{1,0:T(1,128)}) custom-call(bf16[16,4,16,3456]{3,2,1,0:T(8,128)(2,1)} %bitcast.261, bf16[16,4,16,1152]{3,2,1,0:T(8,128)(2,1)} %bitcast.259, f32[4,16,256]{2,1,0:T(8,128)} %get-tuple-element.185.refs_2_, ...), custom_call_target="tpu_custom_call" | custom-call | flops 12884901888 | bytes 23592960 | tf_op jit(solution)/shard_map/pallas_call | solution.py:49
  647.0 17.2 %shard_map.272 = (bf16[1024,1152]{1,0:T(8,128)(2,1)}, f32[8,1152]{1,0:T(8,128)}) custom-call(bf16[1024,3456]{1,0:T(8,128)(2,1)} %get-tuple-element.192.refs_0_, bf16[1152,3456]{1,0:T(8,128)(2,1)} %get-tuple-element.157.refs_2_.refs_1_, bf16[1024,1152]{1,0:T(8,128)(2,1)} %bitcast.217, f32[1024,1152]{1,0:T(8,128)} %get-tuple-element.187.refs_2_.refs_3_, ...), custom_call_target="tpu_custom_call" | custom-call | flops 8153726976 | bytes 26836992 | tf_op jit(solution)/shard_map/pallas_call | solution.py:49
  668.9 21.7 %shard_map.274 = (bf16[4,4,144,1152]{3,2,1,0:T(8,128)(2,1)}, bf16[4,4,144,1152]{3,2,1,0:T(8,128)(2,1)}) custom-call(s32[3]{0:T(128)} %pad_add_fusion.2.refs_0_, bf16[1024,1152]{1,0:T(8,128)(2,1)} %get-tuple-element.178.refs_1_, bf16[1024,1152]{1,0:T(8,128)(2,1)} %bitcast.235, bf16[4,1024,864]{2,1,0:T(8,128)(2,1)} %get-tuple-element.190.refs_3_, ...), custom_call_target="tpu_custom_call" | custom-call | flops 10871635968 | bytes 20054016 | tf_op jit(solution)/shard_map/pallas_call | solution.py:49
  690.7 9.0 all-to-all-done.4
  712.3 7.0 shard_map.277.refs_3_
  719.4 18.6 %shard_map.278 = (bf16[4,4,144,1152]{3,2,1,0:T(8,128)(2,1)}, bf16[4,4,144,1152]{3,2,1,0:T(8,128)(2,1)}) custom-call(s32[3]{0:T(128)} %pad_add_fusion.2.refs_0_, bf16[1024,4608]{1,0:T(8,128)(2,1)} %get-tuple-element.150.refs_1_.refs_0_, bf16[1024,1152]{1,0:T(8,128)(2,1)} %get-tuple-element.200.refs_2_.refs_0_, bf16[4,4,144,1152]{3,2,1,0:T(8,128)(2,1)} %shard_map.277.refs_3_), custom_call_target="tpu_custom_call" | custom-call | flops 10871635968 | bytes 22413312 | tf_op jit(solution)/shard_map/pallas_call | solution.py:49
  741.1 37.7 %shard_map.279 = (bf16[1024,4608]{1,0:T(8,128)(2,1)}, f32[1,4608]{1,0:T(1,128)}, f32[1024,1152]{1,0:T(8,128)}) custom-call(bf16[1024,1152]{1,0:T(8,128)(2,1)} %get-tuple-element.200.refs_2_.refs_0_, bf16[1024,4608]{1,0:T(8,128)(2,1)} %get-tuple-element.201.refs_1_, bf16[4608,1152]{1,0:T(8,128)(2,1)} %shard_map.246.refs_3_.refs_2_, ...), custom_call_target="tpu_custom_call" | custom-call | flops 21743271936 | bytes 47185920 | tf_op jit(solution)/shard_map/pallas_call | solution.py:49
  781.5 7.0 shard_map.281.refs_3_
  790.6 17.9 %shard_map.282 = (bf16[4,4,144,1152]{3,2,1,0:T(8,128)(2,1)}, bf16[4,4,144,1152]{3,2,1,0:T(8,128)(2,1)}) custom-call(s32[3]{0:T(128)} %pad_add_fusion.2.refs_0_, bf16[1024,1152]{1,0:T(8,128)(2,1)} %get-tuple-element.145.refs_0_.refs_1_, bf16[1024,4608]{1,0:T(8,128)(2,1)} %get-tuple-element.209.refs_2_, bf16[4,4,144,1152]{3,2,1,0:T(8,128)(2,1)} %shard_map.281.refs_3_, ...), custom_call_target="tpu_custom_call" | custom-call | flops 10871635968 | bytes 22413312 | tf_op jit(solution)/shard_map/pallas_call | solution.py:49
  808.6 14.9 %shard_map.283 = (f32[1024,1152]{1,0:T(8,128)}, bf16[1024,1152]{1,0:T(8,128)(2,1)}, bf16[4,1024,288]{2,1,0:T(8,128)(2,1)}, bf16[1024,1152]{1,0:T(8,128)(2,1)}, f32[8,1152]{1,0:T(8,128)}) custom-call(f32[1024,1152]{1,0:T(8,128)} %get-tuple-element.207.refs_2_.refs_0_, f32[1024,1152]{1,0:T(8,128)} %get-tuple-element.151.refs_1_, ...), custom_call_target="tpu_custom_call" | custom-call | flops 2717908992 | bytes 28606464 | tf_op jit(solution)/shard_map/pallas_call | solution.py:49
  825.7 7.0 shard_map.284.refs_3_
  838.2 26.0 %shard_map.285 = (bf16[4,4,64,3456]{3,2,1,0:T(8,128)(2,1)}, bf16[4,4,4,64,864]{4,3,2,1,0:T(8,128)(2,1)}, f32[1,3456]{1,0:T(1,128)}) custom-call(bf16[4,4,64,3456]{3,2,1,0:T(8,128)(2,1)} %bitcast.223, bf16[4,4,64,1152]{3,2,1,0:T(8,128)(2,1)} %bitcast.258, f32[4,16,256]{2,1,0:T(8,128)} %get-tuple-element.214.refs_2_, bf16[4,4,144,1152]{3,2,1,0:T(8,128)(2,1)} %shard_map.284.refs_3_), custom_call_target="tpu_custom_call" | custom-call | flops 12884901888 | bytes 23592960 | tf_op jit(solution)/shard_map/pallas_call | solution.py:49
  870.2 21.8 %shard_map.287 = (bf16[4,4,144,1152]{3,2,1,0:T(8,128)(2,1)}, bf16[4,4,144,1152]{3,2,1,0:T(8,128)(2,1)}) custom-call(s32[3]{0:T(128)} %pad_add_fusion.2.refs_0_, bf16[1024,1152]{1,0:T(8,128)(2,1)} %get-tuple-element.220.refs_1_, bf16[1024,1152]{1,0:T(8,128)(2,1)} %get-tuple-element.139.refs_0_.refs_2_, bf16[4,1024,864]{2,1,0:T(8,128)(2,1)} %get-tuple-element.221.refs_3_, ...), custom_call_target="tpu_custom_call" | custom-call | flops 10871635968 | bytes 20054016 | tf_op jit(solution)/shard_map/pallas_call | solution.py:49
  896.6 18.1 %shard_map.289 = (f32[4,4,64,1152]{3,2,1,0:T(8,128)}, f32[8,1152]{1,0:T(8,128)}) custom-call(bf16[1024,3456]{1,0:T(8,128)(2,1)} %get-tuple-element.219.refs_0_, bf16[1152,3456]{1,0:T(8,128)(2,1)} %get-tuple-element.132.refs_2_.refs_1_, bf16[1024,1152]{1,0:T(8,128)(2,1)} %bitcast.240, f32[1024,1152]{1,0:T(8,128)} %get-tuple-element.216.refs_2_.refs_3_, ...), custom_call_target="tpu_custom_call" | custom-call | flops 8153726976 | bytes 26836992 | tf_op jit(solution)/shard_map/pallas_call | solution.py:49
  933.5 13.7 %collective-permute-done.39.refs_11_ = bf16[2,144,1152]{2,1,0:T(8,128)(2,1)S(1)} collective-permute-done((bf16[2,144,1152]{2,1,0:T(8,128)(2,1)S(1)}, bf16[2,144,1152]{2,1,0:T(8,128)(2,1)S(1)}, u32[]{:S(2)}, u32[]{:S(2)}) %collective-permute-start.39) | collective-permute-done | bytes 663584 | tf_op jit(solution)/shard_map/ppermute | solution.py:846
  1012.6 14.6 %collective-permute-done.48 = bf16[2,144,1152]{2,1,0:T(8,128)(2,1)S(1)} collective-permute-done((bf16[2,144,1152]{2,1,0:T(8,128)(2,1)S(1)}, bf16[2,144,1152]{2,1,0:T(8,128)(2,1)S(1)}, u32[]{:S(2)}, u32[]{:S(2)}) %collective-permute-start.48) | collective-permute-done | bytes 663584 | tf_op jit(solution)/shard_map/ppermute | solution.py:846
  1031.6 11.8 %collective-permute-done.49 = bf16[144,1152]{1,0:T(8,128)(2,1)S(1)} collective-permute-done((bf16[144,1152]{1,0:T(8,128)(2,1)S(1)}, bf16[144,1152]{1,0:T(8,128)(2,1)S(1)}, u32[]{:S(2)}, u32[]{:S(2)}) %collective-permute-start.49) | collective-permute-done | bytes 331808 | tf_op jit(solution)/shard_map/ppermute | solution.py:846
  (433 shorter events, 288.0 us)
Async XLA Ops:
  10.6 50.8 %all-to-all-start = ((bf16[4,256,1152]{2,1,0:T(8,128)(2,1)}), bf16[4,256,1152]{2,1,0:T(8,128)(2,1)S(1)}, u32[]{:S(2)}, u32[]{:S(2)}) async-start(bf16[4,256,1152]{2,1,0:T(8,128)(2,1)} %bitcast.212), calls=%async_computation | async-start | bytes 4718592 | tf_op jit(solution)/shard_map/all_to_all | solution.py:972
  19.5 17.7 %collective-permute-start.3 = (bf16[1,1,144,1152]{3,2,1,0:T(8,128)(2,1)}, bf16[1,1,144,1152]{3,2,1,0:T(8,128)(2,1)}, u32[]{:S(2)}, u32[]{:S(2)}) collective-permute-start(bf16[1,1,144,1152]{3,2,1,0:T(8,128)(2,1)} %maximum_bitcast_fusion.5), channel_id=1, source_target_pairs={{0,16},{4,20},{8,24},{12,28},{16,0},{20,4},{24,8},{28,12},{1,17},{... | collective-permute-start | bytes 995336 | tf_op jit(solution)/shard_map/ppermute | solution.py:846
  24.1 15.8 %collective-permute-start = (f32[8,1152]{1,0:T(8,128)}, f32[8,1152]{1,0:T(8,128)S(1)}, u32[]{:S(2)}, u32[]{:S(2)}) collective-permute-start(f32[8,1152]{1,0:T(8,128)} %dynamic_update_slice.8), channel_id=1, source_target_pairs={{0,4},{4,0},{8,12},{12,8},{16,20},{20,16},{24,28},{28,24},{1,5},{5... | collective-permute-start | bytes 110600 | tf_op jit(solution)/shard_map/ppermute | solution.py:883
  39.2 22.2 %collective-permute-start.4 = (bf16[1,2,144,1152]{3,2,1,0:T(8,128)(2,1)}, bf16[1,2,144,1152]{3,2,1,0:T(8,128)(2,1)}, u32[]{:S(2)}, u32[]{:S(2)}) collective-permute-start(bf16[1,2,144,1152]{3,2,1,0:T(8,128)(2,1)} %pad_maximum_fusion.9), channel_id=1, source_target_pairs={{0,8},{4,12},{8,0},{12,4},{16,24},{20,28},{24,16},{28,20},{1,9},{5... | collective-permute-start | bytes 1990664 | tf_op jit(solution)/shard_map/ppermute | solution.py:846
  40.1 15.9 %collective-permute-start.1 = (f32[8,1152]{1,0:T(8,128)S(1)}, f32[8,1152]{1,0:T(8,128)S(1)}, u32[]{:S(2)}, u32[]{:S(2)}) collective-permute-start(f32[8,1152]{1,0:T(8,128)S(1)} %add.157), channel_id=1, source_target_pairs={{0,8},{4,12},{8,0},{12,4},{16,24},{20,28},{24,16},{28,20},{1,9},{5... | collective-permute-start | bytes 110600 | tf_op jit(solution)/shard_map/ppermute | solution.py:883
  62.8 17.2 %collective-permute-start.11 = (bf16[1,1,144,1152]{3,2,1,0:T(8,128)(2,1)}, bf16[1,1,144,1152]{3,2,1,0:T(8,128)(2,1)S(1)}, u32[]{:S(2)}, u32[]{:S(2)}) collective-permute-start(bf16[1,1,144,1152]{3,2,1,0:T(8,128)(2,1)} %shard_map.228), channel_id=1, source_target_pairs={{0,16},{4,20},{8,24},{12,28},{16,0},{20,4},{24,8},{28,12},{1,17},{... | collective-permute-start | bytes 995336 | tf_op jit(solution)/shard_map/ppermute | solution.py:846
  62.9 45.4 %collective-permute-start.5 = (bf16[1,2,144,1152]{3,2,1,0:T(8,128)(2,1)}, bf16[1,2,144,1152]{3,2,1,0:T(8,128)(2,1)}, u32[]{:S(2)}, u32[]{:S(2)}) collective-permute-start(bf16[1,2,144,1152]{3,2,1,0:T(8,128)(2,1)} %pad_maximum_fusion.9), channel_id=1, source_target_pairs={{0,1},{1,0},{2,3},{3,2},{4,5},{5,4},{6,7},{7,6},{8,9},{9,8},{10,11... | collective-permute-start | bytes 1990664 | tf_op jit(solution)/shard_map/ppermute | solution.py:910
  64.6 47.1 %collective-permute-start.8 = (bf16[1,2,144,1152]{3,2,1,0:T(8,128)(2,1)}, bf16[1,2,144,1152]{3,2,1,0:T(8,128)(2,1)}, u32[]{:S(2)}, u32[]{:S(2)}) collective-permute-start(bf16[1,2,144,1152]{3,2,1,0:T(8,128)(2,1)} %shard_map.227.refs_1_), channel_id=1, source_target_pairs={{0,2},{1,3},{2,0},{3,1},{4,6},{5,7},{6,4},{7,5},{8,10},{9,11},{10,... | collective-permute-start | bytes 1990664 | tf_op jit(solution)/shard_map/ppermute | solution.py:910
  81.9 31.3 %collective-permute-start.12 = (bf16[1,2,144,1152]{3,2,1,0:T(8,128)(2,1)}, bf16[1,2,144,1152]{3,2,1,0:T(8,128)(2,1)}, u32[]{:S(2)}, u32[]{:S(2)}) collective-permute-start(bf16[1,2,144,1152]{3,2,1,0:T(8,128)(2,1)} %pad_maximum_fusion.10), channel_id=1, source_target_pairs={{0,8},{4,12},{8,0},{12,4},{16,24},{20,28},{24,16},{28,20},{1,9},{5... | collective-permute-start | bytes 1990664 | tf_op jit(solution)/shard_map/ppermute | solution.py:846
  83.0 15.6 %all-to-all-start.1 = ((f32[8,2,216]{2,1,0:T(2,128)}), f32[8,2,216]{2,1,0:T(2,128)S(1)}, u32[]{:S(2)}, u32[]{:S(2)}) async-start(f32[8,2,216]{2,1,0:T(2,128)} %copy.154), calls=%async_computation.1 | async-start | bytes 32768 | tf_op jit(solution)/shard_map/all_to_all | solution.py:898
  86.3 147.7 %all-gather.12.cloned.1.call-start = ((), (), s32[]{:S(2)}) async-start(), calls=%async_computation.18 | async-start | bytes 6635520 | tf_op jit(solution)/shard_map/all_gather | solution.py:924
  86.3 31.8 %collective-permute-start.7 = (bf16[1,2,144,1152]{3,2,1,0:T(8,128)(2,1)}, bf16[1,2,144,1152]{3,2,1,0:T(8,128)(2,1)}, u32[]{:S(2)}, u32[]{:S(2)}) collective-permute-start(bf16[1,2,144,1152]{3,2,1,0:T(8,128)(2,1)} %pad_maximum_fusion.9), channel_id=1, source_target_pairs={{0,2},{1,3},{2,0},{3,1},{4,6},{5,7},{6,4},{7,5},{8,10},{9,11},{10,... | collective-permute-start | bytes 1990664 | tf_op jit(solution)/shard_map/ppermute | solution.py:910
  108.2 25.9 %collective-permute-start.9 = (bf16[1,2,144,1152]{3,2,1,0:T(8,128)(2,1)}, bf16[1,2,144,1152]{3,2,1,0:T(8,128)(2,1)}, u32[]{:S(2)}, u32[]{:S(2)}) collective-permute-start(bf16[1,2,144,1152]{3,2,1,0:T(8,128)(2,1)} %collective-permute-done.5), channel_id=1, source_target_pairs={{0,2},{1,3},{2,0},{3,1},{4,6},{5,7},{6,4},{7,5},{8,10},{9,11},{10,... | collective-permute-start | bytes 1990664 | tf_op jit(solution)/shard_map/ppermute | solution.py:910
  109.7 18.2 %collective-permute-start.6 = (bf16[1,2,144,1152]{3,2,1,0:T(8,128)(2,1)}, bf16[1,2,144,1152]{3,2,1,0:T(8,128)(2,1)}, u32[]{:S(2)}, u32[]{:S(2)}) collective-permute-start(bf16[1,2,144,1152]{3,2,1,0:T(8,128)(2,1)} %shard_map.227.refs_1_), channel_id=1, source_target_pairs={{0,1},{1,0},{2,3},{3,2},{4,5},{5,4},{6,7},{7,6},{8,9},{9,8},{10,11... | collective-permute-start | bytes 1990664 | tf_op jit(solution)/shard_map/ppermute | solution.py:910
  111.7 39.9 %collective-permute-start.10 = (bf16[1,2,144,1152]{3,2,1,0:T(8,128)(2,1)}, bf16[1,2,144,1152]{3,2,1,0:T(8,128)(2,1)}, u32[]{:S(2)}, u32[]{:S(2)}) collective-permute-start(bf16[1,2,144,1152]{3,2,1,0:T(8,128)(2,1)} %collective-permute-done.8), channel_id=1, source_target_pairs={{0,1},{1,0},{2,3},{3,2},{4,5},{5,4},{6,7},{7,6},{8,9},{9,8},{10,11... | collective-permute-start | bytes 1990664 | tf_op jit(solution)/shard_map/ppermute | solution.py:910
  115.6 15.8 %collective-permute-start.13 = (bf16[1,1,144,1152]{3,2,1,0:T(8,128)(2,1)}, bf16[1,1,144,1152]{3,2,1,0:T(8,128)(2,1)S(1)}, u32[]{:S(2)}, u32[]{:S(2)}) collective-permute-start(bf16[1,1,144,1152]{3,2,1,0:T(8,128)(2,1)} %shard_map.229), channel_id=1, source_target_pairs={{0,16},{4,20},{8,24},{12,28},{16,0},{20,4},{24,8},{28,12},{1,17},{... | collective-permute-start | bytes 995336 | tf_op jit(solution)/shard_map/ppermute | solution.py:846
  120.6 155.5 %all-gather.14.cloned.1.call-start = ((), (), s32[]{:S(2)}) async-start(), calls=%async_computation.19 | async-start | bytes 6635520 | tf_op jit(solution)/shard_map/all_gather | solution.py:924
  162.0 29.6 %collective-permute-start.15 = (bf16[1,2,144,1152]{3,2,1,0:T(8,128)(2,1)S(1)}, bf16[1,2,144,1152]{3,2,1,0:T(8,128)(2,1)S(1)}, u32[]{:S(2)}, u32[]{:S(2)}) collective-permute-start(bf16[1,2,144,1152]{3,2,1,0:T(8,128)(2,1)S(1)} %copy-done.27), channel_id=1, source_target_pairs={{0,8},{4,12},{8,0},{12,4},{16,24},{20,28},{24,16},{28,20},{1,9},{5... | collective-permute-start | bytes 1990664 | tf_op jit(solution)/shard_map/ppermute | solution.py:846
  195.7 127.4 %all-gather.16.cloned.1.call-start = ((), (), s32[]{:S(2)}) async-start(), calls=%async_computation.20 | async-start | bytes 6635520 | tf_op jit(solution)/shard_map/all_gather | solution.py:924
  196.9 18.2 %collective-permute-start.16 = (bf16[1,1,144,1152]{3,2,1,0:T(8,128)(2,1)}, bf16[1,1,144,1152]{3,2,1,0:T(8,128)(2,1)S(1)}, u32[]{:S(2)}, u32[]{:S(2)}) collective-permute-start(bf16[1,1,144,1152]{3,2,1,0:T(8,128)(2,1)} %shard_map.236), channel_id=1, source_target_pairs={{0,16},{4,20},{8,24},{12,28},{16,0},{20,4},{24,8},{28,12},{1,17},{... | collective-permute-start | bytes 995336 | tf_op jit(solution)/shard_map/ppermute | solution.py:846
  216.9 16.3 %collective-permute-start.17 = (bf16[1,2,144,1152]{3,2,1,0:T(8,128)(2,1)S(1)}, bf16[1,2,144,1152]{3,2,1,0:T(8,128)(2,1)S(1)}, u32[]{:S(2)}, u32[]{:S(2)}) collective-permute-start(bf16[1,2,144,1152]{3,2,1,0:T(8,128)(2,1)S(1)} %pad_maximum_fusion.12), channel_id=1, source_target_pairs={{0,8},{4,12},{8,0},{12,4},{16,24},{20,28},{24,16},{28,20},{1,9},{5... | collective-permute-start | bytes 1990664 | tf_op jit(solution)/shard_map/ppermute | solution.py:846
  238.9 36.5 %collective-permute-start.19 = (bf16[2,1,144,1152]{3,2,1,0:T(8,128)(2,1)}, bf16[2,1,144,1152]{3,2,1,0:T(8,128)(2,1)S(1)}, u32[]{:S(2)}, u32[]{:S(2)}) collective-permute-start(bf16[2,1,144,1152]{3,2,1,0:T(8,128)(2,1)} %shard_map.243), channel_id=1, source_target_pairs={{0,16},{4,20},{8,24},{12,28},{16,0},{20,4},{24,8},{28,12},{1,17},{... | collective-permute-start | bytes 1990664 | tf_op jit(solution)/shard_map/ppermute | solution.py:846
  243.0 172.7 %all-gather.18.cloned.1.call-start = ((), (), s32[]{:S(2)}) async-start(), calls=%async_computation.21 | async-start | bytes 6635520 | tf_op jit(solution)/shard_map/all_gather | solution.py:924
  277.6 37.7 %collective-permute-start.21 = (bf16[2,2,144,1152]{3,2,1,0:T(8,128)(2,1)S(1)}, bf16[2,2,144,1152]{3,2,1,0:T(8,128)(2,1)}, u32[]{:S(2)}, u32[]{:S(2)}) collective-permute-start(bf16[2,2,144,1152]{3,2,1,0:T(8,128)(2,1)S(1)} %pad_maximum_fusion.6.refs_3_), channel_id=1, source_target_pairs={{0,8},{4,12},{8,0},{12,4},{16,24},{20,28},{24,16},{28,20},{1,9},{5... | collective-permute-start | bytes 3981320 | tf_op jit(solution)/shard_map/ppermute | solution.py:846
  319.4 46.1 %all-to-all-start.2 = ((bf16[4,256,1152]{2,1,0:T(8,128)(2,1)}), bf16[4,256,1152]{2,1,0:T(8,128)(2,1)S(1)}, u32[]{:S(2)}, u32[]{:S(2)}) async-start(bf16[4,256,1152]{2,1,0:T(8,128)(2,1)} %bitcast.36), calls=%async_computation.2 | async-start | bytes 4718592 | tf_op jit(solution)/shard_map/all_to_all | solution.py:972
  323.1 157.6 %all-gather.20.cloned.1.call-start = ((), (), s32[]{:S(2)}) async-start(), calls=%async_computation.22 | async-start | bytes 6635520 | tf_op jit(solution)/shard_map/all_gather | solution.py:924
  367.7 243.7 %reduce-scatter.7.cloned.1.call-start = ((), (), s32[]{:S(2)}) async-start(), calls=%async_computation.12 | async-start | bytes 6635520 | tf_op jit(solution)/shard_map/reduce_scatter | solution.py:950
  480.7 16.7 %collective-permute-start.25 = (bf16[4,1,4,144,1152]{4,3,2,1,0:T(8,128)(2,1)}, bf16[4,1,4,144,1152]{4,3,2,1,0:T(8,128)(2,1)}, u32[]{:S(2)}, u32[]{:S(2)}) collective-permute-start(bf16[4,1,4,144,1152]{4,3,2,1,0:T(8,128)(2,1)} %shard_map.260.refs_2_.refs_1_), channel_id=1, source_target_pairs={{0,4},{4,0},{8,12},{12,8},{16,20},{20,16},{24,28},{28,24},{1,5},{5... | collective-permute-start | bytes 15925256 | tf_op jit(solution)/shard_map/ppermute | solution.py:846
  527.1 41.1 %all-to-all-start.3 = ((bf16[4,256,1152]{2,1,0:T(8,128)(2,1)}), bf16[4,256,1152]{2,1,0:T(8,128)(2,1)S(1)}, u32[]{:S(2)}, u32[]{:S(2)}) async-start(bf16[4,256,1152]{2,1,0:T(8,128)(2,1)} %bitcast.242), calls=%async_computation.3 | async-start | bytes 4718592 | tf_op jit(solution)/shard_map/all_to_all | solution.py:972
  530.8 207.3 %reduce-scatter.9.cloned.1.call-start = ((), (), s32[]{:S(2)}) async-start(), calls=%async_computation.13 | async-start | bytes 6635520 | tf_op jit(solution)/shard_map/reduce_scatter | solution.py:950
  612.7 26.9 %collective-permute-start.27 = (bf16[2,144,1152]{2,1,0:T(8,128)(2,1)S(1)}, bf16[2,144,1152]{2,1,0:T(8,128)(2,1)S(1)}, u32[]{:S(2)}, u32[]{:S(2)}) collective-permute-start(bf16[2,144,1152]{2,1,0:T(8,128)(2,1)S(1)} %bitcast.252), channel_id=1, source_target_pairs={{0,8},{4,12},{8,0},{12,4},{16,24},{20,28},{24,16},{28,20},{1,9},{5... | collective-permute-start | bytes 1990664 | tf_op jit(solution)/shard_map/ppermute | solution.py:846
  642.7 21.6 %collective-permute-start.28 = (bf16[144,1152]{1,0:T(8,128)(2,1)S(1)}, bf16[144,1152]{1,0:T(8,128)(2,1)S(1)}, u32[]{:S(2)}, u32[]{:S(2)}) collective-permute-start(bf16[144,1152]{1,0:T(8,128)(2,1)S(1)} %slice_bitcast_fusion.13), channel_id=1, source_target_pairs={{0,16},{4,20},{8,24},{12,28},{16,0},{20,4},{24,8},{28,12},{1,17},{... | collective-permute-start | bytes 995336 | tf_op jit(solution)/shard_map/ppermute | solution.py:846
  665.0 34.7 %all-to-all-start.4 = ((bf16[4,256,1152]{2,1,0:T(8,128)(2,1)}), bf16[4,256,1152]{2,1,0:T(8,128)(2,1)S(1)}, u32[]{:S(2)}, u32[]{:S(2)}) async-start(bf16[4,256,1152]{2,1,0:T(8,128)(2,1)} %bitcast.213), calls=%async_computation.5 | async-start | bytes 4718592 | tf_op jit(solution)/shard_map/all_to_all | solution.py:972
  668.9 112.6 %reduce-scatter.11.cloned.1.call-start = ((), (), s32[]{:S(2)}) async-start(), calls=%async_computation.14 | async-start | bytes 6635520 | tf_op jit(solution)/shard_map/reduce_scatter | solution.py:950
  719.4 148.5 %reduce-scatter.13.cloned.1.call-start = ((), (), s32[]{:S(2)}) async-start(), calls=%async_computation.15 | async-start | bytes 6635520 | tf_op jit(solution)/shard_map/reduce_scatter | solution.py:950
  738.0 41.6 %collective-permute-start.31 = (bf16[4,4,144,1152]{3,2,1,0:T(8,128)(2,1)}, bf16[4,4,144,1152]{3,2,1,0:T(8,128)(2,1)}, u32[]{:S(2)}, u32[]{:S(2)}) collective-permute-start(bf16[4,4,144,1152]{3,2,1,0:T(8,128)(2,1)} %get-tuple-element.210), channel_id=1, source_target_pairs={{0,4},{4,0},{8,12},{12,8},{16,20},{20,16},{24,28},{28,24},{1,5},{5... | collective-permute-start | bytes 15925256 | tf_op jit(solution)/shard_map/ppermute | solution.py:846
  739.5 39.2 %collective-permute-start.30 = (bf16[2,144,1152]{2,1,0:T(8,128)(2,1)S(1)}, bf16[2,144,1152]{2,1,0:T(8,128)(2,1)S(1)}, u32[]{:S(2)}, u32[]{:S(2)}) collective-permute-start(bf16[2,144,1152]{2,1,0:T(8,128)(2,1)S(1)} %bitcast.251), channel_id=1, source_target_pairs={{0,8},{4,12},{8,0},{12,4},{16,24},{20,28},{24,16},{28,20},{1,9},{5... | collective-permute-start | bytes 1990664 | tf_op jit(solution)/shard_map/ppermute | solution.py:846
  788.6 140.0 %reduce-scatter.15.cloned.1.call-start = ((), (), s32[]{:S(2)}) async-start(), calls=%async_computation.16 | async-start | bytes 6635520 | tf_op jit(solution)/shard_map/reduce_scatter | solution.py:950
  808.6 14.9 %collective-permute-start.32 = (bf16[4,4,144,1152]{3,2,1,0:T(8,128)(2,1)}, bf16[4,4,144,1152]{3,2,1,0:T(8,128)(2,1)S(1)}, u32[]{:S(2)}, u32[]{:S(2)}) collective-permute-start(bf16[4,4,144,1152]{3,2,1,0:T(8,128)(2,1)} %get-tuple-element.215), channel_id=1, source_target_pairs={{0,4},{4,0},{8,12},{12,8},{16,20},{20,16},{24,28},{28,24},{1,5},{5... | collective-permute-start | bytes 15925256 | tf_op jit(solution)/shard_map/ppermute | solution.py:846
  832.8 178.3 %reduce-scatter.17.cloned.1.call-start = ((), (), s32[]{:S(2)}) async-start(), calls=%async_computation.17 | async-start | bytes 6635520 | tf_op jit(solution)/shard_map/reduce_scatter | solution.py:950
  834.1 30.1 %collective-permute-start.34 = (bf16[144,1152]{1,0:T(8,128)(2,1)S(1)}, bf16[144,1152]{1,0:T(8,128)(2,1)S(1)}, u32[]{:S(2)}, u32[]{:S(2)}) collective-permute-start(bf16[144,1152]{1,0:T(8,128)(2,1)S(1)} %slice_bitcast_fusion.12), channel_id=1, source_target_pairs={{0,16},{4,20},{8,24},{12,28},{16,0},{20,4},{24,8},{28,12},{1,17},{... | collective-permute-start | bytes 995336 | tf_op jit(solution)/shard_map/ppermute | solution.py:846
  836.7 27.5 %collective-permute-start.33 = (bf16[2,144,1152]{2,1,0:T(8,128)(2,1)S(1)}, bf16[2,144,1152]{2,1,0:T(8,128)(2,1)S(1)}, u32[]{:S(2)}, u32[]{:S(2)}) collective-permute-start(bf16[2,144,1152]{2,1,0:T(8,128)(2,1)S(1)} %bitcast.250), channel_id=1, source_target_pairs={{0,8},{4,12},{8,0},{12,4},{16,24},{20,28},{24,16},{28,20},{1,9},{5... | collective-permute-start | bytes 1990664 | tf_op jit(solution)/shard_map/ppermute | solution.py:846
  867.3 24.8 %collective-permute-start.36 = (bf16[144,1152]{1,0:T(8,128)(2,1)}, bf16[144,1152]{1,0:T(8,128)(2,1)S(1)}, u32[]{:S(2)}, u32[]{:S(2)}) collective-permute-start(bf16[144,1152]{1,0:T(8,128)(2,1)} %slice_bitcast_fusion.11), channel_id=1, source_target_pairs={{0,16},{4,20},{8,24},{12,28},{16,0},{20,4},{24,8},{28,12},{1,17},{... | collective-permute-start | bytes 995336 | tf_op jit(solution)/shard_map/ppermute | solution.py:846
  869.3 23.7 %collective-permute-start.35 = (bf16[2,144,1152]{2,1,0:T(8,128)(2,1)S(1)}, bf16[2,144,1152]{2,1,0:T(8,128)(2,1)S(1)}, u32[]{:S(2)}, u32[]{:S(2)}) collective-permute-start(bf16[2,144,1152]{2,1,0:T(8,128)(2,1)S(1)} %bitcast.249), channel_id=1, source_target_pairs={{0,8},{4,12},{8,0},{12,4},{16,24},{20,28},{24,16},{28,20},{1,9},{5... | collective-permute-start | bytes 1990664 | tf_op jit(solution)/shard_map/ppermute | solution.py:846
  893.9 21.6 %collective-permute-start.38 = (bf16[4,4,144,1152]{3,2,1,0:T(8,128)(2,1)}, bf16[4,4,144,1152]{3,2,1,0:T(8,128)(2,1)}, u32[]{:S(2)}, u32[]{:S(2)}) collective-permute-start(bf16[4,4,144,1152]{3,2,1,0:T(8,128)(2,1)} %get-tuple-element.241), channel_id=1, source_target_pairs={{0,4},{4,0},{8,12},{12,8},{16,20},{20,16},{24,28},{28,24},{1,5},{5... | collective-permute-start | bytes 15925256 | tf_op jit(solution)/shard_map/ppermute | solution.py:846
  895.2 19.5 %collective-permute-start.37 = (bf16[144,1152]{1,0:T(8,128)(2,1)S(1)}, bf16[144,1152]{1,0:T(8,128)(2,1)S(1)}, u32[]{:S(2)}, u32[]{:S(2)}) collective-permute-start(bf16[144,1152]{1,0:T(8,128)(2,1)S(1)} %slice_bitcast_fusion.10), channel_id=1, source_target_pairs={{0,16},{4,20},{8,24},{12,28},{16,0},{20,4},{24,8},{28,12},{1,17},{... | collective-permute-start | bytes 995336 | tf_op jit(solution)/shard_map/ppermute | solution.py:846
  930.0 17.2 %collective-permute-start.39 = (bf16[2,144,1152]{2,1,0:T(8,128)(2,1)S(1)}, bf16[2,144,1152]{2,1,0:T(8,128)(2,1)S(1)}, u32[]{:S(2)}, u32[]{:S(2)}) collective-permute-start(bf16[2,144,1152]{2,1,0:T(8,128)(2,1)S(1)} %bitcast.253), channel_id=1, source_target_pairs={{0,8},{4,12},{8,0},{12,4},{16,24},{20,28},{24,16},{28,20},{1,9},{5... | collective-permute-start | bytes 1990664 | tf_op jit(solution)/shard_map/ppermute | solution.py:846
  974.5 21.8 %collective-permute-start.47 = (bf16[144,1152]{1,0:T(8,128)(2,1)}, bf16[144,1152]{1,0:T(8,128)(2,1)}, u32[]{:S(2)}, u32[]{:S(2)}) collective-permute-start(bf16[144,1152]{1,0:T(8,128)(2,1)} %slice_bitcast_fusion.8), channel_id=1, source_target_pairs={{0,16},{4,20},{8,24},{12,28},{16,0},{20,4},{24,8},{28,12},{1,17},{... | collective-permute-start | bytes 995336 | tf_op jit(solution)/shard_map/ppermute | solution.py:846
  (88 other events, 646.3 us)
Sparse Core Ops, SparseCore 0:
  120.8 69.4 all-gather.11
  195.9 62.2 all-gather.13
  260.6 61.9 all-gather.15
  324.9 77.4 all-gather.17
  404.7 61.9 all-gather.19
  497.5 78.9 reduce-scatter.6
  611.4 79.9 reduce-scatter.8
  719.5 62.0 reduce-scatter.10
  788.7 61.9 reduce-scatter.12
  853.6 61.9 reduce-scatter.14
  922.6 62.0 reduce-scatter.16

commit v4 on v3

--- a/solution.py
+++ b/solution.py
@@ -721,6 +721,26 @@
     )(*flat)
 
 
+def laid_out(pairs):
+    count = len(pairs)
+    flat = [item for pair in pairs for item in pair]
+    _, half, rows, d = flat[0].shape
+
+    def body(*refs):
+        for k in range(count):
+            refs[-1][k, 0, :half] = refs[2 * k][0]
+            refs[-1][k, 0, half:] = refs[2 * k + 1][0]
+
+    return call(
+        body,
+        (1,),
+        [whole(item.shape) for item in flat],
+        whole((count, 1, 2 * half, rows, d)),
+        sds((count, 1, 2 * half, rows, d), BF16),
+        nbytes=8 * count * half * rows * d,
+    )(*flat)
+
+
 def add_pieces(left, right, deps=()):
     seq, zs, rows, d = left.shape
 
@@ -872,7 +892,6 @@
     clip_index = lax.axis_index(CLIP)
     seq_index = lax.axis_index("seq")
     place = jnp.stack([clip_index % 2, clip_index // 2, 0 * seq_index]).astype(jnp.int32)
-    turned = jnp.stack([clip_index % 2, clip_index // 2, seq_index]).astype(jnp.int32)
     packed = zs == 4 and seq == 4 and rows % 16 == 0 and down_weight.shape[1] % rows == 0 and d % seq == 0
     cuts = seq if packed else 1
 
@@ -884,30 +903,28 @@
                 step *= 2
         return v
 
-    every_condition = total(
-        lax.dynamic_update_slice(
-            jnp.zeros((clips, d), F32), conditioning, (clip_index, jnp.zeros_like(clip_index))
-        ),
-        (CLIP, clips),
-    )
-    squashed = jax.nn.silu(every_condition).astype(BF16)
-    local_mods = (
-        jnp.einsum("kd,ldc->klc", squashed, ada_weight, preferred_element_type=F32)
-        + ada_bias[None, :, :]
-    )
-    own_mods = lax.all_to_all(local_mods, CLIP, 0, 0, tiled=True)
-    every_mod = lax.all_gather(own_mods, "seq", axis=0, tiled=False)
-    modulation = every_mod.transpose(2, 1, 0, 3).reshape(layers, 6, d)
-    modulation = jnp.pad(modulation, ((0, 0), (0, 2), (0, 0)))
+    def modulate(first, second):
+        own_place = (clip_index, jnp.zeros_like(clip_index))
+        placed = lax.dynamic_update_slice(jnp.zeros((clips, d), F32), conditioning, own_place)
+        if first:
+            placed = gate(placed, first)
+        squashed = jax.nn.silu(total(placed, (CLIP, clips))).astype(BF16)
+        local_mods = (
+            jnp.einsum("kd,ldc->klc", squashed, ada_weight, preferred_element_type=F32)
+            + ada_bias[None, :, :]
+        )
+        if second:
+            local_mods = gate(local_mods, second)
+        own_mods = lax.all_to_all(local_mods, CLIP, 0, 0, tiled=True)
+        every_mod = lax.all_gather(own_mods, "seq", axis=0, tiled=False)
+        modulation = every_mod.transpose(2, 1, 0, 3).reshape(layers, 6, d)
+        return squashed, jnp.pad(modulation, ((0, 0), (0, 2), (0, 0)))
 
     def far(block):
         return hop(block, 4, clips)
 
     def near(block):
         return hop(block, 2, clips)
-
-    def side(block, distance):
-        return lax.ppermute(block, "seq", [(i, i ^ distance) for i in range(seq)])
 
     def put(*parts):
         return jnp.concatenate(parts, axis=1)
@@ -923,17 +940,6 @@
     def along_seq(blocks):
         return lax.all_gather(blocks, "seq", axis=0, tiled=False)
 
-    def across(upper, lower):
-        upper_x, lower_y = side(upper, 1), side(lower, 2)
-        upper_y, lower_x = side(upper, 2), side(lower, 1)
-        blocks = (
-            (upper, lower),
-            (upper_x, lower_x),
-            (upper_y, lower_y),
-            (side(upper_x, 2), side(lower_y, 1)),
-        )
-        return jnp.stack([put(*pair) for pair in blocks])
-
     def both_cores(own, deps):
         own = gate(own, deps)
         return own, hop(own, 1, clips)
@@ -990,7 +996,7 @@
         bias = attention_bias[layer]
         return jnp.concatenate([bias[0], jnp.zeros_like(bias[0]), bias[1]])[None]
 
-    def forward_natural(layer, x):
+    def forward_natural(layer, x, modulation):
         mods = modulation[layer]
         qkv_full, out_full, up_full, down_full = fetch_natural(layer)
         hidden, qkv = qkv_forward(x, mods, qkv_full, qkv_bias_of(layer))
@@ -1007,7 +1013,7 @@
         weights = (qkv_full, out_full, up_full, down_full)
         return result, kept, weights, jnp.max(peak, axis=(0, 1))
 
-    def backward_natural(layer, grad_out, kept, weights):
+    def backward_natural(layer, grad_out, kept, weights, modulation):
         x, hidden, qkv, lse, attended, branch, middle, hidden_two, active, slope, update = kept
         qkv_full, out_full, up_full, down_full = weights
         mods = modulation[layer]
@@ -1039,25 +1045,26 @@
         return both[:, :own_columns], both[:, own_columns:], up_g, down_g
 
     def run_natural():
+        squashed, modulation = modulate((), ())
         first_in = by_places(video_latents)
         second_go = swap_tokens(by_places(cotangent))
-        first_out, first_kept, first_weights, first_peak = forward_natural(0, first_in)
+        first_out, first_kept, first_weights, first_peak = forward_natural(0, first_in, modulation)
         second_in = swap_tokens(first_out)
-        second_out, second_kept, second_weights, second_peak = forward_natural(1, second_in)
+        second_out, second_kept, second_weights, second_peak = forward_natural(1, second_in, modulation)
         second_grad, second_sums, second_parts = backward_natural(
-            1, second_go, second_kept, second_weights
+            1, second_go, second_kept, second_weights, modulation
         )
         first_grad, first_sums, first_parts = backward_natural(
-            0, swap_tokens(second_grad), first_kept, first_weights
+            0, swap_tokens(second_grad), first_kept, first_weights, modulation
         )
         peaks = (first_peak, second_peak)
         sums = (first_sums, second_sums)
         second_out = swap_tokens(second_out)
 
-        def finish(small, own_mod_grad):
-            return total(small, (CLIP, clips), ("seq", seq)), first_parts
-
-        return second_out, first_grad, peaks, collect(sums), finish, second_parts
+        def finish(small, own_mod_grad, exchanged):
+            return total(small, (CLIP, clips), ("seq", seq)), first_parts, second_parts
+
+        return squashed, second_out, first_grad, peaks, collect(sums), finish
 
     def run_packed():
         first_pack, second_pack = pack_rows(0), pack_rows(1)
@@ -1066,13 +1073,14 @@
 
         block = first_pack[0][None, None]
         pair = put(block, far(block))
-        rest = gate(near(pair), (second_go,))
-        whole_q0 = across(pair, rest)
-        block = gate(first_pack[1][None, None], (rest,))
+        squashed, modulation = modulate((), ())
+        line_q0 = put(pair, gate(near(pair), (second_go,)))
+        block = gate(first_pack[1][None, None], (line_q0,))
         pair = put(block, far(block))
-        line_u0 = put(pair, near(pair))
+        line_u0 = put(pair, gate(near(pair), (modulation,)))
         block = gate(first_pack[2][None, None], (line_u0,))
-        pair_d0 = put(block, gate(far(block), (modulation,)))
+        pair_d0 = put(block, far(block))
+        whole_q0 = along_seq(line_q0)
         whole_u0 = along_seq(line_u0)
 
         def attention_part(layer, x, qkv, out_full):
@@ -1081,7 +1089,7 @@
             return qkv, attended.reshape(n, d), lse, jnp.max(peak, axis=(0, 1))
 
         mods = modulation[0]
-        qkv_full, out_full = join_qkv_out(turned, *both_cores(whole_q0, (pair_d0,)), 0)
+        qkv_full, out_full = join_qkv_out(place, *both_cores(whole_q0, (pair_d0,)), 0)
         hidden, qkv = qkv_forward(first_in, mods, qkv_full, qkv_bias_of(0))
         hidden, qkv, got = joint(hidden, qkv, near(pair_d0))
         line_d0 = put(pair_d0, got)
@@ -1214,27 +1222,31 @@
         first_sums = (stream_sums, middle_sums, update_sums, qkv_sums, up_sums)
         half = add_pieces(last_m, hop(last_o, 1, clips), deps=(first_grad,))
         part_q0 = reduce_seq(half)
-        got = first_half(part_u0)
-        rows_of = collect((first_sums, second_sums), deps=(half, got))
-        sum_u0 = add_first(part_u0, got)
-        second_parts = unpack((down_g1, up_g1, both_g1))
-
-        def finish(small, own_mod_grad):
-            up_g0 = add_second(sum_u0, gate(second_half(sum_u0), (own_mod_grad,)))
+        rows_of = collect((first_sums, second_sums), deps=(half,))
+
+        def finish(small, own_mod_grad, exchanged):
+            sum_u0 = add_first(part_u0, exchanged)
+            up_g0 = add_second(sum_u0, second_half(sum_u0))
             part = gate(part_q0, (up_g0,))
             sum_q0 = add_first(part, first_half(part))
             both_g0 = add_second(sum_q0, second_half(sum_q0))
-            return total(small, (CLIP, clips), ("seq", seq)), unpack((down_g0, up_g0, both_g0))
-
-        return second_out, first_grad, (peak0, peak1), rows_of, finish, second_parts
+            early = [gate(item, (own_mod_grad,)) for item in (down_g1, up_g1, both_g1, down_g0)]
+            small = total(small, (CLIP, clips), ("seq", seq))
+            return small, unpack((early[3], up_g0, both_g0)), unpack(early[:3])
+
+        finish.exchange = lambda: first_half(part_u0)
+        return squashed, second_out, first_grad, (peak0, peak1), rows_of, finish
 
     run = run_packed if packed else run_natural
-    second_out, latents_grad, peaks, (mod_grads, bias_rows), finish, second_shed = run()
+    squashed, second_out, latents_grad, peaks, (mod_grads, bias_rows), finish = run()
     output_latents = by_frames(second_out)
 
     mod_grads = total(mod_grads, ("seq", seq)).reshape(layers, clips, seq, -1)
     of_columns = lax.dynamic_index_in_dim(mod_grads, lax.axis_index("seq"), 2, keepdims=False)
     own_mod_grad = lax.all_to_all(of_columns.transpose(1, 0, 2), CLIP, 0, 0, tiled=True)
+    exchanged = None
+    if packed:
+        own_mod_grad, exchanged = joint(own_mod_grad, finish.exchange())
     ada_bias_grad = jnp.sum(own_mod_grad, axis=0)
     rounded_mod = own_mod_grad.astype(BF16)
     ada_weight_grad = jnp.einsum("kd,klc->ldc", squashed, rounded_mod, preferred_element_type=F32)
@@ -1248,8 +1260,8 @@
         jnp.zeros((devices, layers * HEADS), F32), own_peaks, (device, 0)
     ).reshape(-1)
     placed = jnp.pad(placed, (0, peak_rows * d - placed.shape[0])).reshape(peak_rows, d)
-    summed, first_shed = finish(
-        jnp.concatenate([bias_rows, squash_part, placed], axis=0), own_mod_grad
+    summed, first_shed, second_shed = finish(
+        jnp.concatenate([bias_rows, squash_part, placed], axis=0), own_mod_grad, exchanged
     )
     bias_sums = summed[:bias_count].reshape(layers, -1, d)
     own_squash = lax.dynamic_slice_in_dim(summed, bias_count + clip_index, 1, axis=0)

time: 1060 us -> 1040 us (0.981)
  starting transfers between devices: 88.1 us -> 60.3 us
  blocking collectives: 8.86 us -> 26.2 us
  other arithmetic: 53.8 us -> 41.1 us
    all_gather x5 -> x6, waiting for transfers between devices: 0.02 us -> 55 us  [along_seq(): return lax.all_gather(blocks, 'seq', axis=0, tiled=False)]
    all_to_all x4, waiting for transfers between devices: 51.4 us -> 13.6 us  [swap_tokens(): return lax.all_to_all(block, 'seq', 0, 0, tiled=True).reshape(n, d)]
    ppermute x6 -> x0, waiting for transfers between devices: 24.7 us -> none  [side(): return lax.ppermute(block, 'seq', [(i, i ^ distance) for i in range(seq)])]
    ppermute x34, waiting for transfers between devices: 103 us -> 126 us  [hop(): return lax.ppermute(x, CLIP, [(i, i ^ distance) for i in range(count)])]
    all_to_all x0 -> x1, blocking collectives: none -> 17.4 us  [modulate(): own_mods = lax.all_to_all(local_mods, CLIP, 0, 0, tiled=True)]
    another operation x6 -> x0, other arithmetic: 11.7 us -> none  [the longest x5 11.1 us: across(): return jnp.stack([put(*pair) for pair in blocks])]
    unnamed x146 -> x148, local copies, waits for them, and re-layouts: 34.8 us -> 34.8 us
  transfers between devices with their start and end apart: 67 -> 61, of which waited for: 29 -> 30; matrix products, arithmetic and copies ran while one was open for 9% -> 7% of each run, Pallas kernels for 55% -> 56%
where the time goes in v4:
time: 1040 us; the launch traced here: 1030 us
  Pallas kernels  582 us (56%)
  waiting for transfers between devices  230 us (22%)
  local copies, waits for them, and re-layouts  72.8 us (7%)
  starting transfers between devices  60.3 us (6%)
  other arithmetic  41.1 us (4%)
  blocking collectives  26.2 us (3%)
  between operations  15.4 us (1%)
    pallas_call x39, Pallas kernels, call(): return lambda *args: kernel(*args, *deps)  582 us
    ppermute x34, waiting for transfers between devices, hop(): return lax.ppermute(x, CLIP, [(i, i ^ distance) for i in range(count)])  126 us
    all_gather x6, waiting for transfers between devices, along_seq(): return lax.all_gather(blocks, 'seq', axis=0, tiled=False)  55 us
    unnamed x148, local copies, waits for them, and re-layouts  34.8 us
    ppermute x10, waiting for transfers between devices, total(): v = v + lax.ppermute(v, axis, [(i, i ^ step) for i in range(count)])  29.5 us
    ppermute x34, starting transfers between devices, hop(): return lax.ppermute(x, CLIP, [(i, i ^ distance) for i in range(count)])  24.9 us
  transfers between devices with their start and end apart: 61, of which 30 were waited for; matrix products, arithmetic and copies ran while one was open for 7% of the time, Pallas kernels for 56%

profile of v4, /device:TPU:0, one launch (start us, length us, event | category | flops | bytes accessed | tf_op | source)
XLA Modules:
  0.0 1030.4 jit_solution(9377316035316189696)
XLA Ops:
  21.3 14.9 %collective-permute-done.3 = bf16[1,1,144,1152]{3,2,1,0:T(8,128)(2,1)S(1)} collective-permute-done((bf16[1,1,144,1152]{3,2,1,0:T(8,128)(2,1)S(1)}, bf16[1,1,144,1152]{3,2,1,0:T(8,128)(2,1)S(1)}, u32[]{:S(2)}, u32[]{:S(2)}) %collective-permute-start.3) | collective-permute-done | bytes 331808 | tf_op jit(solution)/shard_map/ppermute | solution.py:866
  37.1 15.2 %collective-permute-done.4.refs_0_ = bf16[1,2,144,1152]{3,2,1,0:T(8,128)(2,1)} collective-permute-done((bf16[1,2,144,1152]{3,2,1,0:T(8,128)(2,1)S(1)}, bf16[1,2,144,1152]{3,2,1,0:T(8,128)(2,1)}, u32[]{:S(2)}, u32[]{:S(2)}) %collective-permute-start.4) | collective-permute-done | bytes 663584 | tf_op jit(solution)/shard_map/ppermute | solution.py:866
  80.0 17.4 %all_to_all.30 = f32[8,2,216]{2,1,0:T(2,128)S(1)} all-to-all(f32[8,2,216]{2,1,0:T(2,128)S(1)} %copy.159), channel_id=1, replica_groups=mesh['z'=4,'core'=2,'seq'=4] {'z','core'}, dimensions={0} | all-to-all | bytes 27648 | tf_op jit(solution)/shard_map/all_to_all | solution.py:918
  97.4 8.8 all-gather
  113.5 15.9 %collective-permute-done.7 = bf16[1,1,144,1152]{3,2,1,0:T(8,128)(2,1)S(1)} collective-permute-done((bf16[1,1,144,1152]{3,2,1,0:T(8,128)(2,1)}, bf16[1,1,144,1152]{3,2,1,0:T(8,128)(2,1)S(1)}, u32[]{:S(2)}, u32[]{:S(2)}) %collective-permute-start.7) | collective-permute-done | bytes 331808 | tf_op jit(solution)/shard_map/ppermute | solution.py:866
  140.4 9.8 shard_map.232
  150.2 16.6 %shard_map.233 = (bf16[1024,1152]{1,0:T(8,128)(2,1)}, bf16[1024,3456]{1,0:T(8,128)(2,1)}) custom-call(bf16[1024,1152]{1,0:T(8,128)(2,1)} %bitcast.231, f32[8,1152]{1,0:T(8,128)} %get-tuple-element.336.refs_1_.refs_2_.refs_5_.refs_4_, bf16[1152,3456]{1,0:T(8,128)(2,1)} %get-tuple-element.134.refs_2_.refs_1_, f32[1,3456]{1,0:T(1,128)} %broadcast_in_dim.45.refs_3_), custom_call_target="tpu_custom_call" | custom-call | flops 8153726976 | bytes 19759104 | tf_op jit(solution)/shard_map/pallas_call | solution.py:49
  172.0 12.9 %shard_map.235 = (bf16[4,4,64,1152]{3,2,1,0:T(8,128)(2,1)}, f32[4,16,256]{2,1,0:T(8,128)}, f32[4,1,16]{2,1,0:T(1,128)}) custom-call(bf16[4,4,64,3456]{3,2,1,0:T(8,128)(2,1)} %bitcast.214), custom_call_target="tpu_custom_call" | custom-call | flops 4294967296 | bytes 9437184 | tf_op jit(solution)/shard_map/pallas_call | solution.py:49
  191.1 9.4 shard_map.238
  200.5 7.4 collective-permute-done.11.refs_3_
  217.9 9.8 shard_map.241.refs_1_.refs_3_
  227.7 23.0 %shard_map.242 = (bf16[1024,4608]{1,0:T(8,128)(2,1)}, bf16[1024,4608]{1,0:T(8,128)(2,1)}) custom-call(bf16[1024,1152]{1,0:T(8,128)(2,1)} %get-tuple-element.147.refs_0_.refs_1_, bf16[1152,4608]{1,0:T(8,128)(2,1)} %shard_map.241.refs_1_.refs_3_, f32[1,4608]{1,0:T(1,128)} %get-tuple-element.339.refs_2_), custom_call_target="tpu_custom_call" | custom-call | flops 10871635968 | bytes 31850496 | tf_op jit(solution)/shard_map/pallas_call | solution.py:49
  260.7 10.4 %shard_map.246.refs_3_.refs_2_ = bf16[4608,1152]{1,0:T(8,128)(2,1)} custom-call(s32[3]{0:T(128)} %pad_add_fusion.refs_0_, bf16[4,1,4,144,1152]{4,3,2,1,0:T(8,128)(2,1)} %shard_map.245.refs_1_, bf16[4,1,4,144,1152]{4,3,2,1,0:T(8,128)(2,1)} %collective-permute-done.14.refs_2_, bf16[2,2,144,1152]{3,2,1,0:T(8,128)(2,1)} %copy-done.20), custom_call_target="tpu_custom_call" | custom-call | bytes 21233664 | tf_op jit(solution)/shard_map/pallas_call | solution.py:49
  271.1 19.2 %shard_map.247 = (bf16[1024,1152]{1,0:T(8,128)(2,1)}, bf16[1024,1152]{1,0:T(8,128)(2,1)}) custom-call(bf16[1024,4608]{1,0:T(8,128)(2,1)} %get-tuple-element.152.refs_1_.refs_0_, f32[1024,1152]{1,0:T(8,128)} %get-tuple-element.153.refs_1_, f32[8,1152]{1,0:T(8,128)} %get-tuple-element.336.refs_1_.refs_2_.refs_5_.refs_4_, ...), custom_call_target="tpu_custom_call" | custom-call | flops 10871635968 | bytes 29491200 | tf_op jit(solution)/shard_map/pallas_call | solution.py:49
  298.1 41.5 %all-gather.20.cloned.1.call-done = bf16[4,4,144,1152]{3,2,1,0:T(8,128)(2,1)} async-done(((bf16[1,4,144,1152]{3,2,1,0:T(8,128)(2,1)}), bf16[4,4,144,1152]{3,2,1,0:T(8,128)(2,1)}) %all-gather.20.cloned.1.call-update) | async-done | bytes 5308432 | tf_op jit(solution)/shard_map/all_gather | solution.py:941
  342.3 7.9 collective-permute-done.16.refs_2_
  350.2 9.9 shard_map.250
  360.1 16.5 %shard_map.251 = (bf16[1024,1152]{1,0:T(8,128)(2,1)}, bf16[1024,3456]{1,0:T(8,128)(2,1)}) custom-call(bf16[1024,1152]{1,0:T(8,128)(2,1)} %bitcast.207, f32[8,1152]{1,0:T(8,128)} %get-tuple-element.337.refs_1_.refs_2_.refs_5_.refs_4_, bf16[1152,3456]{1,0:T(8,128)(2,1)} %get-tuple-element.159.refs_2_.refs_1_, f32[1,3456]{1,0:T(1,128)} %broadcast_in_dim.48.refs_3_), custom_call_target="tpu_custom_call" | custom-call | flops 8153726976 | bytes 19759104 | tf_op jit(solution)/shard_map/pallas_call | solution.py:49
  376.7 12.8 %shard_map.252 = (bf16[16,4,16,1152]{3,2,1,0:T(8,128)(2,1)}, f32[4,16,256]{2,1,0:T(8,128)}, f32[4,1,16]{2,1,0:T(1,128)}) custom-call(bf16[16,4,16,3456]{3,2,1,0:T(8,128)(2,1)} %bitcast.252), custom_call_target="tpu_custom_call" | custom-call | flops 4294967296 | bytes 9437184 | tf_op jit(solution)/shard_map/pallas_call | solution.py:49
  389.5 13.5 %all-gather.22.cloned.1.call-done = bf16[4,4,144,1152]{3,2,1,0:T(8,128)(2,1)} async-done(((bf16[1,4,144,1152]{3,2,1,0:T(8,128)(2,1)}), bf16[4,4,144,1152]{3,2,1,0:T(8,128)(2,1)}) %all-gather.22.cloned.1.call-update) | async-done | bytes 5308432 | tf_op jit(solution)/shard_map/all_gather | solution.py:941
  403.0 9.1 shard_map.253
  412.1 9.2 shard_map.256.refs_1_.refs_3_
  421.3 23.0 %shard_map.257 = (bf16[1024,4608]{1,0:T(8,128)(2,1)}, bf16[1024,4608]{1,0:T(8,128)(2,1)}) custom-call(bf16[1024,1152]{1,0:T(8,128)(2,1)} %get-tuple-element.166.refs_0_.refs_1_, bf16[1152,4608]{1,0:T(8,128)(2,1)} %shard_map.256.refs_1_.refs_3_, f32[1,4608]{1,0:T(1,128)} %get-tuple-element.338.refs_2_), custom_call_target="tpu_custom_call" | custom-call | flops 10871635968 | bytes 31850496 | tf_op jit(solution)/shard_map/pallas_call | solution.py:49
  448.7 18.2 %shard_map.259 = (bf16[4,4,144,1152]{3,2,1,0:T(8,128)(2,1)}, bf16[4,4,144,1152]{3,2,1,0:T(8,128)(2,1)}) custom-call(s32[3]{0:T(128)} %pad_add_fusion.refs_0_, bf16[1024,4608]{1,0:T(8,128)(2,1)} %get-tuple-element.168.refs_2_.refs_1_.refs_0_, bf16[1024,1152]{1,0:T(8,128)(2,1)} %get-tuple-element.169.refs_2_.refs_0_), custom_call_target="tpu_custom_call" | custom-call | flops 10871635968 | bytes 22413312 | tf_op jit(solution)/shard_map/pallas_call | solution.py:49
  467.5 8.6 collective-permute-done.18.refs_1_
  476.1 7.0 shard_map.261.refs_0_
  483.8 10.8 %shard_map.263.refs_3_.refs_2_ = bf16[4608,1152]{1,0:T(8,128)(2,1)} custom-call(s32[3]{0:T(128)} %pad_add_fusion.refs_0_, bf16[4,1,4,144,1152]{4,3,2,1,0:T(8,128)(2,1)} %shard_map.260.refs_2_.refs_1_, bf16[4,1,4,144,1152]{4,3,2,1,0:T(8,128)(2,1)} %get-tuple-element.173.refs_2_), custom_call_target="tpu_custom_call" | custom-call | bytes 21233664 | tf_op jit(solution)/shard_map/pallas_call | solution.py:49
  494.5 19.5 %shard_map.264 = (bf16[1024,1152]{1,0:T(8,128)(2,1)}, bf16[1024,1152]{1,0:T(8,128)(2,1)}) custom-call(bf16[1024,4608]{1,0:T(8,128)(2,1)} %get-tuple-element.168.refs_2_.refs_1_.refs_0_, f32[1024,1152]{1,0:T(8,128)} %get-tuple-element.174.refs_1_, f32[8,1152]{1,0:T(8,128)} %get-tuple-element.337.refs_1_.refs_2_.refs_5_.refs_4_, ...), custom_call_target="tpu_custom_call" | custom-call | flops 10871635968 | bytes 29491200 | tf_op jit(solution)/shard_map/pallas_call | solution.py:49
  517.7 37.2 %shard_map.265 = (bf16[1024,4608]{1,0:T(8,128)(2,1)}, f32[1,4608]{1,0:T(1,128)}, f32[1024,1152]{1,0:T(8,128)}) custom-call(bf16[1024,1152]{1,0:T(8,128)(2,1)} %get-tuple-element.169.refs_2_.refs_0_, bf16[1024,4608]{1,0:T(8,128)(2,1)} %get-tuple-element.170.refs_1_, bf16[4608,1152]{1,0:T(8,128)(2,1)} %shard_map.263.refs_3_.refs_2_, ...), custom_call_target="tpu_custom_call" | custom-call | flops 21743271936 | bytes 47185920 | tf_op jit(solution)/shard_map/pallas_call | solution.py:49
  562.0 17.8 %shard_map.267 = (bf16[4,4,144,1152]{3,2,1,0:T(8,128)(2,1)}, bf16[4,4,144,1152]{3,2,1,0:T(8,128)(2,1)}) custom-call(s32[3]{0:T(128)} %pad_add_fusion.refs_0_, bf16[1024,1152]{1,0:T(8,128)(2,1)} %get-tuple-element.166.refs_0_.refs_1_, bf16[1024,4608]{1,0:T(8,128)(2,1)} %get-tuple-element.184.refs_2_), custom_call_target="tpu_custom_call" | custom-call | flops 10871635968 | bytes 22413312 | tf_op jit(solution)/shard_map/pallas_call | solution.py:49
  579.8 14.9 %shard_map.268 = (f32[1024,1152]{1,0:T(8,128)}, bf16[1024,1152]{1,0:T(8,128)(2,1)}, bf16[4,1024,288]{2,1,0:T(8,128)(2,1)}, bf16[1024,1152]{1,0:T(8,128)(2,1)}, f32[8,1152]{1,0:T(8,128)}) custom-call(f32[1024,1152]{1,0:T(8,128)} %get-tuple-element.181.refs_0_, f32[1024,1152]{1,0:T(8,128)} %get-tuple-element.174.refs_1_, ...), custom_call_target="tpu_custom_call" | custom-call | flops 2717908992 | bytes 28606464 | tf_op jit(solution)/shard_map/pallas_call | solution.py:49
  607.0 26.1 %shard_map.270 = (bf16[16,4,16,3456]{3,2,1,0:T(8,128)(2,1)}, bf16[4,16,4,16,864]{4,3,2,1,0:T(8,128)(2,1)}, f32[1,3456]{1,0:T(1,128)}) custom-call(bf16[16,4,16,3456]{3,2,1,0:T(8,128)(2,1)} %bitcast.253, bf16[16,4,16,1152]{3,2,1,0:T(8,128)(2,1)} %bitcast.251, f32[4,16,256]{2,1,0:T(8,128)} %get-tuple-element.187.refs_2_, ...), custom_call_target="tpu_custom_call" | custom-call | flops 12884901888 | bytes 23592960 | tf_op jit(solution)/shard_map/pallas_call | solution.py:49
  638.5 17.3 %shard_map.272 = (bf16[1024,1152]{1,0:T(8,128)(2,1)}, f32[8,1152]{1,0:T(8,128)}) custom-call(bf16[1024,3456]{1,0:T(8,128)(2,1)} %get-tuple-element.194.refs_0_, bf16[1152,3456]{1,0:T(8,128)(2,1)} %get-tuple-element.159.refs_2_.refs_1_, bf16[1024,1152]{1,0:T(8,128)(2,1)} %bitcast.209, f32[1024,1152]{1,0:T(8,128)} %get-tuple-element.189.refs_2_.refs_3_, ...), custom_call_target="tpu_custom_call" | custom-call | flops 8153726976 | bytes 26836992 | tf_op jit(solution)/shard_map/pallas_call | solution.py:49
  660.2 21.8 %shard_map.274 = (bf16[4,4,144,1152]{3,2,1,0:T(8,128)(2,1)}, bf16[4,4,144,1152]{3,2,1,0:T(8,128)(2,1)}) custom-call(s32[3]{0:T(128)} %pad_add_fusion.refs_0_, bf16[1024,1152]{1,0:T(8,128)(2,1)} %get-tuple-element.180.refs_1_, bf16[1024,1152]{1,0:T(8,128)(2,1)} %bitcast.228, bf16[4,1024,864]{2,1,0:T(8,128)(2,1)} %get-tuple-element.192.refs_3_, ...), custom_call_target="tpu_custom_call" | custom-call | flops 10871635968 | bytes 20054016 | tf_op jit(solution)/shard_map/pallas_call | solution.py:49
  682.0 7.9 all-to-all-done.4
  709.5 18.5 %shard_map.278 = (bf16[4,4,144,1152]{3,2,1,0:T(8,128)(2,1)}, bf16[4,4,144,1152]{3,2,1,0:T(8,128)(2,1)}) custom-call(s32[3]{0:T(128)} %pad_add_fusion.refs_0_, bf16[1024,4608]{1,0:T(8,128)(2,1)} %get-tuple-element.152.refs_1_.refs_0_, bf16[1024,1152]{1,0:T(8,128)(2,1)} %get-tuple-element.202.refs_2_.refs_0_, bf16[4,4,144,1152]{3,2,1,0:T(8,128)(2,1)} %shard_map.277.refs_3_), custom_call_target="tpu_custom_call" | custom-call | flops 10871635968 | bytes 22413312 | tf_op jit(solution)/shard_map/pallas_call | solution.py:49
  731.1 37.5 %shard_map.279 = (bf16[1024,4608]{1,0:T(8,128)(2,1)}, f32[1,4608]{1,0:T(1,128)}, f32[1024,1152]{1,0:T(8,128)}) custom-call(bf16[1024,1152]{1,0:T(8,128)(2,1)} %get-tuple-element.202.refs_2_.refs_0_, bf16[1024,4608]{1,0:T(8,128)(2,1)} %get-tuple-element.203.refs_1_, bf16[4608,1152]{1,0:T(8,128)(2,1)} %shard_map.246.refs_3_.refs_2_, ...), custom_call_target="tpu_custom_call" | custom-call | flops 21743271936 | bytes 47185920 | tf_op jit(solution)/shard_map/pallas_call | solution.py:49
  771.7 7.0 shard_map.281.refs_3_
  780.8 18.2 %shard_map.282 = (bf16[4,4,144,1152]{3,2,1,0:T(8,128)(2,1)}, bf16[4,4,144,1152]{3,2,1,0:T(8,128)(2,1)}) custom-call(s32[3]{0:T(128)} %pad_add_fusion.refs_0_, bf16[1024,1152]{1,0:T(8,128)(2,1)} %get-tuple-element.147.refs_0_.refs_1_, bf16[1024,4608]{1,0:T(8,128)(2,1)} %get-tuple-element.211.refs_2_, bf16[4,4,144,1152]{3,2,1,0:T(8,128)(2,1)} %shard_map.281.refs_3_, ...), custom_call_target="tpu_custom_call" | custom-call | flops 10871635968 | bytes 22413312 | tf_op jit(solution)/shard_map/pallas_call | solution.py:49
  799.0 14.9 %shard_map.283 = (f32[1024,1152]{1,0:T(8,128)}, bf16[1024,1152]{1,0:T(8,128)(2,1)}, bf16[4,1024,288]{2,1,0:T(8,128)(2,1)}, bf16[1024,1152]{1,0:T(8,128)(2,1)}, f32[8,1152]{1,0:T(8,128)}) custom-call(f32[1024,1152]{1,0:T(8,128)} %get-tuple-element.209.refs_2_.refs_0_, f32[1024,1152]{1,0:T(8,128)} %get-tuple-element.153.refs_1_, ...), custom_call_target="tpu_custom_call" | custom-call | flops 2717908992 | bytes 28606464 | tf_op jit(solution)/shard_map/pallas_call | solution.py:49
  816.2 7.1 shard_map.284.refs_3_
  828.8 25.9 %shard_map.285 = (bf16[4,4,64,3456]{3,2,1,0:T(8,128)(2,1)}, bf16[4,4,4,64,864]{4,3,2,1,0:T(8,128)(2,1)}, f32[1,3456]{1,0:T(1,128)}) custom-call(bf16[4,4,64,3456]{3,2,1,0:T(8,128)(2,1)} %bitcast.215, bf16[4,4,64,1152]{3,2,1,0:T(8,128)(2,1)} %bitcast.250, f32[4,16,256]{2,1,0:T(8,128)} %get-tuple-element.216.refs_2_, bf16[4,4,144,1152]{3,2,1,0:T(8,128)(2,1)} %shard_map.284.refs_3_), custom_call_target="tpu_custom_call" | custom-call | flops 12884901888 | bytes 23592960 | tf_op jit(solution)/shard_map/pallas_call | solution.py:49
  860.5 21.7 %shard_map.287 = (bf16[4,4,144,1152]{3,2,1,0:T(8,128)(2,1)}, bf16[4,4,144,1152]{3,2,1,0:T(8,128)(2,1)}) custom-call(s32[3]{0:T(128)} %pad_add_fusion.refs_0_, bf16[1024,1152]{1,0:T(8,128)(2,1)} %get-tuple-element.222.refs_1_, bf16[1024,1152]{1,0:T(8,128)(2,1)} %get-tuple-element.141.refs_0_.refs_2_, bf16[4,1024,864]{2,1,0:T(8,128)(2,1)} %get-tuple-element.223.refs_3_, ...), custom_call_target="tpu_custom_call" | custom-call | flops 10871635968 | bytes 20054016 | tf_op jit(solution)/shard_map/pallas_call | solution.py:49
  887.0 18.0 %shard_map.289 = (f32[4,4,64,1152]{3,2,1,0:T(8,128)}, f32[8,1152]{1,0:T(8,128)}) custom-call(bf16[1024,3456]{1,0:T(8,128)(2,1)} %get-tuple-element.221.refs_0_, bf16[1152,3456]{1,0:T(8,128)(2,1)} %get-tuple-element.134.refs_2_.refs_1_, bf16[1024,1152]{1,0:T(8,128)(2,1)} %bitcast.233, f32[1024,1152]{1,0:T(8,128)} %get-tuple-element.218.refs_2_.refs_3_, ...), custom_call_target="tpu_custom_call" | custom-call | flops 8153726976 | bytes 26836992 | tf_op jit(solution)/shard_map/pallas_call | solution.py:49
  905.7 7.0 shard_map.291.refs_10_
  969.0 7.2 collective-permute-done.38
  990.5 14.6 %collective-permute-done.42 = bf16[2,144,1152]{2,1,0:T(8,128)(2,1)S(1)} collective-permute-done((bf16[2,144,1152]{2,1,0:T(8,128)(2,1)S(1)}, bf16[2,144,1152]{2,1,0:T(8,128)(2,1)S(1)}, u32[]{:S(2)}, u32[]{:S(2)}) %collective-permute-start.42) | collective-permute-done | bytes 663584 | tf_op jit(solution)/shard_map/ppermute | solution.py:866
  1009.5 11.8 %collective-permute-done.43 = bf16[144,1152]{1,0:T(8,128)(2,1)S(1)} collective-permute-done((bf16[144,1152]{1,0:T(8,128)(2,1)S(1)}, bf16[144,1152]{1,0:T(8,128)(2,1)S(1)}, u32[]{:S(2)}, u32[]{:S(2)}) %collective-permute-start.43) | collective-permute-done | bytes 331808 | tf_op jit(solution)/shard_map/ppermute | solution.py:866
  (424 shorter events, 264.3 us)
Async XLA Ops:
  10.6 41.7 %all-to-all-start = ((bf16[4,256,1152]{2,1,0:T(8,128)(2,1)}), bf16[4,256,1152]{2,1,0:T(8,128)(2,1)S(1)}, u32[]{:S(2)}, u32[]{:S(2)}) async-start(bf16[4,256,1152]{2,1,0:T(8,128)(2,1)} %bitcast.204), calls=%async_computation | async-start | bytes 4718592 | tf_op jit(solution)/shard_map/all_to_all | solution.py:978
  15.7 115.6 %all-gather.14.cloned.1.call-start = ((), (), s32[]{:S(2)}) async-start(), calls=%async_computation.18 | async-start | bytes 6635520 | tf_op jit(solution)/shard_map/all_gather | solution.py:941
  18.6 17.5 %collective-permute-start.3 = (bf16[1,1,144,1152]{3,2,1,0:T(8,128)(2,1)S(1)}, bf16[1,1,144,1152]{3,2,1,0:T(8,128)(2,1)S(1)}, u32[]{:S(2)}, u32[]{:S(2)}) collective-permute-start(bf16[1,1,144,1152]{3,2,1,0:T(8,128)(2,1)S(1)} %maximum_bitcast_fusion.1), channel_id=1, source_target_pairs={{0,16},{4,20},{8,24},{12,28},{16,0},{20,4},{24,8},{28,12},{1,17},{... | collective-permute-start | bytes 995336 | tf_op jit(solution)/shard_map/ppermute | solution.py:866
  36.3 16.0 %collective-permute-start.4 = (bf16[1,2,144,1152]{3,2,1,0:T(8,128)(2,1)S(1)}, bf16[1,2,144,1152]{3,2,1,0:T(8,128)(2,1)}, u32[]{:S(2)}, u32[]{:S(2)}) collective-permute-start(bf16[1,2,144,1152]{3,2,1,0:T(8,128)(2,1)S(1)} %pad_maximum_fusion.9), channel_id=1, source_target_pairs={{0,8},{4,12},{8,0},{12,4},{16,24},{20,28},{24,16},{28,20},{1,9},{5... | collective-permute-start | bytes 1990664 | tf_op jit(solution)/shard_map/ppermute | solution.py:866
  56.2 152.5 %all-gather.16.cloned.1.call-start = ((), (), s32[]{:S(2)}) async-start(), calls=%async_computation.19 | async-start | bytes 6635520 | tf_op jit(solution)/shard_map/all_gather | solution.py:941
  57.4 20.2 %collective-permute-start.5 = (bf16[1,1,144,1152]{3,2,1,0:T(8,128)(2,1)}, bf16[1,1,144,1152]{3,2,1,0:T(8,128)(2,1)S(1)}, u32[]{:S(2)}, u32[]{:S(2)}) collective-permute-start(bf16[1,1,144,1152]{3,2,1,0:T(8,128)(2,1)} %shard_map.228), channel_id=1, source_target_pairs={{0,16},{4,20},{8,24},{12,28},{16,0},{20,4},{24,8},{28,12},{1,17},{... | collective-permute-start | bytes 995336 | tf_op jit(solution)/shard_map/ppermute | solution.py:866
  69.6 9.8 collective-permute-start.2
  78.7 28.4 %collective-permute-start.6 = (bf16[1,2,144,1152]{3,2,1,0:T(8,128)(2,1)S(1)}, bf16[1,2,144,1152]{3,2,1,0:T(8,128)(2,1)S(1)}, u32[]{:S(2)}, u32[]{:S(2)}) collective-permute-start(bf16[1,2,144,1152]{3,2,1,0:T(8,128)(2,1)S(1)} %pad_maximum_fusion.10), channel_id=1, source_target_pairs={{0,8},{4,12},{8,0},{12,4},{16,24},{20,28},{24,16},{28,20},{1,9},{5... | collective-permute-start | bytes 1990664 | tf_op jit(solution)/shard_map/ppermute | solution.py:866
  110.2 141.3 %all-gather.18.cloned.1.call-start = ((), (), s32[]{:S(2)}) async-start(), calls=%async_computation.20 | async-start | bytes 6635520 | tf_op jit(solution)/shard_map/all_gather | solution.py:941
  112.9 16.4 %collective-permute-start.7 = (bf16[1,1,144,1152]{3,2,1,0:T(8,128)(2,1)}, bf16[1,1,144,1152]{3,2,1,0:T(8,128)(2,1)S(1)}, u32[]{:S(2)}, u32[]{:S(2)}) collective-permute-start(bf16[1,1,144,1152]{3,2,1,0:T(8,128)(2,1)} %shard_map.230), channel_id=1, source_target_pairs={{0,16},{4,20},{8,24},{12,28},{16,0},{20,4},{24,8},{28,12},{1,17},{... | collective-permute-start | bytes 995336 | tf_op jit(solution)/shard_map/ppermute | solution.py:866
  137.3 29.4 %collective-permute-start.9 = (bf16[1,2,144,1152]{3,2,1,0:T(8,128)(2,1)S(1)}, bf16[1,2,144,1152]{3,2,1,0:T(8,128)(2,1)S(1)}, u32[]{:S(2)}, u32[]{:S(2)}) collective-permute-start(bf16[1,2,144,1152]{3,2,1,0:T(8,128)(2,1)S(1)} %copy-done.27), channel_id=1, source_target_pairs={{0,8},{4,12},{8,0},{12,4},{16,24},{20,28},{24,16},{28,20},{1,9},{5... | collective-permute-start | bytes 1990664 | tf_op jit(solution)/shard_map/ppermute | solution.py:866
  170.9 168.7 %all-gather.20.cloned.1.call-start = ((), (), s32[]{:S(2)}) async-start(), calls=%async_computation.21 | async-start | bytes 6635520 | tf_op jit(solution)/shard_map/all_gather | solution.py:941
  172.0 17.2 %collective-permute-start.10 = (bf16[1,1,144,1152]{3,2,1,0:T(8,128)(2,1)}, bf16[1,1,144,1152]{3,2,1,0:T(8,128)(2,1)S(1)}, u32[]{:S(2)}, u32[]{:S(2)}) collective-permute-start(bf16[1,1,144,1152]{3,2,1,0:T(8,128)(2,1)} %shard_map.236), channel_id=1, source_target_pairs={{0,16},{4,20},{8,24},{12,28},{16,0},{20,4},{24,8},{28,12},{1,17},{... | collective-permute-start | bytes 995336 | tf_op jit(solution)/shard_map/ppermute | solution.py:866
  191.0 16.9 %collective-permute-start.11 = (bf16[1,2,144,1152]{3,2,1,0:T(8,128)(2,1)S(1)}, bf16[1,2,144,1152]{3,2,1,0:T(8,128)(2,1)S(1)}, u32[]{:S(2)}, u32[]{:S(2)}) collective-permute-start(bf16[1,2,144,1152]{3,2,1,0:T(8,128)(2,1)S(1)} %pad_maximum_fusion.12), channel_id=1, source_target_pairs={{0,8},{4,12},{8,0},{12,4},{16,24},{20,28},{24,16},{28,20},{1,9},{5... | collective-permute-start | bytes 1990664 | tf_op jit(solution)/shard_map/ppermute | solution.py:866
  212.1 38.6 %collective-permute-start.13 = (bf16[2,1,144,1152]{3,2,1,0:T(8,128)(2,1)}, bf16[2,1,144,1152]{3,2,1,0:T(8,128)(2,1)S(1)}, u32[]{:S(2)}, u32[]{:S(2)}) collective-permute-start(bf16[2,1,144,1152]{3,2,1,0:T(8,128)(2,1)} %shard_map.243), channel_id=1, source_target_pairs={{0,16},{4,20},{8,24},{12,28},{16,0},{20,4},{24,8},{28,12},{1,17},{... | collective-permute-start | bytes 1990664 | tf_op jit(solution)/shard_map/ppermute | solution.py:866
  214.2 188.8 %all-gather.22.cloned.1.call-start = ((), (), s32[]{:S(2)}) async-start(), calls=%async_computation.22 | async-start | bytes 6635520 | tf_op jit(solution)/shard_map/all_gather | solution.py:941
  251.6 9.2 collective-permute-start.14
  253.0 37.3 %collective-permute-start.15 = (bf16[2,2,144,1152]{3,2,1,0:T(8,128)(2,1)S(1)}, bf16[2,2,144,1152]{3,2,1,0:T(8,128)(2,1)}, u32[]{:S(2)}, u32[]{:S(2)}) collective-permute-start(bf16[2,2,144,1152]{3,2,1,0:T(8,128)(2,1)S(1)} %pad_maximum_fusion.6.refs_3_), channel_id=1, source_target_pairs={{0,8},{4,12},{8,0},{12,4},{16,24},{20,28},{24,16},{28,20},{1,9},{5... | collective-permute-start | bytes 3981320 | tf_op jit(solution)/shard_map/ppermute | solution.py:866
  294.4 45.2 %all-to-all-start.2 = ((bf16[4,256,1152]{2,1,0:T(8,128)(2,1)}), bf16[4,256,1152]{2,1,0:T(8,128)(2,1)S(1)}, u32[]{:S(2)}, u32[]{:S(2)}) async-start(bf16[4,256,1152]{2,1,0:T(8,128)(2,1)} %bitcast.32), calls=%async_computation.2 | async-start | bytes 4718592 | tf_op jit(solution)/shard_map/all_to_all | solution.py:978
  298.1 169.3 %all-gather.24.cloned.1.call-start = ((), (), s32[]{:S(2)}) async-start(), calls=%async_computation.23 | async-start | bytes 6635520 | tf_op jit(solution)/shard_map/all_gather | solution.py:941
  341.7 262.2 %reduce-scatter.7.cloned.1.call-start = ((), (), s32[]{:S(2)}) async-start(), calls=%async_computation.12 | async-start | bytes 6635520 | tf_op jit(solution)/shard_map/reduce_scatter | solution.py:956
  467.0 9.2 collective-permute-start.18
  467.4 16.3 %collective-permute-start.19 = (bf16[4,1,4,144,1152]{4,3,2,1,0:T(8,128)(2,1)}, bf16[4,1,4,144,1152]{4,3,2,1,0:T(8,128)(2,1)}, u32[]{:S(2)}, u32[]{:S(2)}) collective-permute-start(bf16[4,1,4,144,1152]{4,3,2,1,0:T(8,128)(2,1)} %shard_map.260.refs_2_.refs_1_), channel_id=1, source_target_pairs={{0,4},{4,0},{8,12},{12,8},{16,20},{20,16},{24,28},{28,24},{1,5},{5... | collective-permute-start | bytes 15925256 | tf_op jit(solution)/shard_map/ppermute | solution.py:866
  514.0 46.6 %all-to-all-start.3 = ((bf16[4,256,1152]{2,1,0:T(8,128)(2,1)}), bf16[4,256,1152]{2,1,0:T(8,128)(2,1)S(1)}, u32[]{:S(2)}, u32[]{:S(2)}) async-start(bf16[4,256,1152]{2,1,0:T(8,128)(2,1)} %bitcast.235), calls=%async_computation.3 | async-start | bytes 4718592 | tf_op jit(solution)/shard_map/all_to_all | solution.py:978
  517.7 210.5 %reduce-scatter.9.cloned.1.call-start = ((), (), s32[]{:S(2)}) async-start(), calls=%async_computation.13 | async-start | bytes 6635520 | tf_op jit(solution)/shard_map/reduce_scatter | solution.py:956
  579.8 14.9 %collective-permute-start.20 = (bf16[4,4,144,1152]{3,2,1,0:T(8,128)(2,1)}, bf16[4,4,144,1152]{3,2,1,0:T(8,128)(2,1)S(1)}, u32[]{:S(2)}, u32[]{:S(2)}) collective-permute-start(bf16[4,4,144,1152]{3,2,1,0:T(8,128)(2,1)} %get-tuple-element.188), channel_id=1, source_target_pairs={{0,4},{4,0},{8,12},{12,8},{16,20},{20,16},{24,28},{28,24},{1,5},{5... | collective-permute-start | bytes 15925256 | tf_op jit(solution)/shard_map/ppermute | solution.py:866
  605.4 27.6 %collective-permute-start.21 = (bf16[2,144,1152]{2,1,0:T(8,128)(2,1)S(1)}, bf16[2,144,1152]{2,1,0:T(8,128)(2,1)S(1)}, u32[]{:S(2)}, u32[]{:S(2)}) collective-permute-start(bf16[2,144,1152]{2,1,0:T(8,128)(2,1)S(1)} %bitcast.245), channel_id=1, source_target_pairs={{0,8},{4,12},{8,0},{12,4},{16,24},{20,28},{24,16},{28,20},{1,9},{5... | collective-permute-start | bytes 1990664 | tf_op jit(solution)/shard_map/ppermute | solution.py:866
  636.0 19.7 %collective-permute-start.22 = (bf16[144,1152]{1,0:T(8,128)(2,1)S(1)}, bf16[144,1152]{1,0:T(8,128)(2,1)S(1)}, u32[]{:S(2)}, u32[]{:S(2)}) collective-permute-start(bf16[144,1152]{1,0:T(8,128)(2,1)S(1)} %slice_bitcast_fusion.13), channel_id=1, source_target_pairs={{0,16},{4,20},{8,24},{12,28},{16,0},{20,4},{24,8},{28,12},{1,17},{... | collective-permute-start | bytes 995336 | tf_op jit(solution)/shard_map/ppermute | solution.py:866
  656.5 33.3 %all-to-all-start.4 = ((bf16[4,256,1152]{2,1,0:T(8,128)(2,1)}), bf16[4,256,1152]{2,1,0:T(8,128)(2,1)S(1)}, u32[]{:S(2)}, u32[]{:S(2)}) async-start(bf16[4,256,1152]{2,1,0:T(8,128)(2,1)} %bitcast.205), calls=%async_computation.5 | async-start | bytes 4718592 | tf_op jit(solution)/shard_map/all_to_all | solution.py:978
  660.2 111.5 %reduce-scatter.11.cloned.1.call-start = ((), (), s32[]{:S(2)}) async-start(), calls=%async_computation.14 | async-start | bytes 6635520 | tf_op jit(solution)/shard_map/reduce_scatter | solution.py:956
  709.5 148.8 %reduce-scatter.13.cloned.1.call-start = ((), (), s32[]{:S(2)}) async-start(), calls=%async_computation.15 | async-start | bytes 6635520 | tf_op jit(solution)/shard_map/reduce_scatter | solution.py:956
  728.0 41.4 %collective-permute-start.25 = (bf16[4,4,144,1152]{3,2,1,0:T(8,128)(2,1)}, bf16[4,4,144,1152]{3,2,1,0:T(8,128)(2,1)}, u32[]{:S(2)}, u32[]{:S(2)}) collective-permute-start(bf16[4,4,144,1152]{3,2,1,0:T(8,128)(2,1)} %get-tuple-element.212), channel_id=1, source_target_pairs={{0,4},{4,0},{8,12},{12,8},{16,20},{20,16},{24,28},{28,24},{1,5},{5... | collective-permute-start | bytes 15925256 | tf_op jit(solution)/shard_map/ppermute | solution.py:866
  729.6 39.0 %collective-permute-start.24 = (bf16[2,144,1152]{2,1,0:T(8,128)(2,1)S(1)}, bf16[2,144,1152]{2,1,0:T(8,128)(2,1)S(1)}, u32[]{:S(2)}, u32[]{:S(2)}) collective-permute-start(bf16[2,144,1152]{2,1,0:T(8,128)(2,1)S(1)} %bitcast.244), channel_id=1, source_target_pairs={{0,8},{4,12},{8,0},{12,4},{16,24},{20,28},{24,16},{28,20},{1,9},{5... | collective-permute-start | bytes 1990664 | tf_op jit(solution)/shard_map/ppermute | solution.py:866
  778.7 142.5 %reduce-scatter.15.cloned.1.call-start = ((), (), s32[]{:S(2)}) async-start(), calls=%async_computation.16 | async-start | bytes 6635520 | tf_op jit(solution)/shard_map/reduce_scatter | solution.py:956
  799.0 14.9 %collective-permute-start.26 = (bf16[4,4,144,1152]{3,2,1,0:T(8,128)(2,1)}, bf16[4,4,144,1152]{3,2,1,0:T(8,128)(2,1)S(1)}, u32[]{:S(2)}, u32[]{:S(2)}) collective-permute-start(bf16[4,4,144,1152]{3,2,1,0:T(8,128)(2,1)} %get-tuple-element.217), channel_id=1, source_target_pairs={{0,4},{4,0},{8,12},{12,8},{16,20},{20,16},{24,28},{28,24},{1,5},{5... | collective-permute-start | bytes 15925256 | tf_op jit(solution)/shard_map/ppermute | solution.py:866
  823.3 165.7 %reduce-scatter.17.cloned.1.call-start = ((), (), s32[]{:S(2)}) async-start(), calls=%async_computation.17 | async-start | bytes 6635520 | tf_op jit(solution)/shard_map/reduce_scatter | solution.py:956
  824.4 30.2 %collective-permute-start.28 = (bf16[144,1152]{1,0:T(8,128)(2,1)S(1)}, bf16[144,1152]{1,0:T(8,128)(2,1)S(1)}, u32[]{:S(2)}, u32[]{:S(2)}) collective-permute-start(bf16[144,1152]{1,0:T(8,128)(2,1)S(1)} %slice_bitcast_fusion.12), channel_id=1, source_target_pairs={{0,16},{4,20},{8,24},{12,28},{16,0},{20,4},{24,8},{28,12},{1,17},{... | collective-permute-start | bytes 995336 | tf_op jit(solution)/shard_map/ppermute | solution.py:866
  827.2 27.5 %collective-permute-start.27 = (bf16[2,144,1152]{2,1,0:T(8,128)(2,1)S(1)}, bf16[2,144,1152]{2,1,0:T(8,128)(2,1)S(1)}, u32[]{:S(2)}, u32[]{:S(2)}) collective-permute-start(bf16[2,144,1152]{2,1,0:T(8,128)(2,1)S(1)} %bitcast.243), channel_id=1, source_target_pairs={{0,8},{4,12},{8,0},{12,4},{16,24},{20,28},{24,16},{28,20},{1,9},{5... | collective-permute-start | bytes 1990664 | tf_op jit(solution)/shard_map/ppermute | solution.py:866
  857.8 24.5 %collective-permute-start.30 = (bf16[144,1152]{1,0:T(8,128)(2,1)}, bf16[144,1152]{1,0:T(8,128)(2,1)S(1)}, u32[]{:S(2)}, u32[]{:S(2)}) collective-permute-start(bf16[144,1152]{1,0:T(8,128)(2,1)} %slice_bitcast_fusion.11), channel_id=1, source_target_pairs={{0,16},{4,20},{8,24},{12,28},{16,0},{20,4},{24,8},{28,12},{1,17},{... | collective-permute-start | bytes 995336 | tf_op jit(solution)/shard_map/ppermute | solution.py:866
  859.6 23.5 %collective-permute-start.29 = (bf16[2,144,1152]{2,1,0:T(8,128)(2,1)S(1)}, bf16[2,144,1152]{2,1,0:T(8,128)(2,1)S(1)}, u32[]{:S(2)}, u32[]{:S(2)}) collective-permute-start(bf16[2,144,1152]{2,1,0:T(8,128)(2,1)S(1)} %bitcast.242), channel_id=1, source_target_pairs={{0,8},{4,12},{8,0},{12,4},{16,24},{20,28},{24,16},{28,20},{1,9},{5... | collective-permute-start | bytes 1990664 | tf_op jit(solution)/shard_map/ppermute | solution.py:866
  884.0 21.7 %collective-permute-start.32 = (bf16[4,4,144,1152]{3,2,1,0:T(8,128)(2,1)}, bf16[4,4,144,1152]{3,2,1,0:T(8,128)(2,1)}, u32[]{:S(2)}, u32[]{:S(2)}) collective-permute-start(bf16[4,4,144,1152]{3,2,1,0:T(8,128)(2,1)} %get-tuple-element.243), channel_id=1, source_target_pairs={{0,4},{4,0},{8,12},{12,8},{16,20},{20,16},{24,28},{28,24},{1,5},{5... | collective-permute-start | bytes 15925256 | tf_op jit(solution)/shard_map/ppermute | solution.py:866
  885.3 19.7 %collective-permute-start.31 = (bf16[144,1152]{1,0:T(8,128)(2,1)S(1)}, bf16[144,1152]{1,0:T(8,128)(2,1)S(1)}, u32[]{:S(2)}, u32[]{:S(2)}) collective-permute-start(bf16[144,1152]{1,0:T(8,128)(2,1)S(1)} %slice_bitcast_fusion.10), channel_id=1, source_target_pairs={{0,16},{4,20},{8,24},{12,28},{16,0},{20,4},{24,8},{28,12},{1,17},{... | collective-permute-start | bytes 995336 | tf_op jit(solution)/shard_map/ppermute | solution.py:866
  923.4 17.1 %collective-permute-start.35 = (bf16[2,144,1152]{2,1,0:T(8,128)(2,1)}, bf16[2,144,1152]{2,1,0:T(8,128)(2,1)}, u32[]{:S(2)}, u32[]{:S(2)}) collective-permute-start(bf16[2,144,1152]{2,1,0:T(8,128)(2,1)} %bitcast.78), channel_id=1, source_target_pairs={{0,8},{4,12},{8,0},{12,4},{16,24},{20,28},{24,16},{28,20},{1,9},{5... | collective-permute-start | bytes 1990664 | tf_op jit(solution)/shard_map/ppermute | solution.py:866
  951.4 27.3 %collective-permute-start.41 = (bf16[144,1152]{1,0:T(8,128)(2,1)}, bf16[144,1152]{1,0:T(8,128)(2,1)}, u32[]{:S(2)}, u32[]{:S(2)}) collective-permute-start(bf16[144,1152]{1,0:T(8,128)(2,1)} %slice_bitcast_fusion.8), channel_id=1, source_target_pairs={{0,16},{4,20},{8,24},{12,28},{16,0},{20,4},{24,8},{28,12},{1,17},{... | collective-permute-start | bytes 995336 | tf_op jit(solution)/shard_map/ppermute | solution.py:866
  952.1 10.9 %collective-permute-start.37 = (f32[25,1152]{1,0:T(8,128)S(1)}, f32[25,1152]{1,0:T(8,128)S(1)}, u32[]{:S(2)}, u32[]{:S(2)}) collective-permute-start(f32[25,1152]{1,0:T(8,128)S(1)} %fusion.20), channel_id=1, source_target_pairs={{0,8},{4,12},{8,0},{12,4},{16,24},{20,28},{24,16},{28,20},{1,9},{5... | collective-permute-start | bytes 345608 | tf_op jit(solution)/shard_map/ppermute | solution.py:902
  963.7 12.5 %collective-permute-start.38 = (f32[25,1152]{1,0:T(8,128)}, f32[25,1152]{1,0:T(8,128)}, u32[]{:S(2)}, u32[]{:S(2)}) collective-permute-start(f32[25,1152]{1,0:T(8,128)} %add.173), channel_id=1, source_target_pairs={{0,16},{4,20},{8,24},{12,28},{16,0},{20,4},{24,8},{28,12},{1,17},{... | collective-permute-start | bytes 345608 | tf_op jit(solution)/shard_map/ppermute | solution.py:902
  990.3 14.8 %collective-permute-start.42 = (bf16[2,144,1152]{2,1,0:T(8,128)(2,1)S(1)}, bf16[2,144,1152]{2,1,0:T(8,128)(2,1)S(1)}, u32[]{:S(2)}, u32[]{:S(2)}) collective-permute-start(bf16[2,144,1152]{2,1,0:T(8,128)(2,1)S(1)} %slice.282), channel_id=1, source_target_pairs={{0,8},{4,12},{8,0},{12,4},{16,24},{20,28},{24,16},{28,20},{1,9},{5... | collective-permute-start | bytes 1990664 | tf_op jit(solution)/shard_map/ppermute | solution.py:866
  1006.5 14.8 %collective-permute-start.43 = (bf16[144,1152]{1,0:T(8,128)(2,1)S(1)}, bf16[144,1152]{1,0:T(8,128)(2,1)S(1)}, u32[]{:S(2)}, u32[]{:S(2)}) collective-permute-start(bf16[144,1152]{1,0:T(8,128)(2,1)S(1)} %slice_bitcast_fusion.6), channel_id=1, source_target_pairs={{0,16},{4,20},{8,24},{12,28},{16,0},{20,4},{24,8},{28,12},{1,17},{... | collective-permute-start | bytes 995336 | tf_op jit(solution)/shard_map/ppermute | solution.py:866
  (83 other events, 524.3 us)
Sparse Core Ops, SparseCore 0:
  56.4 64.8 all-gather.13
  123.6 61.9 all-gather.15
  188.1 61.9 all-gather.17
  252.3 87.2 all-gather.19
  341.9 61.0 all-gather.21
  405.3 62.0 all-gather.23
  483.9 78.3 reduce-scatter.6
  604.1 76.3 reduce-scatter.8
  709.6 62.0 reduce-scatter.10
  778.8 61.9 reduce-scatter.12
  843.9 61.9 reduce-scatter.14
  912.9 62.1 reduce-scatter.16

commit v5 on v4

--- a/solution.py
+++ b/solution.py
@@ -1093,7 +1093,6 @@
         hidden, qkv = qkv_forward(first_in, mods, qkv_full, qkv_bias_of(0))
         hidden, qkv, got = joint(hidden, qkv, near(pair_d0))
         line_d0 = put(pair_d0, got)
-        whole_d0 = along_seq(line_d0)
         block_q1 = gate(second_pack[0][None, None], (got,))
         qkv, attended, lse, peak0 = attention_part(0, first_in, qkv, out_full)
         attended, lse, got = joint(attended, lse, far(block_q1))
@@ -1103,13 +1102,14 @@
         )
         branch, middle, hidden_two, got = joint(branch, middle, hidden_two, near(pair_q1))
         line_q1 = put(pair_q1, got)
-        whole_q1 = along_seq(line_q1)
+        whole_dq = along_seq(jnp.concatenate([line_d0, line_q1], axis=0))
         block_f1 = gate(jnp.stack(second_pack[1:])[:, None], (got,))
         up_full = join_up(place, *both_cores(whole_u0, (branch,)), 0, deps=(line_q1, line_d0))
         active, slope = up_forward(hidden_two, up_full, up_bias[:1])
         active, slope, got = joint(active, slope, far(block_f1))
         pair_f1 = put(block_f1, got)
-        down_full = join_down(place, *both_cores(whole_d0, (active,)), 0, deps=(pair_f1,))
+        own_dq, got_dq = both_cores(whole_dq, (active,))
+        down_full = join_down(place, own_dq, got_dq, 0, deps=(pair_f1,))
         update, result = down_forward(active, middle, mods, down_full, down_bias[:1])
         update, result, got = joint(update, result, near(pair_f1))
         line_f1 = put(pair_f1, got)
@@ -1121,8 +1121,7 @@
         second_in = swap_tokens(result)
 
         mods = modulation[1]
-        own, got = both_cores(whole_q1, (second_in, line_f1))
-        qkv_full, out_full = join_qkv_out(place, own, got, 0)
+        qkv_full, out_full = join_qkv_out(place, own_dq, got_dq, 1, deps=(result, line_f1))
         hidden, qkv = qkv_forward(second_in, mods, qkv_full, qkv_bias_of(1))
         qkv, attended, lse, peak1 = attention_part(1, second_in, qkv, out_full)
         branch, middle, hidden_two = out_forward(
@@ -1227,8 +1226,7 @@
         def finish(small, own_mod_grad, exchanged):
             sum_u0 = add_first(part_u0, exchanged)
             up_g0 = add_second(sum_u0, second_half(sum_u0))
-            part = gate(part_q0, (up_g0,))
-            sum_q0 = add_first(part, first_half(part))
+            sum_q0 = add_first(part_q0, first_half(part_q0))
             both_g0 = add_second(sum_q0, second_half(sum_q0))
             early = [gate(item, (own_mod_grad,)) for item in (down_g1, up_g1, both_g1, down_g0)]
             small = total(small, (CLIP, clips), ("seq", seq))

time: 1040 us -> 1080 us (1.038)
  waiting for transfers between devices: 230 us -> 277 us
  blocking collectives: 26.2 us -> 8.84 us
    all_to_all x4, waiting for transfers between devices: 13.6 us -> 44.4 us  [swap_tokens(): return lax.all_to_all(block, 'seq', 0, 0, tiled=True).reshape(n, d)]
    all_to_all x1 -> x0, blocking collectives: 17.4 us -> none  [modulate(): own_mods = lax.all_to_all(local_mods, CLIP, 0, 0, tiled=True)]
    all_gather x6 -> x5, waiting for transfers between devices: 55 us -> 66.7 us  [along_seq(): return lax.all_gather(blocks, 'seq', axis=0, tiled=False)]
    ppermute x34 -> x33, waiting for transfers between devices: 126 us -> 121 us  [hop(): return lax.ppermute(x, CLIP, [(i, i ^ distance) for i in range(count)])]
    unnamed x148 -> x156, local copies, waits for them, and re-layouts: 34.8 us -> 37.8 us
    ppermute x34 -> x33, starting transfers between devices: 24.9 us -> 26.1 us  [hop(): return lax.ppermute(x, CLIP, [(i, i ^ distance) for i in range(count)])]
  transfers between devices with their start and end apart: 61 -> 60, of which waited for: 30 -> 30; matrix products, arithmetic and copies ran while one was open for 7% -> 7% of each run, Pallas kernels for 56% -> 54%
where the time goes in v5:
time: 1080 us; the launch traced here: 1070 us
  Pallas kernels  582 us (54%)
  waiting for transfers between devices  277 us (26%)
  local copies, waits for them, and re-layouts  78.8 us (7%)
  starting transfers between devices  66 us (6%)
  other arithmetic  42.6 us (4%)
  between operations  15.1 us (1%)
    pallas_call x39, Pallas kernels, call(): return lambda *args: kernel(*args, *deps)  582 us
    ppermute x33, waiting for transfers between devices, hop(): return lax.ppermute(x, CLIP, [(i, i ^ distance) for i in range(count)])  121 us
    all_gather x5, waiting for transfers between devices, along_seq(): return lax.all_gather(blocks, 'seq', axis=0, tiled=False)  66.7 us
    all_to_all x4, waiting for transfers between devices, swap_tokens(): return lax.all_to_all(block, 'seq', 0, 0, tiled=True).reshape(n, d)  44.4 us
    unnamed x156, local copies, waits for them, and re-layouts  37.8 us
    ppermute x10, waiting for transfers between devices, total(): v = v + lax.ppermute(v, axis, [(i, i ^ step) for i in range(count)])  30.3 us
    ppermute x33, starting transfers between devices, hop(): return lax.ppermute(x, CLIP, [(i, i ^ distance) for i in range(count)])  26.1 us
  transfers between devices with their start and end apart: 60, of which 30 were waited for; matrix products, arithmetic and copies ran while one was open for 7% of the time, Pallas kernels for 54%

profile of v5, /device:TPU:0, one launch (start us, length us, event | category | flops | bytes accessed | tf_op | source)
XLA Modules:
  0.0 1072.3 jit_solution(71150658379677885)
XLA Ops:
  21.3 14.9 %collective-permute-done.3 = bf16[1,1,144,1152]{3,2,1,0:T(8,128)(2,1)S(1)} collective-permute-done((bf16[1,1,144,1152]{3,2,1,0:T(8,128)(2,1)S(1)}, bf16[1,1,144,1152]{3,2,1,0:T(8,128)(2,1)S(1)}, u32[]{:S(2)}, u32[]{:S(2)}) %collective-permute-start.3) | collective-permute-done | bytes 331808 | tf_op jit(solution)/shard_map/ppermute | solution.py:866
  37.0 15.2 %collective-permute-done.4.refs_0_ = bf16[1,2,144,1152]{3,2,1,0:T(8,128)(2,1)} collective-permute-done((bf16[1,2,144,1152]{3,2,1,0:T(8,128)(2,1)S(1)}, bf16[1,2,144,1152]{3,2,1,0:T(8,128)(2,1)}, u32[]{:S(2)}, u32[]{:S(2)}) %collective-permute-start.4) | collective-permute-done | bytes 663584 | tf_op jit(solution)/shard_map/ppermute | solution.py:866
  89.1 9.2 all-to-all-done.1
  98.3 8.8 all-gather
  111.7 15.9 %collective-permute-done.7 = bf16[1,1,144,1152]{3,2,1,0:T(8,128)(2,1)S(1)} collective-permute-done((bf16[1,1,144,1152]{3,2,1,0:T(8,128)(2,1)}, bf16[1,1,144,1152]{3,2,1,0:T(8,128)(2,1)S(1)}, u32[]{:S(2)}, u32[]{:S(2)}) %collective-permute-start.7) | collective-permute-done | bytes 331808 | tf_op jit(solution)/shard_map/ppermute | solution.py:866
  139.3 9.8 shard_map.232
  149.1 17.0 %shard_map.233 = (bf16[1024,1152]{1,0:T(8,128)(2,1)}, bf16[1024,3456]{1,0:T(8,128)(2,1)}) custom-call(bf16[1024,1152]{1,0:T(8,128)(2,1)} %bitcast.225, f32[8,1152]{1,0:T(8,128)} %get-tuple-element.336.refs_1_.refs_2_.refs_5_.refs_4_, bf16[1152,3456]{1,0:T(8,128)(2,1)} %get-tuple-element.134.refs_2_.refs_1_, f32[1,3456]{1,0:T(1,128)} %broadcast_in_dim.45.refs_3_), custom_call_target="tpu_custom_call" | custom-call | flops 8153726976 | bytes 19759104 | tf_op jit(solution)/shard_map/pallas_call | solution.py:49
  167.2 13.0 %shard_map.235 = (bf16[4,4,64,1152]{3,2,1,0:T(8,128)(2,1)}, f32[4,16,256]{2,1,0:T(8,128)}, f32[4,1,16]{2,1,0:T(1,128)}) custom-call(bf16[4,4,64,3456]{3,2,1,0:T(8,128)(2,1)} %bitcast.208), custom_call_target="tpu_custom_call" | custom-call | flops 4294967296 | bytes 9437184 | tf_op jit(solution)/shard_map/pallas_call | solution.py:49
  186.3 9.1 shard_map.238
  195.4 7.7 collective-permute-done.11.refs_3_
  218.7 9.0 shard_map.241.refs_1_.refs_3_
  227.7 23.1 %shard_map.242 = (bf16[1024,4608]{1,0:T(8,128)(2,1)}, bf16[1024,4608]{1,0:T(8,128)(2,1)}) custom-call(bf16[1024,1152]{1,0:T(8,128)(2,1)} %get-tuple-element.147.refs_0_.refs_1_, bf16[1152,4608]{1,0:T(8,128)(2,1)} %shard_map.241.refs_1_.refs_3_, f32[1,4608]{1,0:T(1,128)} %get-tuple-element.339.refs_2_), custom_call_target="tpu_custom_call" | custom-call | flops 10871635968 | bytes 31850496 | tf_op jit(solution)/shard_map/pallas_call | solution.py:49
  251.6 61.2 %all-gather.16.cloned.1.call-done = bf16[8,4,144,1152]{3,2,1,0:T(8,128)(2,1)} async-done(((bf16[2,4,144,1152]{3,2,1,0:T(8,128)(2,1)}), bf16[8,4,144,1152]{3,2,1,0:T(8,128)(2,1)}) %all-gather.16.cloned.1.call-update) | async-done | bytes 10616848 | tf_op jit(solution)/shard_map/all_gather | solution.py:941
  316.5 13.1 %collective-permute-done.14.refs_2_ = bf16[4,2,4,144,1152]{4,3,2,1,0:T(8,128)(2,1)} collective-permute-done((bf16[4,2,4,144,1152]{4,3,2,1,0:T(8,128)(2,1)}, bf16[4,2,4,144,1152]{4,3,2,1,0:T(8,128)(2,1)}, u32[]{:S(2)}, u32[]{:S(2)}) %collective-permute-start.14) | collective-permute-done | bytes 10616864 | tf_op jit(solution)/shard_map/ppermute | solution.py:866
  329.6 10.0 shard_map.246.refs_3_.refs_2_
  339.6 19.1 %shard_map.247 = (bf16[1024,1152]{1,0:T(8,128)(2,1)}, bf16[1024,1152]{1,0:T(8,128)(2,1)}) custom-call(bf16[1024,4608]{1,0:T(8,128)(2,1)} %get-tuple-element.152.refs_1_.refs_0_, f32[1024,1152]{1,0:T(8,128)} %get-tuple-element.153.refs_1_, f32[8,1152]{1,0:T(8,128)} %get-tuple-element.336.refs_1_.refs_2_.refs_5_.refs_4_, ...), custom_call_target="tpu_custom_call" | custom-call | flops 10871635968 | bytes 29491200 | tf_op jit(solution)/shard_map/pallas_call | solution.py:49
  368.6 10.4 shard_map.249
  379.1 30.8 %all-to-all-done.2 = bf16[4,256,1152]{2,1,0:T(8,128)(2,1)S(1)} async-done(((bf16[4,256,1152]{2,1,0:T(8,128)(2,1)}), bf16[4,256,1152]{2,1,0:T(8,128)(2,1)S(1)}, u32[]{:S(2)}, u32[]{:S(2)}) %all-to-all-start.2) | async-done | bytes 2359328 | tf_op jit(solution)/shard_map/all_to_all | solution.py:978
  411.3 16.6 %shard_map.250 = (bf16[1024,1152]{1,0:T(8,128)(2,1)}, bf16[1024,3456]{1,0:T(8,128)(2,1)}) custom-call(bf16[1024,1152]{1,0:T(8,128)(2,1)} %bitcast.229, f32[8,1152]{1,0:T(8,128)} %get-tuple-element.337.refs_1_.refs_2_.refs_5_.refs_4_, bf16[1152,3456]{1,0:T(8,128)(2,1)} %get-tuple-element.159.refs_2_.refs_1_, f32[1,3456]{1,0:T(1,128)} %broadcast_in_dim.48.refs_3_), custom_call_target="tpu_custom_call" | custom-call | flops 8153726976 | bytes 19759104 | tf_op jit(solution)/shard_map/pallas_call | solution.py:49
  427.9 12.8 %shard_map.251 = (bf16[16,4,16,1152]{3,2,1,0:T(8,128)(2,1)}, f32[4,16,256]{2,1,0:T(8,128)}, f32[4,1,16]{2,1,0:T(1,128)}) custom-call(bf16[16,4,16,3456]{3,2,1,0:T(8,128)(2,1)} %bitcast.250), custom_call_target="tpu_custom_call" | custom-call | flops 4294967296 | bytes 9437184 | tf_op jit(solution)/shard_map/pallas_call | solution.py:49
  446.2 9.1 shard_map.252
  455.3 9.2 shard_map.255.refs_1_.refs_3_
  464.5 23.1 %shard_map.256 = (bf16[1024,4608]{1,0:T(8,128)(2,1)}, bf16[1024,4608]{1,0:T(8,128)(2,1)}) custom-call(bf16[1024,1152]{1,0:T(8,128)(2,1)} %get-tuple-element.166.refs_0_.refs_1_, bf16[1152,4608]{1,0:T(8,128)(2,1)} %shard_map.255.refs_1_.refs_3_, f32[1,4608]{1,0:T(1,128)} %get-tuple-element.338.refs_2_), custom_call_target="tpu_custom_call" | custom-call | flops 10871635968 | bytes 31850496 | tf_op jit(solution)/shard_map/pallas_call | solution.py:49
  492.0 18.2 %shard_map.258 = (bf16[4,4,144,1152]{3,2,1,0:T(8,128)(2,1)}, bf16[4,4,144,1152]{3,2,1,0:T(8,128)(2,1)}) custom-call(s32[3]{0:T(128)} %pad_add_fusion.refs_0_, bf16[1024,4608]{1,0:T(8,128)(2,1)} %get-tuple-element.168.refs_2_.refs_1_.refs_0_, bf16[1024,1152]{1,0:T(8,128)(2,1)} %get-tuple-element.169.refs_2_.refs_0_), custom_call_target="tpu_custom_call" | custom-call | flops 10871635968 | bytes 22413312 | tf_op jit(solution)/shard_map/pallas_call | solution.py:49
  510.7 8.6 collective-permute-done.17.refs_1_
  519.4 7.0 shard_map.260.refs_0_
  527.0 10.8 %shard_map.262.refs_3_.refs_2_ = bf16[4608,1152]{1,0:T(8,128)(2,1)} custom-call(s32[3]{0:T(128)} %pad_add_fusion.refs_0_, bf16[4,1,4,144,1152]{4,3,2,1,0:T(8,128)(2,1)} %shard_map.259.refs_2_.refs_1_, bf16[4,1,4,144,1152]{4,3,2,1,0:T(8,128)(2,1)} %get-tuple-element.173.refs_2_), custom_call_target="tpu_custom_call" | custom-call | bytes 21233664 | tf_op jit(solution)/shard_map/pallas_call | solution.py:49
  537.8 19.5 %shard_map.263 = (bf16[1024,1152]{1,0:T(8,128)(2,1)}, bf16[1024,1152]{1,0:T(8,128)(2,1)}) custom-call(bf16[1024,4608]{1,0:T(8,128)(2,1)} %get-tuple-element.168.refs_2_.refs_1_.refs_0_, f32[1024,1152]{1,0:T(8,128)} %get-tuple-element.174.refs_1_, f32[8,1152]{1,0:T(8,128)} %get-tuple-element.337.refs_1_.refs_2_.refs_5_.refs_4_, ...), custom_call_target="tpu_custom_call" | custom-call | flops 10871635968 | bytes 29491200 | tf_op jit(solution)/shard_map/pallas_call | solution.py:49
  561.0 37.2 %shard_map.264 = (bf16[1024,4608]{1,0:T(8,128)(2,1)}, f32[1,4608]{1,0:T(1,128)}, f32[1024,1152]{1,0:T(8,128)}) custom-call(bf16[1024,1152]{1,0:T(8,128)(2,1)} %get-tuple-element.169.refs_2_.refs_0_, bf16[1024,4608]{1,0:T(8,128)(2,1)} %get-tuple-element.170.refs_1_, bf16[4608,1152]{1,0:T(8,128)(2,1)} %shard_map.262.refs_3_.refs_2_, ...), custom_call_target="tpu_custom_call" | custom-call | flops 21743271936 | bytes 47185920 | tf_op jit(solution)/shard_map/pallas_call | solution.py:49
  605.3 17.7 %shard_map.266 = (bf16[4,4,144,1152]{3,2,1,0:T(8,128)(2,1)}, bf16[4,4,144,1152]{3,2,1,0:T(8,128)(2,1)}) custom-call(s32[3]{0:T(128)} %pad_add_fusion.refs_0_, bf16[1024,1152]{1,0:T(8,128)(2,1)} %get-tuple-element.166.refs_0_.refs_1_, bf16[1024,4608]{1,0:T(8,128)(2,1)} %get-tuple-element.184.refs_2_), custom_call_target="tpu_custom_call" | custom-call | flops 10871635968 | bytes 22413312 | tf_op jit(solution)/shard_map/pallas_call | solution.py:49
  623.0 14.9 %shard_map.267 = (f32[1024,1152]{1,0:T(8,128)}, bf16[1024,1152]{1,0:T(8,128)(2,1)}, bf16[4,1024,288]{2,1,0:T(8,128)(2,1)}, bf16[1024,1152]{1,0:T(8,128)(2,1)}, f32[8,1152]{1,0:T(8,128)}) custom-call(f32[1024,1152]{1,0:T(8,128)} %get-tuple-element.181.refs_0_, f32[1024,1152]{1,0:T(8,128)} %get-tuple-element.174.refs_1_, ...), custom_call_target="tpu_custom_call" | custom-call | flops 2717908992 | bytes 28606464 | tf_op jit(solution)/shard_map/pallas_call | solution.py:49
  650.2 26.0 %shard_map.269 = (bf16[16,4,16,3456]{3,2,1,0:T(8,128)(2,1)}, bf16[4,16,4,16,864]{4,3,2,1,0:T(8,128)(2,1)}, f32[1,3456]{1,0:T(1,128)}) custom-call(bf16[16,4,16,3456]{3,2,1,0:T(8,128)(2,1)} %bitcast.251, bf16[16,4,16,1152]{3,2,1,0:T(8,128)(2,1)} %bitcast.249, f32[4,16,256]{2,1,0:T(8,128)} %get-tuple-element.187.refs_2_, ...), custom_call_target="tpu_custom_call" | custom-call | flops 12884901888 | bytes 23592960 | tf_op jit(solution)/shard_map/pallas_call | solution.py:49
  681.6 17.3 %shard_map.271 = (bf16[1024,1152]{1,0:T(8,128)(2,1)}, f32[8,1152]{1,0:T(8,128)}) custom-call(bf16[1024,3456]{1,0:T(8,128)(2,1)} %get-tuple-element.194.refs_0_, bf16[1152,3456]{1,0:T(8,128)(2,1)} %get-tuple-element.159.refs_2_.refs_1_, bf16[1024,1152]{1,0:T(8,128)(2,1)} %bitcast.231, f32[1024,1152]{1,0:T(8,128)} %get-tuple-element.189.refs_2_.refs_3_, ...), custom_call_target="tpu_custom_call" | custom-call | flops 8153726976 | bytes 26836992 | tf_op jit(solution)/shard_map/pallas_call | solution.py:49
  703.4 21.8 %shard_map.273 = (bf16[4,4,144,1152]{3,2,1,0:T(8,128)(2,1)}, bf16[4,4,144,1152]{3,2,1,0:T(8,128)(2,1)}) custom-call(s32[3]{0:T(128)} %pad_add_fusion.refs_0_, bf16[1024,1152]{1,0:T(8,128)(2,1)} %get-tuple-element.180.refs_1_, bf16[1024,1152]{1,0:T(8,128)(2,1)} %bitcast.222, bf16[4,1024,864]{2,1,0:T(8,128)(2,1)} %get-tuple-element.192.refs_3_, ...), custom_call_target="tpu_custom_call" | custom-call | flops 10871635968 | bytes 20054016 | tf_op jit(solution)/shard_map/pallas_call | solution.py:49
  725.1 8.0 all-to-all-done.4
  745.7 7.0 shard_map.276.refs_3_
  752.8 18.5 %shard_map.277 = (bf16[4,4,144,1152]{3,2,1,0:T(8,128)(2,1)}, bf16[4,4,144,1152]{3,2,1,0:T(8,128)(2,1)}) custom-call(s32[3]{0:T(128)} %pad_add_fusion.refs_0_, bf16[1024,4608]{1,0:T(8,128)(2,1)} %get-tuple-element.152.refs_1_.refs_0_, bf16[1024,1152]{1,0:T(8,128)(2,1)} %get-tuple-element.202.refs_2_.refs_0_, bf16[4,4,144,1152]{3,2,1,0:T(8,128)(2,1)} %shard_map.276.refs_3_), custom_call_target="tpu_custom_call" | custom-call | flops 10871635968 | bytes 22413312 | tf_op jit(solution)/shard_map/pallas_call | solution.py:49
  774.4 37.5 %shard_map.278 = (bf16[1024,4608]{1,0:T(8,128)(2,1)}, f32[1,4608]{1,0:T(1,128)}, f32[1024,1152]{1,0:T(8,128)}) custom-call(bf16[1024,1152]{1,0:T(8,128)(2,1)} %get-tuple-element.202.refs_2_.refs_0_, bf16[1024,4608]{1,0:T(8,128)(2,1)} %get-tuple-element.203.refs_1_, bf16[4608,1152]{1,0:T(8,128)(2,1)} %shard_map.246.refs_3_.refs_2_, ...), custom_call_target="tpu_custom_call" | custom-call | flops 21743271936 | bytes 47185920 | tf_op jit(solution)/shard_map/pallas_call | solution.py:49
  814.9 7.0 shard_map.280.refs_3_
  824.0 18.2 %shard_map.281 = (bf16[4,4,144,1152]{3,2,1,0:T(8,128)(2,1)}, bf16[4,4,144,1152]{3,2,1,0:T(8,128)(2,1)}) custom-call(s32[3]{0:T(128)} %pad_add_fusion.refs_0_, bf16[1024,1152]{1,0:T(8,128)(2,1)} %get-tuple-element.147.refs_0_.refs_1_, bf16[1024,4608]{1,0:T(8,128)(2,1)} %get-tuple-element.211.refs_2_, bf16[4,4,144,1152]{3,2,1,0:T(8,128)(2,1)} %shard_map.280.refs_3_, ...), custom_call_target="tpu_custom_call" | custom-call | flops 10871635968 | bytes 22413312 | tf_op jit(solution)/shard_map/pallas_call | solution.py:49
  842.3 14.9 %shard_map.282 = (f32[1024,1152]{1,0:T(8,128)}, bf16[1024,1152]{1,0:T(8,128)(2,1)}, bf16[4,1024,288]{2,1,0:T(8,128)(2,1)}, bf16[1024,1152]{1,0:T(8,128)(2,1)}, f32[8,1152]{1,0:T(8,128)}) custom-call(f32[1024,1152]{1,0:T(8,128)} %get-tuple-element.209.refs_2_.refs_0_, f32[1024,1152]{1,0:T(8,128)} %get-tuple-element.153.refs_1_, ...), custom_call_target="tpu_custom_call" | custom-call | flops 2717908992 | bytes 28606464 | tf_op jit(solution)/shard_map/pallas_call | solution.py:49
  859.5 7.1 shard_map.283.refs_3_
  872.0 26.0 %shard_map.284 = (bf16[4,4,64,3456]{3,2,1,0:T(8,128)(2,1)}, bf16[4,4,4,64,864]{4,3,2,1,0:T(8,128)(2,1)}, f32[1,3456]{1,0:T(1,128)}) custom-call(bf16[4,4,64,3456]{3,2,1,0:T(8,128)(2,1)} %bitcast.209, bf16[4,4,64,1152]{3,2,1,0:T(8,128)(2,1)} %bitcast.248, f32[4,16,256]{2,1,0:T(8,128)} %get-tuple-element.216.refs_2_, bf16[4,4,144,1152]{3,2,1,0:T(8,128)(2,1)} %shard_map.283.refs_3_), custom_call_target="tpu_custom_call" | custom-call | flops 12884901888 | bytes 23592960 | tf_op jit(solution)/shard_map/pallas_call | solution.py:49
  903.7 21.7 %shard_map.286 = (bf16[4,4,144,1152]{3,2,1,0:T(8,128)(2,1)}, bf16[4,4,144,1152]{3,2,1,0:T(8,128)(2,1)}) custom-call(s32[3]{0:T(128)} %pad_add_fusion.refs_0_, bf16[1024,1152]{1,0:T(8,128)(2,1)} %get-tuple-element.222.refs_1_, bf16[1024,1152]{1,0:T(8,128)(2,1)} %get-tuple-element.141.refs_0_.refs_2_, bf16[4,1024,864]{2,1,0:T(8,128)(2,1)} %get-tuple-element.223.refs_3_, ...), custom_call_target="tpu_custom_call" | custom-call | flops 10871635968 | bytes 20054016 | tf_op jit(solution)/shard_map/pallas_call | solution.py:49
  930.2 18.0 %shard_map.288 = (f32[4,4,64,1152]{3,2,1,0:T(8,128)}, f32[8,1152]{1,0:T(8,128)}) custom-call(bf16[1024,3456]{1,0:T(8,128)(2,1)} %get-tuple-element.221.refs_0_, bf16[1152,3456]{1,0:T(8,128)(2,1)} %get-tuple-element.134.refs_2_.refs_1_, bf16[1024,1152]{1,0:T(8,128)(2,1)} %bitcast.227, f32[1024,1152]{1,0:T(8,128)} %get-tuple-element.218.refs_2_.refs_3_, ...), custom_call_target="tpu_custom_call" | custom-call | flops 8153726976 | bytes 26836992 | tf_op jit(solution)/shard_map/pallas_call | solution.py:49
  1012.1 7.3 collective-permute-done.37
  1033.9 14.6 %collective-permute-done.40 = bf16[2,144,1152]{2,1,0:T(8,128)(2,1)S(1)} collective-permute-done((bf16[2,144,1152]{2,1,0:T(8,128)(2,1)S(1)}, bf16[2,144,1152]{2,1,0:T(8,128)(2,1)S(1)}, u32[]{:S(2)}, u32[]{:S(2)}) %collective-permute-start.40) | collective-permute-done | bytes 663584 | tf_op jit(solution)/shard_map/ppermute | solution.py:866
  1051.7 11.8 %collective-permute-done.41 = bf16[144,1152]{1,0:T(8,128)(2,1)S(1)} collective-permute-done((bf16[144,1152]{1,0:T(8,128)(2,1)S(1)}, bf16[144,1152]{1,0:T(8,128)(2,1)S(1)}, u32[]{:S(2)}, u32[]{:S(2)}) %collective-permute-start.41) | collective-permute-done | bytes 331808 | tf_op jit(solution)/shard_map/ppermute | solution.py:866
  (427 shorter events, 272.6 us)
Async XLA Ops:
  10.6 41.7 %all-to-all-start = ((bf16[4,256,1152]{2,1,0:T(8,128)(2,1)}), bf16[4,256,1152]{2,1,0:T(8,128)(2,1)S(1)}, u32[]{:S(2)}, u32[]{:S(2)}) async-start(bf16[4,256,1152]{2,1,0:T(8,128)(2,1)} %bitcast.202), calls=%async_computation | async-start | bytes 4718592 | tf_op jit(solution)/shard_map/all_to_all | solution.py:978
  15.7 114.5 %all-gather.12.cloned.1.call-start = ((), (), s32[]{:S(2)}) async-start(), calls=%async_computation.18 | async-start | bytes 6635520 | tf_op jit(solution)/shard_map/all_gather | solution.py:941
  18.6 17.5 %collective-permute-start.3 = (bf16[1,1,144,1152]{3,2,1,0:T(8,128)(2,1)S(1)}, bf16[1,1,144,1152]{3,2,1,0:T(8,128)(2,1)S(1)}, u32[]{:S(2)}, u32[]{:S(2)}) collective-permute-start(bf16[1,1,144,1152]{3,2,1,0:T(8,128)(2,1)S(1)} %maximum_bitcast_fusion.1), channel_id=1, source_target_pairs={{0,16},{4,20},{8,24},{12,28},{16,0},{20,4},{24,8},{28,12},{1,17},{... | collective-permute-start | bytes 995336 | tf_op jit(solution)/shard_map/ppermute | solution.py:866
  36.3 16.0 %collective-permute-start.4 = (bf16[1,2,144,1152]{3,2,1,0:T(8,128)(2,1)S(1)}, bf16[1,2,144,1152]{3,2,1,0:T(8,128)(2,1)}, u32[]{:S(2)}, u32[]{:S(2)}) collective-permute-start(bf16[1,2,144,1152]{3,2,1,0:T(8,128)(2,1)S(1)} %pad_maximum_fusion.9), channel_id=1, source_target_pairs={{0,8},{4,12},{8,0},{12,4},{16,24},{20,28},{24,16},{28,20},{1,9},{5... | collective-permute-start | bytes 1990664 | tf_op jit(solution)/shard_map/ppermute | solution.py:866
  57.4 20.1 %collective-permute-start.5 = (bf16[1,1,144,1152]{3,2,1,0:T(8,128)(2,1)}, bf16[1,1,144,1152]{3,2,1,0:T(8,128)(2,1)S(1)}, u32[]{:S(2)}, u32[]{:S(2)}) collective-permute-start(bf16[1,1,144,1152]{3,2,1,0:T(8,128)(2,1)} %shard_map.228), channel_id=1, source_target_pairs={{0,16},{4,20},{8,24},{12,28},{16,0},{20,4},{24,8},{28,12},{1,17},{... | collective-permute-start | bytes 995336 | tf_op jit(solution)/shard_map/ppermute | solution.py:866
  69.5 10.6 collective-permute-start.2
  79.4 28.6 %collective-permute-start.6 = (bf16[1,2,144,1152]{3,2,1,0:T(8,128)(2,1)}, bf16[1,2,144,1152]{3,2,1,0:T(8,128)(2,1)S(1)}, u32[]{:S(2)}, u32[]{:S(2)}) collective-permute-start(bf16[1,2,144,1152]{3,2,1,0:T(8,128)(2,1)} %pad_maximum_fusion.10), channel_id=1, source_target_pairs={{0,8},{4,12},{8,0},{12,4},{16,24},{20,28},{24,16},{28,20},{1,9},{5... | collective-permute-start | bytes 1990664 | tf_op jit(solution)/shard_map/ppermute | solution.py:866
  81.2 17.2 %all-to-all-start.1 = ((f32[8,2,216]{2,1,0:T(2,128)}), f32[8,2,216]{2,1,0:T(2,128)S(1)}, u32[]{:S(2)}, u32[]{:S(2)}) async-start(f32[8,2,216]{2,1,0:T(2,128)} %copy.157), calls=%async_computation.1 | async-start | bytes 32768 | tf_op jit(solution)/shard_map/all_to_all | solution.py:918
  85.7 122.6 %all-gather.14.cloned.1.call-start = ((), (), s32[]{:S(2)}) async-start(), calls=%async_computation.19 | async-start | bytes 6635520 | tf_op jit(solution)/shard_map/all_gather | solution.py:941
  111.1 16.4 %collective-permute-start.7 = (bf16[1,1,144,1152]{3,2,1,0:T(8,128)(2,1)}, bf16[1,1,144,1152]{3,2,1,0:T(8,128)(2,1)S(1)}, u32[]{:S(2)}, u32[]{:S(2)}) collective-permute-start(bf16[1,1,144,1152]{3,2,1,0:T(8,128)(2,1)} %shard_map.230), channel_id=1, source_target_pairs={{0,16},{4,20},{8,24},{12,28},{16,0},{20,4},{24,8},{28,12},{1,17},{... | collective-permute-start | bytes 995336 | tf_op jit(solution)/shard_map/ppermute | solution.py:866
  130.2 182.6 %all-gather.16.cloned.1.call-start = ((), (), s32[]{:S(2)}) async-start(), calls=%async_computation.20 | async-start | bytes 13271040 | tf_op jit(solution)/shard_map/all_gather | solution.py:941
  137.2 28.9 %collective-permute-start.9 = (bf16[1,2,144,1152]{3,2,1,0:T(8,128)(2,1)S(1)}, bf16[1,2,144,1152]{3,2,1,0:T(8,128)(2,1)S(1)}, u32[]{:S(2)}, u32[]{:S(2)}) collective-permute-start(bf16[1,2,144,1152]{3,2,1,0:T(8,128)(2,1)S(1)} %copy-done.30), channel_id=1, source_target_pairs={{0,8},{4,12},{8,0},{12,4},{16,24},{20,28},{24,16},{28,20},{1,9},{5... | collective-permute-start | bytes 1990664 | tf_op jit(solution)/shard_map/ppermute | solution.py:866
  167.0 17.4 %collective-permute-start.10 = (bf16[1,1,144,1152]{3,2,1,0:T(8,128)(2,1)}, bf16[1,1,144,1152]{3,2,1,0:T(8,128)(2,1)S(1)}, u32[]{:S(2)}, u32[]{:S(2)}) collective-permute-start(bf16[1,1,144,1152]{3,2,1,0:T(8,128)(2,1)} %shard_map.236), channel_id=1, source_target_pairs={{0,16},{4,20},{8,24},{12,28},{16,0},{20,4},{24,8},{28,12},{1,17},{... | collective-permute-start | bytes 995336 | tf_op jit(solution)/shard_map/ppermute | solution.py:866
  186.2 16.9 %collective-permute-start.11 = (bf16[1,2,144,1152]{3,2,1,0:T(8,128)(2,1)S(1)}, bf16[1,2,144,1152]{3,2,1,0:T(8,128)(2,1)S(1)}, u32[]{:S(2)}, u32[]{:S(2)}) collective-permute-start(bf16[1,2,144,1152]{3,2,1,0:T(8,128)(2,1)S(1)} %pad_maximum_fusion.12), channel_id=1, source_target_pairs={{0,8},{4,12},{8,0},{12,4},{16,24},{20,28},{24,16},{28,20},{1,9},{5... | collective-permute-start | bytes 1990664 | tf_op jit(solution)/shard_map/ppermute | solution.py:866
  208.0 238.2 %all-gather.18.cloned.1.call-start = ((), (), s32[]{:S(2)}) async-start(), calls=%async_computation.21 | async-start | bytes 6635520 | tf_op jit(solution)/shard_map/all_gather | solution.py:941
  208.4 10.4 collective-permute-start.12
  215.8 35.0 %collective-permute-start.13 = (bf16[2,1,144,1152]{3,2,1,0:T(8,128)(2,1)}, bf16[2,1,144,1152]{3,2,1,0:T(8,128)(2,1)S(1)}, u32[]{:S(2)}, u32[]{:S(2)}) collective-permute-start(bf16[2,1,144,1152]{3,2,1,0:T(8,128)(2,1)} %shard_map.243), channel_id=1, source_target_pairs={{0,16},{4,20},{8,24},{12,28},{16,0},{20,4},{24,8},{28,12},{1,17},{... | collective-permute-start | bytes 1990664 | tf_op jit(solution)/shard_map/ppermute | solution.py:866
  312.9 16.7 %collective-permute-start.14 = (bf16[4,2,4,144,1152]{4,3,2,1,0:T(8,128)(2,1)}, bf16[4,2,4,144,1152]{4,3,2,1,0:T(8,128)(2,1)}, u32[]{:S(2)}, u32[]{:S(2)}) collective-permute-start(bf16[4,2,4,144,1152]{4,3,2,1,0:T(8,128)(2,1)} %shard_map.245.refs_1_), channel_id=1, source_target_pairs={{0,4},{4,0},{8,12},{12,8},{16,20},{20,16},{24,28},{28,24},{1,5},{5... | collective-permute-start | bytes 31850504 | tf_op jit(solution)/shard_map/ppermute | solution.py:866
  314.3 44.4 %collective-permute-start.15 = (bf16[2,2,144,1152]{3,2,1,0:T(8,128)(2,1)S(1)}, bf16[2,2,144,1152]{3,2,1,0:T(8,128)(2,1)S(1)}, u32[]{:S(2)}, u32[]{:S(2)}) collective-permute-start(bf16[2,2,144,1152]{3,2,1,0:T(8,128)(2,1)S(1)} %pad_maximum_fusion.6.refs_3_), channel_id=1, source_target_pairs={{0,8},{4,12},{8,0},{12,4},{16,24},{20,28},{24,16},{28,20},{1,9},{5... | collective-permute-start | bytes 3981320 | tf_op jit(solution)/shard_map/ppermute | solution.py:866
  363.8 46.1 %all-to-all-start.2 = ((bf16[4,256,1152]{2,1,0:T(8,128)(2,1)}), bf16[4,256,1152]{2,1,0:T(8,128)(2,1)S(1)}, u32[]{:S(2)}, u32[]{:S(2)}) async-start(bf16[4,256,1152]{2,1,0:T(8,128)(2,1)} %bitcast.32), calls=%async_computation.2 | async-start | bytes 4718592 | tf_op jit(solution)/shard_map/all_to_all | solution.py:978
  367.4 143.2 %all-gather.20.cloned.1.call-start = ((), (), s32[]{:S(2)}) async-start(), calls=%async_computation.22 | async-start | bytes 6635520 | tf_op jit(solution)/shard_map/all_gather | solution.py:941
  368.1 279.1 %reduce-scatter.7.cloned.1.call-start = ((), (), s32[]{:S(2)}) async-start(), calls=%async_computation.12 | async-start | bytes 6635520 | tf_op jit(solution)/shard_map/reduce_scatter | solution.py:956
  510.7 16.3 %collective-permute-start.18 = (bf16[4,1,4,144,1152]{4,3,2,1,0:T(8,128)(2,1)}, bf16[4,1,4,144,1152]{4,3,2,1,0:T(8,128)(2,1)}, u32[]{:S(2)}, u32[]{:S(2)}) collective-permute-start(bf16[4,1,4,144,1152]{4,3,2,1,0:T(8,128)(2,1)} %shard_map.259.refs_2_.refs_1_), channel_id=1, source_target_pairs={{0,4},{4,0},{8,12},{12,8},{16,20},{20,16},{24,28},{28,24},{1,5},{5... | collective-permute-start | bytes 15925256 | tf_op jit(solution)/shard_map/ppermute | solution.py:866
  557.3 46.6 %all-to-all-start.3 = ((bf16[4,256,1152]{2,1,0:T(8,128)(2,1)}), bf16[4,256,1152]{2,1,0:T(8,128)(2,1)S(1)}, u32[]{:S(2)}, u32[]{:S(2)}) async-start(bf16[4,256,1152]{2,1,0:T(8,128)(2,1)} %bitcast.232), calls=%async_computation.3 | async-start | bytes 4718592 | tf_op jit(solution)/shard_map/all_to_all | solution.py:978
  560.9 210.5 %reduce-scatter.9.cloned.1.call-start = ((), (), s32[]{:S(2)}) async-start(), calls=%async_computation.13 | async-start | bytes 6635520 | tf_op jit(solution)/shard_map/reduce_scatter | solution.py:956
  623.0 14.9 %collective-permute-start.19 = (bf16[4,4,144,1152]{3,2,1,0:T(8,128)(2,1)}, bf16[4,4,144,1152]{3,2,1,0:T(8,128)(2,1)S(1)}, u32[]{:S(2)}, u32[]{:S(2)}) collective-permute-start(bf16[4,4,144,1152]{3,2,1,0:T(8,128)(2,1)} %get-tuple-element.188), channel_id=1, source_target_pairs={{0,4},{4,0},{8,12},{12,8},{16,20},{20,16},{24,28},{28,24},{1,5},{5... | collective-permute-start | bytes 15925256 | tf_op jit(solution)/shard_map/ppermute | solution.py:866
  648.6 27.6 %collective-permute-start.20 = (bf16[2,144,1152]{2,1,0:T(8,128)(2,1)S(1)}, bf16[2,144,1152]{2,1,0:T(8,128)(2,1)S(1)}, u32[]{:S(2)}, u32[]{:S(2)}) collective-permute-start(bf16[2,144,1152]{2,1,0:T(8,128)(2,1)S(1)} %bitcast.242), channel_id=1, source_target_pairs={{0,8},{4,12},{8,0},{12,4},{16,24},{20,28},{24,16},{28,20},{1,9},{5... | collective-permute-start | bytes 1990664 | tf_op jit(solution)/shard_map/ppermute | solution.py:866
  679.2 19.7 %collective-permute-start.21 = (bf16[144,1152]{1,0:T(8,128)(2,1)S(1)}, bf16[144,1152]{1,0:T(8,128)(2,1)S(1)}, u32[]{:S(2)}, u32[]{:S(2)}) collective-permute-start(bf16[144,1152]{1,0:T(8,128)(2,1)S(1)} %slice_bitcast_fusion.13), channel_id=1, source_target_pairs={{0,16},{4,20},{8,24},{12,28},{16,0},{20,4},{24,8},{28,12},{1,17},{... | collective-permute-start | bytes 995336 | tf_op jit(solution)/shard_map/ppermute | solution.py:866
  699.6 33.4 %all-to-all-start.4 = ((bf16[4,256,1152]{2,1,0:T(8,128)(2,1)}), bf16[4,256,1152]{2,1,0:T(8,128)(2,1)S(1)}, u32[]{:S(2)}, u32[]{:S(2)}) async-start(bf16[4,256,1152]{2,1,0:T(8,128)(2,1)} %bitcast.203), calls=%async_computation.5 | async-start | bytes 4718592 | tf_op jit(solution)/shard_map/all_to_all | solution.py:978
  703.3 111.6 %reduce-scatter.11.cloned.1.call-start = ((), (), s32[]{:S(2)}) async-start(), calls=%async_computation.14 | async-start | bytes 6635520 | tf_op jit(solution)/shard_map/reduce_scatter | solution.py:956
  752.7 148.8 %reduce-scatter.13.cloned.1.call-start = ((), (), s32[]{:S(2)}) async-start(), calls=%async_computation.15 | async-start | bytes 6635520 | tf_op jit(solution)/shard_map/reduce_scatter | solution.py:956
  771.3 41.4 %collective-permute-start.24 = (bf16[4,4,144,1152]{3,2,1,0:T(8,128)(2,1)}, bf16[4,4,144,1152]{3,2,1,0:T(8,128)(2,1)}, u32[]{:S(2)}, u32[]{:S(2)}) collective-permute-start(bf16[4,4,144,1152]{3,2,1,0:T(8,128)(2,1)} %get-tuple-element.212), channel_id=1, source_target_pairs={{0,4},{4,0},{8,12},{12,8},{16,20},{20,16},{24,28},{28,24},{1,5},{5... | collective-permute-start | bytes 15925256 | tf_op jit(solution)/shard_map/ppermute | solution.py:866
  772.9 39.0 %collective-permute-start.23 = (bf16[2,144,1152]{2,1,0:T(8,128)(2,1)S(1)}, bf16[2,144,1152]{2,1,0:T(8,128)(2,1)S(1)}, u32[]{:S(2)}, u32[]{:S(2)}) collective-permute-start(bf16[2,144,1152]{2,1,0:T(8,128)(2,1)S(1)} %bitcast.241), channel_id=1, source_target_pairs={{0,8},{4,12},{8,0},{12,4},{16,24},{20,28},{24,16},{28,20},{1,9},{5... | collective-permute-start | bytes 1990664 | tf_op jit(solution)/shard_map/ppermute | solution.py:866
  822.0 142.3 %reduce-scatter.15.cloned.1.call-start = ((), (), s32[]{:S(2)}) async-start(), calls=%async_computation.16 | async-start | bytes 6635520 | tf_op jit(solution)/shard_map/reduce_scatter | solution.py:956
  842.3 14.9 %collective-permute-start.25 = (bf16[4,4,144,1152]{3,2,1,0:T(8,128)(2,1)}, bf16[4,4,144,1152]{3,2,1,0:T(8,128)(2,1)S(1)}, u32[]{:S(2)}, u32[]{:S(2)}) collective-permute-start(bf16[4,4,144,1152]{3,2,1,0:T(8,128)(2,1)} %get-tuple-element.217), channel_id=1, source_target_pairs={{0,4},{4,0},{8,12},{12,8},{16,20},{20,16},{24,28},{28,24},{1,5},{5... | collective-permute-start | bytes 15925256 | tf_op jit(solution)/shard_map/ppermute | solution.py:866
  866.6 165.6 %reduce-scatter.17.cloned.1.call-start = ((), (), s32[]{:S(2)}) async-start(), calls=%async_computation.17 | async-start | bytes 6635520 | tf_op jit(solution)/shard_map/reduce_scatter | solution.py:956
  867.7 30.3 %collective-permute-start.27 = (bf16[144,1152]{1,0:T(8,128)(2,1)S(1)}, bf16[144,1152]{1,0:T(8,128)(2,1)S(1)}, u32[]{:S(2)}, u32[]{:S(2)}) collective-permute-start(bf16[144,1152]{1,0:T(8,128)(2,1)S(1)} %slice_bitcast_fusion.12), channel_id=1, source_target_pairs={{0,16},{4,20},{8,24},{12,28},{16,0},{20,4},{24,8},{28,12},{1,17},{... | collective-permute-start | bytes 995336 | tf_op jit(solution)/shard_map/ppermute | solution.py:866
  870.5 27.6 %collective-permute-start.26 = (bf16[2,144,1152]{2,1,0:T(8,128)(2,1)S(1)}, bf16[2,144,1152]{2,1,0:T(8,128)(2,1)S(1)}, u32[]{:S(2)}, u32[]{:S(2)}) collective-permute-start(bf16[2,144,1152]{2,1,0:T(8,128)(2,1)S(1)} %bitcast.240), channel_id=1, source_target_pairs={{0,8},{4,12},{8,0},{12,4},{16,24},{20,28},{24,16},{28,20},{1,9},{5... | collective-permute-start | bytes 1990664 | tf_op jit(solution)/shard_map/ppermute | solution.py:866
  901.1 24.3 %collective-permute-start.29 = (bf16[144,1152]{1,0:T(8,128)(2,1)}, bf16[144,1152]{1,0:T(8,128)(2,1)S(1)}, u32[]{:S(2)}, u32[]{:S(2)}) collective-permute-start(bf16[144,1152]{1,0:T(8,128)(2,1)} %slice_bitcast_fusion.11), channel_id=1, source_target_pairs={{0,16},{4,20},{8,24},{12,28},{16,0},{20,4},{24,8},{28,12},{1,17},{... | collective-permute-start | bytes 995336 | tf_op jit(solution)/shard_map/ppermute | solution.py:866
  903.0 23.5 %collective-permute-start.28 = (bf16[2,144,1152]{2,1,0:T(8,128)(2,1)S(1)}, bf16[2,144,1152]{2,1,0:T(8,128)(2,1)S(1)}, u32[]{:S(2)}, u32[]{:S(2)}) collective-permute-start(bf16[2,144,1152]{2,1,0:T(8,128)(2,1)S(1)} %bitcast.239), channel_id=1, source_target_pairs={{0,8},{4,12},{8,0},{12,4},{16,24},{20,28},{24,16},{28,20},{1,9},{5... | collective-permute-start | bytes 1990664 | tf_op jit(solution)/shard_map/ppermute | solution.py:866
  927.3 21.6 %collective-permute-start.31 = (bf16[4,4,144,1152]{3,2,1,0:T(8,128)(2,1)}, bf16[4,4,144,1152]{3,2,1,0:T(8,128)(2,1)}, u32[]{:S(2)}, u32[]{:S(2)}) collective-permute-start(bf16[4,4,144,1152]{3,2,1,0:T(8,128)(2,1)} %get-tuple-element.243), channel_id=1, source_target_pairs={{0,4},{4,0},{8,12},{12,8},{16,20},{20,16},{24,28},{28,24},{1,5},{5... | collective-permute-start | bytes 15925256 | tf_op jit(solution)/shard_map/ppermute | solution.py:866
  928.7 19.5 %collective-permute-start.30 = (bf16[144,1152]{1,0:T(8,128)(2,1)S(1)}, bf16[144,1152]{1,0:T(8,128)(2,1)S(1)}, u32[]{:S(2)}, u32[]{:S(2)}) collective-permute-start(bf16[144,1152]{1,0:T(8,128)(2,1)S(1)} %slice_bitcast_fusion.10), channel_id=1, source_target_pairs={{0,16},{4,20},{8,24},{12,28},{16,0},{20,4},{24,8},{28,12},{1,17},{... | collective-permute-start | bytes 995336 | tf_op jit(solution)/shard_map/ppermute | solution.py:866
  966.5 17.1 %collective-permute-start.34 = (bf16[2,144,1152]{2,1,0:T(8,128)(2,1)}, bf16[2,144,1152]{2,1,0:T(8,128)(2,1)}, u32[]{:S(2)}, u32[]{:S(2)}) collective-permute-start(bf16[2,144,1152]{2,1,0:T(8,128)(2,1)} %bitcast.77), channel_id=1, source_target_pairs={{0,8},{4,12},{8,0},{12,4},{16,24},{20,28},{24,16},{28,20},{1,9},{5... | collective-permute-start | bytes 1990664 | tf_op jit(solution)/shard_map/ppermute | solution.py:866
  994.5 27.3 %collective-permute-start.42 = (bf16[144,1152]{1,0:T(8,128)(2,1)}, bf16[144,1152]{1,0:T(8,128)(2,1)}, u32[]{:S(2)}, u32[]{:S(2)}) collective-permute-start(bf16[144,1152]{1,0:T(8,128)(2,1)} %slice_bitcast_fusion.5), channel_id=1, source_target_pairs={{0,16},{4,20},{8,24},{12,28},{16,0},{20,4},{24,8},{28,12},{1,17},{... | collective-permute-start | bytes 995336 | tf_op jit(solution)/shard_map/ppermute | solution.py:866
  995.2 10.9 %collective-permute-start.36 = (f32[25,1152]{1,0:T(8,128)S(1)}, f32[25,1152]{1,0:T(8,128)S(1)}, u32[]{:S(2)}, u32[]{:S(2)}) collective-permute-start(f32[25,1152]{1,0:T(8,128)S(1)} %fusion.22), channel_id=1, source_target_pairs={{0,8},{4,12},{8,0},{12,4},{16,24},{20,28},{24,16},{28,20},{1,9},{5... | collective-permute-start | bytes 345608 | tf_op jit(solution)/shard_map/ppermute | solution.py:902
  1006.8 12.5 %collective-permute-start.37 = (f32[25,1152]{1,0:T(8,128)}, f32[25,1152]{1,0:T(8,128)}, u32[]{:S(2)}, u32[]{:S(2)}) collective-permute-start(f32[25,1152]{1,0:T(8,128)} %add.173), channel_id=1, source_target_pairs={{0,16},{4,20},{8,24},{12,28},{16,0},{20,4},{24,8},{28,12},{1,17},{... | collective-permute-start | bytes 345608 | tf_op jit(solution)/shard_map/ppermute | solution.py:902
  1033.7 14.8 %collective-permute-start.40 = (bf16[2,144,1152]{2,1,0:T(8,128)(2,1)S(1)}, bf16[2,144,1152]{2,1,0:T(8,128)(2,1)S(1)}, u32[]{:S(2)}, u32[]{:S(2)}) collective-permute-start(bf16[2,144,1152]{2,1,0:T(8,128)(2,1)S(1)} %bitcast.243), channel_id=1, source_target_pairs={{0,8},{4,12},{8,0},{12,4},{16,24},{20,28},{24,16},{28,20},{1,9},{5... | collective-permute-start | bytes 1990664 | tf_op jit(solution)/shard_map/ppermute | solution.py:866
  1048.7 14.8 %collective-permute-start.41 = (bf16[144,1152]{1,0:T(8,128)(2,1)S(1)}, bf16[144,1152]{1,0:T(8,128)(2,1)S(1)}, u32[]{:S(2)}, u32[]{:S(2)}) collective-permute-start(bf16[144,1152]{1,0:T(8,128)(2,1)S(1)} %slice_bitcast_fusion.8), channel_id=1, source_target_pairs={{0,16},{4,20},{8,24},{12,28},{16,0},{20,4},{24,8},{28,12},{1,17},{... | collective-permute-start | bytes 995336 | tf_op jit(solution)/shard_map/ppermute | solution.py:866
  (86 other events, 529.4 us)
Sparse Core Ops, SparseCore 0:
  56.4 64.8 all-gather.11
  130.4 60.6 all-gather.13
  208.1 104.7 all-gather.15
  363.9 82.2 all-gather.17
  448.5 61.9 all-gather.19
  527.1 78.3 reduce-scatter.6
  647.3 76.4 reduce-scatter.8
  752.9 62.0 reduce-scatter.10
  822.1 61.9 reduce-scatter.12
  887.0 61.9 reduce-scatter.14
  956.0 62.2 reduce-scatter.16
